TPU v7x, 32 devices: a whole 2x2x4 slice. The times are simulated.
32 devices in a mesh: seq: 4 (over y, core), cp: 8 (over z, x).
Axes of the slice: x: 2, y: 2, z: 4, core: 2. Of those that a mesh axis runs over, the one named last changes fastest.
Arguments:
- query: bfloat16 [4096, 4608], P(('seq', 'cp')), may hold values from -6 to 6
- key_proj: bfloat16 [4096, 4608], P(('seq', 'cp')), may hold values from -6 to 6
- value_proj: bfloat16 [4096, 4608], P(('seq', 'cp')), may hold values from -6 to 6
- featurizer: float32 [3, 7, 288], replicated, may hold values from -2 to 2
- rates: float32 [16, 4608], replicated, may hold values from 6.1035156e-05 to 0.25
- residues: float32 [16, 4608], replicated, may hold values from -5 to 5
- skip: float32 [4608], replicated, may hold values from -4 to 4
Outputs:
- operator_out: bfloat16 [4096, 4608], P(('seq', 'cp'))
All inputs are finite; a program needn't handle non-finite values.
Results may differ from a plain program's by a relative error of at most 0.0064.
Values may be sent and summed in bfloat16 or wider, within the bound.
No kernel may reach another device: no remote copies, remote signals or barrier semaphores. Data moves between devices by JAX's collectives and lax.ppermute only.
A program may use at most 128 MiB of HBM per device.

v0:
```python
import math

import jax
import jax.numpy as jnp
from jax import lax
from jax.sharding import PartitionSpec as P

precise = lax.Precision.HIGHEST


def from_behind(value, axis, steps):
    count = lax.axis_size(axis)
    first, last = (max(0, -steps), min(count, count - steps))
    return lax.ppermute(value, axis, [(source, source + steps) for source in range(first, last)])


def prefix(value, axis, join, neutral):
    count, mine = (lax.axis_size(axis), lax.axis_index(axis))
    pieces = jax.tree.map(lambda part: lax.all_gather(part, axis), value)
    so_far = jax.tree.map(
        lambda part, zero: jnp.full_like(part, 0) + jnp.asarray(zero, part.dtype), value, neutral
    )

    def lap(position, so_far):
        longer = join(so_far, jax.tree.map(lambda part: part[position], pieces))
        return jax.tree.map(lambda new, old: jnp.where(position < mine, new, old), longer, so_far)

    return lax.fori_loop(0, count - 1, lap, so_far)


def mode_terms(decay_rate, residue_part):
    mode_count = decay_rate.shape[1]
    return residue_part * jnp.sqrt(-jnp.expm1(-2.0 * decay_rate) / mode_count)


def short_conv(extended, tap_table, row_count):
    tap_count = tap_table.shape[0]
    running = jnp.zeros((row_count, extended.shape[1]), jnp.float32)
    for lag_index in range(tap_count):
        first_row = tap_count - 1 - lag_index
        running = running + tap_table[lag_index][None, :] * extended[
            first_row : first_row + row_count
        ].astype(jnp.float32)
    return running


def link_blocks(earlier, later):
    return (earlier[0] * later[0], later[0] * earlier[1] + later[1])


def modal_local(signal, decay_rate, mode_coef, block_len):
    row_count, chan_count = signal.shape
    block_count = row_count // block_len
    blocks = signal.reshape(block_count, block_len, chan_count)
    offsets = jnp.arange(block_len, dtype=jnp.float32)
    falloff = jnp.exp(-decay_rate[None, :, :] * offsets[:, None, None])
    kernel = jnp.sum(mode_coef[None] * falloff, axis=2)
    lag_table = (
        jnp.arange(block_len, dtype=jnp.int32)[:, None]
        - jnp.arange(block_len, dtype=jnp.int32)[None, :]
    )
    toeplitz = jnp.where((lag_table >= 0)[:, :, None], kernel[jnp.maximum(lag_table, 0)], 0.0)
    within = jnp.einsum("ijc,bjc->bic", toeplitz, blocks, precision=precise)
    block_state = jnp.einsum("jcr,bjc->bcr", falloff[::-1], blocks, precision=precise)
    factor = jnp.broadcast_to(jnp.exp(-decay_rate * block_len)[None], block_state.shape)
    _, through = lax.associative_scan(link_blocks, (factor, block_state))
    entering = jnp.concatenate([jnp.zeros_like(through[:1]), through[:-1]], axis=0)
    leading = mode_coef[None] * falloff * jnp.exp(-decay_rate)[None]
    carried = jnp.einsum("icr,bcr->bic", leading, entering, precision=precise)
    return ((within + carried).reshape(row_count, chan_count), through[-1])


def modal_all(signal, decay_rate, mode_coef):
    row_count, chan_count = signal.shape
    chan_block = math.gcd(chan_count, 128)
    block_total = chan_count // chan_block
    block_len = min(row_count, 32)
    pieces = signal.reshape(row_count, block_total, chan_block).transpose(1, 0, 2)

    def modal_one_block(packed):
        return modal_local(packed[0], packed[1], packed[2], block_len)

    within, end_state = lax.map(
        modal_one_block,
        (
            pieces,
            decay_rate.reshape(block_total, chan_block, -1),
            mode_coef.reshape(block_total, chan_block, -1),
        ),
    )
    return (
        within.transpose(1, 0, 2).reshape(row_count, chan_count),
        end_state.reshape(chan_count, -1),
    )


def incoming(enter_state, decay_rate, mode_coef, row_count):
    chan_count = enter_state.shape[0]
    chan_block = math.gcd(chan_count, 128)
    block_total = chan_count // chan_block
    block_len = min(row_count, 128)

    def incoming_one_block(packed):
        state_part, rate_part, coef_part = packed
        offsets = jnp.arange(block_len, dtype=jnp.float32)
        leading = coef_part[None] * jnp.exp(-rate_part[None] * (offsets[:, None, None] + 1.0))
        starts = jnp.arange(row_count // block_len, dtype=jnp.float32) * block_len
        entering = jnp.exp(-rate_part[None] * starts[:, None, None]) * state_part[None]
        return jnp.einsum("icr,bcr->bic", leading, entering, precision=precise).reshape(
            row_count, chan_block
        )

    pieces = lax.map(
        incoming_one_block,
        (
            enter_state.reshape(block_total, chan_block, -1),
            decay_rate.reshape(block_total, chan_block, -1),
            mode_coef.reshape(block_total, chan_block, -1),
        ),
    )
    return pieces.transpose(1, 0, 2).reshape(row_count, chan_count)


def local(query, key_proj, value_proj, featurizer, rates, residues, skip):
    row_count, feature_width = query.shape
    tap_count = featurizer.shape[1]
    filters = jnp.repeat(featurizer, feature_width // featurizer.shape[2], axis=2)
    tail_start = row_count - tap_count + 1
    received = from_behind(
        (query[tail_start:], key_proj[tail_start:], value_proj[tail_start:]), ("seq", "cp"), 1
    )
    featured = []
    for member, source in enumerate((query, key_proj, value_proj)):
        extended = jnp.concatenate([received[member], source], axis=0)
        featured.append(short_conv(extended, filters[member], row_count))
    gate_half = featured[0].astype(jnp.bfloat16)
    gate = lax.optimization_barrier(gate_half).astype(jnp.float32)
    signal_half = (featured[1] * featured[2]).astype(jnp.bfloat16)
    rate_all = rates.T
    coef_all = mode_terms(rate_all, residues.T)
    unit = jnp.ones((), jnp.float32)
    nothing = jnp.zeros((), jnp.float32)
    owned = feature_width // lax.axis_size("cp")
    col_start = lax.axis_index("cp") * owned
    decay_rate = lax.dynamic_slice_in_dim(rate_all, col_start, owned, 0)
    mode_coef = lax.dynamic_slice_in_dim(coef_all, col_start, owned, 0)
    skip_part = lax.dynamic_slice_in_dim(skip, col_start, owned, 0)
    grouped = lax.all_to_all(signal_half, "cp", split_axis=1, concat_axis=0, tiled=True)
    group_rows = grouped.shape[0]
    signal = grouped.astype(jnp.float32)
    within, end_state = modal_all(signal, decay_rate, mode_coef)

    def link_groups(earlier, later):
        return (
            earlier[0] + later[0],
            jnp.exp(-decay_rate * (group_rows * later[0][..., None, None])) * earlier[1] + later[1],
        )

    prior = prefix((unit, end_state), "seq", link_groups, (nothing, jnp.zeros_like(end_state)))
    convolved = (
        within + incoming(prior[1], decay_rate, mode_coef, group_rows) + skip_part[None, :] * signal
    )
    conv_half = lax.all_to_all(
        convolved.astype(jnp.bfloat16), "cp", split_axis=0, concat_axis=1, tiled=True
    )
    return (gate * conv_half.astype(jnp.float32)).astype(jnp.bfloat16)


def solution(mesh):
    placed = (
        P(("seq", "cp"), None),
        P(("seq", "cp"), None),
        P(("seq", "cp"), None),
        P(),
        P(),
        P(),
        P(),
    )
    return jax.shard_map(
        local, mesh=mesh, in_specs=placed, out_specs=P(("seq", "cp"), None), check_vma=False
    )
```

profile of v0, /device:TPU:1, one launch (start us, length us, event | category | flops | bytes accessed | tf_op | source)
XLA Modules:
  0.0 366.1 jit_solution(7591305965350173999)
XLA Ops:
  1.6 3.9 %collective-permute-start.1 = (bf16[6,4608]{1,0:T(8,128)(2,1)}, bf16[6,4608]{1,0:T(8,128)(2,1)}, u32[]{:S(2)}, u32[]{:S(2)}) collective-permute-start(bf16[6,4608]{1,0:T(8,128)(2,1)} %slice.389), channel_id=1, source_target_pairs={{0,1},{1,2},{2,3},{3,4},{4,5},{5,6},{6,7},{7,8},{8,9},{9,10},{10,1... | collective-permute-start | bytes 165896 | tf_op jit(solution)/shard_map/ppermute | solution.py:14
  7.1 3.2 collective-permute-start.2
  36.4 23.8 %multiply_convert_fusion = bf16[128,4608]{0,1:T(8,128)(2,1)} fusion(bf16[128,4608]{0,1:T(8,128)(2,1)S(1)} %copy.196, bf16[128,4608]{0,1:T(8,128)(2,1)S(1)} %copy.193, bf16[6,4608]{0,1:T(8,128)(2,1)} %copy.197, bf16[6,4608]{0,1:T(8,128)(2,1)S(1)} %copy.194, f32[4608]{0:T(1024)} %broadcast_in_dim.176, f32[4608]{0:T(1024)} %broadcast_in_dim.174, ...), kind=kLoop, calls=%fused_computation.113 | loop fusion | flops 46006272 | bytes 3907584 | tf_op jit(solution)/shard_map/convert_element_type | solution.py:138
  60.2 6.0 %all-to-all-start = ((bf16[128,8,576]{0,2,1:T(8,128)(2,1)}), bf16[128,8,576]{0,2,1:T(8,128)(2,1)S(1)}, u32[]{:S(2)}, u32[]{:S(2)}) async-start(bf16[128,8,576]{0,2,1:T(8,128)(2,1)} %bitcast.13), calls=%async_computation | async-start | bytes 2359296 | tf_op jit(solution)/shard_map/all_to_all | solution.py:148
  67.6 6.1 %all-reduce.11 = f32[4]{0:T(128)} all-reduce(f32[4]{0:T(128)S(1)} %dynamic-update-slice), channel_id=1, replica_groups=mesh['seq'=4,'cp'=8] {'seq'}, use_global_device_ids=true, to_apply=%add.11 | all-reduce | flops 4 | bytes 32
  78.4 16.5 %all-to-all-done = bf16[128,8,576]{0,2,1:T(8,128)(2,1)S(1)} async-done(((bf16[128,8,576]{0,2,1:T(8,128)(2,1)}), bf16[128,8,576]{0,2,1:T(8,128)(2,1)S(1)}, u32[]{:S(2)}, u32[]{:S(2)}) %all-to-all-start) | async-done | bytes 1179680 | tf_op jit(solution)/shard_map/all_to_all | solution.py:148
  99.8 172.9 %while.38 = (s32[]{:T(128)}, f32[9,1024,64]{1,2,0:T(8,128)}, f32[9,64,16]{1,0,2:T(8,128)}, f32[9,1024,64]{1,2,0:T(8,128)}, f32[9,64,16]{2,1,0:T(8,128)}, /*index...) while((s32[]{:T(128)}, f32[9,1024,64]{1,2,0:T(8,128)}, f32[9,64,16]{1,0,2:T(8,128)}, ...), condition=%wide.region_2.3_spmd, body=%wide.region_0.2_spmd.sunk | while | flops 50917376 | bytes 10017425 | solution.py:83
  107.8 2.8 gather_fusion
  113.4 2.4 fusion.93
  127.0 2.8 gather_fusion
  146.2 2.8 gather_fusion
  165.4 2.8 gather_fusion
  184.7 2.8 gather_fusion
  203.9 2.8 gather_fusion
  223.1 2.8 gather_fusion
  242.3 2.8 gather_fusion
  261.5 2.8 gather_fusion
  273.6 6.4 %all_gather.7 = f32[4,576,16]{1,2,0:T(8,128)S(1)} all-gather(f32[1,576,16]{1,2,0:T(8,128)S(1)} %all_gather_reshape.3), channel_id=1, replica_groups=mesh['seq'=4,'cp'=8] {'seq'}, dimensions={0}, use_global_device_ids=true | all-gather | bytes 184320 | tf_op jit(solution)/shard_map/all_gather | solution.py:19
  280.0 3.9 %while.40 = (s32[]{:T(128)}, f32[576,16]{0,1:T(8,128)S(1)}, s32[]{:T(128)}, f32[4]{0:T(128)S(1)}, f32[576,16]{0,1:T(8,128)S(1)}, /*index=5*/f32[4,576,16]{1,2,0:T(8,128)S(1)}, s32[]{:T(128)}, f32[1]{0:T(128)}, s32[]{:T(128)}) while((s32[]{:T(128)}, f32[576,16]{0,1:T(8,128)S(1)}, s32[]{:T(128)}, f32[4]{0:T(128)S(1)}, ...), condition=%wide.region_4.5_spmd.clone, body=%wide.region_3.4_spmd.clone.sunk | while | flops 46085 | bytes 147601 | solution.py:28
  285.8 30.0 %while.39 = (s32[]{:T(128)}, f32[9,1024,64]{1,2,0:T(8,128)}, f32[9,64,16]{1,0,2:T(8,128)}, f32[9,64,16]{2,1,0:T(8,128)S(1)}, f32[9,64,16]{2,1,0:T(8,128)}, /*index=5*/s32[]{:T(128)}) while((s32[]{:T(128)}, f32[9,1024,64]{1,2,0:T(8,128)}, f32[9,64,16]{1,0,2:T(8,128)}, f32[9,64,16]{2,1,0:T(8,128)S(1)}, f32[9,64,16]{2,1,0:T(8,128)}, ...), condition=%wide.region_6.7_spmd, body=%wide.region_5.6_spmd.sunk | while | flops 12862602 | bytes 1365645 | solution.py:113
  320.8 3.7 %all-to-all-start.1 = ((bf16[8,128,576]{1,2,0:T(8,128)(2,1)}), bf16[8,128,576]{1,2,0:T(8,128)(2,1)S(1)}, u32[]{:S(2)}, u32[]{:S(2)}) async-start(bf16[8,128,576]{1,2,0:T(8,128)(2,1)} %fusion.36), calls=%async_computation.1 | async-start | bytes 2359296 | tf_op jit(solution)/shard_map/all_to_all | solution.py:163
  325.2 3.2 collective-permute-start
  336.9 13.7 %collective-permute-done = bf16[6,4608]{1,0:T(8,128)(2,1)} collective-permute-done((bf16[6,4608]{1,0:T(8,128)(2,1)}, bf16[6,4608]{1,0:T(8,128)(2,1)}, u32[]{:S(2)}, u32[]{:S(2)}) %collective-permute-start) | collective-permute-done | bytes 55328 | tf_op jit(solution)/shard_map/ppermute | solution.py:14
  353.0 11.3 %add_convert_fusion = bf16[128,4608]{0,1:T(8,128)(2,1)S(1)} fusion(bf16[128,4608]{0,1:T(8,128)(2,1)S(1)} %copy.190, bf16[6,4608]{0,1:T(8,128)(2,1)} %copy.191, f32[4608]{0:T(1024)} %broadcast_in_dim.147, f32[4608]{0:T(1024)} %broadcast_in_dim.145, f32[4608]{0:T(1024)} %broadcast_in_dim.143, f32[4608]{0:T(1024)} %broadcast_in_dim.141, ...), kind=kLoop, calls=%fused_computation.114 | loop fusion | flops 23003136 | bytes 2543616 | tf_op jit(solution)/shard_map/convert_element_type | solution.py:136
  (707 shorter events, 234.9 us)
Async XLA Ops:
  0.0 15.1 %copy-start.5 = (bf16[128,4608]{1,0:T(8,128)(2,1)S(1)}, bf16[128,4608]{1,0:T(8,128)(2,1)}, u32[]{:S(2)}) copy-start(bf16[128,4608]{1,0:T(8,128)(2,1)} %param.15) | copy-start | bytes 3538948
  1.6 31.0 %collective-permute-start.1 = (bf16[6,4608]{1,0:T(8,128)(2,1)}, bf16[6,4608]{1,0:T(8,128)(2,1)}, u32[]{:S(2)}, u32[]{:S(2)}) collective-permute-start(bf16[6,4608]{1,0:T(8,128)(2,1)} %slice.389), channel_id=1, source_target_pairs={{0,1},{1,2},{2,3},{3,4},{4,5},{5,6},{6,7},{7,8},{8,9},{9,10},{10,1... | collective-permute-start | bytes 165896 | tf_op jit(solution)/shard_map/ppermute | solution.py:14
  7.1 26.9 %collective-permute-start.2 = (bf16[6,4608]{1,0:T(8,128)(2,1)}, bf16[6,4608]{1,0:T(8,128)(2,1)}, u32[]{:S(2)}, u32[]{:S(2)}) collective-permute-start(bf16[6,4608]{1,0:T(8,128)(2,1)} %slice.410), channel_id=1, source_target_pairs={{0,1},{1,2},{2,3},{3,4},{4,5},{5,6},{6,7},{7,8},{8,9},{9,10},{10,1... | collective-permute-start | bytes 165896 | tf_op jit(solution)/shard_map/ppermute | solution.py:14
  15.8 11.9 %copy-start.12 = (f32[288]{0:T(512)S(1)}, f32[288]{0:T(512)}, u32[]{:S(2)}) copy-start(f32[288]{0:T(512)} %get-tuple-element.309) | copy-start | bytes 3460
  15.8 12.7 %copy-start.11 = (f32[288]{0:T(512)S(1)}, f32[288]{0:T(512)}, u32[]{:S(2)}) copy-start(f32[288]{0:T(512)} %get-tuple-element.308) | copy-start | bytes 3460
  15.9 13.5 %copy-start.9 = (f32[288]{0:T(512)S(1)}, f32[288]{0:T(512)}, u32[]{:S(2)}) copy-start(f32[288]{0:T(512)} %get-tuple-element.307) | copy-start | bytes 3460
  15.9 15.1 %copy-start.10 = (f32[288]{0:T(512)S(1)}, f32[288]{0:T(512)}, u32[]{:S(2)}) copy-start(f32[288]{0:T(512)} %get-tuple-element.324) | copy-start | bytes 3460
  15.9 15.9 %copy-start.8 = (f32[288]{0:T(512)S(1)}, f32[288]{0:T(512)}, u32[]{:S(2)}) copy-start(f32[288]{0:T(512)} %get-tuple-element.325) | copy-start | bytes 3460
  60.2 6.0 %copy-start.14 = (u32[32]{0:T(128)S(1)}, u32[32]{0:T(128)}, u32[]{:S(2)}) copy-start(u32[32]{0:T(128)} %constant.123) | copy-start | bytes 388
  60.2 34.7 %all-to-all-start = ((bf16[128,8,576]{0,2,1:T(8,128)(2,1)}), bf16[128,8,576]{0,2,1:T(8,128)(2,1)S(1)}, u32[]{:S(2)}, u32[]{:S(2)}) async-start(bf16[128,8,576]{0,2,1:T(8,128)(2,1)} %bitcast.13), calls=%async_computation | async-start | bytes 2359296 | tf_op jit(solution)/shard_map/all_to_all | solution.py:148
  94.9 1.5 copy-start
  99.8 180.3 %copy-start.3 = (f32[576,16]{0,1:T(8,128)S(1)}, f32[576,16]{0,1:T(8,128)}, u32[]{:S(2)}) copy-start(f32[576,16]{0,1:T(8,128)} %get-tuple-element.540) | copy-start | bytes 110596
  99.8 180.3 %copy-start.4 = (f32[576,16]{0,1:T(8,128)S(1)}, f32[576,16]{0,1:T(8,128)}, u32[]{:S(2)}) copy-start(f32[576,16]{0,1:T(8,128)} %custom-call) | copy-start | bytes 110596
  99.8 180.3 %copy-start.13 = (f32[4]{0:T(128)S(1)}, f32[4]{0:T(128)}, u32[]{:S(2)}) copy-start(f32[4]{0:T(128)} %all-reduce.11) | copy-start | bytes 52
  285.8 30.0 %copy-start.2 = (f32[9,1024,64]{1,2,0:T(8,128)S(1)}, f32[9,1024,64]{1,2,0:T(8,128)}, u32[]{:S(2)}) copy-start(f32[9,1024,64]{1,2,0:T(8,128)} %get-tuple-element.214) | copy-start | bytes 7077892
  318.0 1.3 copy-start.1
  320.8 3.7 %copy-start.6 = (bf16[128,4608]{1,0:T(8,128)(2,1)S(1)}, bf16[128,4608]{1,0:T(8,128)(2,1)}, u32[]{:S(2)}) copy-start(bf16[128,4608]{1,0:T(8,128)(2,1)} %param.13) | copy-start | bytes 3538948
  320.8 12.8 %copy-start.7 = (f32[288]{0:T(512)S(1)}, f32[288]{0:T(512)}, u32[]{:S(2)}) copy-start(f32[288]{0:T(512)} %get-tuple-element.320) | copy-start | bytes 3460
  320.8 43.5 %all-to-all-start.1 = ((bf16[8,128,576]{1,2,0:T(8,128)(2,1)}), bf16[8,128,576]{1,2,0:T(8,128)(2,1)S(1)}, u32[]{:S(2)}, u32[]{:S(2)}) async-start(bf16[8,128,576]{1,2,0:T(8,128)(2,1)} %fusion.36), calls=%async_computation.1 | async-start | bytes 2359296 | tf_op jit(solution)/shard_map/all_to_all | solution.py:163
  325.2 25.4 %collective-permute-start = (bf16[6,4608]{1,0:T(8,128)(2,1)}, bf16[6,4608]{1,0:T(8,128)(2,1)}, u32[]{:S(2)}, u32[]{:S(2)}) collective-permute-start(bf16[6,4608]{1,0:T(8,128)(2,1)} %slice.368), channel_id=1, source_target_pairs={{0,1},{1,2},{2,3},{3,4},{4,5},{5,6},{6,7},{7,8},{8,9},{9,10},{10,1... | collective-permute-start | bytes 165896 | tf_op jit(solution)/shard_map/ppermute | solution.py:14
where the time goes:
time: 373 us; the launch traced here: 366 us
  local copies, waits for them, and re-layouts  189 us (51%)
  matrix products  61.3 us (16%)
  other arithmetic  47.9 us (13%)
  waiting for transfers between devices  30.2 us (8%)
  starting transfers between devices  20 us (5%)
  blocking collectives  12.5 us (3%)
  loops' own time  5.22 us (1%)
    gather x18, local copies, waits for them, and re-layouts, modal_local(): kernel[jnp.maximum(lag_table, 0)]  33.6 us
    dynamic_update_slice x36, local copies, waits for them, and re-layouts, modal_all(): lax.map(modal_one_block, (pieces, decay_rate.reshape(block_total, chan_bl...  28.3 us
    dynamic_slice x45, local copies, waits for them, and re-layouts, modal_all(): lax.map(modal_one_block, (pieces, decay_rate.reshape(block_total, chan_bl...  26.5 us
    broadcast_in_dim x42, local copies, waits for them, and re-layouts, local(): jnp.repeat(featurizer, feature_width // featurizer.shape[2], axis=2)  24.3 us
    convert_element_type x1, other arithmetic, local(): signal_half = (featured[1] * featured[2]).astype(jnp.bfloat16)  23.8 us
    dot_general x9, matrix products, modal_local(): carried = jnp.einsum('icr,bcr->bic', leading, entering, precision=precise)  21.9 us
    all_to_all x1, waiting for transfers between devices, local(): lax.all_to_all(signal_half, 'cp', split_axis=1, concat_axis=0, tiled=True)  16.5 us
    dot_general x9, matrix products, modal_local(): within = jnp.einsum('ijc,bjc->bic', toeplitz, blocks, precision=precise)  16.3 us
  transfers between devices with their start and end apart: 5, of which 2 were waited for; matrix products, arithmetic and copies ran while one was open for 15% of the time, Pallas kernels for 0%

commit v1 on v0

v1 whole, which is shorter than its diff:
```python
import functools
import math

import jax
import jax.numpy as jnp
from jax import lax
from jax.experimental import pallas as pl
from jax.experimental.pallas import tpu as pltpu
from jax.sharding import PartitionSpec as P

LANES = 128
ROWS = 8
TILES = 4
CHUNK = TILES * LANES
f32 = jnp.float32
bf16 = jnp.bfloat16


def params(limit=32 * 2**20):
    return pltpu.CompilerParams(vmem_limit_bytes=limit)


def put_tile(scratch, group, slot, tile):
    scratch[pl.ds((group * ROWS + slot) * ROWS, ROWS), :] = tile


def get_row(scratch, group, row):
    return scratch[pl.ds(group * ROWS * ROWS + row, ROWS, stride=ROWS), :]


def lanes_of(value, tile):
    return value[:, tile * LANES : (tile + 1) * LANES]


def stage_tokens(source, scratch):
    half_groups = source.shape[0] // ROWS // 2
    for pair in range(half_groups):
        block = source[pl.ds(pair * 2 * ROWS, 2 * ROWS), :].astype(f32)
        for part in range(2):
            group = pair * 2 + part
            half, within = group // half_groups, group % half_groups
            for tile in range(TILES):
                piece = lanes_of(block, tile)[part * ROWS : (part + 1) * ROWS]
                put_tile(scratch, within + 1, half * TILES + tile, piece)
                if half == 0 and within == half_groups - 1:
                    put_tile(scratch, 0, TILES + tile, piece)


def stage_table(table, scratch):
    for group in range(table.shape[0] // ROWS):
        for tile in range(TILES):
            piece = lanes_of(table, tile)[group * ROWS : (group + 1) * ROWS]
            put_tile(scratch, group, tile, piece)
            put_tile(scratch, group, TILES + tile, piece)


def fir(taps, now, past):
    total = taps[0] * now
    for lag in range(1, len(taps)):
        total = total + taps[lag] * past[-lag]
    return total


def rounded(value):
    return value.astype(bf16).astype(f32)


def pack_kernel(key_ref, value_ref, query_ref, out_ref):
    tails = [ref[...].astype(f32)[ROWS:] for ref in (key_ref, value_ref, query_ref)]
    out_ref[...] = jnp.concatenate(tails, axis=0).astype(bf16)


def chunk_taps(feat_ref, members, scratch):
    taps, width = feat_ref.shape[-2:]
    share = CHUNK // width
    group = lax.broadcasted_iota(jnp.int32, (width, CHUNK), 0)
    channel = lax.broadcasted_iota(jnp.int32, (width, CHUNK), 1)
    pick = (group == channel // share).astype(f32).astype(bf16)
    for position, member in enumerate(members):
        rest = feat_ref[member]
        wide = jnp.zeros((taps, CHUNK), f32)
        for _ in range(3):
            term = rest.astype(bf16)
            rest = rest - term.astype(f32)
            wide = wide + jnp.dot(term, pick, preferred_element_type=f32)
        wide = jnp.concatenate([wide, jnp.zeros((ROWS - taps, CHUNK), f32)], axis=0)
        for tile in range(TILES):
            put_tile(scratch, position, tile, lanes_of(wide, tile))
            put_tile(scratch, position, TILES + tile, lanes_of(wide, tile))
    return [
        [get_row(scratch, position, lag) for lag in range(taps)] for position in range(len(members))
    ]


def first_half():
    return lax.broadcasted_iota(jnp.int32, (ROWS, LANES), 0) < TILES


def power(base, exponent):
    result = None
    while exponent:
        if exponent & 1:
            result = base if result is None else result * base
        base = base * base
        exponent >>= 1
    return result


def signal_kernel(key_ref, value_ref, feat_ref, rate_ref, u_ref, decay_ref, tap_ref, state_ref, *scratches):
    key_scr, value_scr, table_scr = scratches
    modes = rate_ref.shape[0]
    steps = u_ref.shape[0]
    top = first_half()
    for ref, scr in ((key_ref, key_scr), (value_ref, value_scr)):
        stage_tokens(ref, scr)
        for tile in range(TILES):
            put_tile(scr, 0, tile, jnp.zeros((ROWS, LANES), f32))
    taps = chunk_taps(feat_ref, (1, 2), table_scr)
    for member in range(2):
        for lag, tap in enumerate(taps[member]):
            tap_ref[member * ROWS + lag] = tap
    reach = len(taps[0]) - 1
    stage_table(rate_ref[...], table_scr)
    for mode in range(modes):
        decay_ref[mode] = jnp.exp(-get_row(table_scr, mode // ROWS, mode % ROWS))
    decay = [decay_ref[mode] for mode in range(modes)]

    def eight(group, carry, opening=False):
        state, past = carry
        state = list(state)
        past = [list(past[0]), list(past[1])]
        for row in range(ROWS):
            parts = []
            for member, scr in enumerate((key_scr, value_scr)):
                now = get_row(scr, group + 1, row)
                parts.append(fir(taps[member], now, past[member]))
                past[member] = past[member][1:] + [now]
            u = rounded(parts[0] * parts[1])
            if opening and row < reach:
                u = jnp.where(top, 0.0, u)
            u_ref[group * ROWS + row] = u
            if opening and row == 0:
                state = [u for _ in range(modes)]
            else:
                state = [decay[mode] * state[mode] + u for mode in range(modes)]
        return tuple(state), (tuple(past[0]), tuple(past[1]))

    past = tuple(
        tuple(get_row(scr, 0, ROWS - reach + row) for row in range(reach)) for scr in (key_scr, value_scr)
    )
    carry = eight(0, ((None,) * modes, past), True)
    state, _ = lax.fori_loop(1, steps // ROWS, eight, carry)
    for mode in range(modes):
        through = power(decay[mode], steps) * state[mode]
        state_ref[mode] = pltpu.roll(through, TILES, 0) + state[mode]


def head_kernel(key_ref, value_ref, halo_ref, decay_ref, tap_ref, state_ref, out_ref, head_ref, *scratches, tokens):
    key_scr, value_scr, total_scr = scratches
    chunks, modes = state_ref.shape[:2]
    pieces, piece_rows = out_ref.shape[:2]
    reach = tap_ref.shape[1] // 2 - 2
    top = first_half()
    for chunk in range(chunks):
        span = slice(chunk * CHUNK, (chunk + 1) * CHUNK)
        halo = halo_ref[:, span].astype(f32)
        for member, (ref, scr) in enumerate(((key_ref, key_scr), (value_ref, value_scr))):
            block = ref[:, span].astype(f32)
            for tile in range(TILES):
                before = lanes_of(halo, tile)[member * ROWS : (member + 1) * ROWS]
                after = lanes_of(block, tile)[:ROWS]
                for slot in (tile, TILES + tile):
                    put_tile(scr, 0, slot, before)
                    put_tile(scr, 1, slot, after)
        taps = [[tap_ref[chunk, member * ROWS + lag] for lag in range(reach + 1)] for member in range(2)]
        signals = []
        for row in range(reach):
            parts = []
            for member, scr in enumerate((key_scr, value_scr)):
                seen = [
                    get_row(scr, 1, row - lag) if lag <= row else get_row(scr, 0, ROWS + row - lag)
                    for lag in range(reach + 1)
                ]
                parts.append(fir(taps[member], seen[0], seen[:0:-1]))
            signals.append(jnp.where(top, rounded(parts[0] * parts[1]), 0.0))
            head_ref[chunk, row] = signals[-1]
        for row in range(reach, ROWS):
            head_ref[chunk, row] = jnp.zeros((ROWS, LANES), f32)
        for mode in range(modes):
            decay = decay_ref[chunk, mode]
            head = signals[0]
            for row in range(1, reach):
                head = decay * head + signals[row]
            head = power(decay, tokens - reach) * head
            total = state_ref[chunk, mode] + pltpu.roll(head, TILES, 0)
            total_scr[mode, chunk * TILES : (chunk + 1) * TILES, :] = total[TILES:]
    split = pieces // modes
    for mode in range(modes):
        for part in range(split):
            rows = total_scr[mode, part * piece_rows : (part + 1) * piece_rows, :]
            out_ref[mode * split + part] = rows.astype(out_ref.dtype)


def local_kernel(u_ref, head_ref, decay_ref, coef_ref, skip_ref, y_ref, lead_ref, mid_ref, table_scr):
    steps = u_ref.shape[0]
    modes = decay_ref.shape[0]
    stage_table(coef_ref[...], table_scr)
    for mode in range(modes):
        lead_ref[mode] = get_row(table_scr, mode // ROWS, mode % ROWS)
    coef = [lead_ref[mode] for mode in range(modes)]
    skip_tile = jnp.broadcast_to(skip_ref[...], (ROWS, CHUNK))
    stage_table(skip_tile, table_scr)
    skip = get_row(table_scr, 0, 0)
    decay = [decay_ref[mode] for mode in range(modes)]

    def eight(group, state, opening=False):
        state = list(state)
        for row in range(ROWS):
            u = u_ref[group * ROWS + row]
            if opening:
                u = u + head_ref[row]
            if opening and row == 0:
                state = [u for _ in range(modes)]
            else:
                state = [decay[mode] * state[mode] + u for mode in range(modes)]
            terms = [skip * u] + [coef[mode] * state[mode] for mode in range(modes)]
            while len(terms) > 1:
                terms = [sum(terms[at + 1 : at + 2], terms[at]) for at in range(0, len(terms), 2)]
            y_ref[group * ROWS + row] = terms[0]
        return tuple(state)

    state = eight(0, (None,) * modes, True)
    state = lax.fori_loop(1, steps // ROWS, eight, state)
    for mode in range(modes):
        mid_ref[mode] = pltpu.roll(state[mode], TILES, 0)


def gate_kernel(query_ref, halo_ref, feat_ref, gate_ref, query_scr, table_scr):
    steps = gate_ref.shape[0]
    stage_tokens(query_ref, query_scr)
    halo = halo_ref[...].astype(f32)[2 * ROWS :]
    for tile in range(TILES):
        put_tile(query_scr, 0, tile, lanes_of(halo, tile))
    (taps,) = chunk_taps(feat_ref, (0,), table_scr)
    reach = len(taps) - 1

    def eight(group, past):
        past = list(past)
        for row in range(ROWS):
            now = get_row(query_scr, group + 1, row)
            gate_ref[group * ROWS + row] = rounded(fir(taps, now, past))
            past = past[1:] + [now]
        return tuple(past)

    past = tuple(get_row(query_scr, 0, ROWS - reach + row) for row in range(reach))
    lax.fori_loop(0, steps // ROWS, eight, past)


def prefix_kernel(piece_ref, rate_ref, out_ref, table_scr, *, tokens, axes):
    devices, piece_rows = piece_ref.shape[:2]
    split = devices // rate_ref.shape[0]
    mine = lax.axis_index(axes)
    mode, part = mine // split, mine % split
    group = pl.multiple_of(mode // ROWS * ROWS, ROWS)
    first = pl.multiple_of(part * piece_rows * LANES, LANES)
    rows = rate_ref[pl.ds(group, ROWS), pl.ds(first, piece_rows * LANES)]
    here = lax.broadcasted_iota(jnp.int32, rows.shape, 0) == mode - group
    rate = jnp.sum(jnp.where(here, rows, 0.0), axis=0, keepdims=True)
    for row in range(piece_rows):
        table_scr[row : row + 1, :] = lanes_of(rate, row)
    through = jnp.exp(-float(tokens) * table_scr[:piece_rows, :])

    def lap(source, entering):
        out_ref[source] = entering.astype(out_ref.dtype)
        return through * entering + piece_ref[source].astype(f32)

    lax.fori_loop(0, devices, lap, jnp.zeros((piece_rows, LANES), f32))


def final_kernel(piece_ref, decay_ref, lead_ref, mid_ref, y_ref, gate_ref, out_ref, total_scr, enter_scr, out_scr):
    chunk = pl.program_id(0)
    modes = decay_ref.shape[0]
    steps = y_ref.shape[0]
    top = first_half()

    @pl.when(chunk == 0)
    def _():
        pieces, piece_rows = piece_ref.shape[:2]
        split = pieces // modes
        for mode in range(modes):
            for part in range(split):
                rows = piece_ref[mode * split + part].astype(f32)
                total_scr[mode, part * piece_rows : (part + 1) * piece_rows, :] = rows
        for at in range(enter_scr.shape[0]):
            for mode in range(modes):
                rows = total_scr[mode, at * TILES : (at + 1) * TILES, :]
                enter_scr[at, mode, :TILES, :] = rows
                enter_scr[at, mode, TILES:, :] = rows

    decay = [decay_ref[mode] for mode in range(modes)]
    state = []
    for mode in range(modes):
        enter = enter_scr[chunk, mode]
        later = power(decay[mode], steps) * enter + mid_ref[mode]
        state.append(lead_ref[mode] * jnp.where(top, enter, later))

    def eight(group, state):
        state = list(state)
        for row in range(ROWS):
            state = [decay[mode] * state[mode] for mode in range(modes)]
            terms = state
            while len(terms) > 1:
                terms = [sum(terms[at + 1 : at + 2], terms[at]) for at in range(0, len(terms), 2)]
            at = group * ROWS + row
            value = gate_ref[at] * rounded(y_ref[at] + terms[0])
            out_scr[pl.ds(group * ROWS * ROWS + row, ROWS, stride=ROWS), :] = value
        return tuple(state)

    lax.fori_loop(0, steps // ROWS, eight, tuple(state))
    half_groups = steps // ROWS
    for pair in range(half_groups):
        for tile in range(TILES):
            parts = []
            for group in (pair * 2, pair * 2 + 1):
                half, within = group // half_groups, group % half_groups
                slot = (within * ROWS + half * TILES + tile) * ROWS
                parts.append(out_scr[pl.ds(slot, ROWS), :])
            out_ref[pl.ds(pair * 2 * ROWS, 2 * ROWS), tile * LANES : (tile + 1) * LANES] = jnp.concatenate(
                parts, axis=0
            ).astype(bf16)


def cost(flops, moved):
    return pl.CostEstimate(flops=int(flops), bytes_accessed=int(moved), transcendentals=0)


def local(query, key_proj, value_proj, featurizer, rates, residues, skip, *, axes):
    tokens, width = query.shape
    modes = rates.shape[0]
    members, taps, groups = featurizer.shape
    devices = math.prod(lax.axis_size(axis) for axis in axes)
    chunks = width // CHUNK
    steps = tokens // 2
    tiles = width // LANES
    split = devices // modes
    even = devices % modes == 0 and tiles % split == 0
    shape = jax.ShapeDtypeStruct
    vmem = pltpu.VMEM
    elements = tokens * width

    def blocks(*dims):
        return pl.BlockSpec((None, *dims), lambda at: (at,) + (0,) * len(dims))

    columns = lambda rows: pl.BlockSpec((rows, CHUNK), lambda at: (0, at))
    whole = lambda *dims: pl.BlockSpec(dims, lambda at: (0,) * len(dims))
    tail = pl.BlockSpec((2 * ROWS, width), lambda at: (tokens // (2 * ROWS) - 1, 0))
    front = pl.BlockSpec((2 * ROWS, width), lambda at: (0, 0))
    vectors = lambda count: shape((chunks, count, ROWS, LANES), f32)

    feat = featurizer.reshape(members, taps, chunks, groups // chunks).transpose(2, 0, 1, 3)
    feat_block = blocks(members, taps, groups // chunks)

    packed = pl.pallas_call(
        pack_kernel,
        grid=(1,),
        in_specs=[tail] * 3,
        out_specs=whole(3 * ROWS, width),
        out_shape=shape((3 * ROWS, width), bf16),
        compiler_params=params(),
        name="pack",
    )(key_proj, value_proj, query)
    halo = lax.ppermute(packed, axes, [(at, at + 1) for at in range(devices - 1)])

    stage = vmem(((steps // ROWS + 1) * ROWS * ROWS, LANES), f32)
    table = vmem((2 * ROWS * ROWS, LANES), f32)
    u, decay, wide_taps, state = pl.pallas_call(
        signal_kernel,
        grid=(chunks,),
        in_specs=[columns(tokens)] * 2 + [feat_block, columns(modes)],
        out_specs=[blocks(n, ROWS, LANES) for n in (steps, modes, 2 * ROWS, modes)],
        out_shape=[vectors(n) for n in (steps, modes, 2 * ROWS, modes)],
        scratch_shapes=[stage, stage, table],
        compiler_params=params(),
        cost_estimate=cost(60 * elements, 10 * elements),
        name="signal",
    )(key_proj, value_proj, feat, rates)

    pieces = (modes * split, tiles // split, LANES) if even else (modes, tiles, LANES)
    flat = (modes, width)
    small = vmem((2 * ROWS * ROWS, LANES), f32)
    left, head = pl.pallas_call(
        functools.partial(head_kernel, tokens=tokens),
        grid=(1,),
        in_specs=[front, front, whole(3 * ROWS, width)]
        + [whole(chunks, n, ROWS, LANES) for n in (modes, 2 * ROWS, modes)],
        out_specs=[whole(*pieces), whole(chunks, ROWS, ROWS, LANES)],
        out_shape=[shape(pieces, bf16), vectors(ROWS)],
        scratch_shapes=[small, small, vmem((modes, tiles, LANES), f32)],
        compiler_params=params(),
        name="head",
    )(key_proj, value_proj, halo, decay, wide_taps, state)

    def swap(value):
        return lax.all_to_all(value, axes, split_axis=0, concat_axis=0, tiled=True)

    if even:
        theirs = swap(left)
        entering = pl.pallas_call(
            functools.partial(prefix_kernel, tokens=tokens, axes=axes),
            grid=(1,),
            in_specs=[whole(*pieces), whole(modes, width)],
            out_specs=whole(*pieces),
            out_shape=shape(pieces, bf16),
            scratch_shapes=[vmem((-(-pieces[1] // ROWS) * ROWS, LANES), f32)],
            compiler_params=params(),
            name="prefix",
        )(theirs, rates)
        entered = swap(entering)
    else:
        share = modes * width // devices
        theirs = swap(left.reshape(devices, share))
        mine = lax.axis_index(axes)
        through = jnp.exp(-float(tokens) * lax.dynamic_slice_in_dim(rates.reshape(-1), mine * share, share))
        _, entering = lax.scan(
            lambda so_far, piece: (through * so_far + piece.astype(f32), so_far.astype(bf16)),
            jnp.zeros((share,), f32),
            theirs,
        )
        entered = swap(entering).reshape(pieces)

    coef = residues * jnp.sqrt(-jnp.expm1(-2.0 * rates) / modes)
    y, lead, mid = pl.pallas_call(
        local_kernel,
        grid=(chunks,),
        in_specs=[blocks(n, ROWS, LANES) for n in (steps, ROWS, modes)] + [columns(modes), columns(1)],
        out_specs=[blocks(n, ROWS, LANES) for n in (steps, modes, modes)],
        out_shape=[vectors(n) for n in (steps, modes, modes)],
        scratch_shapes=[table],
        compiler_params=params(),
        cost_estimate=cost(66 * elements, 8 * elements),
        name="within",
    )(u, head, decay, coef, skip[None, :])

    gate = pl.pallas_call(
        gate_kernel,
        grid=(chunks,),
        in_specs=[columns(tokens), columns(3 * ROWS), feat_block],
        out_specs=blocks(steps, ROWS, LANES),
        out_shape=vectors(steps),
        scratch_shapes=[stage, table],
        compiler_params=params(),
        cost_estimate=cost(14 * elements, 6 * elements),
        name="gate",
    )(query, halo, feat)

    return pl.pallas_call(
        final_kernel,
        grid=(chunks,),
        in_specs=[whole(*pieces)] + [blocks(n, ROWS, LANES) for n in (modes, modes, modes, steps, steps)],
        out_specs=columns(tokens),
        out_shape=shape((tokens, width), bf16),
        scratch_shapes=[
            vmem((modes, tiles, LANES), f32),
            vmem((chunks, modes, ROWS, LANES), f32),
            vmem((steps * ROWS, LANES), f32),
        ],
        compiler_params=params(),
        cost_estimate=cost(40 * elements, 10 * elements),
        name="final",
    )(entered, decay, lead, mid, y, gate)


def solution(mesh):
    axes = tuple(mesh.axis_names)
    placed = (P(axes, None),) * 3 + (P(),) * 4
    return jax.shard_map(
        functools.partial(local, axes=axes),
        mesh=mesh,
        in_specs=placed,
        out_specs=P(axes, None),
        check_vma=False,
    )
```

time: 373 us -> 63.6 us (0.17); the launches traced: 366 us -> 62.5 us
  local copies, waits for them, and re-layouts: 189 us -> 12.8 us
  matrix products: 61.3 us -> 0 us
  other arithmetic: 47.9 us -> 0.18 us
  waiting for transfers between devices: 30.2 us -> 1.47 us
  Pallas kernels: 0 us -> 27.9 us
  starting transfers between devices: 20 us -> 7.22 us
  loops' own time: 5.22 us -> 0 us
    dot_general x36 -> x0, matrix products: 61.3 us -> none  [the longest x9 21.9 us: modal_local(): carried = jnp.einsum('icr,bcr->bic', leading, entering, precision=precise)]
    convert_element_type x4 -> x0, other arithmetic: 37.1 us -> none  [the longest x1 23.8 us: local(): signal_half = (featured[1] * featured[2]).astype(jnp.bfloat16)]
    gather x18 -> x0, local copies, waits for them, and re-layouts: 33.6 us -> none  [modal_local(): kernel[jnp.maximum(lag_table, 0)]]
    dynamic_slice x50 -> x0, local copies, waits for them, and re-layouts: 30 us -> none  [the longest x45 26.5 us: modal_all(): lax.map(modal_one_block, (pieces, decay_rate.reshape(block_total, chan_bl...]
    dynamic_update_slice x36 -> x0, local copies, waits for them, and re-layouts: 28.3 us -> none  [modal_all(): lax.map(modal_one_block, (pieces, decay_rate.reshape(block_total, chan_bl...]
    pallas_call x0 -> x7, Pallas kernels: none -> 27.9 us  [the longest x1 7.72 us: local(): pl.pallas_call(signal_kernel, grid=(chunks,), in_specs=[columns(tokens)]...]
    broadcast_in_dim x51 -> x1, local copies, waits for them, and re-layouts: 24.7 us -> 0.01 us  [local(): skip[None, :]]
    all_to_all x2 -> x1, waiting for transfers between devices: 16.5 us -> 0.01 us  [swap(): return lax.all_to_all(value, axes, split_axis=0, concat_axis=0, tiled=True)]
  transfers between devices with their start and end apart: 5 -> 2, of which waited for: 2 -> 1; matrix products, arithmetic and copies ran while one was open for 15% -> 1% of each run, Pallas kernels for 0% -> 31%
where the time goes in v1:
time: 63.6 us; the launch traced here: 62.5 us
  Pallas kernels  27.9 us (44%)
  local copies, waits for them, and re-layouts  12.8 us (20%)
  blocking collectives  12.7 us (20%)
  starting transfers between devices  7.22 us (11%)
  waiting for transfers between devices  1.47 us (2%)
    all_to_all x1, blocking collectives, swap(): return lax.all_to_all(value, axes, split_axis=0, concat_axis=0, tiled=True)  12.7 us
    unnamed x40, local copies, waits for them, and re-layouts  12.7 us
    pallas_call x1, Pallas kernels, local(): pl.pallas_call(signal_kernel, grid=(chunks,), in_specs=[columns(tokens)]...  7.72 us
    pallas_call x1, Pallas kernels, local(): pl.pallas_call(local_kernel, grid=(chunks,), in_specs=[blocks(n, ROWS, LA...  5.77 us
    pallas_call x1, Pallas kernels, local(): pl.pallas_call(gate_kernel, grid=(chunks,), in_specs=[columns(tokens), co...  5.74 us
    pallas_call x1, Pallas kernels, local(): pl.pallas_call(final_kernel, grid=(chunks,), in_specs=[whole(*pieces)] +...  5.37 us
    ppermute x1, starting transfers between devices, local(): lax.ppermute(packed, axes, [(at, at + 1) for at in range(devices - 1)])  4.07 us
    all_to_all x1, starting transfers between devices, swap(): return lax.all_to_all(value, axes, split_axis=0, concat_axis=0, tiled=True)  3.15 us
  transfers between devices with their start and end apart: 2, of which 1 were waited for; matrix products, arithmetic and copies ran while one was open for 1% of the time, Pallas kernels for 31%

profile of v1, /device:TPU:1, one launch (start us, length us, event | category | flops | bytes accessed | tf_op | source)
XLA Modules:
  0.0 62.5 jit_solution(6517805208291486894)
XLA Ops:
  0.0 1.3 %copy-done = bf16[128,4608]{1,0:T(8,128)(2,1)S(1)} copy-done((bf16[128,4608]{1,0:T(8,128)(2,1)S(1)}, bf16[128,4608]{1,0:T(8,128)(2,1)}, u32[]{:S(2)}) %copy-start) | copy-done | bytes 1179672
  1.3 1.3 %copy-done.2 = bf16[128,4608]{1,0:T(8,128)(2,1)S(1)} copy-done((bf16[128,4608]{1,0:T(8,128)(2,1)S(1)}, bf16[128,4608]{1,0:T(8,128)(2,1)}, u32[]{:S(2)}) %copy-start.2) | copy-done | bytes 1179672
  2.5 1.3 %copy-done.4 = bf16[128,4608]{1,0:T(8,128)(2,1)S(1)} copy-done((bf16[128,4608]{1,0:T(8,128)(2,1)S(1)}, bf16[128,4608]{1,0:T(8,128)(2,1)}, u32[]{:S(2)}) %copy-start.4) | copy-done | bytes 1179672
  3.8 0.7 %pack.1 = bf16[24,4608]{1,0:T(8,128)(2,1)} custom-call(bf16[128,4608]{1,0:T(8,128)(2,1)S(1)} %copy-done, bf16[128,4608]{1,0:T(8,128)(2,1)S(1)} %copy-done.2, bf16[128,4608]{1,0:T(8,128)(2,1)S(1)} %copy-done.4), custom_call_target="tpu_custom_call" | custom-call | tf_op jit(solution)/shard_map/pack/pallas_call | solution.py:363
  4.5 4.1 %collective-permute-start = (bf16[24,4608]{1,0:T(8,128)(2,1)}, bf16[24,4608]{1,0:T(8,128)(2,1)}, u32[]{:S(2)}, u32[]{:S(2)}) collective-permute-start(bf16[24,4608]{1,0:T(8,128)(2,1)} %pack.1), channel_id=1, source_target_pairs={{0,1},{1,2},{2,3},{3,4},{4,5},{5,6},{6,7},{7,8},{8,9},{9,10},{10,1... | collective-permute-start | bytes 663560 | tf_op jit(solution)/shard_map/ppermute | solution.py:372
  8.6 0.1 reshape.3
  8.8 7.7 %signal.1 = (f32[9,64,8,128]{3,2,1,0:T(8,128)S(1)}, f32[9,16,8,128]{3,2,1,0:T(8,128)S(1)}, f32[9,16,8,128]{3,2,1,0:T(8,128)S(1)}, f32[9,16,8,128]{3,2,1,0:T(8,128)S(1)}) custom-call(bf16[128,4608]{1,0:T(8,128)(2,1)S(1)} %copy-done.1, bf16[128,4608]{1,0:T(8,128)(2,1)S(1)} %copy-done.3, f32[9,3,7,32]{3,2,1,0:T(8,128)S(1)} %bitcast.3, f32[16,4608]{1,0:T(8,128)S(1)} %copy-done.6), custom_call_target="tpu_custom_call" | custom-call | flops 35389440 | bytes 5898240 | tf_op jit(solution)/shard_map/signal/pallas_call | solution.py:376
  16.5 1.5 %collective-permute-done.halo_ref = bf16[24,4608]{1,0:T(8,128)(2,1)} collective-permute-done((bf16[24,4608]{1,0:T(8,128)(2,1)}, bf16[24,4608]{1,0:T(8,128)(2,1)}, u32[]{:S(2)}, u32[]{:S(2)}) %collective-permute-start) | collective-permute-done | bytes 221216 | tf_op jit(solution)/shard_map/ppermute | solution.py:372
  18.0 1.7 %head.1 = (bf16[32,18,128]{2,1,0:T(8,128)(2,1)S(1)}, f32[9,8,8,128]{3,2,1,0:T(8,128)S(1)}) custom-call(bf16[128,4608]{1,0:T(8,128)(2,1)S(1)} %copy-done.1, bf16[128,4608]{1,0:T(8,128)(2,1)S(1)} %copy-done.3, bf16[24,4608]{1,0:T(8,128)(2,1)} %collective-permute-done.halo_ref, f32[9,16,8,128]{3,2,1,0:T(8,128)S(1)} %get-tuple-element.14.decay_ref, ...), custom_call_target="tpu_custom_call" | custom-call | tf_op jit(solution)/shard_map/head/pallas_call | solution.py:391
  19.8 0.7 %copy-done.15 = f32[9,8,8,128]{3,2,1,0:T(8,128)} copy-done((f32[9,8,8,128]{3,2,1,0:T(8,128)}, f32[9,8,8,128]{3,2,1,0:T(8,128)S(1)}, u32[]{:S(2)}) %copy-start.15) | copy-done | bytes 294936
  20.5 12.7 %all_to_all.10.piece_ref = bf16[32,18,128]{2,1,0:T(8,128)(2,1)S(1)} all-to-all(bf16[32,18,128]{2,1,0:T(8,128)(2,1)S(1)} %get-tuple-element.17), channel_id=1, replica_groups=mesh['seq'=4,'cp'=8] {'seq','cp'}, dimensions={0} | all-to-all | bytes 294912 | tf_op jit(solution)/shard_map/all_to_all | solution.py:404
  33.2 0.9 %prefix.1 = bf16[32,18,128]{2,1,0:T(8,128)(2,1)} custom-call(bf16[32,18,128]{2,1,0:T(8,128)(2,1)S(1)} %all_to_all.10.piece_ref, f32[16,4608]{1,0:T(8,128)S(1)} %copy-done.6), custom_call_target="tpu_custom_call" | custom-call | tf_op jit(solution)/shard_map/prefix/pallas_call | solution.py:408
  34.0 3.1 %all-to-all-start.1 = ((bf16[32,18,128]{2,1,0:T(8,128)(2,1)}), bf16[32,18,128]{2,1,0:T(8,128)(2,1)S(1)}, u32[]{:S(2)}, u32[]{:S(2)}) async-start(bf16[32,18,128]{2,1,0:T(8,128)(2,1)} %prefix.1), calls=%async_computation.1 | async-start | bytes 393216 | tf_op jit(solution)/shard_map/all_to_all | solution.py:404
  37.2 0.2 sqrt_multiply_fusion.coef_ref
  37.5 1.3 %copy-done.5 = bf16[128,4608]{1,0:T(8,128)(2,1)S(1)} copy-done((bf16[128,4608]{1,0:T(8,128)(2,1)S(1)}, bf16[128,4608]{1,0:T(8,128)(2,1)}, u32[]{:S(2)}) %copy-start.5) | copy-done | bytes 1179672
  38.7 5.7 %gate.1.gate_ref = f32[9,64,8,128]{3,2,1,0:T(8,128)S(1)} custom-call(bf16[128,4608]{1,0:T(8,128)(2,1)S(1)} %copy-done.5, bf16[24,4608]{1,0:T(8,128)(2,1)} %collective-permute-done.halo_ref, f32[9,3,7,32]{3,2,1,0:T(8,128)S(1)} %bitcast.4), custom_call_target="tpu_custom_call" | custom-call | flops 8257536 | bytes 3538944 | tf_op jit(solution)/shard_map/gate/pallas_call | solution.py:444
  44.5 5.8 %within.1 = (f32[9,64,8,128]{3,2,1,0:T(8,128)S(1)}, f32[9,16,8,128]{3,2,1,0:T(8,128)S(1)}, f32[9,16,8,128]{3,2,1,0:T(8,128)S(1)}) custom-call(f32[9,64,8,128]{3,2,1,0:T(8,128)S(1)} %copy-done.8, f32[9,8,8,128]{3,2,1,0:T(8,128)S(1)} %copy-done.16, f32[9,16,8,128]{3,2,1,0:T(8,128)S(1)} %get-tuple-element.14.decay_ref, ...), custom_call_target="tpu_custom_call" | custom-call | flops 38928384 | bytes 4718592 | tf_op jit(solution)/shard_map/within/pallas_call | solution.py:432
  50.3 1.4 %copy-done.9 = f32[9,64,8,128]{3,2,1,0:T(8,128)} copy-done((f32[9,64,8,128]{3,2,1,0:T(8,128)}, f32[9,64,8,128]{3,2,1,0:T(8,128)S(1)}, u32[]{:S(2)}) %copy-start.9) | copy-done | bytes 2359320
  51.7 0.8 %copy-done.11 = f32[9,16,8,128]{3,2,1,0:T(8,128)} copy-done((f32[9,16,8,128]{3,2,1,0:T(8,128)}, f32[9,16,8,128]{3,2,1,0:T(8,128)S(1)}, u32[]{:S(2)}) %copy-start.11) | copy-done | bytes 589848
  52.5 0.8 %copy-done.13 = f32[9,16,8,128]{3,2,1,0:T(8,128)} copy-done((f32[9,16,8,128]{3,2,1,0:T(8,128)}, f32[9,16,8,128]{3,2,1,0:T(8,128)S(1)}, u32[]{:S(2)}) %copy-start.13) | copy-done | bytes 589848
  53.3 1.7 %copy-done.10 = f32[9,64,8,128]{3,2,1,0:T(8,128)S(1)} copy-done((f32[9,64,8,128]{3,2,1,0:T(8,128)S(1)}, f32[9,64,8,128]{3,2,1,0:T(8,128)}, u32[]{:S(2)}) %copy-start.10) | copy-done | bytes 2359320
  55.0 1.1 %copy-done.12 = f32[9,16,8,128]{3,2,1,0:T(8,128)S(1)} copy-done((f32[9,16,8,128]{3,2,1,0:T(8,128)S(1)}, f32[9,16,8,128]{3,2,1,0:T(8,128)}, u32[]{:S(2)}) %copy-start.12) | copy-done | bytes 589848
  56.1 1.1 %copy-done.14 = f32[9,16,8,128]{3,2,1,0:T(8,128)S(1)} copy-done((f32[9,16,8,128]{3,2,1,0:T(8,128)S(1)}, f32[9,16,8,128]{3,2,1,0:T(8,128)}, u32[]{:S(2)}) %copy-start.14) | copy-done | bytes 589848
  57.1 5.4 %final.1 = bf16[128,4608]{1,0:T(8,128)(2,1)} custom-call(bf16[32,18,128]{2,1,0:T(8,128)(2,1)S(1)} %all-to-all-done.1.piece_ref, f32[9,16,8,128]{3,2,1,0:T(8,128)S(1)} %get-tuple-element.14.decay_ref, f32[9,16,8,128]{3,2,1,0:T(8,128)S(1)} %copy-done.12, f32[9,16,8,128]{3,2,1,0:T(8,128)S(1)} %copy-done.14, f32[9,64,8,128]{3,2,1,0:T(8,128)S(1)} %copy-done.10, ...), custom_call_target="tpu_custom_call" | custom-call | flops 23592960 | bytes 5898240 | tf_op jit(solution)/shard_map/final/pallas_call | solution.py:456
  (32 shorter events, 0.1 us)
Async XLA Ops:
  0.0 1.3 %copy-start = (bf16[128,4608]{1,0:T(8,128)(2,1)S(1)}, bf16[128,4608]{1,0:T(8,128)(2,1)}, u32[]{:S(2)}) copy-start(bf16[128,4608]{1,0:T(8,128)(2,1)} %key_ref.5) | copy-start | bytes 3538948
  1.3 1.3 %copy-start.2 = (bf16[128,4608]{1,0:T(8,128)(2,1)S(1)}, bf16[128,4608]{1,0:T(8,128)(2,1)}, u32[]{:S(2)}) copy-start(bf16[128,4608]{1,0:T(8,128)(2,1)} %value_ref.5) | copy-start | bytes 3538948
  2.5 1.3 %copy-start.4 = (bf16[128,4608]{1,0:T(8,128)(2,1)S(1)}, bf16[128,4608]{1,0:T(8,128)(2,1)}, u32[]{:S(2)}) copy-start(bf16[128,4608]{1,0:T(8,128)(2,1)} %query_ref.3) | copy-start | bytes 3538948
  3.8 4.8 %copy-start.18 = (f32[3,7,288]{2,1,0:T(8,128)S(1)}, f32[3,7,288]{2,1,0:T(8,128)}, u32[]{:S(2)}) copy-start(f32[3,7,288]{2,1,0:T(8,128)} %param.10) | copy-start | bytes 72580
  3.8 4.9 %copy-start.1 = (bf16[128,4608]{1,0:T(8,128)(2,1)S(1)}, bf16[128,4608]{1,0:T(8,128)(2,1)}, u32[]{:S(2)}) copy-start(bf16[128,4608]{1,0:T(8,128)(2,1)} %key_ref.5) | copy-start | bytes 3538948
  3.8 4.9 %copy-start.3 = (bf16[128,4608]{1,0:T(8,128)(2,1)S(1)}, bf16[128,4608]{1,0:T(8,128)(2,1)}, u32[]{:S(2)}) copy-start(bf16[128,4608]{1,0:T(8,128)(2,1)} %value_ref.5) | copy-start | bytes 3538948
  3.8 5.0 %copy-start.6 = (f32[16,4608]{1,0:T(8,128)S(1)}, f32[16,4608]{1,0:T(8,128)}, u32[]{:S(2)}) copy-start(f32[16,4608]{1,0:T(8,128)} %rate_ref.3) | copy-start | bytes 884740
  4.5 13.5 %collective-permute-start = (bf16[24,4608]{1,0:T(8,128)(2,1)}, bf16[24,4608]{1,0:T(8,128)(2,1)}, u32[]{:S(2)}, u32[]{:S(2)}) collective-permute-start(bf16[24,4608]{1,0:T(8,128)(2,1)} %pack.1), channel_id=1, source_target_pairs={{0,1},{1,2},{2,3},{3,4},{4,5},{5,6},{6,7},{7,8},{8,9},{9,10},{10,1... | collective-permute-start | bytes 663560 | tf_op jit(solution)/shard_map/ppermute | solution.py:372
  16.5 3.2 %copy-start.7 = (f32[9,64,8,128]{3,2,1,0:T(8,128)}, f32[9,64,8,128]{3,2,1,0:T(8,128)S(1)}, u32[]{:S(2)}) copy-start(f32[9,64,8,128]{3,2,1,0:T(8,128)S(1)} %get-tuple-element.18.u_ref) | copy-start | bytes 7077892
  19.8 0.7 %copy-start.15 = (f32[9,8,8,128]{3,2,1,0:T(8,128)}, f32[9,8,8,128]{3,2,1,0:T(8,128)S(1)}, u32[]{:S(2)}) copy-start(f32[9,8,8,128]{3,2,1,0:T(8,128)S(1)} %get-tuple-element.19.head_ref) | copy-start | bytes 884740
  20.5 16.7 %copy-start.17 = (f32[16,4608]{1,0:T(8,128)S(1)}, f32[16,4608]{1,0:T(8,128)}, u32[]{:S(2)}) copy-start(f32[16,4608]{1,0:T(8,128)} %param.12) | copy-start | bytes 884740
  20.5 16.9 %copy-start.19 = (f32[4608]{0:T(1024)S(1)}, f32[4608]{0:T(1024)}, u32[]{:S(2)}) copy-start(f32[4608]{0:T(1024)} %param.13) | copy-start | bytes 55300
  34.0 19.3 %all-to-all-start.1 = ((bf16[32,18,128]{2,1,0:T(8,128)(2,1)}), bf16[32,18,128]{2,1,0:T(8,128)(2,1)S(1)}, u32[]{:S(2)}, u32[]{:S(2)}) async-start(bf16[32,18,128]{2,1,0:T(8,128)(2,1)} %prefix.1), calls=%async_computation.1 | async-start | bytes 393216 | tf_op jit(solution)/shard_map/all_to_all | solution.py:404
  37.4 1.3 %copy-start.5 = (bf16[128,4608]{1,0:T(8,128)(2,1)S(1)}, bf16[128,4608]{1,0:T(8,128)(2,1)}, u32[]{:S(2)}) copy-start(bf16[128,4608]{1,0:T(8,128)(2,1)} %query_ref.3) | copy-start | bytes 3538948
  38.7 5.8 %copy-start.8 = (f32[9,64,8,128]{3,2,1,0:T(8,128)S(1)}, f32[9,64,8,128]{3,2,1,0:T(8,128)}, u32[]{:S(2)}) copy-start(f32[9,64,8,128]{3,2,1,0:T(8,128)} %copy-done.7) | copy-start | bytes 7077892
  38.7 5.8 %copy-start.16 = (f32[9,8,8,128]{3,2,1,0:T(8,128)S(1)}, f32[9,8,8,128]{3,2,1,0:T(8,128)}, u32[]{:S(2)}) copy-start(f32[9,8,8,128]{3,2,1,0:T(8,128)} %copy-done.15) | copy-start | bytes 884740
  50.3 1.4 %copy-start.9 = (f32[9,64,8,128]{3,2,1,0:T(8,128)}, f32[9,64,8,128]{3,2,1,0:T(8,128)S(1)}, u32[]{:S(2)}) copy-start(f32[9,64,8,128]{3,2,1,0:T(8,128)S(1)} %get-tuple-element.22.y_ref) | copy-start | bytes 7077892
  51.7 0.8 %copy-start.11 = (f32[9,16,8,128]{3,2,1,0:T(8,128)}, f32[9,16,8,128]{3,2,1,0:T(8,128)S(1)}, u32[]{:S(2)}) copy-start(f32[9,16,8,128]{3,2,1,0:T(8,128)S(1)} %get-tuple-element.20.lead_ref) | copy-start | bytes 1769476
  52.5 0.8 %copy-start.13 = (f32[9,16,8,128]{3,2,1,0:T(8,128)}, f32[9,16,8,128]{3,2,1,0:T(8,128)S(1)}, u32[]{:S(2)}) copy-start(f32[9,16,8,128]{3,2,1,0:T(8,128)S(1)} %get-tuple-element.21.mid_ref) | copy-start | bytes 1769476
  53.3 1.7 %copy-start.10 = (f32[9,64,8,128]{3,2,1,0:T(8,128)S(1)}, f32[9,64,8,128]{3,2,1,0:T(8,128)}, u32[]{:S(2)}) copy-start(f32[9,64,8,128]{3,2,1,0:T(8,128)} %copy-done.9) | copy-start | bytes 7077892
  55.0 1.1 %copy-start.12 = (f32[9,16,8,128]{3,2,1,0:T(8,128)S(1)}, f32[9,16,8,128]{3,2,1,0:T(8,128)}, u32[]{:S(2)}) copy-start(f32[9,16,8,128]{3,2,1,0:T(8,128)} %copy-done.11) | copy-start | bytes 1769476
  56.1 1.1 %copy-start.14 = (f32[9,16,8,128]{3,2,1,0:T(8,128)S(1)}, f32[9,16,8,128]{3,2,1,0:T(8,128)}, u32[]{:S(2)}) copy-start(f32[9,16,8,128]{3,2,1,0:T(8,128)} %copy-done.13) | copy-start | bytes 1769476

commit v2 on v1

--- a/solution.py
+++ b/solution.py
@@ -16,7 +16,7 @@
 bf16 = jnp.bfloat16
 
 
-def params(limit=32 * 2**20):
+def params(limit=56 * 2**20):
     return pltpu.CompilerParams(vmem_limit_bytes=limit)
 
 
@@ -70,26 +70,18 @@
     out_ref[...] = jnp.concatenate(tails, axis=0).astype(bf16)
 
 
-def chunk_taps(feat_ref, members, scratch):
-    taps, width = feat_ref.shape[-2:]
-    share = CHUNK // width
-    group = lax.broadcasted_iota(jnp.int32, (width, CHUNK), 0)
-    channel = lax.broadcasted_iota(jnp.int32, (width, CHUNK), 1)
-    pick = (group == channel // share).astype(f32).astype(bf16)
-    for position, member in enumerate(members):
-        rest = feat_ref[member]
-        wide = jnp.zeros((taps, CHUNK), f32)
-        for _ in range(3):
-            term = rest.astype(bf16)
-            rest = rest - term.astype(f32)
-            wide = wide + jnp.dot(term, pick, preferred_element_type=f32)
-        wide = jnp.concatenate([wide, jnp.zeros((ROWS - taps, CHUNK), f32)], axis=0)
-        for tile in range(TILES):
-            put_tile(scratch, position, tile, lanes_of(wide, tile))
-            put_tile(scratch, position, TILES + tile, lanes_of(wide, tile))
-    return [
-        [get_row(scratch, position, lag) for lag in range(taps)] for position in range(len(members))
-    ]
+def widened(group_taps):
+    count = group_taps.shape[-1]
+    group = lax.broadcasted_iota(jnp.int32, (count, LANES), 0)
+    lane = lax.broadcasted_iota(jnp.int32, (count, LANES), 1)
+    pick = (group == lane // (LANES // count)).astype(f32).astype(bf16)
+    wide, rest = None, group_taps
+    for _ in range(3):
+        term = rest.astype(bf16)
+        rest = rest - term.astype(f32)
+        part = jnp.dot(term, pick, preferred_element_type=f32)
+        wide = part if wide is None else wide + part
+    return [wide[at : at + ROWS] for at in range(0, wide.shape[0], ROWS)]
 
 
 def first_half():
@@ -115,11 +107,11 @@
         stage_tokens(ref, scr)
         for tile in range(TILES):
             put_tile(scr, 0, tile, jnp.zeros((ROWS, LANES), f32))
-    taps = chunk_taps(feat_ref, (1, 2), table_scr)
-    for member in range(2):
-        for lag, tap in enumerate(taps[member]):
-            tap_ref[member * ROWS + lag] = tap
-    reach = len(taps[0]) - 1
+    reach = tap_ref.shape[0] // 2 - 1
+    both = widened(feat_ref[(reach + 1) * ROWS :, :])
+    taps = (both[: reach + 1], both[reach + 1 :])
+    for lag, tap in enumerate(both):
+        tap_ref[lag] = tap
     stage_table(rate_ref[...], table_scr)
     for mode in range(modes):
         decay_ref[mode] = jnp.exp(-get_row(table_scr, mode // ROWS, mode % ROWS))
@@ -149,7 +141,9 @@
         tuple(get_row(scr, 0, ROWS - reach + row) for row in range(reach)) for scr in (key_scr, value_scr)
     )
     carry = eight(0, ((None,) * modes, past), True)
-    state, _ = lax.fori_loop(1, steps // ROWS, eight, carry)
+    for group in range(1, steps // ROWS):
+        carry = eight(group, carry)
+    state, _ = carry
     for mode in range(modes):
         through = power(decay[mode], steps) * state[mode]
         state_ref[mode] = pltpu.roll(through, TILES, 0) + state[mode]
@@ -159,7 +153,7 @@
     key_scr, value_scr, total_scr = scratches
     chunks, modes = state_ref.shape[:2]
     pieces, piece_rows = out_ref.shape[:2]
-    reach = tap_ref.shape[1] // 2 - 2
+    reach = tap_ref.shape[1] // 2 - 1
     top = first_half()
     for chunk in range(chunks):
         span = slice(chunk * CHUNK, (chunk + 1) * CHUNK)
@@ -172,7 +166,9 @@
                 for slot in (tile, TILES + tile):
                     put_tile(scr, 0, slot, before)
                     put_tile(scr, 1, slot, after)
-        taps = [[tap_ref[chunk, member * ROWS + lag] for lag in range(reach + 1)] for member in range(2)]
+        taps = [
+            [tap_ref[chunk, member * (reach + 1) + lag] for lag in range(reach + 1)] for member in range(2)
+        ]
         signals = []
         for row in range(reach):
             parts = []
@@ -230,19 +226,20 @@
         return tuple(state)
 
     state = eight(0, (None,) * modes, True)
-    state = lax.fori_loop(1, steps // ROWS, eight, state)
+    for group in range(1, steps // ROWS):
+        state = eight(group, state)
     for mode in range(modes):
         mid_ref[mode] = pltpu.roll(state[mode], TILES, 0)
 
 
-def gate_kernel(query_ref, halo_ref, feat_ref, gate_ref, query_scr, table_scr):
+def gate_kernel(query_ref, halo_ref, feat_ref, gate_ref, query_scr):
     steps = gate_ref.shape[0]
     stage_tokens(query_ref, query_scr)
     halo = halo_ref[...].astype(f32)[2 * ROWS :]
     for tile in range(TILES):
         put_tile(query_scr, 0, tile, lanes_of(halo, tile))
-    (taps,) = chunk_taps(feat_ref, (0,), table_scr)
-    reach = len(taps) - 1
+    reach = feat_ref.shape[0] // (3 * ROWS) - 1
+    taps = widened(feat_ref[: (reach + 1) * ROWS, :])
 
     def eight(group, past):
         past = list(past)
@@ -253,7 +250,8 @@
         return tuple(past)
 
     past = tuple(get_row(query_scr, 0, ROWS - reach + row) for row in range(reach))
-    lax.fori_loop(0, steps // ROWS, eight, past)
+    for group in range(steps // ROWS):
+        past = eight(group, past)
 
 
 def prefix_kernel(piece_ref, rate_ref, out_ref, table_scr, *, tokens, axes):
@@ -316,7 +314,8 @@
             out_scr[pl.ds(group * ROWS * ROWS + row, ROWS, stride=ROWS), :] = value
         return tuple(state)
 
-    lax.fori_loop(0, steps // ROWS, eight, tuple(state))
+    for group in range(steps // ROWS):
+        state = eight(group, state)
     half_groups = steps // ROWS
     for pair in range(half_groups):
         for tile in range(TILES):
@@ -357,8 +356,10 @@
     front = pl.BlockSpec((2 * ROWS, width), lambda at: (0, 0))
     vectors = lambda count: shape((chunks, count, ROWS, LANES), f32)
 
-    feat = featurizer.reshape(members, taps, chunks, groups // chunks).transpose(2, 0, 1, 3)
-    feat_block = blocks(members, taps, groups // chunks)
+    feat = featurizer.reshape(members, taps, chunks, 1, TILES, groups // tiles).transpose(2, 0, 1, 3, 4, 5)
+    feat = jnp.broadcast_to(feat, (chunks, members, taps, 2, TILES, groups // tiles))
+    feat = feat.reshape(chunks, members * taps * ROWS, groups // tiles)
+    feat_block = blocks(members * taps * ROWS, groups // tiles)
 
     packed = pl.pallas_call(
         pack_kernel,
@@ -377,8 +378,8 @@
         signal_kernel,
         grid=(chunks,),
         in_specs=[columns(tokens)] * 2 + [feat_block, columns(modes)],
-        out_specs=[blocks(n, ROWS, LANES) for n in (steps, modes, 2 * ROWS, modes)],
-        out_shape=[vectors(n) for n in (steps, modes, 2 * ROWS, modes)],
+        out_specs=[blocks(n, ROWS, LANES) for n in (steps, modes, 2 * taps, modes)],
+        out_shape=[vectors(n) for n in (steps, modes, 2 * taps, modes)],
         scratch_shapes=[stage, stage, table],
         compiler_params=params(),
         cost_estimate=cost(60 * elements, 10 * elements),
@@ -392,7 +393,7 @@
         functools.partial(head_kernel, tokens=tokens),
         grid=(1,),
         in_specs=[front, front, whole(3 * ROWS, width)]
-        + [whole(chunks, n, ROWS, LANES) for n in (modes, 2 * ROWS, modes)],
+        + [whole(chunks, n, ROWS, LANES) for n in (modes, 2 * taps, modes)],
         out_specs=[whole(*pieces), whole(chunks, ROWS, ROWS, LANES)],
         out_shape=[shape(pieces, bf16), vectors(ROWS)],
         scratch_shapes=[small, small, vmem((modes, tiles, LANES), f32)],
@@ -400,11 +401,24 @@
         name="head",
     )(key_proj, value_proj, halo, decay, wide_taps, state)
 
+    left, halo_late = lax.optimization_barrier((left, halo))
+    gate = pl.pallas_call(
+        gate_kernel,
+        grid=(chunks,),
+        in_specs=[columns(tokens), columns(3 * ROWS), feat_block],
+        out_specs=blocks(steps, ROWS, LANES),
+        out_shape=vectors(steps),
+        scratch_shapes=[stage],
+        compiler_params=params(),
+        cost_estimate=cost(14 * elements, 6 * elements),
+        name="gate",
+    )(query, halo_late, feat)
+
     def swap(value):
         return lax.all_to_all(value, axes, split_axis=0, concat_axis=0, tiled=True)
 
     if even:
-        theirs = swap(left)
+        theirs, gate = lax.optimization_barrier((swap(left), gate))
         entering = pl.pallas_call(
             functools.partial(prefix_kernel, tokens=tokens, axes=axes),
             grid=(1,),
@@ -415,10 +429,9 @@
             compiler_params=params(),
             name="prefix",
         )(theirs, rates)
-        entered = swap(entering)
     else:
         share = modes * width // devices
-        theirs = swap(left.reshape(devices, share))
+        theirs, gate = lax.optimization_barrier((swap(left.reshape(devices, share)), gate))
         mine = lax.axis_index(axes)
         through = jnp.exp(-float(tokens) * lax.dynamic_slice_in_dim(rates.reshape(-1), mine * share, share))
         _, entering = lax.scan(
@@ -426,8 +439,9 @@
             jnp.zeros((share,), f32),
             theirs,
         )
-        entered = swap(entering).reshape(pieces)
-
+
+    entering, u_late = lax.optimization_barrier((entering, u))
+    entered = swap(entering).reshape(pieces)
     coef = residues * jnp.sqrt(-jnp.expm1(-2.0 * rates) / modes)
     y, lead, mid = pl.pallas_call(
         local_kernel,
@@ -439,19 +453,7 @@
         compiler_params=params(),
         cost_estimate=cost(66 * elements, 8 * elements),
         name="within",
-    )(u, head, decay, coef, skip[None, :])
-
-    gate = pl.pallas_call(
-        gate_kernel,
-        grid=(chunks,),
-        in_specs=[columns(tokens), columns(3 * ROWS), feat_block],
-        out_specs=blocks(steps, ROWS, LANES),
-        out_shape=vectors(steps),
-        scratch_shapes=[stage, table],
-        compiler_params=params(),
-        cost_estimate=cost(14 * elements, 6 * elements),
-        name="gate",
-    )(query, halo, feat)
+    )(u_late, head, decay, coef, skip[None, :])
 
     return pl.pallas_call(
         final_kernel,

time: 63.6 us -> 64.5 us (1.014)
  Pallas kernels: 27.9 us -> 42.9 us
  blocking collectives: 12.7 us -> 0 us
  local copies, waits for them, and re-layouts: 12.8 us -> 3.95 us
  starting transfers between devices: 7.22 us -> 14.4 us
  other arithmetic: 0.18 us -> 0.9 us
    all_to_all x1 -> x0, blocking collectives: 12.7 us -> none  [swap(): return lax.all_to_all(value, axes, split_axis=0, concat_axis=0, tiled=True)]
    unnamed x40 -> x14, local copies, waits for them, and re-layouts: 12.7 us -> 2.05 us
    all_to_all x1 -> x2, starting transfers between devices: 3.15 us -> 10.5 us  [swap(): return lax.all_to_all(value, axes, split_axis=0, concat_axis=0, tiled=True)]
    pallas_call x1, Pallas kernels: 5.77 us -> 9.3 us  [local(): pl.pallas_call(local_kernel, grid=(chunks,), in_specs=[blocks(n, ROWS, LA...]
    pallas_call x1, Pallas kernels: 5.37 us -> 8.57 us  [local(): pl.pallas_call(final_kernel, grid=(chunks,), in_specs=[whole(*pieces)] +...]
    pallas_call x1, Pallas kernels: 7.72 us -> 10.7 us  [local(): pl.pallas_call(signal_kernel, grid=(chunks,), in_specs=[columns(tokens)]...]
    pallas_call x1, Pallas kernels: 5.74 us -> 7.45 us  [local(): pl.pallas_call(gate_kernel, grid=(chunks,), in_specs=[columns(tokens), co...]
    ppermute x1, waiting for transfers between devices: 1.47 us -> 0.01 us  [local(): lax.ppermute(packed, axes, [(at, at + 1) for at in range(devices - 1)])]
  transfers between devices with their start and end apart: 2 -> 3, of which waited for: 1 -> 1; matrix products, arithmetic and copies ran while one was open for 1% -> 4% of each run, Pallas kernels for 31% -> 43%
where the time goes in v2:
time: 64.5 us; the launch traced here: 63.2 us
  Pallas kernels  42.9 us (67%)
  starting transfers between devices  14.4 us (22%)
  local copies, waits for them, and re-layouts  3.95 us (6%)
  waiting for transfers between devices  0.99 us (2%)
  other arithmetic  0.9 us (1%)
    pallas_call x1, Pallas kernels, local(): pl.pallas_call(signal_kernel, grid=(chunks,), in_specs=[columns(tokens)]...  10.7 us
    all_to_all x2, starting transfers between devices, swap(): return lax.all_to_all(value, axes, split_axis=0, concat_axis=0, tiled=True)  10.5 us
    pallas_call x1, Pallas kernels, local(): pl.pallas_call(local_kernel, grid=(chunks,), in_specs=[blocks(n, ROWS, LA...  9.3 us
    pallas_call x1, Pallas kernels, local(): pl.pallas_call(final_kernel, grid=(chunks,), in_specs=[whole(*pieces)] +...  8.57 us
    pallas_call x1, Pallas kernels, local(): pl.pallas_call(gate_kernel, grid=(chunks,), in_specs=[columns(tokens), co...  7.45 us
    ppermute x1, starting transfers between devices, local(): lax.ppermute(packed, axes, [(at, at + 1) for at in range(devices - 1)])  3.94 us
    pallas_call x1, Pallas kernels, local(): pl.pallas_call(functools.partial(head_kernel, tokens=tokens), grid=(1,),...  3.15 us
    unnamed x14, local copies, waits for them, and re-layouts  2.05 us
  transfers between devices with their start and end apart: 3, of which 1 were waited for; matrix products, arithmetic and copies ran while one was open for 4% of the time, Pallas kernels for 43%

profile of v2, /device:TPU:1, one launch (start us, length us, event | category | flops | bytes accessed | tf_op | source)
XLA Modules:
  0.0 63.2 jit_solution(2862155784463301593)
XLA Ops:
  0.0 1.8 %pack.1 = bf16[24,4608]{1,0:T(8,128)(2,1)} custom-call(bf16[128,4608]{1,0:T(8,128)(2,1)} %key_ref.5, bf16[128,4608]{1,0:T(8,128)(2,1)} %value_ref.5, bf16[128,4608]{1,0:T(8,128)(2,1)} %query_ref.3), custom_call_target="tpu_custom_call" | custom-call | tf_op jit(solution)/shard_map/pack/pallas_call | solution.py:364
  1.8 3.9 %collective-permute-start = (bf16[24,4608]{1,0:T(8,128)(2,1)}, bf16[24,4608]{1,0:T(8,128)(2,1)S(1)}, u32[]{:S(2)}, u32[]{:S(2)}) collective-permute-start(bf16[24,4608]{1,0:T(8,128)(2,1)} %pack.1), channel_id=1, source_target_pairs={{0,1},{1,2},{2,3},{3,4},{4,5},{5,6},{6,7},{7,8},{8,9},{9,10},{10,1... | collective-permute-start | bytes 663560 | tf_op jit(solution)/shard_map/ppermute | solution.py:373
  5.7 0.0 copy-done.5
  5.7 0.2 reshape.6
  6.0 0.1 copy.9
  6.0 1.0 %broadcast_in_dim.11 = f32[9,3,7,2,4,8]{5,4,3,2,1,0:T(4,128)} broadcast(f32[9,3,7,4,8]{4,3,2,1,0:T(4,128)S(1)} %copy.9), dimensions={0,1,2,4,5} | broadcast | bytes 72576 | tf_op jit(solution)/shard_map/broadcast_in_dim | solution.py:360
  7.0 10.7 %signal.1 = (f32[9,64,8,128]{3,2,1,0:T(8,128)}, f32[9,16,8,128]{3,2,1,0:T(8,128)}, f32[9,14,8,128]{3,2,1,0:T(8,128)}, f32[9,16,8,128]{3,2,1,0:T(8,128)}) custom-call(bf16[128,4608]{1,0:T(8,128)(2,1)} %key_ref.5, bf16[128,4608]{1,0:T(8,128)(2,1)} %value_ref.5, f32[9,168,8]{2,1,0:T(8,128)} %bitcast.4, f32[16,4608]{1,0:T(8,128)} %rate_ref.3), custom_call_target="tpu_custom_call" | custom-call | flops 35389440 | bytes 5898240 | tf_op jit(solution)/shard_map/signal/pallas_call | solution.py:377
  17.7 0.0 collective-permute-done.halo_ref
  17.7 0.7 %copy-done.1 = bf16[24,4608]{1,0:T(8,128)(2,1)} copy-done((bf16[24,4608]{1,0:T(8,128)(2,1)}, bf16[24,4608]{1,0:T(8,128)(2,1)S(1)}, u32[]{:S(2)}) %copy-start.1) | copy-done | bytes 221208
  18.4 3.1 %head.1 = (bf16[32,18,128]{2,1,0:T(8,128)(2,1)}, f32[9,8,8,128]{3,2,1,0:T(8,128)}) custom-call(bf16[128,4608]{1,0:T(8,128)(2,1)} %key_ref.5, bf16[128,4608]{1,0:T(8,128)(2,1)} %value_ref.5, bf16[24,4608]{1,0:T(8,128)(2,1)} %copy-done.1, f32[9,16,8,128]{3,2,1,0:T(8,128)} %get-tuple-element.20.decay_ref, f32[9,14,8,128]{3,2,1,0:T(8,128)} %get-tuple-element.21.tap_ref, ...), custom_call_target="tpu_custom_call" | custom-call | tf_op jit(solution)/shard_map/head/pallas_call | solution.py:392
  21.6 5.6 %all-to-all-start = ((bf16[32,18,128]{2,1,0:T(8,128)(2,1)}), bf16[32,18,128]{2,1,0:T(8,128)(2,1)S(1)}, u32[]{:S(2)}, u32[]{:S(2)}) async-start(bf16[32,18,128]{2,1,0:T(8,128)(2,1)} %get-tuple-element.24), calls=%async_computation | async-start | bytes 393216 | tf_op jit(solution)/shard_map/all_to_all | solution.py:418
  27.2 7.5 %gate.1.gate_ref = f32[9,64,8,128]{3,2,1,0:T(8,128)} custom-call(bf16[128,4608]{1,0:T(8,128)(2,1)} %query_ref.3, bf16[24,4608]{1,0:T(8,128)(2,1)} %copy-done.1, f32[9,168,8]{2,1,0:T(8,128)} %bitcast.5), custom_call_target="tpu_custom_call" | custom-call | flops 8257536 | bytes 3538944 | tf_op jit(solution)/shard_map/gate/pallas_call | solution.py:405
  34.6 1.0 %all-to-all-done.piece_ref = bf16[32,18,128]{2,1,0:T(8,128)(2,1)S(1)} async-done(((bf16[32,18,128]{2,1,0:T(8,128)(2,1)}), bf16[32,18,128]{2,1,0:T(8,128)(2,1)S(1)}, u32[]{:S(2)}, u32[]{:S(2)}) %all-to-all-start) | async-done | bytes 147488 | tf_op jit(solution)/shard_map/all_to_all | solution.py:418
  35.6 0.7 %copy-done.2 = bf16[32,18,128]{2,1,0:T(8,128)(2,1)} copy-done((bf16[32,18,128]{2,1,0:T(8,128)(2,1)}, bf16[32,18,128]{2,1,0:T(8,128)(2,1)S(1)}, u32[]{:S(2)}) %copy-start.2) | copy-done | bytes 147480
  36.3 1.9 %prefix.1 = bf16[32,18,128]{2,1,0:T(8,128)(2,1)} custom-call(bf16[32,18,128]{2,1,0:T(8,128)(2,1)} %copy-done.2, f32[16,4608]{1,0:T(8,128)} %rate_ref.3), custom_call_target="tpu_custom_call" | custom-call | tf_op jit(solution)/shard_map/prefix/pallas_call | solution.py:422
  38.3 4.9 %all-to-all-start.1 = ((bf16[32,18,128]{2,1,0:T(8,128)(2,1)}), bf16[32,18,128]{2,1,0:T(8,128)(2,1)S(1)}, u32[]{:S(2)}, u32[]{:S(2)}) async-start(bf16[32,18,128]{2,1,0:T(8,128)(2,1)} %prefix.1), calls=%async_computation.1 | async-start | bytes 393216 | tf_op jit(solution)/shard_map/all_to_all | solution.py:418
  43.1 0.0 copy-done
  43.1 0.0 copy-done.4
  43.1 0.9 %sqrt_multiply_fusion.coef_ref = f32[16,4608]{1,0:T(8,128)} fusion(f32[16,4608]{1,0:T(8,128)S(1)} %copy-done.4, f32[16,4608]{1,0:T(8,128)S(1)} %copy-done), kind=kLoop, calls=%fused_computation | loop fusion | flops 294912 | bytes 884736 | tf_op jit(solution)/shard_map/mul | solution.py:445
  44.0 0.6 broadcast_in_dim.12.skip_ref
  44.7 9.3 %within.1 = (f32[9,64,8,128]{3,2,1,0:T(8,128)}, f32[9,16,8,128]{3,2,1,0:T(8,128)}, f32[9,16,8,128]{3,2,1,0:T(8,128)}) custom-call(f32[9,64,8,128]{3,2,1,0:T(8,128)} %get-tuple-element.29.u_ref, f32[9,8,8,128]{3,2,1,0:T(8,128)} %get-tuple-element.30.head_ref, f32[9,16,8,128]{3,2,1,0:T(8,128)} %get-tuple-element.20.decay_ref, ...), custom_call_target="tpu_custom_call" | custom-call | flops 38928384 | bytes 4718592 | tf_op jit(solution)/shard_map/within/pallas_call | solution.py:446
  54.0 0.0 all-to-all-done.1.piece_ref
  54.0 0.7 %copy-done.3 = bf16[32,18,128]{2,1,0:T(8,128)(2,1)} copy-done((bf16[32,18,128]{2,1,0:T(8,128)(2,1)}, bf16[32,18,128]{2,1,0:T(8,128)(2,1)S(1)}, u32[]{:S(2)}) %copy-start.3) | copy-done | bytes 147480
  54.7 8.6 %final.1 = bf16[128,4608]{1,0:T(8,128)(2,1)} custom-call(bf16[32,18,128]{2,1,0:T(8,128)(2,1)} %copy-done.3, f32[9,16,8,128]{3,2,1,0:T(8,128)} %get-tuple-element.20.decay_ref, f32[9,16,8,128]{3,2,1,0:T(8,128)} %get-tuple-element.31.lead_ref, f32[9,16,8,128]{3,2,1,0:T(8,128)} %get-tuple-element.32.mid_ref, f32[9,64,8,128]{3,2,1,0:T(8,128)} %get-tuple-element.33.y_ref, ...), custom_call_target="tpu_custom_call" | custom-call | flops 23592960 | bytes 5898240 | tf_op jit(solution)/shard_map/final/pallas_call | solution.py:458
  (8 shorter events, 0.0 us)
Async XLA Ops:
  0.0 5.7 %copy-start.5 = (f32[3,7,288]{2,1,0:T(8,128)S(1)}, f32[3,7,288]{2,1,0:T(8,128)}, u32[]{:S(2)}) copy-start(f32[3,7,288]{2,1,0:T(8,128)} %param.10) | copy-start | bytes 72580
  1.8 16.0 %collective-permute-start = (bf16[24,4608]{1,0:T(8,128)(2,1)}, bf16[24,4608]{1,0:T(8,128)(2,1)S(1)}, u32[]{:S(2)}, u32[]{:S(2)}) collective-permute-start(bf16[24,4608]{1,0:T(8,128)(2,1)} %pack.1), channel_id=1, source_target_pairs={{0,1},{1,2},{2,3},{3,4},{4,5},{5,6},{6,7},{7,8},{8,9},{9,10},{10,1... | collective-permute-start | bytes 663560 | tf_op jit(solution)/shard_map/ppermute | solution.py:373
  17.7 0.7 %copy-start.1 = (bf16[24,4608]{1,0:T(8,128)(2,1)}, bf16[24,4608]{1,0:T(8,128)(2,1)S(1)}, u32[]{:S(2)}) copy-start(bf16[24,4608]{1,0:T(8,128)(2,1)S(1)} %collective-permute-done.halo_ref) | copy-start | bytes 663556
  21.6 14.1 %all-to-all-start = ((bf16[32,18,128]{2,1,0:T(8,128)(2,1)}), bf16[32,18,128]{2,1,0:T(8,128)(2,1)S(1)}, u32[]{:S(2)}, u32[]{:S(2)}) async-start(bf16[32,18,128]{2,1,0:T(8,128)(2,1)} %get-tuple-element.24), calls=%async_computation | async-start | bytes 393216 | tf_op jit(solution)/shard_map/all_to_all | solution.py:418
  34.6 8.5 %copy-start = (f32[16,4608]{1,0:T(8,128)S(1)}, f32[16,4608]{1,0:T(8,128)}, u32[]{:S(2)}) copy-start(f32[16,4608]{1,0:T(8,128)} %rate_ref.3) | copy-start | bytes 884740
  34.6 8.5 %copy-start.4 = (f32[16,4608]{1,0:T(8,128)S(1)}, f32[16,4608]{1,0:T(8,128)}, u32[]{:S(2)}) copy-start(f32[16,4608]{1,0:T(8,128)} %param.12) | copy-start | bytes 884740
  34.6 9.4 %copy-start.6 = (f32[4608]{0:T(1024)S(1)}, f32[4608]{0:T(1024)}, u32[]{:S(2)}) copy-start(f32[4608]{0:T(1024)} %param.13) | copy-start | bytes 55300
  35.6 0.7 %copy-start.2 = (bf16[32,18,128]{2,1,0:T(8,128)(2,1)}, bf16[32,18,128]{2,1,0:T(8,128)(2,1)S(1)}, u32[]{:S(2)}) copy-start(bf16[32,18,128]{2,1,0:T(8,128)(2,1)S(1)} %all-to-all-done.piece_ref) | copy-start | bytes 442372
  38.3 15.7 %all-to-all-start.1 = ((bf16[32,18,128]{2,1,0:T(8,128)(2,1)}), bf16[32,18,128]{2,1,0:T(8,128)(2,1)S(1)}, u32[]{:S(2)}, u32[]{:S(2)}) async-start(bf16[32,18,128]{2,1,0:T(8,128)(2,1)} %prefix.1), calls=%async_computation.1 | async-start | bytes 393216 | tf_op jit(solution)/shard_map/all_to_all | solution.py:418
  54.0 0.7 %copy-start.3 = (bf16[32,18,128]{2,1,0:T(8,128)(2,1)}, bf16[32,18,128]{2,1,0:T(8,128)(2,1)S(1)}, u32[]{:S(2)}) copy-start(bf16[32,18,128]{2,1,0:T(8,128)(2,1)S(1)} %all-to-all-done.1.piece_ref) | copy-start | bytes 442372

commit v3 on v2

v3 whole, which is shorter than its diff:
```python
import functools
import math

import jax
import jax.numpy as jnp
from jax import lax
from jax.experimental import pallas as pl
from jax.experimental.pallas import tpu as pltpu
from jax.sharding import PartitionSpec as P

LANES = 128
ROWS = 8
TILES = 4
CHUNK = TILES * LANES
LAP = 16
f32 = jnp.float32
bf16 = jnp.bfloat16


def put_tile(scratch, group, slot, tile):
    scratch[pl.ds((group * ROWS + slot) * ROWS, ROWS), :] = tile


def get_row(scratch, group, row):
    return scratch[pl.ds(group * ROWS * ROWS + row, ROWS, stride=ROWS), :]


def lanes_of(value, tile):
    return value[:, tile * LANES : (tile + 1) * LANES]


def stage_tokens(source, scratch):
    half_groups = source.shape[0] // ROWS // 2
    for pair in range(half_groups):
        block = source[pl.ds(pair * 2 * ROWS, 2 * ROWS), :].astype(f32)
        for part in range(2):
            group = pair * 2 + part
            half, within = group // half_groups, group % half_groups
            for tile in range(TILES):
                piece = lanes_of(block, tile)[part * ROWS : (part + 1) * ROWS]
                put_tile(scratch, within + 1, half * TILES + tile, piece)
                if half == 0 and within == half_groups - 1:
                    put_tile(scratch, 0, TILES + tile, piece)


def stage_table(table, scratch):
    for group in range(table.shape[0] // ROWS):
        for tile in range(TILES):
            piece = lanes_of(table, tile)[group * ROWS : (group + 1) * ROWS]
            put_tile(scratch, group, tile, piece)
            put_tile(scratch, group, TILES + tile, piece)


def fir(taps, now, past):
    total = taps[0] * now
    for lag in range(1, len(taps)):
        total = total + taps[lag] * past[-lag]
    return total


def rounded(value):
    return value.astype(bf16).astype(f32)


def lag_taps(rows, scratch, group):
    for tile in range(TILES):
        put_tile(scratch, group, tile, lanes_of(rows, tile))
        put_tile(scratch, group, TILES + tile, lanes_of(rows, tile))


def widened(group_taps):
    count = group_taps.shape[-1]
    group = lax.broadcasted_iota(jnp.int32, (count, CHUNK), 0)
    lane = lax.broadcasted_iota(jnp.int32, (count, CHUNK), 1)
    pick = (group == lane // (CHUNK // count)).astype(f32).astype(bf16)
    parts, rest = [], group_taps
    for _ in range(3):
        term = rest.astype(bf16)
        rest = rest - term.astype(f32)
        parts.append(jnp.dot(term, pick, preferred_element_type=f32))
    return parts[0] + parts[1] + parts[2]


def first_half():
    return lax.broadcasted_iota(jnp.int32, (ROWS, LANES), 0) < TILES


def power(base, exponent):
    result = None
    while exponent:
        if exponent & 1:
            result = base if result is None else result * base
        base = base * base
        exponent >>= 1
    return result


def tree(terms):
    while len(terms) > 1:
        terms = [sum(terms[at + 1 : at + 2], terms[at]) for at in range(0, len(terms), 2)]
    return terms[0]


def span(at):
    return pl.ds(pl.multiple_of(at * CHUNK, CHUNK), CHUNK)


def laps(steps, body, carry):
    def lap(number, carry):
        for part in range(LAP // ROWS):
            carry = body(number * (LAP // ROWS) + part, carry)
        return carry

    return lax.fori_loop(0, steps // LAP, lap, carry)


def pack_kernel(key_ref, value_ref, query_ref, out_ref, sem):
    tokens = key_ref.shape[0]
    copies = [
        pltpu.make_async_copy(
            ref.at[pl.ds(tokens - 2 * ROWS, 2 * ROWS)], out_ref.at[pl.ds(at * 2 * ROWS, 2 * ROWS)], sem.at[at]
        )
        for at, ref in enumerate((key_ref, value_ref, query_ref))
    ]
    for copy in copies:
        copy.start()
    for copy in copies:
        copy.wait()


def signal_kernel(key_ref, value_ref, feat_ref, rate_ref, u_ref, decay_ref, pair_ref, *scratches):
    key_buf, value_buf, feat_buf, rate_buf, u_buf, decay_buf, pair_buf = scratches[:7]
    wide_scr, key_scr, value_scr, table_scr, in_sem, small_sem, out_sem, last_sem = scratches[7:]
    chunks, steps = u_buf.shape[:2]
    modes = rate_buf.shape[0]
    reach = feat_buf.shape[2] - 2
    top = first_half()

    def fetch(at):
        return [
            pltpu.make_async_copy(ref.at[:, span(at)], buf.at[at], in_sem.at[member, at])
            for member, (ref, buf) in enumerate(((key_ref, key_buf), (value_ref, value_buf)))
        ]

    def send(at):
        return pltpu.make_async_copy(u_buf.at[at], u_ref.at[at], out_sem.at[at])

    small = [
        pltpu.make_async_copy(feat_ref, feat_buf, small_sem.at[0]),
        pltpu.make_async_copy(rate_ref, rate_buf, small_sem.at[1]),
    ]
    for copy in small:
        copy.start()
    for at in range(chunks):
        for copy in fetch(at):
            copy.start()
    small[0].wait()
    for member in range(2):
        rows = feat_buf[:, member + 1].reshape(chunks * ROWS, feat_buf.shape[-1])
        wide_scr[:, member] = widened(rows).reshape(chunks, ROWS, CHUNK)
    small[1].wait()

    def chunk(at, _):
        stage_table(rate_buf[:, span(at)], table_scr)
        decay = []
        for mode in range(modes):
            decay.append(jnp.exp(-get_row(table_scr, mode // ROWS, mode % ROWS)))
            decay_buf[at, mode] = decay[mode]
        taps = []
        for member in range(2):
            lag_taps(wide_scr[at, member], table_scr, member + 2)
            taps.append([get_row(table_scr, member + 2, lag) for lag in range(reach + 1)])
        for copy in fetch(at):
            copy.wait()
        for buf, scr in ((key_buf, key_scr), (value_buf, value_scr)):
            stage_tokens(buf.at[at], scr)
            for tile in range(TILES):
                put_tile(scr, 0, tile, jnp.zeros((ROWS, LANES), f32))

        def eight(group, carry):
            state, past = carry
            state = list(state)
            past = [list(past[0]), list(past[1])]
            for row in range(ROWS):
                parts = []
                for member, scr in enumerate((key_scr, value_scr)):
                    now = get_row(scr, group + 1, row)
                    parts.append(fir(taps[member], now, past[member]))
                    past[member] = past[member][1:] + [now]
                u = rounded(parts[0] * parts[1])
                if row < reach:
                    u = jnp.where(jnp.logical_and(top, group == 0), 0.0, u)
                u_buf[at, group * ROWS + row] = u
                state = [decay[mode] * state[mode] + u for mode in range(modes)]
            return tuple(state), (tuple(past[0]), tuple(past[1]))

        past = tuple(
            tuple(get_row(scr, 0, ROWS - reach + row) for row in range(reach)) for scr in (key_scr, value_scr)
        )
        state, _ = laps(steps, eight, ((jnp.zeros((ROWS, LANES), f32),) * modes, past))
        send(at).start()
        for mode in range(modes // 2):
            whole = []
            for one in (mode, mode + modes // 2):
                whole.append(state[one] + pltpu.roll(power(decay[one], steps) * state[one], TILES, 0))
            pair_buf[at, mode] = jnp.where(top, pltpu.roll(whole[0], TILES, 0), whole[1])
            pair_buf[at, modes // 2 + mode] = jnp.where(top, decay[mode], decay[mode + modes // 2])
        for lag in range(reach + 1):
            pair_buf[at, modes + lag] = jnp.where(top, taps[0][lag], taps[1][lag])
        return 0

    lax.fori_loop(0, chunks, chunk, 0)
    last = [
        pltpu.make_async_copy(decay_buf, decay_ref, last_sem.at[0]),
        pltpu.make_async_copy(pair_buf, pair_ref, last_sem.at[1]),
    ]
    for copy in last:
        copy.start()
    for at in range(chunks):
        send(at).wait()
    for copy in last:
        copy.wait()


def head_kernel(key_ref, value_ref, halo_ref, pair_ref, out_ref, head_ref, *scratches, tokens, reach):
    front_buf, halo_buf, pair_buf, out_buf, head_buf, token_scr, total_scr, in_sem, pair_sem, out_sem = scratches
    chunks = pair_buf.shape[0]
    pieces, piece_rows = out_buf.shape[:2]
    modes = total_scr.shape[0]
    half = modes // 2
    top = first_half()
    copies = [
        pltpu.make_async_copy(halo_ref.at[pl.ds(0, 4 * ROWS)], halo_buf, in_sem.at[0]),
        pltpu.make_async_copy(key_ref.at[pl.ds(0, 2 * ROWS)], front_buf.at[0], in_sem.at[1]),
        pltpu.make_async_copy(value_ref.at[pl.ds(0, 2 * ROWS)], front_buf.at[1], in_sem.at[2]),
    ]
    pairs = [
        pltpu.make_async_copy(pair_ref.at[chunk], pair_buf.at[chunk], pair_sem.at[chunk]) for chunk in range(chunks)
    ]
    for copy in copies + pairs:
        copy.start()
    for copy in copies:
        copy.wait()
    for chunk in range(chunks):
        pairs[chunk].wait()
        lanes = slice(chunk * CHUNK, (chunk + 1) * CHUNK)
        for member in range(2):
            before = halo_buf[member * 2 * ROWS : (member + 1) * 2 * ROWS, lanes].astype(f32)[ROWS:]
            after = front_buf[member, :, lanes].astype(f32)[:ROWS]
            for tile in range(TILES):
                put_tile(token_scr, 0, member * TILES + tile, lanes_of(before, tile))
                put_tile(token_scr, 1, member * TILES + tile, lanes_of(after, tile))
        taps = [pair_buf[chunk, modes + lag] for lag in range(reach + 1)]
        seen = [get_row(token_scr, 0, ROWS - reach + row) for row in range(reach)]
        signals = []
        for row in range(reach):
            now = get_row(token_scr, 1, row)
            both = fir(taps, now, seen)
            seen = seen[1:] + [now]
            signals.append(rounded(both * pltpu.roll(both, TILES, 0)))
            head_buf[chunk, row] = jnp.where(top, signals[-1], 0.0)
        for row in range(reach, ROWS):
            head_buf[chunk, row] = jnp.zeros((ROWS, LANES), f32)
        for mode in range(half):
            decay = pair_buf[chunk, half + mode]
            head = signals[0]
            for row in range(1, reach):
                head = decay * head + signals[row]
            total = pair_buf[chunk, mode] + power(decay, tokens - reach) * head
            rows = slice(chunk * TILES, (chunk + 1) * TILES)
            total_scr[mode, rows, :] = total[:TILES]
            total_scr[half + mode, rows, :] = total[TILES:]
    split = pieces // modes
    for mode in range(modes):
        for part in range(split):
            rows = total_scr[mode, part * piece_rows : (part + 1) * piece_rows, :]
            out_buf[mode * split + part] = rows.astype(out_buf.dtype)
    outs = [
        pltpu.make_async_copy(out_buf, out_ref, out_sem.at[0]),
        pltpu.make_async_copy(head_buf, head_ref, out_sem.at[1]),
    ]
    for copy in outs:
        copy.start()
    for copy in outs:
        copy.wait()


def local_kernel(u_ref, head_ref, decay_ref, coef_ref, skip_ref, y_ref, enter_ref, *scratches):
    u_buf, head_buf, decay_buf, coef_buf, skip_buf, y_buf, enter_buf, table_scr = scratches[:8]
    in_sem, small_sem, out_sem = scratches[8:]
    chunks, steps = u_buf.shape[:2]
    modes = decay_buf.shape[1]
    top = first_half()

    def fetch(at):
        return [
            pltpu.make_async_copy(ref.at[at], buf.at[at], in_sem.at[member, at])
            for member, (ref, buf) in enumerate(((u_ref, u_buf), (decay_ref, decay_buf)))
        ]

    def send(at):
        return [
            pltpu.make_async_copy(buf.at[at], ref.at[at], out_sem.at[member, at])
            for member, (ref, buf) in enumerate(((y_ref, y_buf), (enter_ref, enter_buf)))
        ]

    small = [
        pltpu.make_async_copy(ref, buf, small_sem.at[at])
        for at, (ref, buf) in enumerate(((head_ref, head_buf), (coef_ref, coef_buf), (skip_ref, skip_buf)))
    ]
    for copy in small:
        copy.start()
    for at in range(chunks):
        for copy in fetch(at):
            copy.start()
    for copy in small:
        copy.wait()

    def chunk(at, _):
        stage_table(coef_buf[:, span(at)], table_scr)
        coef = [get_row(table_scr, mode // ROWS, mode % ROWS) for mode in range(modes)]
        lag_taps(jnp.broadcast_to(skip_buf[:, span(at)], (ROWS, CHUNK)), table_scr, modes // ROWS)
        skip = get_row(table_scr, modes // ROWS, 0)
        for copy in fetch(at):
            copy.wait()
        for row in range(ROWS):
            u_buf[at, row] = u_buf[at, row] + head_buf[at, row]
        decay = [decay_buf[at, mode] for mode in range(modes)]

        def eight(group, state):
            state = list(state)
            for row in range(ROWS):
                u = u_buf[at, group * ROWS + row]
                state = [decay[mode] * state[mode] + u for mode in range(modes)]
                y_buf[at, group * ROWS + row] = tree(
                    [skip * u] + [coef[mode] * state[mode] for mode in range(modes)]
                )
            return tuple(state)

        state = laps(steps, eight, (jnp.zeros((ROWS, LANES), f32),) * modes)
        for mode in range(modes):
            middle = pltpu.roll(state[mode], TILES, 0)
            enter_buf[at, mode] = coef[mode] * jnp.where(top, 1.0, power(decay[mode], steps))
            enter_buf[at, modes + mode] = jnp.where(top, 0.0, coef[mode] * middle)
        for copy in send(at):
            copy.start()
        return 0

    lax.fori_loop(0, chunks, chunk, 0)
    for at in range(chunks):
        for copy in send(at):
            copy.wait()


def gate_kernel(query_ref, halo_ref, feat_ref, gate_ref, *scratches):
    query_buf, halo_buf, feat_buf, gate_buf, wide_scr, query_scr, table_scr, in_sem, small_sem, out_sem = scratches
    chunks, steps = gate_buf.shape[0], gate_buf.shape[1] // ROWS
    reach = feat_buf.shape[2] - 2

    def fetch(at):
        return pltpu.make_async_copy(query_ref.at[:, span(at)], query_buf.at[at], in_sem.at[at])

    def send(at):
        return pltpu.make_async_copy(gate_buf.at[at], gate_ref.at[at], out_sem.at[at])

    small = [
        pltpu.make_async_copy(feat_ref, feat_buf, small_sem.at[0]),
        pltpu.make_async_copy(halo_ref.at[pl.ds(4 * ROWS, 2 * ROWS)], halo_buf, small_sem.at[1]),
    ]
    for copy in small:
        copy.start()
    for at in range(chunks):
        fetch(at).start()
    for copy in small:
        copy.wait()
    wide_scr[...] = widened(feat_buf[:, 0].reshape(chunks * ROWS, feat_buf.shape[-1])).reshape(chunks, ROWS, CHUNK)

    def chunk(at, _):
        lag_taps(wide_scr[at], table_scr, 0)
        taps = [get_row(table_scr, 0, lag) for lag in range(reach + 1)]
        fetch(at).wait()
        stage_tokens(query_buf.at[at], query_scr)
        halo = halo_buf[:, span(at)].astype(f32)[ROWS:]
        for tile in range(TILES):
            put_tile(query_scr, 0, tile, lanes_of(halo, tile))

        def eight(group, past):
            past = list(past)
            found = []
            for row in range(ROWS):
                now = get_row(query_scr, group + 1, row)
                found.append(fir(taps, now, past))
                past = past[1:] + [now]
            rows = jnp.concatenate(found, axis=0).astype(bf16)
            gate_buf[at, pl.ds(pl.multiple_of(group * ROWS * ROWS, ROWS * ROWS), ROWS * ROWS), :] = rows
            return tuple(past)

        past = tuple(get_row(query_scr, 0, ROWS - reach + row) for row in range(reach))
        laps(steps, eight, past)
        send(at).start()
        return 0

    lax.fori_loop(0, chunks, chunk, 0)
    for at in range(chunks):
        send(at).wait()


def prefix_kernel(piece_ref, rate_ref, out_ref, table_scr, *, tokens, axes):
    devices, piece_rows = piece_ref.shape[:2]
    split = devices // rate_ref.shape[0]
    mine = lax.axis_index(axes)
    mode, part = mine // split, mine % split
    group = pl.multiple_of(mode // ROWS * ROWS, ROWS)
    first = pl.multiple_of(part * piece_rows * LANES, LANES)
    rows = rate_ref[pl.ds(group, ROWS), pl.ds(first, piece_rows * LANES)]
    here = lax.broadcasted_iota(jnp.int32, rows.shape, 0) == mode - group
    rate = jnp.sum(jnp.where(here, rows, 0.0), axis=0, keepdims=True)
    for row in range(piece_rows):
        table_scr[row : row + 1, :] = lanes_of(rate, row)
    through = jnp.exp(-float(tokens) * table_scr[:piece_rows, :])

    def lap(source, entering):
        out_ref[source] = entering.astype(out_ref.dtype)
        return through * entering + piece_ref[source].astype(f32)

    lax.fori_loop(0, devices, lap, jnp.zeros((piece_rows, LANES), f32))


def final_kernel(piece_ref, decay_ref, enter_ref, y_ref, gate_ref, out_ref, *scratches):
    piece_buf, decay_buf, enter_buf, y_buf, gate_buf, out_buf, total_scr, state_scr, out_scr = scratches[:9]
    piece_sem, in_sem, out_sem = scratches[9:]
    chunks, modes = decay_buf.shape[:2]
    steps = y_buf.shape[1]
    half_groups = steps // ROWS

    def fetch(at):
        sources = ((decay_ref, decay_buf), (enter_ref, enter_buf), (y_ref, y_buf), (gate_ref, gate_buf))
        return [
            pltpu.make_async_copy(ref.at[at], buf.at[at], in_sem.at[member, at])
            for member, (ref, buf) in enumerate(sources)
        ]

    def send(at):
        return pltpu.make_async_copy(out_buf.at[at], out_ref.at[:, span(at)], out_sem.at[at])

    piece_copy = pltpu.make_async_copy(piece_ref, piece_buf, piece_sem.at[0])
    piece_copy.start()
    for at in range(chunks):
        for copy in fetch(at):
            copy.start()
    piece_copy.wait()
    pieces, piece_rows = piece_buf.shape[:2]
    split = pieces // modes
    for mode in range(modes):
        for part in range(split):
            rows = piece_buf[mode * split + part].astype(f32)
            total_scr[mode, part * piece_rows : (part + 1) * piece_rows, :] = rows
    for at in range(chunks):
        for mode in range(modes):
            rows = total_scr[mode, at * TILES : (at + 1) * TILES, :]
            state_scr[at, mode, :TILES, :] = rows
            state_scr[at, mode, TILES:, :] = rows

    def chunk(at, _):
        for copy in fetch(at):
            copy.wait()
        decay = [decay_buf[at, mode] for mode in range(modes)]
        state = tuple(
            enter_buf[at, mode] * state_scr[at, mode] + enter_buf[at, modes + mode] for mode in range(modes)
        )

        def eight(group, state):
            first = pl.multiple_of(group * ROWS * ROWS, ROWS * ROWS)
            gates = gate_buf[at, pl.ds(first, ROWS * ROWS), :].astype(f32)
            for row in range(ROWS):
                state = [decay[mode] * state[mode] for mode in range(modes)]
                conv = rounded(y_buf[at, group * ROWS + row] + tree(state))
                value = gates[row * ROWS : (row + 1) * ROWS] * conv
                out_scr[pl.ds(first + row, ROWS, stride=ROWS), :] = value
            return tuple(state)

        laps(steps, eight, state)
        for pair in range(half_groups):
            for tile in range(TILES):
                parts = []
                for group in (pair * 2, pair * 2 + 1):
                    half, within = group // half_groups, group % half_groups
                    slot = (within * ROWS + half * TILES + tile) * ROWS
                    parts.append(out_scr[pl.ds(slot, ROWS), :])
                rows = jnp.concatenate(parts, axis=0).astype(bf16)
                out_buf[at, pl.ds(pair * 2 * ROWS, 2 * ROWS), tile * LANES : (tile + 1) * LANES] = rows
        send(at).start()
        return 0

    lax.fori_loop(0, chunks, chunk, 0)
    for at in range(chunks):
        send(at).wait()


def cost(flops, moved):
    return pl.CostEstimate(flops=int(flops), bytes_accessed=int(moved), transcendentals=0)


def local(query, key_proj, value_proj, featurizer, rates, residues, skip, *, axes):
    tokens, width = query.shape
    modes = rates.shape[0]
    members, taps, groups = featurizer.shape
    devices = math.prod(lax.axis_size(axis) for axis in axes)
    chunks = width // CHUNK
    steps = tokens // 2
    tiles = width // LANES
    split = devices // modes
    even = devices % modes == 0 and tiles % split == 0
    shape = jax.ShapeDtypeStruct
    vmem = pltpu.VMEM
    dma = pltpu.SemaphoreType.DMA
    elements = tokens * width
    there = pl.BlockSpec(memory_space=pl.ANY)

    def call(kernel, inputs, outputs, scratches, name, **more):
        return pl.pallas_call(
            kernel,
            in_specs=[there] * len(inputs),
            out_specs=[there] * len(outputs),
            out_shape=outputs,
            scratch_shapes=scratches,
            compiler_params=pltpu.CompilerParams(vmem_limit_bytes=60 * 2**20),
            name=name,
            **more,
        )(*inputs)

    def vectors(count, kind=f32):
        return (chunks, count, ROWS, LANES), kind

    (packed,) = call(
        pack_kernel,
        (key_proj, value_proj, query),
        [shape((members * 2 * ROWS, width), bf16)],
        [dma((members,))],
        "pack",
    )
    halo = lax.ppermute(packed, axes, [(at, at + 1) for at in range(devices - 1)])

    feat = featurizer.reshape(members, taps, chunks, groups // chunks).transpose(2, 0, 1, 3)
    feat = jnp.pad(feat, ((0, 0), (0, 0), (0, ROWS - taps), (0, 0)))
    tokens_buf = vmem((chunks, tokens, CHUNK), bf16)
    feat_buf = vmem(feat.shape, f32)
    stage = vmem(((steps // ROWS + 1) * ROWS * ROWS, LANES), f32)
    pairs = vectors(modes + taps)
    u, decay, pair = call(
        signal_kernel,
        (key_proj, value_proj, feat, rates),
        [shape(*vectors(steps)), shape(*vectors(modes)), shape(*pairs)],
        [tokens_buf, tokens_buf, feat_buf, vmem((modes, width), f32)]
        + [vmem(*vectors(steps)), vmem(*vectors(modes)), vmem(*pairs)]
        + [vmem((chunks, 2, ROWS, CHUNK), f32), stage, stage, vmem((4 * ROWS * ROWS, LANES), f32)]
        + [dma((2, chunks)), dma((2,)), dma((chunks,)), dma((2,))],
        "signal",
        cost_estimate=cost(60 * elements, 10 * elements),
    )

    pieces = (modes * split, tiles // split, LANES) if even else (modes, tiles, LANES)
    left, head = call(
        functools.partial(head_kernel, tokens=tokens, reach=taps - 1),
        (key_proj, value_proj, halo, pair),
        [shape(pieces, bf16), shape(*vectors(ROWS))],
        [vmem((2, 2 * ROWS, width), bf16), vmem((4 * ROWS, width), bf16), vmem(*pairs)]
        + [vmem(pieces, bf16), vmem(*vectors(ROWS)), vmem((2 * ROWS * ROWS, LANES), f32)]
        + [vmem((modes, tiles, LANES), f32), dma((3,)), dma((chunks,)), dma((2,))],
        "head",
    )
    left, halo_late = lax.optimization_barrier((left, halo))

    gate_shape = ((chunks, steps * ROWS, LANES), bf16)
    (gate,) = call(
        gate_kernel,
        (query, halo_late, feat),
        [shape(*gate_shape)],
        [tokens_buf, vmem((2 * ROWS, width), bf16), feat_buf, vmem(*gate_shape)]
        + [vmem((chunks, ROWS, CHUNK), f32), stage, vmem((ROWS * ROWS, LANES), f32)]
        + [dma((chunks,)), dma((2,)), dma((chunks,))],
        "gate",
        cost_estimate=cost(14 * elements, 4 * elements),
    )

    def swap(value):
        return lax.all_to_all(value, axes, split_axis=0, concat_axis=0, tiled=True)

    if even:
        theirs, gate = lax.optimization_barrier((swap(left), gate))
        entering = pl.pallas_call(
            functools.partial(prefix_kernel, tokens=tokens, axes=axes),
            out_shape=shape(pieces, bf16),
            scratch_shapes=[vmem((-(-pieces[1] // ROWS) * ROWS, LANES), f32)],
            compiler_params=pltpu.CompilerParams(vmem_limit_bytes=60 * 2**20),
            name="prefix",
        )(theirs, rates)
    else:
        share = modes * width // devices
        theirs, gate = lax.optimization_barrier((swap(left.reshape(devices, share)), gate))
        mine = lax.axis_index(axes)
        through = jnp.exp(-float(tokens) * lax.dynamic_slice_in_dim(rates.reshape(-1), mine * share, share))
        _, entering = lax.scan(
            lambda so_far, piece: (through * so_far + piece.astype(f32), so_far.astype(bf16)),
            jnp.zeros((share,), f32),
            theirs,
        )

    entering, u_late = lax.optimization_barrier((entering, u))
    entered = swap(entering).reshape(pieces)
    coef = residues * jnp.sqrt(-jnp.expm1(-2.0 * rates) / modes)
    y, enter = call(
        local_kernel,
        (u_late, head, decay, coef, skip[None, :]),
        [shape(*vectors(steps)), shape(*vectors(2 * modes))],
        [vmem(*vectors(steps)), vmem(*vectors(ROWS)), vmem(*vectors(modes)), vmem((modes, width), f32)]
        + [vmem((1, width), f32), vmem(*vectors(steps)), vmem(*vectors(2 * modes))]
        + [vmem((3 * ROWS * ROWS, LANES), f32), dma((2, chunks)), dma((3,)), dma((2, chunks))],
        "within",
        cost_estimate=cost(66 * elements, 8 * elements),
    )

    (out,) = call(
        final_kernel,
        (entered, decay, enter, y, gate),
        [shape((tokens, width), bf16)],
        [vmem(pieces, bf16), vmem(*vectors(modes)), vmem(*vectors(2 * modes)), vmem(*vectors(steps))]
        + [vmem(*gate_shape), tokens_buf, vmem((modes, tiles, LANES), f32), vmem(*vectors(modes))]
        + [vmem((steps * ROWS, LANES), f32), dma((1,)), dma((4, chunks)), dma((chunks,))],
        "final",
        cost_estimate=cost(40 * elements, 10 * elements),
    )
    return out


def solution(mesh):
    axes = tuple(mesh.axis_names)
    placed = (P(axes, None),) * 3 + (P(),) * 4
    return jax.shard_map(
        functools.partial(local, axes=axes),
        mesh=mesh,
        in_specs=placed,
        out_specs=P(axes, None),
        check_vma=False,
    )
```

time: 64.5 us -> 72.1 us (1.12)
  waiting for transfers between devices: 0.99 us -> 7.91 us
  Pallas kernels: 42.9 us -> 48.8 us
  starting transfers between devices: 14.4 us -> 10.2 us
    pallas_call x6, Pallas kernels: 40.9 us -> 46.8 us  [call(): pl.pallas_call(kernel, in_specs=[there] * len(inputs), out_specs=[there]...]
    all_to_all x2, starting transfers between devices: 10.5 us -> 6.28 us  [swap(): return lax.all_to_all(value, axes, split_axis=0, concat_axis=0, tiled=True)]
    ppermute x1, waiting for transfers between devices: 0.01 us -> 3.63 us  [local(): lax.ppermute(packed, axes, [(at, at + 1) for at in range(devices - 1)])]
    all_to_all x2, waiting for transfers between devices: 0.99 us -> 4.28 us  [swap(): return lax.all_to_all(value, axes, split_axis=0, concat_axis=0, tiled=True)]
    broadcast_in_dim x2 -> x0, local copies, waits for them, and re-layouts: 1.04 us -> none  [local(): jnp.broadcast_to(feat, (chunks, members, taps, 2, TILES, groups // tiles))]
  transfers between devices with their start and end apart: 3 -> 3, of which waited for: 1 -> 2; matrix products, arithmetic and copies ran while one was open for 4% -> 3% of each run, Pallas kernels for 43% -> 31%
where the time goes in v3:
time: 72.1 us; the launch traced here: 71.5 us
  Pallas kernels  48.8 us (68%)
  starting transfers between devices  10.2 us (14%)
  waiting for transfers between devices  7.91 us (11%)
  local copies, waits for them, and re-layouts  3.55 us (5%)
  other arithmetic  0.9 us (1%)
    pallas_call x6, Pallas kernels, call(): pl.pallas_call(kernel, in_specs=[there] * len(inputs), out_specs=[there]...  46.8 us
    all_to_all x2, starting transfers between devices, swap(): return lax.all_to_all(value, axes, split_axis=0, concat_axis=0, tiled=True)  6.28 us
    all_to_all x2, waiting for transfers between devices, swap(): return lax.all_to_all(value, axes, split_axis=0, concat_axis=0, tiled=True)  4.28 us
    ppermute x1, starting transfers between devices, local(): lax.ppermute(packed, axes, [(at, at + 1) for at in range(devices - 1)])  3.95 us
    ppermute x1, waiting for transfers between devices, local(): lax.ppermute(packed, axes, [(at, at + 1) for at in range(devices - 1)])  3.63 us
    unnamed x14, local copies, waits for them, and re-layouts  2.16 us
    pallas_call x1, Pallas kernels, local(): pl.pallas_call(functools.partial(prefix_kernel, tokens=tokens, axes=axes)...  1.97 us
  transfers between devices with their start and end apart: 3, of which 2 were waited for; matrix products, arithmetic and copies ran while one was open for 3% of the time, Pallas kernels for 31%

profile of v3, /device:TPU:1, one launch (start us, length us, event | category | flops | bytes accessed | tf_op | source)
XLA Modules:
  0.0 71.5 jit_solution(11495277597613632204)
XLA Ops:
  0.0 14.5 %pack.1 = bf16[48,4608]{1,0:T(8,128)(2,1)} custom-call(bf16[128,4608]{1,0:T(8,128)(2,1)} %key_ref.5, bf16[128,4608]{1,0:T(8,128)(2,1)} %value_ref.5, bf16[128,4608]{1,0:T(8,128)(2,1)} %query_ref.3), custom_call_target="tpu_custom_call" | custom-call | tf_op jit(solution)/shard_map/pack/pallas_call | solution.py:521
  14.5 3.9 %collective-permute-start = (bf16[48,4608]{1,0:T(8,128)(2,1)}, bf16[48,4608]{1,0:T(8,128)(2,1)S(1)}, u32[]{:S(2)}, u32[]{:S(2)}) collective-permute-start(bf16[48,4608]{1,0:T(8,128)(2,1)} %pack.1), channel_id=1, source_target_pairs={{0,1},{1,2},{2,3},{3,4},{4,5},{5,6},{6,7},{7,8},{8,9},{9,10},{10,1... | collective-permute-start | bytes 1327112 | tf_op jit(solution)/shard_map/ppermute | solution.py:542
  18.5 0.0 copy-done.5
  18.5 0.1 reshape.3
  18.6 0.7 pad.4.feat_ref
  19.3 9.6 %signal.1 = (f32[9,64,8,128]{3,2,1,0:T(8,128)}, f32[9,16,8,128]{3,2,1,0:T(8,128)}, f32[9,23,8,128]{3,2,1,0:T(8,128)}) custom-call(bf16[128,4608]{1,0:T(8,128)(2,1)} %key_ref.5, bf16[128,4608]{1,0:T(8,128)(2,1)} %value_ref.5, f32[9,3,8,32]{3,2,1,0:T(8,128)} %pad.4.feat_ref, f32[16,4608]{1,0:T(8,128)} %rate_ref.3), custom_call_target="tpu_custom_call" | custom-call | flops 35389440 | bytes 5898240 | tf_op jit(solution)/shard_map/signal/pallas_call | solution.py:521
  28.9 3.6 %collective-permute-done.halo_ref = bf16[48,4608]{1,0:T(8,128)(2,1)S(1)} collective-permute-done((bf16[48,4608]{1,0:T(8,128)(2,1)}, bf16[48,4608]{1,0:T(8,128)(2,1)S(1)}, u32[]{:S(2)}, u32[]{:S(2)}) %collective-permute-start) | collective-permute-done | bytes 442400 | tf_op jit(solution)/shard_map/ppermute | solution.py:542
  32.5 0.8 %copy-done.1 = bf16[48,4608]{1,0:T(8,128)(2,1)} copy-done((bf16[48,4608]{1,0:T(8,128)(2,1)}, bf16[48,4608]{1,0:T(8,128)(2,1)S(1)}, u32[]{:S(2)}) %copy-start.1) | copy-done | bytes 442392
  33.3 2.8 %head.1 = (bf16[32,18,128]{2,1,0:T(8,128)(2,1)}, f32[9,8,8,128]{3,2,1,0:T(8,128)}) custom-call(bf16[128,4608]{1,0:T(8,128)(2,1)} %key_ref.5, bf16[128,4608]{1,0:T(8,128)(2,1)} %value_ref.5, bf16[48,4608]{1,0:T(8,128)(2,1)} %copy-done.1, f32[9,23,8,128]{3,2,1,0:T(8,128)} %get-tuple-element.18.pair_ref), custom_call_target="tpu_custom_call" | custom-call | tf_op jit(solution)/shard_map/head/pallas_call | solution.py:521
  36.2 3.1 %all-to-all-start = ((bf16[32,18,128]{2,1,0:T(8,128)(2,1)}), bf16[32,18,128]{2,1,0:T(8,128)(2,1)S(1)}, u32[]{:S(2)}, u32[]{:S(2)}) async-start(bf16[32,18,128]{2,1,0:T(8,128)(2,1)} %get-tuple-element.20), calls=%async_computation | async-start | bytes 393216 | tf_op jit(solution)/shard_map/all_to_all | solution.py:587
  39.3 4.1 %gate.1.gate_ref = bf16[9,512,128]{2,1,0:T(8,128)(2,1)} custom-call(bf16[128,4608]{1,0:T(8,128)(2,1)} %query_ref.3, bf16[48,4608]{1,0:T(8,128)(2,1)} %copy-done.1, f32[9,3,8,32]{3,2,1,0:T(8,128)} %pad.4.feat_ref), custom_call_target="tpu_custom_call" | custom-call | flops 8257536 | bytes 2359296 | tf_op jit(solution)/shard_map/gate/pallas_call | solution.py:521
  43.4 0.0 copy-start
  43.4 0.0 copy-start.4
  43.5 0.0 copy-start.6
  43.5 4.3 %all-to-all-done.piece_ref = bf16[32,18,128]{2,1,0:T(8,128)(2,1)S(1)} async-done(((bf16[32,18,128]{2,1,0:T(8,128)(2,1)}), bf16[32,18,128]{2,1,0:T(8,128)(2,1)S(1)}, u32[]{:S(2)}, u32[]{:S(2)}) %all-to-all-start) | async-done | bytes 147488 | tf_op jit(solution)/shard_map/all_to_all | solution.py:587
  47.7 0.7 copy-done.3
  48.4 2.0 %prefix.1 = bf16[32,18,128]{2,1,0:T(8,128)(2,1)} custom-call(bf16[32,18,128]{2,1,0:T(8,128)(2,1)} %copy-done.3, f32[16,4608]{1,0:T(8,128)} %rate_ref.3), custom_call_target="tpu_custom_call" | custom-call | tf_op jit(solution)/shard_map/prefix/pallas_call | solution.py:591
  50.4 3.1 %all-to-all-start.1 = ((bf16[32,18,128]{2,1,0:T(8,128)(2,1)}), bf16[32,18,128]{2,1,0:T(8,128)(2,1)S(1)}, u32[]{:S(2)}, u32[]{:S(2)}) async-start(bf16[32,18,128]{2,1,0:T(8,128)(2,1)} %prefix.1), calls=%async_computation.1 | async-start | bytes 393216 | tf_op jit(solution)/shard_map/all_to_all | solution.py:587
  53.6 0.9 %sqrt_multiply_fusion.coef_ref = f32[16,4608]{1,0:T(8,128)} fusion(f32[16,4608]{1,0:T(8,128)S(1)} %copy-done.4, f32[16,4608]{1,0:T(8,128)S(1)} %copy-done), kind=kLoop, calls=%fused_computation | loop fusion | flops 294912 | bytes 884736 | tf_op jit(solution)/shard_map/mul | solution.py:611
  54.5 0.6 broadcast_in_dim.3.skip_ref
  55.1 8.7 %within.1 = (f32[9,64,8,128]{3,2,1,0:T(8,128)}, f32[9,32,8,128]{3,2,1,0:T(8,128)}) custom-call(f32[9,64,8,128]{3,2,1,0:T(8,128)} %get-tuple-element.26.u_ref, f32[9,8,8,128]{3,2,1,0:T(8,128)} %get-tuple-element.27.head_ref, f32[9,16,8,128]{3,2,1,0:T(8,128)} %get-tuple-element.25.decay_ref, f32[16,4608]{1,0:T(8,128)} %sqrt_multiply_fusion.coef_ref, ...), custom_call_target="tpu_custom_call" | custom-call | flops 38928384 | bytes 4718592 | tf_op jit(solution)/shard_map/within/pallas_call | solution.py:521
  63.8 0.0 all-to-all-done.1.piece_ref
  63.8 0.7 copy-done.2
  64.5 7.0 %final.1 = bf16[128,4608]{1,0:T(8,128)(2,1)} custom-call(bf16[32,18,128]{2,1,0:T(8,128)(2,1)} %copy-done.2, f32[9,16,8,128]{3,2,1,0:T(8,128)} %get-tuple-element.25.decay_ref, f32[9,32,8,128]{3,2,1,0:T(8,128)} %get-tuple-element.28.enter_ref, f32[9,64,8,128]{3,2,1,0:T(8,128)} %get-tuple-element.29.y_ref, bf16[9,512,128]{2,1,0:T(8,128)(2,1)} %gate.1.gate_ref), custom_call_target="tpu_custom_call" | custom-call | flops 23592960 | bytes 5898240 | tf_op jit(solution)/shard_map/final/pallas_call | solution.py:521
  (8 shorter events, 0.1 us)
Async XLA Ops:
  0.0 18.5 %copy-start.5 = (f32[3,7,288]{2,1,0:T(8,128)S(1)}, f32[3,7,288]{2,1,0:T(8,128)}, u32[]{:S(2)}) copy-start(f32[3,7,288]{2,1,0:T(8,128)} %param.10) | copy-start | bytes 72580
  14.5 18.0 %collective-permute-start = (bf16[48,4608]{1,0:T(8,128)(2,1)}, bf16[48,4608]{1,0:T(8,128)(2,1)S(1)}, u32[]{:S(2)}, u32[]{:S(2)}) collective-permute-start(bf16[48,4608]{1,0:T(8,128)(2,1)} %pack.1), channel_id=1, source_target_pairs={{0,1},{1,2},{2,3},{3,4},{4,5},{5,6},{6,7},{7,8},{8,9},{9,10},{10,1... | collective-permute-start | bytes 1327112 | tf_op jit(solution)/shard_map/ppermute | solution.py:542
  32.5 0.8 %copy-start.1 = (bf16[48,4608]{1,0:T(8,128)(2,1)}, bf16[48,4608]{1,0:T(8,128)(2,1)S(1)}, u32[]{:S(2)}) copy-start(bf16[48,4608]{1,0:T(8,128)(2,1)S(1)} %collective-permute-done.halo_ref) | copy-start | bytes 1327108
  36.2 11.6 %all-to-all-start = ((bf16[32,18,128]{2,1,0:T(8,128)(2,1)}), bf16[32,18,128]{2,1,0:T(8,128)(2,1)S(1)}, u32[]{:S(2)}, u32[]{:S(2)}) async-start(bf16[32,18,128]{2,1,0:T(8,128)(2,1)} %get-tuple-element.20), calls=%async_computation | async-start | bytes 393216 | tf_op jit(solution)/shard_map/all_to_all | solution.py:587
  43.4 10.1 %copy-start = (f32[16,4608]{1,0:T(8,128)S(1)}, f32[16,4608]{1,0:T(8,128)}, u32[]{:S(2)}) copy-start(f32[16,4608]{1,0:T(8,128)} %rate_ref.3) | copy-start | bytes 884740
  43.4 10.1 %copy-start.4 = (f32[16,4608]{1,0:T(8,128)S(1)}, f32[16,4608]{1,0:T(8,128)}, u32[]{:S(2)}) copy-start(f32[16,4608]{1,0:T(8,128)} %param.12) | copy-start | bytes 884740
  43.5 11.0 %copy-start.6 = (f32[4608]{0:T(1024)S(1)}, f32[4608]{0:T(1024)}, u32[]{:S(2)}) copy-start(f32[4608]{0:T(1024)} %param.13) | copy-start | bytes 55300
  47.7 0.7 copy-start.3
  50.4 13.4 %all-to-all-start.1 = ((bf16[32,18,128]{2,1,0:T(8,128)(2,1)}), bf16[32,18,128]{2,1,0:T(8,128)(2,1)S(1)}, u32[]{:S(2)}, u32[]{:S(2)}) async-start(bf16[32,18,128]{2,1,0:T(8,128)(2,1)} %prefix.1), calls=%async_computation.1 | async-start | bytes 393216 | tf_op jit(solution)/shard_map/all_to_all | solution.py:587
  63.8 0.7 copy-start.2

commit v4 on v3

v4 whole, which is shorter than its diff:
```python
import functools
import math

import jax
import jax.numpy as jnp
from jax import lax
from jax.experimental import pallas as pl
from jax.experimental.pallas import tpu as pltpu
from jax.sharding import PartitionSpec as P

LANES = 128
ROWS = 8
TILES = 4
CHUNK = TILES * LANES
LAP = 16
BLOCK = LAP * ROWS
AHEAD = 3
f32 = jnp.float32
bf16 = jnp.bfloat16


def put_tile(scratch, group, slot, tile):
    scratch[pl.ds((group * ROWS + slot) * ROWS, ROWS), :] = tile


def get_row(scratch, group, row):
    return scratch[pl.ds(group * ROWS * ROWS + row, ROWS, stride=ROWS), :]


def lanes_of(value, tile):
    return value[:, tile * LANES : (tile + 1) * LANES]


def place(row, step=1):
    return pl.ds(pl.multiple_of(row * ROWS, ROWS), step * ROWS)


def spread(row_of):
    slot = lax.broadcasted_iota(jnp.int32, (ROWS, LANES), 0) % TILES
    result = jnp.broadcast_to(row_of(TILES - 1), (ROWS, LANES))
    for tile in range(TILES - 1):
        result = jnp.where(slot == tile, jnp.broadcast_to(row_of(tile), (ROWS, LANES)), result)
    return result


def spread_rows(ref, at, rows):
    def one(row):
        return spread(lambda tile: ref[row : row + 1, pl.ds(pl.multiple_of((at * TILES + tile) * LANES, LANES), LANES)])

    return [one(row) for row in rows]


def relayout():
    row = lax.broadcasted_iota(jnp.int32, (BLOCK, BLOCK), 0)
    column = lax.broadcasted_iota(jnp.int32, (BLOCK, BLOCK), 1)
    same = jnp.logical_and(row // ROWS == column % LAP, row % ROWS == column // LAP)
    return same.astype(f32).astype(bf16)


def block_of(buf, at, number, steps):
    return jnp.concatenate(
        [
            buf[at, pl.ds(pl.multiple_of(half * steps + number * LAP, LAP), LAP), tile * LANES : (tile + 1) * LANES]
            for half in range(2)
            for tile in range(TILES)
        ],
        axis=0,
    )


def move_block(bufs, scrs, at, slot, number, steps, matrix):
    wide = jnp.concatenate([block_of(buf, at, number, steps) for buf in bufs], axis=1)
    moved = jnp.dot(matrix, wide, preferred_element_type=f32)
    rows = pl.ds(pl.multiple_of(number * BLOCK, BLOCK), BLOCK)
    for position, scr in enumerate(scrs):
        scr[slot, rows, :] = lanes_of(moved, position)


def fir(taps, now, past):
    total = taps[0] * now
    for lag in range(1, len(taps)):
        total = total + taps[lag] * past[-lag]
    return total


def rounded(value):
    return value.astype(bf16).astype(f32)


def widened(group_taps):
    count = group_taps.shape[-1]
    group = lax.broadcasted_iota(jnp.int32, (count, CHUNK), 0)
    lane = lax.broadcasted_iota(jnp.int32, (count, CHUNK), 1)
    pick = (group == lane // (CHUNK // count)).astype(f32).astype(bf16)
    parts, rest = [], group_taps
    for _ in range(3):
        term = rest.astype(bf16)
        rest = rest - term.astype(f32)
        parts.append(jnp.dot(term, pick, preferred_element_type=f32))
    return parts[0] + parts[1] + parts[2]


def chunk_taps(wide_scr, at, member):
    def one(lag):
        return spread(lambda tile: wide_scr[at, member, lag : lag + 1, tile * LANES : (tile + 1) * LANES])

    return one


def first_half():
    return lax.broadcasted_iota(jnp.int32, (ROWS, LANES), 0) < TILES


def power(base, exponent):
    result = None
    while exponent:
        if exponent & 1:
            result = base if result is None else result * base
        base = base * base
        exponent >>= 1
    return result


def tree(terms):
    while len(terms) > 1:
        terms = [sum(terms[at + 1 : at + 2], terms[at]) for at in range(0, len(terms), 2)]
    return terms[0]


def span(at):
    return pl.ds(pl.multiple_of(at * CHUNK, CHUNK), CHUNK)


def start_all(copies):
    for copy in copies:
        copy.start()


def wait_all(copies):
    for copy in copies:
        copy.wait()


def over_chunks(chunks, fetch, body):
    for at in range(min(AHEAD, chunks)):
        start_all(fetch(at))

    def one(at, _):
        @pl.when(at + AHEAD < chunks)
        def _():
            start_all(fetch(at + AHEAD))

        body(at)
        return 0

    return lambda: lax.fori_loop(0, chunks, one, 0)


def pack_kernel(key_ref, value_ref, query_ref, out_ref, in_buf, out_buf, in_sem, out_sem):
    tokens = key_ref.shape[0]
    copies = [
        pltpu.make_async_copy(ref.at[pl.ds(tokens - 2 * ROWS, 2 * ROWS)], in_buf.at[at], in_sem.at[at])
        for at, ref in enumerate((key_ref, value_ref, query_ref))
    ]
    start_all(copies)
    wait_all(copies)
    tails = [in_buf[at].astype(f32)[ROWS:] for at in range(len(copies))]
    out_buf[...] = jnp.concatenate(tails, axis=0).astype(bf16)
    last = pltpu.make_async_copy(out_buf, out_ref, out_sem.at[0])
    last.start()
    last.wait()


def signal_kernel(key_ref, value_ref, feat_ref, rate_ref, u_ref, decay_ref, pair_ref, *scratches):
    key_buf, value_buf, feat_buf, rate_buf, u_buf, decay_buf, pair_buf = scratches[:7]
    wide_scr, key_scr, value_scr, in_sem, small_sem, out_sem = scratches[7:]
    chunks, steps = u_buf.shape[0], u_buf.shape[1] // ROWS
    modes = rate_buf.shape[0]
    reach = feat_buf.shape[2] - 1
    top = first_half()
    matrix = relayout()
    bufs, scrs = (key_buf, value_buf), (key_scr, value_scr)

    def fetch(at):
        return [
            pltpu.make_async_copy(ref.at[:, span(at)], buf.at[at], in_sem.at[member, at])
            for member, (ref, buf) in enumerate(((key_ref, key_buf), (value_ref, value_buf)))
        ]

    def send(at):
        sources = ((u_buf, u_ref), (decay_buf, decay_ref), (pair_buf, pair_ref))
        return [
            pltpu.make_async_copy(buf.at[at], ref.at[at], out_sem.at[member, at])
            for member, (buf, ref) in enumerate(sources)
        ]

    small = [
        pltpu.make_async_copy(feat_ref, feat_buf, small_sem.at[0]),
        pltpu.make_async_copy(rate_ref, rate_buf, small_sem.at[1]),
    ]
    start_all(small)

    def chunk(at):
        @pl.when(at + 1 < chunks)
        def _():
            wait_all(fetch(at + 1))

        decay = [jnp.exp(-rate) for rate in spread_rows(rate_buf, at, range(modes))]
        for mode in range(modes):
            decay_buf[at, mode] = decay[mode]
        taps = [[chunk_taps(wide_scr, at, member)(lag) for lag in range(reach + 1)] for member in range(2)]
        slot, later = at % 2, jnp.minimum(at + 1, chunks - 1)

        def lap(number, carry):
            state, past = carry
            state = list(state)
            past = [list(past[0]), list(past[1])]
            move_block(bufs, scrs, later, 1 - slot, number, steps, matrix)
            opening = jnp.logical_and(top, number == 0)
            for row in range(0, LAP, 2):
                found = []
                for step in (row, row + 1):
                    parts = []
                    for member, scr in enumerate(scrs):
                        now = scr[slot, place(number * LAP + step), :]
                        parts.append(fir(taps[member], now, past[member]))
                        past[member] = past[member][1:] + [now]
                    u = parts[0] * parts[1]
                    found.append(jnp.where(opening, 0.0, u) if step < reach else u)
                both = jnp.concatenate(found, axis=0).astype(bf16)
                u_buf[at, place(number * LAP + row, 2), :] = both
                both = both.astype(f32)
                for u in (both[:ROWS], both[ROWS:]):
                    state = [decay[mode] * state[mode] + u for mode in range(modes)]
            return tuple(state), (tuple(past[0]), tuple(past[1]))

        past = tuple(
            tuple(pltpu.roll(scr[slot, place(steps - reach + row), :], TILES, 0) for row in range(reach))
            for scr in scrs
        )
        zero = jnp.zeros((ROWS, LANES), f32)
        state, _ = lax.fori_loop(0, steps // LAP, lap, ((zero,) * modes, past))
        for mode in range(modes // 2):
            whole = []
            for one in (mode, mode + modes // 2):
                whole.append(state[one] + pltpu.roll(power(decay[one], steps) * state[one], TILES, 0))
            pair_buf[at, mode] = jnp.where(top, pltpu.roll(whole[0], TILES, 0), whole[1])
            pair_buf[at, modes // 2 + mode] = jnp.where(top, decay[mode], decay[mode + modes // 2])
        for lag in range(reach + 1):
            pair_buf[at, modes + lag] = jnp.where(top, taps[0][lag], taps[1][lag])
        start_all(send(at))

    run = over_chunks(chunks, fetch, chunk)
    small[0].wait()
    count = feat_buf.shape[-1]
    for member in range(2):
        rows = [feat_buf[at, member + 1] for at in range(chunks)]
        rows = [jnp.concatenate([row, jnp.zeros((ROWS - reach - 1, count), f32)], axis=0) for row in rows]
        wide = widened(jnp.concatenate(rows, axis=0))
        wide_scr[:, member] = wide.reshape(chunks, ROWS, CHUNK)
    small[1].wait()
    wait_all(fetch(0))
    for number in range(steps // LAP):
        move_block(bufs, scrs, 0, 0, number, steps, matrix)
    run()
    for at in range(chunks):
        wait_all(send(at))


def head_kernel(key_ref, value_ref, halo_ref, pair_ref, out_ref, head_ref, *scratches, tokens, reach):
    front_buf, pair_buf, out_buf, head_buf, token_scr, total_scr, in_sem, pair_sem, out_sem = scratches
    chunks = pair_buf.shape[0]
    pieces, piece_rows = out_buf.shape[:2]
    modes = total_scr.shape[0]
    half = modes // 2
    top = first_half()
    copies = [
        pltpu.make_async_copy(key_ref.at[pl.ds(0, 2 * ROWS)], front_buf.at[0], in_sem.at[0]),
        pltpu.make_async_copy(value_ref.at[pl.ds(0, 2 * ROWS)], front_buf.at[1], in_sem.at[1]),
    ]
    pairs = [
        pltpu.make_async_copy(pair_ref.at[chunk], pair_buf.at[chunk], pair_sem.at[chunk]) for chunk in range(chunks)
    ]
    start_all(copies + pairs)
    wait_all(copies)
    nothing = jnp.zeros((ROWS, LANES), f32)
    for chunk in range(chunks):
        pairs[chunk].wait()
        lanes = slice(chunk * CHUNK, (chunk + 1) * CHUNK)
        halo = halo_ref[:, lanes].astype(f32)
        for member in range(2):
            before = halo[member * ROWS : (member + 1) * ROWS]
            after = front_buf[member, :, lanes].astype(f32)[:ROWS]
            for tile in range(TILES):
                put_tile(token_scr, 0, member * TILES + tile, lanes_of(before, tile))
                put_tile(token_scr, 1, member * TILES + tile, lanes_of(after, tile))
        taps = [pair_buf[chunk, modes + lag] for lag in range(reach + 1)]
        seen = [get_row(token_scr, 0, ROWS - reach + row) for row in range(reach)]
        signals = []
        for row in range(reach):
            now = get_row(token_scr, 1, row)
            both = fir(taps, now, seen)
            seen = seen[1:] + [now]
            signals.append(rounded(both * pltpu.roll(both, TILES, 0)))
        kept = [jnp.where(top, one, 0.0) for one in signals] + [nothing] * (ROWS - reach)
        head_buf[chunk] = jnp.concatenate(kept, axis=0).astype(bf16)
        for mode in range(half):
            decay = pair_buf[chunk, half + mode]
            head = signals[0]
            for row in range(1, reach):
                head = decay * head + signals[row]
            total = pair_buf[chunk, mode] + power(decay, tokens - reach) * head
            rows = slice(chunk * TILES, (chunk + 1) * TILES)
            total_scr[mode, rows, :] = total[:TILES]
            total_scr[half + mode, rows, :] = total[TILES:]
    split = pieces // modes
    for mode in range(modes):
        for part in range(split):
            rows = total_scr[mode, part * piece_rows : (part + 1) * piece_rows, :]
            out_buf[mode * split + part] = rows.astype(out_buf.dtype)
    outs = [
        pltpu.make_async_copy(out_buf, out_ref, out_sem.at[0]),
        pltpu.make_async_copy(head_buf, head_ref, out_sem.at[1]),
    ]
    start_all(outs)
    wait_all(outs)


def local_kernel(u_ref, head_ref, decay_ref, coef_ref, skip_ref, y_ref, enter_ref, *scratches):
    u_buf, head_buf, decay_buf, coef_buf, skip_buf, y_buf, enter_buf = scratches[:7]
    in_sem, small_sem, out_sem = scratches[7:]
    chunks, steps = u_buf.shape[0], u_buf.shape[1] // ROWS
    modes = decay_buf.shape[1]
    top = first_half()

    def fetch(at):
        return [
            pltpu.make_async_copy(ref.at[at], buf.at[at], in_sem.at[member, at])
            for member, (ref, buf) in enumerate(((u_ref, u_buf), (decay_ref, decay_buf)))
        ]

    def send(at):
        return [
            pltpu.make_async_copy(buf.at[at], ref.at[at], out_sem.at[member, at])
            for member, (ref, buf) in enumerate(((y_ref, y_buf), (enter_ref, enter_buf)))
        ]

    small = [
        pltpu.make_async_copy(ref, buf, small_sem.at[at])
        for at, (ref, buf) in enumerate(((head_ref, head_buf), (coef_ref, coef_buf), (skip_ref, skip_buf)))
    ]
    start_all(small)

    def chunk(at):
        coef = spread_rows(coef_buf, at, range(modes))
        (skip,) = spread_rows(skip_buf, at, range(1))
        wait_all(fetch(at))
        front = slice(0, ROWS * ROWS)
        u_buf[at, front] = (u_buf[at, front].astype(f32) + head_buf[at].astype(f32)).astype(bf16)
        decay = [decay_buf[at, mode] for mode in range(modes)]

        def lap(number, state):
            state = list(state)
            for row in range(0, LAP, 2):
                both = u_buf[at, place(number * LAP + row, 2), :].astype(f32)
                for step, u in ((row, both[:ROWS]), (row + 1, both[ROWS:])):
                    state = [decay[mode] * state[mode] + u for mode in range(modes)]
                    y_buf[at, number * LAP + step] = tree(
                        [skip * u] + [coef[mode] * state[mode] for mode in range(modes)]
                    )
            return tuple(state)

        state = lax.fori_loop(0, steps // LAP, lap, (jnp.zeros((ROWS, LANES), f32),) * modes)
        for mode in range(modes):
            middle = pltpu.roll(state[mode], TILES, 0)
            enter_buf[at, mode] = coef[mode] * jnp.where(top, 1.0, power(decay[mode], steps))
            enter_buf[at, modes + mode] = jnp.where(top, 0.0, coef[mode] * middle)
        start_all(send(at))

    run = over_chunks(chunks, fetch, chunk)
    wait_all(small)
    run()
    for at in range(chunks):
        wait_all(send(at))


def gate_kernel(query_ref, halo_ref, feat_ref, gate_ref, *scratches):
    query_buf, halo_buf, feat_buf, gate_buf, wide_scr, query_scr, halo_scr = scratches[:7]
    in_sem, small_sem, out_sem = scratches[7:]
    chunks, steps = gate_buf.shape[0], gate_buf.shape[1] // ROWS
    reach = feat_buf.shape[2] - 1
    top = first_half()
    matrix = relayout()

    def fetch(at):
        return [pltpu.make_async_copy(query_ref.at[:, span(at)], query_buf.at[at], in_sem.at[at])]

    def send(at):
        return pltpu.make_async_copy(gate_buf.at[at], gate_ref.at[at], out_sem.at[at])

    small = [
        pltpu.make_async_copy(feat_ref, feat_buf, small_sem.at[0]),
        pltpu.make_async_copy(halo_ref, halo_buf, small_sem.at[1]),
    ]
    start_all(small)

    def chunk(at):
        @pl.when(at + 1 < chunks)
        def _():
            wait_all(fetch(at + 1))

        taps = [chunk_taps(wide_scr, at, 0)(lag) for lag in range(reach + 1)]
        slot, later = at % 2, jnp.minimum(at + 1, chunks - 1)
        halo = halo_buf[:, span(at)].astype(f32)[2 * ROWS :]
        for tile in range(TILES):
            put_tile(halo_scr, 0, tile, lanes_of(halo, tile))
            put_tile(halo_scr, 0, TILES + tile, lanes_of(halo, tile))

        def lap(number, past):
            past = list(past)
            move_block((query_buf,), (query_scr,), later, 1 - slot, number, steps, matrix)
            found = []
            for row in range(LAP):
                now = query_scr[slot, place(number * LAP + row), :]
                found.append(fir(taps, now, past))
                past = past[1:] + [now]
            gate_buf[at, place(number * LAP, LAP), :] = jnp.concatenate(found, axis=0).astype(bf16)
            return tuple(past)

        past = tuple(
            jnp.where(
                top,
                get_row(halo_scr, 0, ROWS - reach + row),
                pltpu.roll(query_scr[slot, place(steps - reach + row), :], TILES, 0),
            )
            for row in range(reach)
        )
        lax.fori_loop(0, steps // LAP, lap, past)
        send(at).start()

    run = over_chunks(chunks, fetch, chunk)
    wait_all(small)
    count = feat_buf.shape[-1]
    rows = [feat_buf[at, 0] for at in range(chunks)]
    rows = [jnp.concatenate([row, jnp.zeros((ROWS - reach - 1, count), f32)], axis=0) for row in rows]
    wide_scr[:, 0] = widened(jnp.concatenate(rows, axis=0)).reshape(chunks, ROWS, CHUNK)
    wait_all(fetch(0))
    for number in range(steps // LAP):
        move_block((query_buf,), (query_scr,), 0, 0, number, steps, matrix)
    run()
    for at in range(chunks):
        send(at).wait()


def prefix_kernel(piece_ref, rate_ref, out_ref, rate_buf, out_buf, table_scr, sem, *, tokens, axes):
    devices, piece_rows = piece_ref.shape[:2]
    split = devices // rate_ref.shape[0]
    mine = lax.axis_index(axes)
    mode, part = mine // split, mine % split
    group = pl.multiple_of(mode // ROWS * ROWS, ROWS)
    first_copy = pltpu.make_async_copy(rate_ref.at[pl.ds(group, ROWS)], rate_buf, sem.at[0])
    first_copy.start()
    first_copy.wait()
    first = pl.multiple_of(part * piece_rows * LANES, LANES)
    rows = rate_buf[:, pl.ds(first, piece_rows * LANES)]
    here = lax.broadcasted_iota(jnp.int32, rows.shape, 0) == mode - group
    rate = jnp.sum(jnp.where(here, rows, 0.0), axis=0, keepdims=True)
    for row in range(piece_rows):
        table_scr[row : row + 1, :] = lanes_of(rate, row)
    through = jnp.exp(-float(tokens) * table_scr[:piece_rows, :])

    def lap(number, entering):
        for part in range(4):
            source = number * 4 + part
            out_buf[source] = entering.astype(out_buf.dtype)
            entering = through * entering + piece_ref[source].astype(f32)
        return entering

    lax.fori_loop(0, devices // 4, lap, jnp.zeros((piece_rows, LANES), f32))
    last = pltpu.make_async_copy(out_buf, out_ref, sem.at[1])
    last.start()
    last.wait()


def final_kernel(piece_ref, decay_ref, enter_ref, y_ref, gate_ref, out_ref, *scratches):
    decay_buf, enter_buf, y_buf, gate_buf, out_buf, total_scr, state_scr, value_scr = scratches[:8]
    in_sem, out_sem = scratches[8:]
    chunks, modes = decay_buf.shape[:2]
    steps = y_buf.shape[1]
    count = steps // LAP
    matrix = relayout()

    def fetch(at):
        sources = ((decay_ref, decay_buf), (enter_ref, enter_buf), (y_ref, y_buf), (gate_ref, gate_buf))
        return [
            pltpu.make_async_copy(ref.at[at], buf.at[at], in_sem.at[member, at])
            for member, (ref, buf) in enumerate(sources)
        ]

    def send(at):
        return pltpu.make_async_copy(out_buf.at[at], out_ref.at[:, span(at)], out_sem.at[at])

    def settle(number):
        at, within = number // count, number % count
        moved = lax.dot_general(
            matrix, value_scr[number % 2], (((0,), (0,)), ((), ())), preferred_element_type=f32
        ).astype(bf16)
        for half in range(2):
            for tile in range(TILES):
                slot = half * TILES + tile
                rows = pl.ds(pl.multiple_of(half * steps + within * LAP, LAP), LAP)
                out_buf[at, rows, tile * LANES : (tile + 1) * LANES] = moved[slot * LAP : (slot + 1) * LAP]

    def chunk(at):
        wait_all(fetch(at))
        decay = [decay_buf[at, mode] for mode in range(modes)]
        state = tuple(
            enter_buf[at, mode] * state_scr[at, mode] + enter_buf[at, modes + mode] for mode in range(modes)
        )

        def lap(number, state):
            settle(jnp.maximum(at * count + number - 1, 0))
            found = []
            for row in range(0, LAP, 2):
                gates = gate_buf[at, place(number * LAP + row, 2), :].astype(f32)
                sums = []
                for step in (row, row + 1):
                    state = [decay[mode] * state[mode] for mode in range(modes)]
                    sums.append(y_buf[at, number * LAP + step] + tree(state))
                found.append((gates * rounded(jnp.concatenate(sums, axis=0))).astype(bf16))
            value_scr[(at * count + number) % 2] = jnp.concatenate(found, axis=0)
            return tuple(state)

        lax.fori_loop(0, count, lap, state)

        @pl.when(at > 0)
        def _():
            send(at - 1).start()

    run = over_chunks(chunks, fetch, chunk)
    value_scr[...] = jnp.zeros(value_scr.shape, bf16)
    pieces, piece_rows = piece_ref.shape[:2]
    split = pieces // modes
    for mode in range(modes):
        for part in range(split):
            rows = piece_ref[mode * split + part].astype(f32)
            total_scr[mode, part * piece_rows : (part + 1) * piece_rows, :] = rows
    for at in range(chunks):
        for mode in range(modes):
            rows = total_scr[mode, at * TILES : (at + 1) * TILES, :]
            state_scr[at, mode, :TILES, :] = rows
            state_scr[at, mode, TILES:, :] = rows
    run()
    settle(chunks * count - 1)
    send(chunks - 1).start()
    for at in range(chunks):
        send(at).wait()


def cost(flops, moved):
    return pl.CostEstimate(flops=int(flops), bytes_accessed=int(moved), transcendentals=0)


def local(query, key_proj, value_proj, featurizer, rates, residues, skip, *, axes):
    tokens, width = query.shape
    modes = rates.shape[0]
    members, taps, groups = featurizer.shape
    devices = math.prod(lax.axis_size(axis) for axis in axes)
    chunks = width // CHUNK
    steps = tokens // 2
    tiles = width // LANES
    split = devices // modes
    even = devices % modes == 0 and tiles % split == 0
    shape = jax.ShapeDtypeStruct
    vmem = pltpu.VMEM
    dma = pltpu.SemaphoreType.DMA
    elements = tokens * width
    there = pl.BlockSpec(memory_space=pltpu.HBM)

    def call(kernel, inputs, outputs, scratches, name, near=(), **more):
        inputs = [
            value if at in near else pltpu.with_memory_space_constraint(value, pltpu.HBM)
            for at, value in enumerate(inputs)
        ]
        return pl.pallas_call(
            kernel,
            in_specs=[pl.BlockSpec(memory_space=vmem) if at in near else there for at in range(len(inputs))],
            out_specs=[there] * len(outputs),
            out_shape=[pltpu.HBM(one.shape, one.dtype) for one in outputs],
            scratch_shapes=scratches,
            compiler_params=pltpu.CompilerParams(vmem_limit_bytes=32 * 2**20),
            name=name,
            **more,
        )(*inputs)

    def vectors(count, kind=f32):
        return (chunks, count, ROWS, LANES), kind

    packed_shape = ((members * ROWS, width), bf16)
    (packed,) = call(
        pack_kernel,
        (key_proj, value_proj, query),
        [shape(*packed_shape)],
        [vmem((members, 2 * ROWS, width), bf16), vmem(*packed_shape), dma((members,)), dma((1,))],
        "pack",
    )
    halo = lax.ppermute(packed, axes, [(at, at + 1) for at in range(devices - 1)])

    feat = featurizer.reshape(members, taps, chunks, groups // chunks).transpose(2, 0, 1, 3)
    tokens_buf = vmem((chunks, tokens, CHUNK), bf16)
    feat_buf = vmem(feat.shape, f32)
    moved = vmem((2, steps * ROWS, LANES), f32)
    pairs = vectors(modes + taps)
    flat = ((chunks, steps * ROWS, LANES), bf16)
    u, decay, pair = call(
        signal_kernel,
        (key_proj, value_proj, feat, rates),
        [shape(*flat), shape(*vectors(modes)), shape(*pairs)],
        [tokens_buf, tokens_buf, feat_buf, vmem((modes, width), f32)]
        + [vmem(*flat), vmem(*vectors(modes)), vmem(*pairs)]
        + [vmem((chunks, 2, ROWS, CHUNK), f32), moved, moved]
        + [dma((2, chunks)), dma((2,)), dma((3, chunks))],
        "signal",
        cost_estimate=cost(60 * elements, 10 * elements),
    )

    pieces = (modes * split, tiles // split, LANES) if even else (modes, tiles, LANES)
    front = ((chunks, ROWS * ROWS, LANES), bf16)
    left, head = call(
        functools.partial(head_kernel, tokens=tokens, reach=taps - 1),
        (key_proj, value_proj, halo, pair),
        [shape(pieces, bf16), shape(*front)],
        [vmem((2, 2 * ROWS, width), bf16), vmem(*pairs)]
        + [vmem(pieces, bf16), vmem(*front), vmem((2 * ROWS * ROWS, LANES), f32)]
        + [vmem((modes, tiles, LANES), f32), dma((2,)), dma((chunks,)), dma((2,))],
        "head",
        near=(2,),
    )
    left, halo_late, rates_late, skip_late = lax.optimization_barrier((left, halo, rates, skip))
    coef = residues * jnp.sqrt(-jnp.expm1(-2.0 * rates_late) / modes)
    skip_row = skip_late[None, :]
    (gate,) = call(
        gate_kernel,
        (query, halo_late, feat),
        [shape(*flat)],
        [tokens_buf, vmem(*packed_shape), feat_buf, vmem(*flat)]
        + [vmem((chunks, 1, ROWS, CHUNK), f32), moved, vmem((ROWS * ROWS, LANES), f32)]
        + [dma((chunks,)), dma((2,)), dma((chunks,))],
        "gate",
        cost_estimate=cost(14 * elements, 4 * elements),
    )

    def swap(value):
        return lax.all_to_all(value, axes, split_axis=0, concat_axis=0, tiled=True)

    share = modes * width // devices
    theirs = swap(left if even else left.reshape(devices, share))
    theirs, gate, coef, skip_row = lax.optimization_barrier((theirs, gate, coef, skip_row))
    if even:
        (entering,) = call(
            functools.partial(prefix_kernel, tokens=tokens, axes=axes),
            (theirs, rates),
            [shape(pieces, bf16)],
            [vmem((ROWS, width), f32), vmem(pieces, bf16)]
            + [vmem((-(-pieces[1] // ROWS) * ROWS, LANES), f32), dma((2,))],
            "prefix",
            near=(0,),
        )
    else:
        mine = lax.axis_index(axes)
        through = jnp.exp(-float(tokens) * lax.dynamic_slice_in_dim(rates.reshape(-1), mine * share, share))
        _, entering = lax.scan(
            lambda so_far, piece: (through * so_far + piece.astype(f32), so_far.astype(bf16)),
            jnp.zeros((share,), f32),
            theirs,
        )

    entering, u_late = lax.optimization_barrier((entering, u))
    entered = swap(entering).reshape(pieces)
    y, enter = call(
        local_kernel,
        (u_late, head, decay, coef, skip_row),
        [shape(*vectors(steps)), shape(*vectors(2 * modes))],
        [vmem(*flat), vmem(*front), vmem(*vectors(modes)), vmem((modes, width), f32)]
        + [vmem((1, width), f32), vmem(*vectors(steps)), vmem(*vectors(2 * modes))]
        + [dma((2, chunks)), dma((3,)), dma((2, chunks))],
        "within",
        cost_estimate=cost(66 * elements, 8 * elements),
    )

    (out,) = call(
        final_kernel,
        (entered, decay, enter, y, gate),
        [shape((tokens, width), bf16)],
        [vmem(*vectors(modes)), vmem(*vectors(2 * modes)), vmem(*vectors(steps))]
        + [vmem(*flat), tokens_buf, vmem((modes, tiles, LANES), f32), vmem(*vectors(modes))]
        + [vmem((2, BLOCK, LANES), bf16), dma((4, chunks)), dma((chunks,))],
        "final",
        near=(0,),
        cost_estimate=cost(40 * elements, 10 * elements),
    )
    return out


def solution(mesh):
    axes = tuple(mesh.axis_names)
    placed = (P(axes, None),) * 3 + (P(),) * 4
    return jax.shard_map(
        functools.partial(local, axes=axes),
        mesh=mesh,
        in_specs=placed,
        out_specs=P(axes, None),
        check_vma=False,
    )
```

time: 72.1 us -> 65.1 us (0.903)
  waiting for transfers between devices: 7.91 us -> 0.27 us
  starting transfers between devices: 10.2 us -> 15.4 us
  Pallas kernels: 48.8 us -> 46.2 us
  local copies, waits for them, and re-layouts: 3.55 us -> 1.41 us
    all_to_all x2, starting transfers between devices: 6.28 us -> 11.5 us  [swap(): return lax.all_to_all(value, axes, split_axis=0, concat_axis=0, tiled=True)]
    all_to_all x2, waiting for transfers between devices: 4.28 us -> 0.27 us  [swap(): return lax.all_to_all(value, axes, split_axis=0, concat_axis=0, tiled=True)]
    ppermute x1, waiting for transfers between devices: 3.63 us -> 0.01 us  [local(): lax.ppermute(packed, axes, [(at, at + 1) for at in range(devices - 1)])]
    pallas_call x7, Pallas kernels: 48.8 us -> 46.2 us  [call(): pl.pallas_call(kernel, in_specs=[pl.BlockSpec(memory_space=vmem) if at in...]
    unnamed x14 -> x10, local copies, waits for them, and re-layouts: 2.16 us -> 0.03 us
  transfers between devices with their start and end apart: 3 -> 3, of which waited for: 2 -> 1; matrix products, arithmetic and copies ran while one was open for 3% -> 4% of each run, Pallas kernels for 31% -> 48%
where the time goes in v4:
time: 65.1 us; the launch traced here: 64.4 us
  Pallas kernels  46.2 us (71%)
  starting transfers between devices  15.4 us (24%)
  local copies, waits for them, and re-layouts  1.41 us (2%)
  other arithmetic  0.93 us (1%)
    pallas_call x7, Pallas kernels, call(): pl.pallas_call(kernel, in_specs=[pl.BlockSpec(memory_space=vmem) if at in...  46.2 us
    all_to_all x2, starting transfers between devices, swap(): return lax.all_to_all(value, axes, split_axis=0, concat_axis=0, tiled=True)  11.5 us
    ppermute x1, starting transfers between devices, local(): lax.ppermute(packed, axes, [(at, at + 1) for at in range(devices - 1)])  3.95 us
  transfers between devices with their start and end apart: 3, of which 1 were waited for; matrix products, arithmetic and copies ran while one was open for 4% of the time, Pallas kernels for 48%

profile of v4, /device:TPU:1, one launch (start us, length us, event | category | flops | bytes accessed | tf_op | source)
XLA Modules:
  0.0 64.4 jit_solution(3931824976077660933)
XLA Ops:
  0.0 1.8 %pack.1 = bf16[24,4608]{1,0:T(8,128)(2,1)} custom-call(bf16[128,4608]{1,0:T(8,128)(2,1)} %key_ref.5, bf16[128,4608]{1,0:T(8,128)(2,1)} %value_ref.5, bf16[128,4608]{1,0:T(8,128)(2,1)} %query_ref.3), custom_call_target="tpu_custom_call" | custom-call | tf_op jit(solution)/shard_map/pack/pallas_call | solution.py:585
  1.8 3.9 %collective-permute-start = (bf16[24,4608]{1,0:T(8,128)(2,1)}, bf16[24,4608]{1,0:T(8,128)(2,1)S(1)}, u32[]{:S(2)}, u32[]{:S(2)}) collective-permute-start(bf16[24,4608]{1,0:T(8,128)(2,1)} %pack.1), channel_id=1, source_target_pairs={{0,1},{1,2},{2,3},{3,4},{4,5},{5,6},{6,7},{7,8},{8,9},{9,10},{10,1... | collective-permute-start | bytes 663560 | tf_op jit(solution)/shard_map/ppermute | solution.py:607
  5.8 0.0 copy-done.3
  5.8 0.1 reshape.3
  5.9 0.7 %copy.10 = f32[3,7,9,32]{3,1,0,2:T(8,128)} copy(f32[3,7,9,32]{3,2,1,0:T(8,128)S(1)} %reshape.3) | data formatting | bytes 48384 | tf_op jit(solution)/shard_map/reshape | solution.py:609
  6.6 13.8 %signal.1 = (bf16[9,512,128]{2,1,0:T(8,128)(2,1)}, f32[9,16,8,128]{3,2,1,0:T(8,128)}, f32[9,23,8,128]{3,2,1,0:T(8,128)}) custom-call(bf16[128,4608]{1,0:T(8,128)(2,1)} %key_ref.5, bf16[128,4608]{1,0:T(8,128)(2,1)} %value_ref.5, f32[9,3,7,32]{3,2,1,0:T(8,128)} %bitcast.3, f32[16,4608]{1,0:T(8,128)} %rate_ref.3), custom_call_target="tpu_custom_call" | custom-call | flops 35389440 | bytes 5898240 | tf_op jit(solution)/shard_map/signal/pallas_call | solution.py:585
  20.4 0.0 collective-permute-done.halo_ref
  20.4 0.0 copy-start
  20.4 0.0 copy-start.1
  20.4 0.0 copy-start.2
  20.4 2.8 %head.1 = (bf16[32,18,128]{2,1,0:T(8,128)(2,1)}, bf16[9,64,128]{2,1,0:T(8,128)(2,1)}) custom-call(bf16[128,4608]{1,0:T(8,128)(2,1)} %key_ref.5, bf16[128,4608]{1,0:T(8,128)(2,1)} %value_ref.5, bf16[24,4608]{1,0:T(8,128)(2,1)S(1)} %collective-permute-done.halo_ref, f32[9,23,8,128]{3,2,1,0:T(8,128)} %get-tuple-element.22.pair_ref), custom_call_target="tpu_custom_call" | custom-call | tf_op jit(solution)/shard_map/head/pallas_call | solution.py:585
  23.2 0.0 copy-done
  23.2 0.0 copy-start.4
  23.2 5.6 %all-to-all-start = ((bf16[32,18,128]{2,1,0:T(8,128)(2,1)}), bf16[32,18,128]{2,1,0:T(8,128)(2,1)S(1)}, u32[]{:S(2)}, u32[]{:S(2)}) async-start(bf16[32,18,128]{2,1,0:T(8,128)(2,1)} %get-tuple-element.24), calls=%async_computation | async-start | bytes 393216 | tf_op jit(solution)/shard_map/all_to_all | solution.py:654
  28.8 0.0 copy-done.1
  28.9 0.9 %sqrt_multiply_fusion.coef_ref = f32[16,4608]{1,0:T(8,128)} fusion(f32[16,4608]{1,0:T(8,128)S(1)} %copy-done.2, f32[16,4608]{1,0:T(8,128)S(1)} %copy-done.1), kind=kLoop, calls=%fused_computation | loop fusion | flops 294912 | bytes 884736 | tf_op jit(solution)/shard_map/mul | solution.py:640
  29.8 0.6 broadcast_in_dim.3.skip_ref
  30.4 8.6 %gate.1.gate_ref = bf16[9,512,128]{2,1,0:T(8,128)(2,1)} custom-call(bf16[128,4608]{1,0:T(8,128)(2,1)} %query_ref.3, bf16[24,4608]{1,0:T(8,128)(2,1)} %copy-done, f32[9,3,7,32]{3,2,1,0:T(8,128)} %bitcast.4), custom_call_target="tpu_custom_call" | custom-call | flops 8257536 | bytes 2359296 | tf_op jit(solution)/shard_map/gate/pallas_call | solution.py:585
  39.1 0.0 all-to-all-done.piece_ref
  39.1 1.8 %prefix.1 = bf16[32,18,128]{2,1,0:T(8,128)(2,1)} custom-call(bf16[32,18,128]{2,1,0:T(8,128)(2,1)S(1)} %all-to-all-done.piece_ref, f32[16,4608]{1,0:T(8,128)} %rate_ref.3), custom_call_target="tpu_custom_call" | custom-call | tf_op jit(solution)/shard_map/prefix/pallas_call | solution.py:585
  40.8 5.8 %all-to-all-start.1 = ((bf16[32,18,128]{2,1,0:T(8,128)(2,1)}), bf16[32,18,128]{2,1,0:T(8,128)(2,1)S(1)}, u32[]{:S(2)}, u32[]{:S(2)}) async-start(bf16[32,18,128]{2,1,0:T(8,128)(2,1)} %prefix.1), calls=%async_computation.1 | async-start | bytes 393216 | tf_op jit(solution)/shard_map/all_to_all | solution.py:654
  46.7 8.2 %within.1 = (f32[9,64,8,128]{3,2,1,0:T(8,128)}, f32[9,32,8,128]{3,2,1,0:T(8,128)}) custom-call(bf16[9,512,128]{2,1,0:T(8,128)(2,1)} %get-tuple-element.32.u_ref, bf16[9,64,128]{2,1,0:T(8,128)(2,1)} %get-tuple-element.33.head_ref, f32[9,16,8,128]{3,2,1,0:T(8,128)} %get-tuple-element.31.decay_ref, f32[16,4608]{1,0:T(8,128)} %sqrt_multiply_fusion.coef_ref, ...), custom_call_target="tpu_custom_call" | custom-call | flops 38928384 | bytes 4718592 | tf_op jit(solution)/shard_map/within/pallas_call | solution.py:585
  54.9 0.3 all-to-all-done.1.piece_ref
  55.1 9.2 %final.1 = bf16[128,4608]{1,0:T(8,128)(2,1)} custom-call(bf16[32,18,128]{2,1,0:T(8,128)(2,1)S(1)} %all-to-all-done.1.piece_ref, f32[9,16,8,128]{3,2,1,0:T(8,128)} %get-tuple-element.31.decay_ref, f32[9,32,8,128]{3,2,1,0:T(8,128)} %get-tuple-element.36.enter_ref, f32[9,64,8,128]{3,2,1,0:T(8,128)} %get-tuple-element.37.y_ref, bf16[9,512,128]{2,1,0:T(8,128)(2,1)} %gate.1.gate_ref), custom_call_target="tpu_custom_call" | custom-call | flops 23592960 | bytes 5898240 | tf_op jit(solution)/shard_map/final/pallas_call | solution.py:585
  (3 shorter events, 0.0 us)
Async XLA Ops:
  0.0 5.8 %copy-start.3 = (f32[3,7,288]{2,1,0:T(8,128)S(1)}, f32[3,7,288]{2,1,0:T(8,128)}, u32[]{:S(2)}) copy-start(f32[3,7,288]{2,1,0:T(8,128)} %param.10) | copy-start | bytes 72580
  1.8 18.6 %collective-permute-start = (bf16[24,4608]{1,0:T(8,128)(2,1)}, bf16[24,4608]{1,0:T(8,128)(2,1)S(1)}, u32[]{:S(2)}, u32[]{:S(2)}) collective-permute-start(bf16[24,4608]{1,0:T(8,128)(2,1)} %pack.1), channel_id=1, source_target_pairs={{0,1},{1,2},{2,3},{3,4},{4,5},{5,6},{6,7},{7,8},{8,9},{9,10},{10,1... | collective-permute-start | bytes 663560 | tf_op jit(solution)/shard_map/ppermute | solution.py:607
  20.4 2.8 %copy-start = (bf16[24,4608]{1,0:T(8,128)(2,1)}, bf16[24,4608]{1,0:T(8,128)(2,1)S(1)}, u32[]{:S(2)}) copy-start(bf16[24,4608]{1,0:T(8,128)(2,1)S(1)} %collective-permute-done.halo_ref) | copy-start | bytes 663556
  20.4 8.5 %copy-start.1 = (f32[16,4608]{1,0:T(8,128)S(1)}, f32[16,4608]{1,0:T(8,128)}, u32[]{:S(2)}) copy-start(f32[16,4608]{1,0:T(8,128)} %rate_ref.3) | copy-start | bytes 884740
  20.4 8.5 %copy-start.2 = (f32[16,4608]{1,0:T(8,128)S(1)}, f32[16,4608]{1,0:T(8,128)}, u32[]{:S(2)}) copy-start(f32[16,4608]{1,0:T(8,128)} %param.12) | copy-start | bytes 884740
  23.2 6.6 %copy-start.4 = (f32[4608]{0:T(1024)S(1)}, f32[4608]{0:T(1024)}, u32[]{:S(2)}) copy-start(f32[4608]{0:T(1024)} %param.13) | copy-start | bytes 55300
  23.2 15.8 %all-to-all-start = ((bf16[32,18,128]{2,1,0:T(8,128)(2,1)}), bf16[32,18,128]{2,1,0:T(8,128)(2,1)S(1)}, u32[]{:S(2)}, u32[]{:S(2)}) async-start(bf16[32,18,128]{2,1,0:T(8,128)(2,1)} %get-tuple-element.24), calls=%async_computation | async-start | bytes 393216 | tf_op jit(solution)/shard_map/all_to_all | solution.py:654
  40.8 14.3 %all-to-all-start.1 = ((bf16[32,18,128]{2,1,0:T(8,128)(2,1)}), bf16[32,18,128]{2,1,0:T(8,128)(2,1)S(1)}, u32[]{:S(2)}, u32[]{:S(2)}) async-start(bf16[32,18,128]{2,1,0:T(8,128)(2,1)} %prefix.1), calls=%async_computation.1 | async-start | bytes 393216 | tf_op jit(solution)/shard_map/all_to_all | solution.py:654

commit v5 on v0

v5 whole, which is shorter than its diff:
```python
import functools
import math

import jax
import jax.numpy as jnp
from jax import lax
from jax.experimental import pallas as pl
from jax.experimental.pallas import tpu as pltpu
from jax.sharding import PartitionSpec as P

LANES = 128
ROWS = 8
TILES = 4
CHUNK = TILES * LANES
AHEAD = 3
f32 = jnp.float32
bf16 = jnp.bfloat16


def put_tile(scratch, group, slot, tile):
    scratch[pl.ds((group * ROWS + slot) * ROWS, ROWS), :] = tile


def get_row(scratch, group, row):
    return scratch[pl.ds(group * ROWS * ROWS + row, ROWS, stride=ROWS), :]


def lanes_of(value, tile):
    return value[:, tile * LANES : (tile + 1) * LANES]


def tile_lanes(tile):
    return pl.ds(pl.multiple_of(tile * LANES, LANES), LANES)


def span(at):
    return pl.ds(pl.multiple_of(at * CHUNK, CHUNK), CHUNK)


def wide(row):
    return jnp.broadcast_to(row, (ROWS, LANES))


def sublane():
    return lax.broadcasted_iota(jnp.int32, (ROWS, LANES), 0)


def spread(row_of):
    slot = sublane() % TILES
    result = wide(row_of(TILES - 1))
    for tile in range(TILES - 1):
        result = jnp.where(slot == tile, wide(row_of(tile)), result)
    return result


def spread_rows(ref, at, rows):
    def one(row):
        return spread(lambda tile: ref[row : row + 1, tile_lanes(at * TILES + tile)])

    return [one(row) for row in rows]


def rounded(value):
    return value.astype(bf16).astype(f32)


def tiles_of(block):
    block = block.astype(f32)
    return [block[at : at + ROWS] for at in range(0, block.shape[0], ROWS)]


def shifted(now, last, by):
    turned = pltpu.roll(now, by, 0)
    return jnp.where(sublane() < by, last, turned), turned


def fir_step(tile, taps, past):
    one, kept = shifted(tile, past[0], 1)
    nested = taps[6] * tile
    after = [kept]
    for level in (4, 2, 0):
        moved, kept = shifted(nested, past[1 + level // 2], 2)
        after.insert(1, kept)
        nested = taps[level] * tile + taps[level + 1] * one + moved
    return nested, after


def fir_start():
    return [jnp.zeros((ROWS, LANES), f32)] * 4


def chunk_taps(wide_ref, at, member, tile, count):
    return [wide(wide_ref[at, member, lag : lag + 1, tile_lanes(tile)]) for lag in range(count)]


def widened(feat_ref, member, out_ref, position):
    chunks, _, taps, count = feat_ref.shape
    rows = [feat_ref[at, member] for at in range(chunks)]
    rows = [jnp.concatenate([row, jnp.zeros((ROWS - taps, count), f32)], axis=0) for row in rows]
    group = lax.broadcasted_iota(jnp.int32, (count, CHUNK), 0)
    lane = lax.broadcasted_iota(jnp.int32, (count, CHUNK), 1)
    pick = (group == lane // (CHUNK // count)).astype(f32).astype(bf16)
    parts, rest = [], jnp.concatenate(rows, axis=0)
    for _ in range(3):
        term = rest.astype(bf16)
        rest = rest - term.astype(f32)
        parts.append(jnp.dot(term, pick, preferred_element_type=f32))
    out_ref[:, position] = (parts[0] + parts[1] + parts[2]).reshape(chunks, ROWS, CHUNK)


def power(base, exponent):
    result = None
    while exponent:
        if exponent & 1:
            result = base if result is None else result * base
        base = base * base
        exponent >>= 1
    return result


def tree(terms):
    while len(terms) > 1:
        terms = [sum(terms[at + 1 : at + 2], terms[at]) for at in range(0, len(terms), 2)]
    return terms[0]


def start_all(copies):
    for copy in copies:
        copy.start()


def wait_all(copies):
    for copy in copies:
        copy.wait()


def begin(chunks, fetch):
    for at in range(min(AHEAD, chunks)):
        start_all(fetch(at))


def over_chunks(chunks, fetch, body, send):
    def one(at, _):
        @pl.when(at + AHEAD < chunks)
        def _():
            start_all(fetch(at + AHEAD))

        wait_all(fetch(at))
        body(at)
        start_all(send(at))
        return 0

    lax.fori_loop(0, chunks, one, 0)
    for at in range(chunks):
        wait_all(send(at))


def columns_in(pairs, sem):
    def fetch(at):
        return [
            pltpu.make_async_copy(ref.at[:, span(at)], buf.at[at], sem.at[member, at])
            for member, (ref, buf) in enumerate(pairs)
        ]

    return fetch


def columns_out(ref, buf, sem):
    return lambda at: [pltpu.make_async_copy(buf.at[at], ref.at[:, span(at)], sem.at[0, at])]


def pack_kernel(key_ref, value_ref, query_ref, out_ref, in_buf, in_sem):
    tokens = key_ref.shape[0]
    copies = [
        pltpu.make_async_copy(ref.at[pl.ds(tokens - 2 * ROWS, 2 * ROWS)], in_buf.at[at], in_sem.at[at])
        for at, ref in enumerate((key_ref, value_ref, query_ref))
    ]
    start_all(copies)
    wait_all(copies)
    tails = [in_buf[at].astype(f32)[ROWS:] for at in range(len(copies))]
    out_ref[...] = jnp.concatenate(tails, axis=0).astype(bf16)


def signal_kernel(key_ref, value_ref, feat_ref, rate_ref, u_ref, wide_ref, state_ref, *scratches):
    key_buf, value_buf, u_buf, power_scr, in_sem, out_sem = scratches
    chunks, tokens = u_buf.shape[:2]
    modes = rate_ref.shape[0]
    count = feat_ref.shape[2]
    fetch = columns_in(((key_ref, key_buf), (value_ref, value_buf)), in_sem)
    begin(chunks, fetch)
    for member in range(2):
        widened(feat_ref, member + 1, wide_ref, member)

    def chunk(at):
        through = jnp.exp(-rate_ref[:, span(at)])
        for level in range(4):
            power_scr[level] = through
            through = through * through

        def tile(number, _):
            lanes = tile_lanes(number)
            taps = [chunk_taps(wide_ref, at, member, number, count) for member in range(2)]
            past = [fir_start(), fir_start()]
            for pair in range(tokens // (2 * ROWS)):
                rows = slice(pair * 2 * ROWS, (pair + 1) * 2 * ROWS)
                sources = [tiles_of(buf[at, rows, lanes]) for buf in (key_buf, value_buf)]
                found = []
                for part in range(2):
                    both = []
                    for member in range(2):
                        value, past[member] = fir_step(sources[member][part], taps[member], past[member])
                        both.append(value)
                    u = both[0] * both[1]
                    if pair == 0 and part == 0:
                        u = jnp.where(sublane() < count - 1, 0.0, u)
                    found.append(u)
                u_buf[at, rows, lanes] = jnp.concatenate(found, axis=0).astype(bf16)
            return 0

        lax.fori_loop(0, TILES, tile, 0)

        def gather(number, _):
            lanes = tile_lanes(number)
            decay = [wide(power_scr[3, mode : mode + 1, lanes]) for mode in range(modes)]
            state = None
            for pair in range(tokens // (2 * ROWS)):
                for u in tiles_of(u_buf[at, pair * 2 * ROWS : (pair + 1) * 2 * ROWS, lanes]):
                    if state is None:
                        state = [u] * modes
                    else:
                        state = [decay[mode] * state[mode] + u for mode in range(modes)]
            for mode in range(modes):
                whole = state[mode]
                for level in (2, 1, 0):
                    factor = wide(power_scr[level, mode : mode + 1, lanes])
                    whole = factor * whole + pltpu.roll(whole, ROWS - (1 << level), 0)
                state_ref[mode, pl.ds(at * TILES + number, 1), :] = whole[:1]
            return 0

        lax.fori_loop(0, TILES, gather, 0)

    over_chunks(chunks, fetch, chunk, columns_out(u_ref, u_buf, out_sem))


def head_kernel(key_ref, value_ref, halo_ref, rate_ref, wide_ref, state_ref, out_ref, head_ref, *scratches, tokens, reach):
    front_buf, rate_scr, token_scr, total_scr, in_sem = scratches
    modes, tiles = state_ref.shape[:2]
    pieces, piece_rows = out_ref.shape[:2]
    copies = [
        pltpu.make_async_copy(ref.at[pl.ds(0, 2 * ROWS)], front_buf.at[member], in_sem.at[member])
        for member, ref in enumerate((key_ref, value_ref))
    ]
    start_all(copies)
    for group in range(modes // ROWS):
        for tile in range(tiles):
            rows = pl.ds((group * tiles + tile) * ROWS, ROWS)
            rate_scr[rows, :] = rate_ref[group * ROWS : (group + 1) * ROWS, tile * LANES : (tile + 1) * LANES]
    wait_all(copies)

    def one(tile, _):
        lanes = tile_lanes(tile)
        halo = tiles_of(halo_ref[:, lanes])
        parts = []
        for member in range(2):
            taps = chunk_taps(wide_ref, tile // TILES, member, tile % TILES, reach + 1)
            _, past = fir_step(halo[member], taps, fir_start())
            value, _ = fir_step(tiles_of(front_buf[member, :, lanes])[0], taps, past)
            parts.append(value)
        u = jnp.where(sublane() < reach, rounded(parts[0] * parts[1]), 0.0)
        token_scr[pl.ds(pl.multiple_of(tile * ROWS, ROWS), ROWS), :] = u
        head_ref[:, lanes] = jnp.concatenate([u, jnp.zeros((ROWS, LANES), f32)], axis=0).astype(bf16)
        return 0

    lax.fori_loop(0, tiles, one, 0)
    signals = [token_scr[pl.ds(row, tiles, stride=ROWS), :] for row in range(reach)]
    split = pieces // modes
    for mode in range(modes):
        start = mode // ROWS * tiles * ROWS + mode % ROWS
        decay = jnp.exp(-rate_scr[pl.ds(start, tiles, stride=ROWS), :])
        head = signals[0]
        for row in range(1, reach):
            head = decay * head + signals[row]
        total_scr[mode] = state_ref[mode] + power(decay, tokens - reach) * head
        for part in range(split):
            rows = total_scr[mode, part * piece_rows : (part + 1) * piece_rows, :]
            out_ref[mode * split + part] = rows.astype(out_ref.dtype)


def gate_kernel(query_ref, halo_ref, feat_ref, rate_ref, coef_ref, gate_ref, lead_ref, *scratches):
    query_buf, halo_buf, gate_buf, lead_buf, wide_scr, in_sem, small_sem, out_sem, lead_sem = scratches
    chunks, tokens = gate_buf.shape[:2]
    modes = rate_ref.shape[0]
    count = feat_ref.shape[2]
    fetch = columns_in(((query_ref, query_buf),), in_sem)
    halo_copy = pltpu.make_async_copy(halo_ref, halo_buf, small_sem.at[0])
    halo_copy.start()
    begin(chunks, fetch)
    widened(feat_ref, 0, wide_scr, 0)
    halo_copy.wait()
    steps = (sublane() + 1).astype(f32)

    def send(at):
        return [
            pltpu.make_async_copy(gate_buf.at[at], gate_ref.at[:, span(at)], out_sem.at[0, at]),
            pltpu.make_async_copy(lead_buf.at[at], lead_ref.at[at], lead_sem.at[at]),
        ]

    def chunk(at):
        def tile(number, _):
            lanes = tile_lanes(number)
            all_lanes = tile_lanes(at * TILES + number)
            taps = chunk_taps(wide_scr, at, 0, number, count)
            _, past = fir_step(tiles_of(halo_buf[:, all_lanes])[2], taps, fir_start())
            for pair in range(tokens // (2 * ROWS)):
                rows = slice(pair * 2 * ROWS, (pair + 1) * 2 * ROWS)
                found = []
                for source in tiles_of(query_buf[at, rows, lanes]):
                    value, past = fir_step(source, taps, past)
                    found.append(value)
                gate_buf[at, rows, lanes] = jnp.concatenate(found, axis=0).astype(bf16)
            for mode in range(modes):
                rate = wide(rate_ref[mode : mode + 1, all_lanes])
                coef = wide(coef_ref[mode : mode + 1, all_lanes])
                lead_buf[at, number * modes + mode] = coef * jnp.exp(-rate * steps)
            return 0

        lax.fori_loop(0, TILES, tile, 0)

    over_chunks(chunks, fetch, chunk, send)


def prefix_kernel(piece_ref, rate_ref, out_ref, table_scr, *, tokens, axes):
    devices, piece_rows = piece_ref.shape[:2]
    split = devices // rate_ref.shape[0]
    mine = lax.axis_index(axes)
    mode, part = mine // split, mine % split
    group = pl.multiple_of(mode // ROWS * ROWS, ROWS)
    first = pl.multiple_of(part * piece_rows * LANES, LANES)
    rows = rate_ref[pl.ds(group, ROWS), pl.ds(first, piece_rows * LANES)]
    here = lax.broadcasted_iota(jnp.int32, rows.shape, 0) == mode - group
    rate = jnp.sum(jnp.where(here, rows, 0.0), axis=0, keepdims=True)
    for row in range(piece_rows):
        table_scr[row : row + 1, :] = lanes_of(rate, row)
    through = jnp.exp(-float(tokens) * table_scr[:piece_rows, :])

    def lap(number, entering):
        for step in range(4):
            source = number * 4 + step
            out_ref[source] = entering.astype(out_ref.dtype)
            entering = through * entering + piece_ref[source].astype(f32)
        return entering

    lax.fori_loop(0, devices // 4, lap, jnp.zeros((piece_rows, LANES), f32))


def local_kernel(u_ref, head_ref, rate_ref, coef_ref, skip_ref, y_ref, mid_ref, *scratches):
    u_buf, y_buf, mid_buf, token_scr, sum_scr, in_sem, out_sem, mid_sem = scratches
    chunks, tokens = u_buf.shape[:2]
    modes = rate_ref.shape[0]
    half_groups = tokens // ROWS // 2
    fetch = columns_in(((u_ref, u_buf),), in_sem)
    begin(chunks, fetch)

    def send(at):
        return [
            pltpu.make_async_copy(y_buf.at[at], y_ref.at[:, span(at)], out_sem.at[0, at]),
            pltpu.make_async_copy(mid_buf.at[at], mid_ref.at[at], mid_sem.at[at]),
        ]

    def chunk(at):
        front = u_buf[at, : 2 * ROWS].astype(f32) + head_ref[:, span(at)].astype(f32)
        u_buf[at, : 2 * ROWS] = front.astype(bf16)
        for pair in range(half_groups):
            block = u_buf[at, pair * 2 * ROWS : (pair + 1) * 2 * ROWS, :].astype(f32)
            for part in range(2):
                group = pair * 2 + part
                half, within = group // half_groups, group % half_groups
                for tile in range(TILES):
                    piece = lanes_of(block, tile)[part * ROWS : (part + 1) * ROWS]
                    put_tile(token_scr, within, half * TILES + tile, piece)
        (skip,) = spread_rows(skip_ref, at, range(1))
        for first in range(0, modes, ROWS):
            some = range(first, first + ROWS)
            coef = spread_rows(coef_ref, at, some)
            decay = [jnp.exp(-rate) for rate in spread_rows(rate_ref, at, some)]

            def eight(group, state):
                state = list(state)
                for row in range(ROWS):
                    u = get_row(token_scr, group, row)
                    state = [factor * one + u for factor, one in zip(decay, state)]
                    terms = [factor * one for factor, one in zip(coef, state)]
                    place = pl.ds(group * ROWS * ROWS + row, ROWS, stride=ROWS)
                    so_far = skip * u if first == 0 else sum_scr[place, :]
                    sum_scr[place, :] = so_far + tree(terms)
                return tuple(state)

            state = lax.fori_loop(0, half_groups, eight, (jnp.zeros((ROWS, LANES), f32),) * ROWS)
            for at_mode, one in zip(some, state):
                mid_buf[at, at_mode] = one
        for group in range(2 * half_groups):
            half, within = group // half_groups, group % half_groups
            for tile in range(TILES):
                slot = (within * ROWS + half * TILES + tile) * ROWS
                rows = slice(group * ROWS, (group + 1) * ROWS)
                y_buf[at, rows, tile * LANES : (tile + 1) * LANES] = sum_scr[pl.ds(slot, ROWS), :]

    over_chunks(chunks, fetch, chunk, send)


def final_kernel(piece_ref, rate_ref, lead_ref, mid_ref, y_ref, gate_ref, out_ref, *scratches):
    lead_buf, mid_buf, y_buf, gate_buf, out_buf, total_scr, power_scr, in_sem, wide_sem, out_sem = scratches
    chunks, modes = mid_buf.shape[:2]
    tokens = y_buf.shape[1]
    columns = columns_in(((y_ref, y_buf), (gate_ref, gate_buf)), in_sem)

    def fetch(at):
        return columns(at) + [
            pltpu.make_async_copy(ref.at[at], buf.at[at], wide_sem.at[member, at])
            for member, (ref, buf) in enumerate(((lead_ref, lead_buf), (mid_ref, mid_buf)))
        ]

    begin(chunks, fetch)
    pieces, piece_rows = piece_ref.shape[:2]
    split = pieces // modes
    for mode in range(modes):
        for part in range(split):
            rows = piece_ref[mode * split + part].astype(f32)
            total_scr[mode, part * piece_rows : (part + 1) * piece_rows, :] = rows

    def chunk(at):
        power_scr[...] = jnp.exp(-float(ROWS) * rate_ref[:, span(at)])

        def tile(number, _):
            lanes = tile_lanes(number)
            decay = [wide(power_scr[mode : mode + 1, lanes]) for mode in range(modes)]
            state = [
                lead_buf[at, number * modes + mode] * wide(total_scr[mode, pl.ds(at * TILES + number, 1), :])
                for mode in range(modes)
            ]
            for pair in range(tokens // (2 * ROWS)):
                rows = slice(pair * 2 * ROWS, (pair + 1) * 2 * ROWS)
                gates = gate_buf[at, rows, lanes].astype(f32)
                sums = []
                for part in range(2):
                    if pair == tokens // (4 * ROWS) and part == 0:
                        state = [
                            one + lead_buf[at, number * modes + mode] * wide(mid_buf[at, mode, pl.ds(number, 1), :])
                            for mode, one in enumerate(state)
                        ]
                    here = slice((pair * 2 + part) * ROWS, (pair * 2 + part + 1) * ROWS)
                    sums.append(y_buf[at, here, lanes] + tree(state))
                    state = [factor * one for factor, one in zip(decay, state)]
                out_buf[at, rows, lanes] = (gates * rounded(jnp.concatenate(sums, axis=0))).astype(bf16)
            return 0

        lax.fori_loop(0, TILES, tile, 0)

    over_chunks(chunks, fetch, chunk, columns_out(out_ref, out_buf, out_sem))


def cost(flops, moved):
    return pl.CostEstimate(flops=int(flops), bytes_accessed=int(moved), transcendentals=0)


def local(query, key_proj, value_proj, featurizer, rates, residues, skip, *, axes):
    tokens, width = query.shape
    modes = rates.shape[0]
    members, taps, groups = featurizer.shape
    devices = math.prod(lax.axis_size(axis) for axis in axes)
    chunks = width // CHUNK
    tiles = width // LANES
    split = devices // modes
    even = devices % modes == 0 and tiles % split == 0
    vmem = pltpu.VMEM
    far = pltpu.HBM
    near = jax.ShapeDtypeStruct
    dma = pltpu.SemaphoreType.DMA
    elements = tokens * width

    def call(kernel, inputs, outputs, scratches, name, close=(), **more):
        inputs = [
            value if at in close else pltpu.with_memory_space_constraint(value, far)
            for at, value in enumerate(inputs)
        ]
        beside, there = pl.BlockSpec(memory_space=vmem), pl.BlockSpec(memory_space=far)
        return pl.pallas_call(
            kernel,
            in_specs=[beside if at in close else there for at in range(len(inputs))],
            out_specs=[beside if isinstance(one, near) else there for one in outputs],
            out_shape=outputs,
            scratch_shapes=scratches,
            compiler_params=pltpu.CompilerParams(vmem_limit_bytes=32 * 2**20),
            name=name,
            **more,
        )(*inputs)

    (packed,) = call(
        pack_kernel,
        (key_proj, value_proj, query),
        [near((members * ROWS, width), bf16)],
        [vmem((members, 2 * ROWS, width), bf16), dma((members,))],
        "pack",
    )
    halo = lax.ppermute(packed, axes, [(at, at + 1) for at in range(devices - 1)])

    feat = featurizer.reshape(members, taps, chunks, groups // chunks).transpose(2, 0, 1, 3)
    half_buf, whole_buf = vmem((chunks, tokens, CHUNK), bf16), vmem((chunks, tokens, CHUNK), f32)
    u, wide_taps, state = call(
        signal_kernel,
        (key_proj, value_proj, feat, rates),
        [far((tokens, width), bf16), near((chunks, 2, ROWS, CHUNK), f32), near((modes, tiles, LANES), f32)],
        [half_buf, half_buf, half_buf, vmem((4, modes, CHUNK), f32), dma((2, chunks)), dma((1, chunks))],
        "signal",
        close=(2, 3),
        cost_estimate=cost(60 * elements, 10 * elements),
    )

    pieces = (modes * split, tiles // split, LANES) if even else (modes, tiles, LANES)
    left, head = call(
        functools.partial(head_kernel, tokens=tokens, reach=taps - 1),
        (key_proj, value_proj, halo, rates, wide_taps, state),
        [near(pieces, bf16), near((2 * ROWS, width), bf16)],
        [vmem((2, 2 * ROWS, width), bf16), vmem((modes * tiles, LANES), f32)]
        + [vmem((tiles * ROWS, LANES), f32), vmem((modes, tiles, LANES), f32), dma((2,))],
        "head",
        close=(2, 3, 4, 5),
    )
    left, halo_late, rates_late, skip_late = lax.optimization_barrier((left, halo, rates, skip))
    coef = residues * jnp.sqrt(-jnp.expm1(-2.0 * rates_late) / modes)
    skip_row = skip_late[None, :]
    gate, lead = call(
        gate_kernel,
        (query, halo_late, feat, rates, coef),
        [far((tokens, width), bf16), far((chunks, TILES * modes, ROWS, LANES), f32)],
        [half_buf, vmem((members * ROWS, width), bf16), half_buf]
        + [vmem((chunks, TILES * modes, ROWS, LANES), f32), vmem((chunks, 1, ROWS, CHUNK), f32)]
        + [dma((1, chunks)), dma((1,)), dma((1, chunks)), dma((chunks,))],
        "gate",
        close=(2, 3, 4),
        cost_estimate=cost(30 * elements, 8 * elements),
    )

    def swap(value):
        return lax.all_to_all(value, axes, split_axis=0, concat_axis=0, tiled=True)

    share = modes * width // devices
    theirs = swap(left if even else left.reshape(devices, share))
    theirs, gate, lead, coef, skip_row = lax.optimization_barrier((theirs, gate, lead, coef, skip_row))
    if even:
        (entering,) = call(
            functools.partial(prefix_kernel, tokens=tokens, axes=axes),
            (theirs, rates),
            [near(pieces, bf16)],
            [vmem((-(-pieces[1] // ROWS) * ROWS, LANES), f32)],
            "prefix",
            close=(0, 1),
        )
    else:
        mine = lax.axis_index(axes)
        through = jnp.exp(-float(tokens) * lax.dynamic_slice_in_dim(rates.reshape(-1), mine * share, share))
        _, entering = lax.scan(
            lambda so_far, piece: (through * so_far + piece.astype(f32), so_far.astype(bf16)),
            jnp.zeros((share,), f32),
            theirs,
        )

    entering, u_late = lax.optimization_barrier((entering, u))
    entered = swap(entering).reshape(pieces)
    stage = vmem((tokens // ROWS // 2 * ROWS * ROWS, LANES), f32)
    y, mid = call(
        local_kernel,
        (u_late, head, rates, coef, skip_row),
        [far((tokens, width), f32), far((chunks, modes, ROWS, LANES), f32)],
        [half_buf, whole_buf, vmem((chunks, modes, ROWS, LANES), f32), stage, stage]
        + [dma((1, chunks)), dma((1, chunks)), dma((chunks,))],
        "within",
        close=(1, 2, 3, 4),
        cost_estimate=cost(66 * elements, 8 * elements),
    )

    (out,) = call(
        final_kernel,
        (entered, rates, lead, mid, y, gate),
        [far((tokens, width), bf16)],
        [vmem((chunks, TILES * modes, ROWS, LANES), f32), vmem((chunks, modes, ROWS, LANES), f32)]
        + [whole_buf, half_buf, half_buf, vmem((modes, tiles, LANES), f32), vmem((modes, CHUNK), f32)]
        + [dma((2, chunks)), dma((2, chunks)), dma((1, chunks))],
        "final",
        close=(0, 1),
        cost_estimate=cost(40 * elements, 10 * elements),
    )
    return out


def solution(mesh):
    axes = tuple(mesh.axis_names)
    placed = (P(axes, None),) * 3 + (P(),) * 4
    return jax.shard_map(
        functools.partial(local, axes=axes),
        mesh=mesh,
        in_specs=placed,
        out_specs=P(axes, None),
        check_vma=False,
    )
```

time: 373 us -> 51.2 us (0.14); the launches traced: 366 us -> 50.4 us
  local copies, waits for them, and re-layouts: 189 us -> 0.16 us
  matrix products: 61.3 us -> 0 us
  other arithmetic: 47.9 us -> 0.19 us
  Pallas kernels: 0 us -> 34.1 us
  waiting for transfers between devices: 30.2 us -> 3.12 us
  blocking collectives: 12.5 us -> 0 us
  starting transfers between devices: 20 us -> 12.7 us
  loops' own time: 5.22 us -> 0 us
    dot_general x36 -> x0, matrix products: 61.3 us -> none  [the longest x9 21.9 us: modal_local(): carried = jnp.einsum('icr,bcr->bic', leading, entering, precision=precise)]
    convert_element_type x4 -> x0, other arithmetic: 37.1 us -> none  [the longest x1 23.8 us: local(): signal_half = (featured[1] * featured[2]).astype(jnp.bfloat16)]
    pallas_call x0 -> x7, Pallas kernels: none -> 34.1 us  [call(): pl.pallas_call(kernel, in_specs=[beside if at in close else there for at...]
    gather x18 -> x0, local copies, waits for them, and re-layouts: 33.6 us -> none  [modal_local(): kernel[jnp.maximum(lag_table, 0)]]
    dynamic_slice x50 -> x0, local copies, waits for them, and re-layouts: 30 us -> none  [the longest x45 26.5 us: modal_all(): lax.map(modal_one_block, (pieces, decay_rate.reshape(block_total, chan_bl...]
    dynamic_update_slice x36 -> x0, local copies, waits for them, and re-layouts: 28.3 us -> none  [modal_all(): lax.map(modal_one_block, (pieces, decay_rate.reshape(block_total, chan_bl...]
    broadcast_in_dim x51 -> x1, local copies, waits for them, and re-layouts: 24.7 us -> 0.01 us  [local(): skip_row = skip_late[None, :]]
    mul x36 -> x0, local copies, waits for them, and re-layouts: 15.4 us -> none  [the longest x9 7.01 us: incoming_one_block(): coef_part[None] * jnp.exp(-rate_part[None] * (offsets[:, None, None] + 1.0))]
  transfers between devices with their start and end apart: 5 -> 3, of which waited for: 2 -> 1; matrix products, arithmetic and copies ran while one was open for 15% -> 1% of each run, Pallas kernels for 0% -> 46%
where the time goes in v5:
time: 51.2 us; the launch traced here: 50.4 us
  Pallas kernels  34.1 us (67%)
  starting transfers between devices  12.7 us (25%)
  waiting for transfers between devices  3.12 us (6%)
    pallas_call x7, Pallas kernels, call(): pl.pallas_call(kernel, in_specs=[beside if at in close else there for at...  34.1 us
    all_to_all x2, starting transfers between devices, swap(): return lax.all_to_all(value, axes, split_axis=0, concat_axis=0, tiled=True)  8.77 us
    ppermute x1, starting transfers between devices, local(): lax.ppermute(packed, axes, [(at, at + 1) for at in range(devices - 1)])  3.95 us
    all_to_all x2, waiting for transfers between devices, swap(): return lax.all_to_all(value, axes, split_axis=0, concat_axis=0, tiled=True)  3.12 us
  transfers between devices with their start and end apart: 3, of which 1 were waited for; matrix products, arithmetic and copies ran while one was open for 1% of the time, Pallas kernels for 46%

profile of v5, /device:TPU:1, one launch (start us, length us, event | category | flops | bytes accessed | tf_op | source)
XLA Modules:
  0.0 50.4 jit_solution(5353143601558789287)
XLA Ops:
  0.0 0.0 copy-start.3
  0.0 1.1 %pack.1 = bf16[24,4608]{1,0:T(8,128)(2,1)S(1)} custom-call(bf16[128,4608]{1,0:T(8,128)(2,1)} %key_ref.5, bf16[128,4608]{1,0:T(8,128)(2,1)} %value_ref.5, bf16[128,4608]{1,0:T(8,128)(2,1)} %query_ref.3), custom_call_target="tpu_custom_call" | custom-call | tf_op jit(solution)/shard_map/pack/pallas_call | solution.py:487
  1.1 3.9 %collective-permute-start = (bf16[24,4608]{1,0:T(8,128)(2,1)S(1)}, bf16[24,4608]{1,0:T(8,128)(2,1)S(1)}, u32[]{:S(2)}, u32[]{:S(2)}) collective-permute-start(bf16[24,4608]{1,0:T(8,128)(2,1)S(1)} %pack.1), channel_id=1, source_target_pairs={{0,1},{1,2},{2,3},{3,4},{4,5},{5,6},{6,7},{7,8},{8,9},{9,10},{10,1... | collective-permute-start | bytes 663560 | tf_op jit(solution)/shard_map/ppermute | solution.py:505
  5.1 0.0 copy-done.3
  5.1 0.1 reshape.3
  5.3 0.0 copy-done
  5.3 9.4 %signal.1 = (bf16[128,4608]{1,0:T(8,128)(2,1)}, f32[9,2,8,512]{3,2,1,0:T(8,128)S(1)}, f32[16,36,128]{2,1,0:T(8,128)S(1)}) custom-call(bf16[128,4608]{1,0:T(8,128)(2,1)} %key_ref.5, bf16[128,4608]{1,0:T(8,128)(2,1)} %value_ref.5, f32[9,3,7,32]{3,2,1,0:T(8,128)S(1)} %bitcast.3, f32[16,4608]{1,0:T(8,128)S(1)} %copy-done), custom_call_target="tpu_custom_call" | custom-call | flops 35389440 | bytes 5898240 | tf_op jit(solution)/shard_map/signal/pallas_call | solution.py:487
  14.7 0.0 collective-permute-done.halo_ref
  14.7 0.0 copy-start.1
  14.7 0.0 copy-start.2
  14.7 3.1 %head.1 = (bf16[32,18,128]{2,1,0:T(8,128)(2,1)}, bf16[16,4608]{1,0:T(8,128)(2,1)S(1)}) custom-call(bf16[128,4608]{1,0:T(8,128)(2,1)} %key_ref.5, bf16[128,4608]{1,0:T(8,128)(2,1)} %value_ref.5, bf16[24,4608]{1,0:T(8,128)(2,1)S(1)} %collective-permute-done.halo_ref, f32[16,4608]{1,0:T(8,128)S(1)} %copy-done, f32[9,2,8,512]{3,2,1,0:T(8,128)S(1)} %get-tuple-element.25.wide_ref, ...), custom_call_target="tpu_custom_call" | custom-call | tf_op jit(solution)/shard_map/head/pallas_call | solution.py:487
  17.8 0.0 copy-done.1
  17.8 0.0 copy-start.4
  17.8 5.6 %all-to-all-start = ((bf16[32,18,128]{2,1,0:T(8,128)(2,1)}), bf16[32,18,128]{2,1,0:T(8,128)(2,1)S(1)}, u32[]{:S(2)}, u32[]{:S(2)}) async-start(bf16[32,18,128]{2,1,0:T(8,128)(2,1)} %get-tuple-element.28), calls=%async_computation | async-start | bytes 393216 | tf_op jit(solution)/shard_map/all_to_all | solution.py:545
  23.5 0.0 copy-done.2
  23.5 0.2 sqrt_multiply_fusion.coef_ref
  23.7 0.0 copy-done.4
  23.7 5.1 %gate.1 = (bf16[128,4608]{1,0:T(8,128)(2,1)}, f32[9,64,8,128]{3,2,1,0:T(8,128)}) custom-call(bf16[128,4608]{1,0:T(8,128)(2,1)} %query_ref.3, bf16[24,4608]{1,0:T(8,128)(2,1)} %copy-done.1, f32[9,3,7,32]{3,2,1,0:T(8,128)S(1)} %bitcast.4, f32[16,4608]{1,0:T(8,128)S(1)} %copy-done, f32[16,4608]{1,0:T(8,128)S(1)} %sqrt_multiply_fusion.coef_ref), custom_call_target="tpu_custom_call" | custom-call | flops 17694720 | bytes 4718592 | tf_op jit(solution)/shard_map/gate/pallas_call | solution.py:487
  28.8 3.1 %all-to-all-done.piece_ref = bf16[32,18,128]{2,1,0:T(8,128)(2,1)S(1)} async-done(((bf16[32,18,128]{2,1,0:T(8,128)(2,1)}), bf16[32,18,128]{2,1,0:T(8,128)(2,1)S(1)}, u32[]{:S(2)}, u32[]{:S(2)}) %all-to-all-start) | async-done | bytes 147488 | tf_op jit(solution)/shard_map/all_to_all | solution.py:545
  31.9 0.8 %prefix.1 = bf16[32,18,128]{2,1,0:T(8,128)(2,1)} custom-call(bf16[32,18,128]{2,1,0:T(8,128)(2,1)S(1)} %all-to-all-done.piece_ref, f32[16,4608]{1,0:T(8,128)S(1)} %copy-done), custom_call_target="tpu_custom_call" | custom-call | tf_op jit(solution)/shard_map/prefix/pallas_call | solution.py:487
  32.7 3.1 %all-to-all-start.1 = ((bf16[32,18,128]{2,1,0:T(8,128)(2,1)}), bf16[32,18,128]{2,1,0:T(8,128)(2,1)S(1)}, u32[]{:S(2)}, u32[]{:S(2)}) async-start(bf16[32,18,128]{2,1,0:T(8,128)(2,1)} %prefix.1), calls=%async_computation.1 | async-start | bytes 393216 | tf_op jit(solution)/shard_map/all_to_all | solution.py:545
  35.9 8.8 %within.1 = (f32[128,4608]{1,0:T(8,128)}, f32[9,16,8,128]{3,2,1,0:T(8,128)}) custom-call(bf16[128,4608]{1,0:T(8,128)(2,1)} %get-tuple-element.38.u_ref, bf16[16,4608]{1,0:T(8,128)(2,1)S(1)} %get-tuple-element.39.head_ref, f32[16,4608]{1,0:T(8,128)S(1)} %copy-done, f32[16,4608]{1,0:T(8,128)S(1)} %sqrt_multiply_fusion.coef_ref, ...), custom_call_target="tpu_custom_call" | custom-call | flops 38928384 | bytes 4718592 | tf_op jit(solution)/shard_map/within/pallas_call | solution.py:487
  44.7 0.0 all-to-all-done.1.piece_ref
  44.7 5.7 %final.1 = bf16[128,4608]{1,0:T(8,128)(2,1)} custom-call(bf16[32,18,128]{2,1,0:T(8,128)(2,1)S(1)} %all-to-all-done.1.piece_ref, f32[16,4608]{1,0:T(8,128)S(1)} %copy-done, f32[9,64,8,128]{3,2,1,0:T(8,128)} %get-tuple-element.37.lead_ref, f32[9,16,8,128]{3,2,1,0:T(8,128)} %get-tuple-element.42.mid_ref, f32[128,4608]{1,0:T(8,128)} %get-tuple-element.43.y_ref, ...), custom_call_target="tpu_custom_call" | custom-call | flops 23592960 | bytes 5898240 | tf_op jit(solution)/shard_map/final/pallas_call | solution.py:487
  (3 shorter events, 0.1 us)
Async XLA Ops:
  0.0 5.1 %copy-start.3 = (f32[3,7,288]{2,1,0:T(8,128)S(1)}, f32[3,7,288]{2,1,0:T(8,128)}, u32[]{:S(2)}) copy-start(f32[3,7,288]{2,1,0:T(8,128)} %param.10) | copy-start | bytes 72580
  0.0 5.3 %copy-start = (f32[16,4608]{1,0:T(8,128)S(1)}, f32[16,4608]{1,0:T(8,128)}, u32[]{:S(2)}) copy-start(f32[16,4608]{1,0:T(8,128)} %rate_ref.11) | copy-start | bytes 884740
  1.1 13.5 %collective-permute-start = (bf16[24,4608]{1,0:T(8,128)(2,1)S(1)}, bf16[24,4608]{1,0:T(8,128)(2,1)S(1)}, u32[]{:S(2)}, u32[]{:S(2)}) collective-permute-start(bf16[24,4608]{1,0:T(8,128)(2,1)S(1)} %pack.1), channel_id=1, source_target_pairs={{0,1},{1,2},{2,3},{3,4},{4,5},{5,6},{6,7},{7,8},{8,9},{9,10},{10,1... | collective-permute-start | bytes 663560 | tf_op jit(solution)/shard_map/ppermute | solution.py:505
  14.7 3.1 %copy-start.1 = (bf16[24,4608]{1,0:T(8,128)(2,1)}, bf16[24,4608]{1,0:T(8,128)(2,1)S(1)}, u32[]{:S(2)}) copy-start(bf16[24,4608]{1,0:T(8,128)(2,1)S(1)} %collective-permute-done.halo_ref) | copy-start | bytes 663556
  14.7 8.8 %copy-start.2 = (f32[16,4608]{1,0:T(8,128)S(1)}, f32[16,4608]{1,0:T(8,128)}, u32[]{:S(2)}) copy-start(f32[16,4608]{1,0:T(8,128)} %param.12) | copy-start | bytes 884740
  17.8 5.8 %copy-start.4 = (f32[4608]{0:T(1024)S(1)}, f32[4608]{0:T(1024)}, u32[]{:S(2)}) copy-start(f32[4608]{0:T(1024)} %param.13) | copy-start | bytes 55300
  17.8 14.1 %all-to-all-start = ((bf16[32,18,128]{2,1,0:T(8,128)(2,1)}), bf16[32,18,128]{2,1,0:T(8,128)(2,1)S(1)}, u32[]{:S(2)}, u32[]{:S(2)}) async-start(bf16[32,18,128]{2,1,0:T(8,128)(2,1)} %get-tuple-element.28), calls=%async_computation | async-start | bytes 393216 | tf_op jit(solution)/shard_map/all_to_all | solution.py:545
  32.7 12.0 %all-to-all-start.1 = ((bf16[32,18,128]{2,1,0:T(8,128)(2,1)}), bf16[32,18,128]{2,1,0:T(8,128)(2,1)S(1)}, u32[]{:S(2)}, u32[]{:S(2)}) async-start(bf16[32,18,128]{2,1,0:T(8,128)(2,1)} %prefix.1), calls=%async_computation.1 | async-start | bytes 393216 | tf_op jit(solution)/shard_map/all_to_all | solution.py:545

commit v6 on v5

--- a/solution.py
+++ b/solution.py
@@ -69,24 +69,17 @@
     return [block[at : at + ROWS] for at in range(0, block.shape[0], ROWS)]
 
 
-def shifted(now, last, by):
-    turned = pltpu.roll(now, by, 0)
-    return jnp.where(sublane() < by, last, turned), turned
-
-
-def fir_step(tile, taps, past):
-    one, kept = shifted(tile, past[0], 1)
-    nested = taps[6] * tile
-    after = [kept]
-    for level in (4, 2, 0):
-        moved, kept = shifted(nested, past[1 + level // 2], 2)
-        after.insert(1, kept)
-        nested = taps[level] * tile + taps[level + 1] * one + moved
-    return nested, after
-
-
-def fir_start():
-    return [jnp.zeros((ROWS, LANES), f32)] * 4
+def fir(column, taps, first):
+    total = taps[0] * column[pl.ds(first, ROWS), :]
+    for lag in range(1, len(taps)):
+        total = total + taps[lag] * column[pl.ds(first - lag, ROWS), :]
+    return total
+
+
+def lay_column(column, source, lanes):
+    for pair in range(source.shape[0] // (2 * ROWS)):
+        rows = slice(pair * 2 * ROWS, (pair + 1) * 2 * ROWS)
+        column[pl.ds(ROWS + pair * 2 * ROWS, 2 * ROWS), :] = source[rows, lanes].astype(f32)
 
 
 def chunk_taps(wide_ref, at, member, tile, count):
@@ -182,7 +175,7 @@
 
 
 def signal_kernel(key_ref, value_ref, feat_ref, rate_ref, u_ref, wide_ref, state_ref, *scratches):
-    key_buf, value_buf, u_buf, power_scr, in_sem, out_sem = scratches
+    key_buf, value_buf, u_buf, power_scr, *columns, in_sem, out_sem = scratches
     chunks, tokens = u_buf.shape[:2]
     modes = rate_ref.shape[0]
     count = feat_ref.shape[2]
@@ -200,20 +193,15 @@
         def tile(number, _):
             lanes = tile_lanes(number)
             taps = [chunk_taps(wide_ref, at, member, number, count) for member in range(2)]
-            past = [fir_start(), fir_start()]
+            for column, buf in zip(columns, (key_buf, value_buf)):
+                column[pl.ds(0, ROWS), :] = jnp.zeros((ROWS, LANES), f32)
+                lay_column(column, buf.at[at], lanes)
             for pair in range(tokens // (2 * ROWS)):
+                found = []
+                for first in (pair * 2 * ROWS + ROWS, pair * 2 * ROWS + 2 * ROWS):
+                    u = fir(columns[0], taps[0], first) * fir(columns[1], taps[1], first)
+                    found.append(jnp.where(sublane() < count - 1, 0.0, u) if first == ROWS else u)
                 rows = slice(pair * 2 * ROWS, (pair + 1) * 2 * ROWS)
-                sources = [tiles_of(buf[at, rows, lanes]) for buf in (key_buf, value_buf)]
-                found = []
-                for part in range(2):
-                    both = []
-                    for member in range(2):
-                        value, past[member] = fir_step(sources[member][part], taps[member], past[member])
-                        both.append(value)
-                    u = both[0] * both[1]
-                    if pair == 0 and part == 0:
-                        u = jnp.where(sublane() < count - 1, 0.0, u)
-                    found.append(u)
                 u_buf[at, rows, lanes] = jnp.concatenate(found, axis=0).astype(bf16)
             return 0
 
@@ -243,7 +231,7 @@
 
 
 def head_kernel(key_ref, value_ref, halo_ref, rate_ref, wide_ref, state_ref, out_ref, head_ref, *scratches, tokens, reach):
-    front_buf, rate_scr, token_scr, total_scr, in_sem = scratches
+    front_buf, rate_scr, column_scr, token_scr, total_scr, in_sem = scratches
     modes, tiles = state_ref.shape[:2]
     pieces, piece_rows = out_ref.shape[:2]
     copies = [
@@ -257,21 +245,23 @@
             rate_scr[rows, :] = rate_ref[group * ROWS : (group + 1) * ROWS, tile * LANES : (tile + 1) * LANES]
     wait_all(copies)
 
-    def one(tile, _):
-        lanes = tile_lanes(tile)
-        halo = tiles_of(halo_ref[:, lanes])
-        parts = []
-        for member in range(2):
-            taps = chunk_taps(wide_ref, tile // TILES, member, tile % TILES, reach + 1)
-            _, past = fir_step(halo[member], taps, fir_start())
-            value, _ = fir_step(tiles_of(front_buf[member, :, lanes])[0], taps, past)
-            parts.append(value)
-        u = jnp.where(sublane() < reach, rounded(parts[0] * parts[1]), 0.0)
-        token_scr[pl.ds(pl.multiple_of(tile * ROWS, ROWS), ROWS), :] = u
-        head_ref[:, lanes] = jnp.concatenate([u, jnp.zeros((ROWS, LANES), f32)], axis=0).astype(bf16)
+    def some(chunk, _):
+        for number in range(TILES):
+            lanes = tile_lanes(chunk * TILES + number)
+            halo = halo_ref[:, lanes].astype(f32)
+            parts = []
+            for member in range(2):
+                taps = chunk_taps(wide_ref, chunk, member, number, reach + 1)
+                column = column_scr.at[number, member]
+                column[pl.ds(0, ROWS), :] = halo[member * ROWS : (member + 1) * ROWS]
+                column[pl.ds(ROWS, ROWS), :] = front_buf[member, :, lanes].astype(f32)[:ROWS]
+                parts.append(fir(column, taps, ROWS))
+            u = jnp.where(sublane() < reach, rounded(parts[0] * parts[1]), 0.0)
+            token_scr[pl.ds(pl.multiple_of((chunk * TILES + number) * ROWS, ROWS), ROWS), :] = u
+            head_ref[:, lanes] = jnp.concatenate([u, jnp.zeros((ROWS, LANES), f32)], axis=0).astype(bf16)
         return 0
 
-    lax.fori_loop(0, tiles, one, 0)
+    lax.fori_loop(0, tiles // TILES, some, 0)
     signals = [token_scr[pl.ds(row, tiles, stride=ROWS), :] for row in range(reach)]
     split = pieces // modes
     for mode in range(modes):
@@ -286,10 +276,9 @@
             out_ref[mode * split + part] = rows.astype(out_ref.dtype)
 
 
-def gate_kernel(query_ref, halo_ref, feat_ref, rate_ref, coef_ref, gate_ref, lead_ref, *scratches):
-    query_buf, halo_buf, gate_buf, lead_buf, wide_scr, in_sem, small_sem, out_sem, lead_sem = scratches
+def gate_kernel(query_ref, halo_ref, feat_ref, gate_ref, *scratches):
+    query_buf, halo_buf, gate_buf, wide_scr, column, in_sem, small_sem, out_sem = scratches
     chunks, tokens = gate_buf.shape[:2]
-    modes = rate_ref.shape[0]
     count = feat_ref.shape[2]
     fetch = columns_in(((query_ref, query_buf),), in_sem)
     halo_copy = pltpu.make_async_copy(halo_ref, halo_buf, small_sem.at[0])
@@ -297,56 +286,49 @@
     begin(chunks, fetch)
     widened(feat_ref, 0, wide_scr, 0)
     halo_copy.wait()
-    steps = (sublane() + 1).astype(f32)
-
-    def send(at):
-        return [
-            pltpu.make_async_copy(gate_buf.at[at], gate_ref.at[:, span(at)], out_sem.at[0, at]),
-            pltpu.make_async_copy(lead_buf.at[at], lead_ref.at[at], lead_sem.at[at]),
-        ]
 
     def chunk(at):
         def tile(number, _):
             lanes = tile_lanes(number)
-            all_lanes = tile_lanes(at * TILES + number)
             taps = chunk_taps(wide_scr, at, 0, number, count)
-            _, past = fir_step(tiles_of(halo_buf[:, all_lanes])[2], taps, fir_start())
+            halo = halo_buf[:, tile_lanes(at * TILES + number)].astype(f32)
+            column[pl.ds(0, ROWS), :] = halo[2 * ROWS :]
+            lay_column(column, query_buf.at[at], lanes)
             for pair in range(tokens // (2 * ROWS)):
+                first = pair * 2 * ROWS + ROWS
+                found = [fir(column, taps, first), fir(column, taps, first + ROWS)]
                 rows = slice(pair * 2 * ROWS, (pair + 1) * 2 * ROWS)
-                found = []
-                for source in tiles_of(query_buf[at, rows, lanes]):
-                    value, past = fir_step(source, taps, past)
-                    found.append(value)
                 gate_buf[at, rows, lanes] = jnp.concatenate(found, axis=0).astype(bf16)
-            for mode in range(modes):
-                rate = wide(rate_ref[mode : mode + 1, all_lanes])
-                coef = wide(coef_ref[mode : mode + 1, all_lanes])
-                lead_buf[at, number * modes + mode] = coef * jnp.exp(-rate * steps)
             return 0
 
         lax.fori_loop(0, TILES, tile, 0)
 
-    over_chunks(chunks, fetch, chunk, send)
-
-
-def prefix_kernel(piece_ref, rate_ref, out_ref, table_scr, *, tokens, axes):
+    over_chunks(chunks, fetch, chunk, columns_out(gate_ref, gate_buf, out_sem))
+
+
+def prefix_kernel(piece_ref, rate_ref, coef_ref, out_ref, table_scr, *, tokens, axes):
     devices, piece_rows = piece_ref.shape[:2]
     split = devices // rate_ref.shape[0]
     mine = lax.axis_index(axes)
     mode, part = mine // split, mine % split
     group = pl.multiple_of(mode // ROWS * ROWS, ROWS)
     first = pl.multiple_of(part * piece_rows * LANES, LANES)
-    rows = rate_ref[pl.ds(group, ROWS), pl.ds(first, piece_rows * LANES)]
-    here = lax.broadcasted_iota(jnp.int32, rows.shape, 0) == mode - group
-    rate = jnp.sum(jnp.where(here, rows, 0.0), axis=0, keepdims=True)
-    for row in range(piece_rows):
-        table_scr[row : row + 1, :] = lanes_of(rate, row)
-    through = jnp.exp(-float(tokens) * table_scr[:piece_rows, :])
+
+    def mine_of(ref):
+        rows = ref[pl.ds(group, ROWS), pl.ds(first, piece_rows * LANES)]
+        here = lax.broadcasted_iota(jnp.int32, rows.shape, 0) == mode - group
+        row = jnp.sum(jnp.where(here, rows, 0.0), axis=0, keepdims=True)
+        for number in range(piece_rows):
+            table_scr[number : number + 1, :] = lanes_of(row, number)
+        return table_scr[:piece_rows, :]
+
+    coef = mine_of(coef_ref)
+    through = jnp.exp(-float(tokens) * mine_of(rate_ref))
 
     def lap(number, entering):
         for step in range(4):
             source = number * 4 + step
-            out_ref[source] = entering.astype(out_ref.dtype)
+            out_ref[source] = (coef * entering).astype(out_ref.dtype)
             entering = through * entering + piece_ref[source].astype(f32)
         return entering
 
@@ -354,7 +336,7 @@
 
 
 def local_kernel(u_ref, head_ref, rate_ref, coef_ref, skip_ref, y_ref, mid_ref, *scratches):
-    u_buf, y_buf, mid_buf, token_scr, sum_scr, in_sem, out_sem, mid_sem = scratches
+    u_buf, y_buf, mid_buf, token_scr, vector_scr, part_scr, sum_scr, in_sem, out_sem, mid_sem = scratches
     chunks, tokens = u_buf.shape[:2]
     modes = rate_ref.shape[0]
     half_groups = tokens // ROWS // 2
@@ -387,17 +369,26 @@
             def eight(group, state):
                 state = list(state)
                 for row in range(ROWS):
-                    u = get_row(token_scr, group, row)
+                    strided = pl.ds(group * ROWS * ROWS + row, ROWS, stride=ROWS)
+                    dense = pl.ds(pl.multiple_of((group * ROWS + row) * ROWS, ROWS), ROWS)
+                    if first == 0:
+                        u = token_scr[strided, :]
+                        vector_scr[dense, :] = u
+                        so_far = skip * u
+                    else:
+                        u = vector_scr[dense, :]
+                        so_far = part_scr[dense, :]
                     state = [factor * one + u for factor, one in zip(decay, state)]
-                    terms = [factor * one for factor, one in zip(coef, state)]
-                    place = pl.ds(group * ROWS * ROWS + row, ROWS, stride=ROWS)
-                    so_far = skip * u if first == 0 else sum_scr[place, :]
-                    sum_scr[place, :] = so_far + tree(terms)
+                    value = so_far + tree([factor * one for factor, one in zip(coef, state)])
+                    if first + ROWS < modes:
+                        part_scr[dense, :] = value
+                    else:
+                        sum_scr[strided, :] = value
                 return tuple(state)
 
             state = lax.fori_loop(0, half_groups, eight, (jnp.zeros((ROWS, LANES), f32),) * ROWS)
-            for at_mode, one in zip(some, state):
-                mid_buf[at, at_mode] = one
+            for at_mode, factor, one in zip(some, coef, state):
+                mid_buf[at, at_mode] = factor * one
         for group in range(2 * half_groups):
             half, within = group // half_groups, group % half_groups
             for tile in range(TILES):
@@ -408,17 +399,14 @@
     over_chunks(chunks, fetch, chunk, send)
 
 
-def final_kernel(piece_ref, rate_ref, lead_ref, mid_ref, y_ref, gate_ref, out_ref, *scratches):
-    lead_buf, mid_buf, y_buf, gate_buf, out_buf, total_scr, power_scr, in_sem, wide_sem, out_sem = scratches
+def final_kernel(piece_ref, rate_ref, mid_ref, y_ref, gate_ref, out_ref, *scratches):
+    mid_buf, y_buf, gate_buf, out_buf, total_scr, power_scr, lead_scr, in_sem, mid_sem, out_sem = scratches
     chunks, modes = mid_buf.shape[:2]
     tokens = y_buf.shape[1]
     columns = columns_in(((y_ref, y_buf), (gate_ref, gate_buf)), in_sem)
 
     def fetch(at):
-        return columns(at) + [
-            pltpu.make_async_copy(ref.at[at], buf.at[at], wide_sem.at[member, at])
-            for member, (ref, buf) in enumerate(((lead_ref, lead_buf), (mid_ref, mid_buf)))
-        ]
+        return columns(at) + [pltpu.make_async_copy(mid_ref.at[at], mid_buf.at[at], mid_sem.at[at])]
 
     begin(chunks, fetch)
     pieces, piece_rows = piece_ref.shape[:2]
@@ -427,17 +415,25 @@
         for part in range(split):
             rows = piece_ref[mode * split + part].astype(f32)
             total_scr[mode, part * piece_rows : (part + 1) * piece_rows, :] = rows
+    bits = [(sublane() >> level) % 2 == 1 for level in range(3)]
 
     def chunk(at):
-        power_scr[...] = jnp.exp(-float(ROWS) * rate_ref[:, span(at)])
+        through = jnp.exp(-rate_ref[:, span(at)])
+        for level in range(4):
+            power_scr[level] = through
+            through = through * through
 
         def tile(number, _):
             lanes = tile_lanes(number)
-            decay = [wide(power_scr[mode : mode + 1, lanes]) for mode in range(modes)]
-            state = [
-                lead_buf[at, number * modes + mode] * wide(total_scr[mode, pl.ds(at * TILES + number, 1), :])
-                for mode in range(modes)
-            ]
+            state = []
+            for mode in range(modes):
+                rows = [wide(power_scr[level, mode : mode + 1, lanes]) for level in range(3)]
+                lead = rows[0]
+                for bit, row in zip(bits, rows):
+                    lead = lead * jnp.where(bit, row, 1.0)
+                lead_scr[mode] = lead
+                state.append(lead * wide(total_scr[mode, pl.ds(at * TILES + number, 1), :]))
+            decay = [wide(power_scr[3, mode : mode + 1, lanes]) for mode in range(modes)]
             for pair in range(tokens // (2 * ROWS)):
                 rows = slice(pair * 2 * ROWS, (pair + 1) * 2 * ROWS)
                 gates = gate_buf[at, rows, lanes].astype(f32)
@@ -445,7 +441,7 @@
                 for part in range(2):
                     if pair == tokens // (4 * ROWS) and part == 0:
                         state = [
-                            one + lead_buf[at, number * modes + mode] * wide(mid_buf[at, mode, pl.ds(number, 1), :])
+                            one + lead_scr[mode] * wide(mid_buf[at, mode, pl.ds(number, 1), :])
                             for mode, one in enumerate(state)
                         ]
                     here = slice((pair * 2 + part) * ROWS, (pair * 2 + part + 1) * ROWS)
@@ -505,12 +501,14 @@
     halo = lax.ppermute(packed, axes, [(at, at + 1) for at in range(devices - 1)])
 
     feat = featurizer.reshape(members, taps, chunks, groups // chunks).transpose(2, 0, 1, 3)
+    column = vmem((ROWS + tokens, LANES), f32)
     half_buf, whole_buf = vmem((chunks, tokens, CHUNK), bf16), vmem((chunks, tokens, CHUNK), f32)
     u, wide_taps, state = call(
         signal_kernel,
         (key_proj, value_proj, feat, rates),
         [far((tokens, width), bf16), near((chunks, 2, ROWS, CHUNK), f32), near((modes, tiles, LANES), f32)],
-        [half_buf, half_buf, half_buf, vmem((4, modes, CHUNK), f32), dma((2, chunks)), dma((1, chunks))],
+        [half_buf, half_buf, half_buf, vmem((4, modes, CHUNK), f32), column, column]
+        + [dma((2, chunks)), dma((1, chunks))],
         "signal",
         close=(2, 3),
         cost_estimate=cost(60 * elements, 10 * elements),
@@ -521,7 +519,7 @@
         functools.partial(head_kernel, tokens=tokens, reach=taps - 1),
         (key_proj, value_proj, halo, rates, wide_taps, state),
         [near(pieces, bf16), near((2 * ROWS, width), bf16)],
-        [vmem((2, 2 * ROWS, width), bf16), vmem((modes * tiles, LANES), f32)]
+        [vmem((2, 2 * ROWS, width), bf16), vmem((modes * tiles, LANES), f32), vmem((TILES, 2, 2 * ROWS, LANES), f32)]
         + [vmem((tiles * ROWS, LANES), f32), vmem((modes, tiles, LANES), f32), dma((2,))],
         "head",
         close=(2, 3, 4, 5),
@@ -529,16 +527,15 @@
     left, halo_late, rates_late, skip_late = lax.optimization_barrier((left, halo, rates, skip))
     coef = residues * jnp.sqrt(-jnp.expm1(-2.0 * rates_late) / modes)
     skip_row = skip_late[None, :]
-    gate, lead = call(
+    (gate,) = call(
         gate_kernel,
-        (query, halo_late, feat, rates, coef),
-        [far((tokens, width), bf16), far((chunks, TILES * modes, ROWS, LANES), f32)],
-        [half_buf, vmem((members * ROWS, width), bf16), half_buf]
-        + [vmem((chunks, TILES * modes, ROWS, LANES), f32), vmem((chunks, 1, ROWS, CHUNK), f32)]
-        + [dma((1, chunks)), dma((1,)), dma((1, chunks)), dma((chunks,))],
+        (query, halo_late, feat),
+        [far((tokens, width), bf16)],
+        [half_buf, vmem((members * ROWS, width), bf16), half_buf, vmem((chunks, 1, ROWS, CHUNK), f32), column]
+        + [dma((1, chunks)), dma((1,)), dma((1, chunks))],
         "gate",
-        close=(2, 3, 4),
-        cost_estimate=cost(30 * elements, 8 * elements),
+        close=(2,),
+        cost_estimate=cost(14 * elements, 4 * elements),
     )
 
     def swap(value):
@@ -546,21 +543,22 @@
 
     share = modes * width // devices
     theirs = swap(left if even else left.reshape(devices, share))
-    theirs, gate, lead, coef, skip_row = lax.optimization_barrier((theirs, gate, lead, coef, skip_row))
+    theirs, gate, coef, skip_row = lax.optimization_barrier((theirs, gate, coef, skip_row))
     if even:
         (entering,) = call(
             functools.partial(prefix_kernel, tokens=tokens, axes=axes),
-            (theirs, rates),
+            (theirs, rates, coef),
             [near(pieces, bf16)],
             [vmem((-(-pieces[1] // ROWS) * ROWS, LANES), f32)],
             "prefix",
-            close=(0, 1),
+            close=(0, 1, 2),
         )
     else:
         mine = lax.axis_index(axes)
         through = jnp.exp(-float(tokens) * lax.dynamic_slice_in_dim(rates.reshape(-1), mine * share, share))
+        factor = lax.dynamic_slice_in_dim(coef.reshape(-1), mine * share, share)
         _, entering = lax.scan(
-            lambda so_far, piece: (through * so_far + piece.astype(f32), so_far.astype(bf16)),
+            lambda so_far, piece: (through * so_far + piece.astype(f32), (factor * so_far).astype(bf16)),
             jnp.zeros((share,), f32),
             theirs,
         )
@@ -572,7 +570,7 @@
         local_kernel,
         (u_late, head, rates, coef, skip_row),
         [far((tokens, width), f32), far((chunks, modes, ROWS, LANES), f32)],
-        [half_buf, whole_buf, vmem((chunks, modes, ROWS, LANES), f32), stage, stage]
+        [half_buf, whole_buf, vmem((chunks, modes, ROWS, LANES), f32)] + [stage] * 4
         + [dma((1, chunks)), dma((1, chunks)), dma((chunks,))],
         "within",
         close=(1, 2, 3, 4),
@@ -581,11 +579,11 @@
 
     (out,) = call(
         final_kernel,
-        (entered, rates, lead, mid, y, gate),
+        (entered, rates, mid, y, gate),
         [far((tokens, width), bf16)],
-        [vmem((chunks, TILES * modes, ROWS, LANES), f32), vmem((chunks, modes, ROWS, LANES), f32)]
-        + [whole_buf, half_buf, half_buf, vmem((modes, tiles, LANES), f32), vmem((modes, CHUNK), f32)]
-        + [dma((2, chunks)), dma((2, chunks)), dma((1, chunks))],
+        [vmem((chunks, modes, ROWS, LANES), f32), whole_buf, half_buf, half_buf]
+        + [vmem((modes, tiles, LANES), f32), vmem((4, modes, CHUNK), f32), vmem((modes, ROWS, LANES), f32)]
+        + [dma((2, chunks)), dma((chunks,)), dma((1, chunks))],
         "final",
         close=(0, 1),
         cost_estimate=cost(40 * elements, 10 * elements),

time: 51.2 us -> 49.7 us (0.971)
  Pallas kernels: 34.1 us -> 31.9 us
  waiting for transfers between devices: 3.12 us -> 4.16 us
    pallas_call x7, Pallas kernels: 34.1 us -> 31.9 us  [call(): pl.pallas_call(kernel, in_specs=[beside if at in close else there for at...]
    all_to_all x2, waiting for transfers between devices: 3.12 us -> 3.81 us  [swap(): return lax.all_to_all(value, axes, split_axis=0, concat_axis=0, tiled=True)]
  transfers between devices with their start and end apart: 3 -> 3, of which waited for: 1 -> 2; matrix products, arithmetic and copies ran while one was open for 1% -> 1% of each run, Pallas kernels for 46% -> 44%
where the time goes in v6:
time: 49.7 us; the launch traced here: 49 us
  Pallas kernels  31.9 us (64%)
  starting transfers between devices  12.4 us (25%)
  waiting for transfers between devices  4.16 us (8%)
    pallas_call x7, Pallas kernels, call(): pl.pallas_call(kernel, in_specs=[beside if at in close else there for at...  31.9 us
    all_to_all x2, starting transfers between devices, swap(): return lax.all_to_all(value, axes, split_axis=0, concat_axis=0, tiled=True)  8.46 us
    ppermute x1, starting transfers between devices, local(): lax.ppermute(packed, axes, [(at, at + 1) for at in range(devices - 1)])  3.95 us
    all_to_all x2, waiting for transfers between devices, swap(): return lax.all_to_all(value, axes, split_axis=0, concat_axis=0, tiled=True)  3.81 us
  transfers between devices with their start and end apart: 3, of which 2 were waited for; matrix products, arithmetic and copies ran while one was open for 1% of the time, Pallas kernels for 44%

profile of v6, /device:TPU:1, one launch (start us, length us, event | category | flops | bytes accessed | tf_op | source)
XLA Modules:
  0.0 49.0 jit_solution(7669684605926998011)
XLA Ops:
  0.0 0.0 copy-start.3
  0.0 0.0 copy-start
  0.0 1.1 %pack.1 = bf16[24,4608]{1,0:T(8,128)(2,1)S(1)} custom-call(bf16[128,4608]{1,0:T(8,128)(2,1)} %key_ref.5, bf16[128,4608]{1,0:T(8,128)(2,1)} %value_ref.5, bf16[128,4608]{1,0:T(8,128)(2,1)} %query_ref.3), custom_call_target="tpu_custom_call" | custom-call | tf_op jit(solution)/shard_map/pack/pallas_call | solution.py:483
  1.1 3.9 %collective-permute-start = (bf16[24,4608]{1,0:T(8,128)(2,1)S(1)}, bf16[24,4608]{1,0:T(8,128)(2,1)S(1)}, u32[]{:S(2)}, u32[]{:S(2)}) collective-permute-start(bf16[24,4608]{1,0:T(8,128)(2,1)S(1)} %pack.1), channel_id=1, source_target_pairs={{0,1},{1,2},{2,3},{3,4},{4,5},{5,6},{6,7},{7,8},{8,9},{9,10},{10,1... | collective-permute-start | bytes 663560 | tf_op jit(solution)/shard_map/ppermute | solution.py:501
  5.1 0.0 copy-done.3
  5.1 0.1 reshape.3
  5.3 0.0 copy-done
  5.3 8.6 %signal.1 = (bf16[128,4608]{1,0:T(8,128)(2,1)}, f32[9,2,8,512]{3,2,1,0:T(8,128)S(1)}, f32[16,36,128]{2,1,0:T(8,128)S(1)}) custom-call(bf16[128,4608]{1,0:T(8,128)(2,1)} %key_ref.5, bf16[128,4608]{1,0:T(8,128)(2,1)} %value_ref.5, f32[9,3,7,32]{3,2,1,0:T(8,128)S(1)} %bitcast.3, f32[16,4608]{1,0:T(8,128)S(1)} %copy-done), custom_call_target="tpu_custom_call" | custom-call | flops 35389440 | bytes 5898240 | tf_op jit(solution)/shard_map/signal/pallas_call | solution.py:483
  13.8 0.3 collective-permute-done.halo_ref
  14.2 0.0 copy-start.1
  14.2 2.5 %head.1 = (bf16[32,18,128]{2,1,0:T(8,128)(2,1)}, bf16[16,4608]{1,0:T(8,128)(2,1)S(1)}) custom-call(bf16[128,4608]{1,0:T(8,128)(2,1)} %key_ref.5, bf16[128,4608]{1,0:T(8,128)(2,1)} %value_ref.5, bf16[24,4608]{1,0:T(8,128)(2,1)S(1)} %collective-permute-done.halo_ref, f32[16,4608]{1,0:T(8,128)S(1)} %copy-done, f32[9,2,8,512]{3,2,1,0:T(8,128)S(1)} %get-tuple-element.22.wide_ref, ...), custom_call_target="tpu_custom_call" | custom-call | tf_op jit(solution)/shard_map/head/pallas_call | solution.py:483
  16.7 0.0 copy-done.1
  16.7 0.0 copy-start.4
  16.7 5.3 %all-to-all-start = ((bf16[32,18,128]{2,1,0:T(8,128)(2,1)}), bf16[32,18,128]{2,1,0:T(8,128)(2,1)S(1)}, u32[]{:S(2)}, u32[]{:S(2)}) async-start(bf16[32,18,128]{2,1,0:T(8,128)(2,1)} %get-tuple-element.25), calls=%async_computation | async-start | bytes 393216 | tf_op jit(solution)/shard_map/all_to_all | solution.py:542
  22.0 0.0 copy-done.2
  22.0 0.2 sqrt_multiply_fusion.coef_ref
  22.2 0.0 copy-done.4
  22.2 4.4 %gate.1.gate_ref = bf16[128,4608]{1,0:T(8,128)(2,1)} custom-call(bf16[128,4608]{1,0:T(8,128)(2,1)} %query_ref.3, bf16[24,4608]{1,0:T(8,128)(2,1)} %copy-done.1, f32[9,3,7,32]{3,2,1,0:T(8,128)S(1)} %bitcast.4), custom_call_target="tpu_custom_call" | custom-call | flops 8257536 | bytes 2359296 | tf_op jit(solution)/shard_map/gate/pallas_call | solution.py:483
  26.7 3.8 %all-to-all-done.piece_ref = bf16[32,18,128]{2,1,0:T(8,128)(2,1)S(1)} async-done(((bf16[32,18,128]{2,1,0:T(8,128)(2,1)}), bf16[32,18,128]{2,1,0:T(8,128)(2,1)S(1)}, u32[]{:S(2)}, u32[]{:S(2)}) %all-to-all-start) | async-done | bytes 147488 | tf_op jit(solution)/shard_map/all_to_all | solution.py:542
  30.5 0.8 %prefix.1 = bf16[32,18,128]{2,1,0:T(8,128)(2,1)} custom-call(bf16[32,18,128]{2,1,0:T(8,128)(2,1)S(1)} %all-to-all-done.piece_ref, f32[16,4608]{1,0:T(8,128)S(1)} %copy-done, f32[16,4608]{1,0:T(8,128)S(1)} %sqrt_multiply_fusion.coef_ref), custom_call_target="tpu_custom_call" | custom-call | tf_op jit(solution)/shard_map/prefix/pallas_call | solution.py:483
  31.3 3.1 %all-to-all-start.1 = ((bf16[32,18,128]{2,1,0:T(8,128)(2,1)}), bf16[32,18,128]{2,1,0:T(8,128)(2,1)S(1)}, u32[]{:S(2)}, u32[]{:S(2)}) async-start(bf16[32,18,128]{2,1,0:T(8,128)(2,1)} %prefix.1), calls=%async_computation.1 | async-start | bytes 393216 | tf_op jit(solution)/shard_map/all_to_all | solution.py:542
  34.5 8.5 %within.1 = (f32[128,4608]{1,0:T(8,128)}, f32[9,16,8,128]{3,2,1,0:T(8,128)}) custom-call(bf16[128,4608]{1,0:T(8,128)(2,1)} %get-tuple-element.33.u_ref, bf16[16,4608]{1,0:T(8,128)(2,1)S(1)} %get-tuple-element.34.head_ref, f32[16,4608]{1,0:T(8,128)S(1)} %copy-done, f32[16,4608]{1,0:T(8,128)S(1)} %sqrt_multiply_fusion.coef_ref, ...), custom_call_target="tpu_custom_call" | custom-call | flops 38928384 | bytes 4718592 | tf_op jit(solution)/shard_map/within/pallas_call | solution.py:483
  43.0 0.0 all-to-all-done.1.piece_ref
  43.0 6.0 %final.1 = bf16[128,4608]{1,0:T(8,128)(2,1)} custom-call(bf16[32,18,128]{2,1,0:T(8,128)(2,1)S(1)} %all-to-all-done.1.piece_ref, f32[16,4608]{1,0:T(8,128)S(1)} %copy-done, f32[9,16,8,128]{3,2,1,0:T(8,128)} %get-tuple-element.36.mid_ref, f32[128,4608]{1,0:T(8,128)} %get-tuple-element.37.y_ref, bf16[128,4608]{1,0:T(8,128)(2,1)} %gate.1.gate_ref), custom_call_target="tpu_custom_call" | custom-call | flops 23592960 | bytes 5898240 | tf_op jit(solution)/shard_map/final/pallas_call | solution.py:483
  (3 shorter events, 0.1 us)
Async XLA Ops:
  0.0 5.1 %copy-start.3 = (f32[3,7,288]{2,1,0:T(8,128)S(1)}, f32[3,7,288]{2,1,0:T(8,128)}, u32[]{:S(2)}) copy-start(f32[3,7,288]{2,1,0:T(8,128)} %param.10) | copy-start | bytes 72580
  0.0 5.3 %copy-start = (f32[16,4608]{1,0:T(8,128)S(1)}, f32[16,4608]{1,0:T(8,128)}, u32[]{:S(2)}) copy-start(f32[16,4608]{1,0:T(8,128)} %rate_ref.9) | copy-start | bytes 884740
  1.1 13.0 %collective-permute-start = (bf16[24,4608]{1,0:T(8,128)(2,1)S(1)}, bf16[24,4608]{1,0:T(8,128)(2,1)S(1)}, u32[]{:S(2)}, u32[]{:S(2)}) collective-permute-start(bf16[24,4608]{1,0:T(8,128)(2,1)S(1)} %pack.1), channel_id=1, source_target_pairs={{0,1},{1,2},{2,3},{3,4},{4,5},{5,6},{6,7},{7,8},{8,9},{9,10},{10,1... | collective-permute-start | bytes 663560 | tf_op jit(solution)/shard_map/ppermute | solution.py:501
  14.2 2.5 %copy-start.1 = (bf16[24,4608]{1,0:T(8,128)(2,1)}, bf16[24,4608]{1,0:T(8,128)(2,1)S(1)}, u32[]{:S(2)}) copy-start(bf16[24,4608]{1,0:T(8,128)(2,1)S(1)} %collective-permute-done.halo_ref) | copy-start | bytes 663556
  14.2 7.8 %copy-start.2 = (f32[16,4608]{1,0:T(8,128)S(1)}, f32[16,4608]{1,0:T(8,128)}, u32[]{:S(2)}) copy-start(f32[16,4608]{1,0:T(8,128)} %param.12) | copy-start | bytes 884740
  16.7 5.5 %copy-start.4 = (f32[4608]{0:T(1024)S(1)}, f32[4608]{0:T(1024)}, u32[]{:S(2)}) copy-start(f32[4608]{0:T(1024)} %param.13) | copy-start | bytes 55300
  16.7 13.8 %all-to-all-start = ((bf16[32,18,128]{2,1,0:T(8,128)(2,1)}), bf16[32,18,128]{2,1,0:T(8,128)(2,1)S(1)}, u32[]{:S(2)}, u32[]{:S(2)}) async-start(bf16[32,18,128]{2,1,0:T(8,128)(2,1)} %get-tuple-element.25), calls=%async_computation | async-start | bytes 393216 | tf_op jit(solution)/shard_map/all_to_all | solution.py:542
  31.3 11.7 %all-to-all-start.1 = ((bf16[32,18,128]{2,1,0:T(8,128)(2,1)}), bf16[32,18,128]{2,1,0:T(8,128)(2,1)S(1)}, u32[]{:S(2)}, u32[]{:S(2)}) async-start(bf16[32,18,128]{2,1,0:T(8,128)(2,1)} %prefix.1), calls=%async_computation.1 | async-start | bytes 393216 | tf_op jit(solution)/shard_map/all_to_all | solution.py:542

commit v7 on v6

--- a/solution.py
+++ b/solution.py
@@ -69,17 +69,36 @@
     return [block[at : at + ROWS] for at in range(0, block.shape[0], ROWS)]
 
 
-def fir(column, taps, first):
-    total = taps[0] * column[pl.ds(first, ROWS), :]
-    for lag in range(1, len(taps)):
-        total = total + taps[lag] * column[pl.ds(first - lag, ROWS), :]
-    return total
+def fir(column, taps, first, count):
+    half = ROWS // 2
+    top = sublane() < half
+
+    def seen(start, lags):
+        return [column[pl.ds(start - lag, ROWS), :] for lag in range(lags)]
+
+    def far_part(rows):
+        total = taps[half] * rows[0]
+        for lag in range(half + 1, len(taps)):
+            total = total + taps[lag] * rows[lag - half]
+        return pltpu.roll(total, half, 0)
+
+    before = far_part(seen(first - ROWS, len(taps) - half))
+    results = []
+    for start in range(first, first + count * ROWS, ROWS):
+        rows = seen(start, half)
+        now = far_part(rows)
+        total = taps[0] * rows[0]
+        for lag in range(1, half):
+            total = total + taps[lag] * rows[lag]
+        results.append(total + jnp.where(top, before, now))
+        before = now
+    return results
 
 
 def lay_column(column, source, lanes):
     for pair in range(source.shape[0] // (2 * ROWS)):
         rows = slice(pair * 2 * ROWS, (pair + 1) * 2 * ROWS)
-        column[pl.ds(ROWS + pair * 2 * ROWS, 2 * ROWS), :] = source[rows, lanes].astype(f32)
+        column[pl.ds((pair + 1) * 2 * ROWS, 2 * ROWS), :] = source[rows, lanes].astype(f32)
 
 
 def chunk_taps(wide_ref, at, member, tile, count):
@@ -193,16 +212,16 @@
         def tile(number, _):
             lanes = tile_lanes(number)
             taps = [chunk_taps(wide_ref, at, member, number, count) for member in range(2)]
-            for column, buf in zip(columns, (key_buf, value_buf)):
-                column[pl.ds(0, ROWS), :] = jnp.zeros((ROWS, LANES), f32)
+            parts = []
+            for member, (column, buf) in enumerate(zip(columns, (key_buf, value_buf))):
+                column[pl.ds(0, 2 * ROWS), :] = jnp.zeros((2 * ROWS, LANES), f32)
                 lay_column(column, buf.at[at], lanes)
+                parts.append(fir(column, taps[member], 2 * ROWS, tokens // ROWS))
+            found = [one * other for one, other in zip(*parts)]
+            found[0] = jnp.where(sublane() < count - 1, 0.0, found[0])
             for pair in range(tokens // (2 * ROWS)):
-                found = []
-                for first in (pair * 2 * ROWS + ROWS, pair * 2 * ROWS + 2 * ROWS):
-                    u = fir(columns[0], taps[0], first) * fir(columns[1], taps[1], first)
-                    found.append(jnp.where(sublane() < count - 1, 0.0, u) if first == ROWS else u)
                 rows = slice(pair * 2 * ROWS, (pair + 1) * 2 * ROWS)
-                u_buf[at, rows, lanes] = jnp.concatenate(found, axis=0).astype(bf16)
+                u_buf[at, rows, lanes] = jnp.concatenate(found[pair * 2 : pair * 2 + 2], axis=0).astype(bf16)
             return 0
 
         lax.fori_loop(0, TILES, tile, 0)
@@ -253,9 +272,10 @@
             for member in range(2):
                 taps = chunk_taps(wide_ref, chunk, member, number, reach + 1)
                 column = column_scr.at[number, member]
-                column[pl.ds(0, ROWS), :] = halo[member * ROWS : (member + 1) * ROWS]
-                column[pl.ds(ROWS, ROWS), :] = front_buf[member, :, lanes].astype(f32)[:ROWS]
-                parts.append(fir(column, taps, ROWS))
+                column[pl.ds(0, ROWS), :] = jnp.zeros((ROWS, LANES), f32)
+                column[pl.ds(ROWS, ROWS), :] = halo[member * ROWS : (member + 1) * ROWS]
+                column[pl.ds(2 * ROWS, ROWS), :] = front_buf[member, :, lanes].astype(f32)[:ROWS]
+                parts += fir(column, taps, 2 * ROWS, 1)
             u = jnp.where(sublane() < reach, rounded(parts[0] * parts[1]), 0.0)
             token_scr[pl.ds(pl.multiple_of((chunk * TILES + number) * ROWS, ROWS), ROWS), :] = u
             head_ref[:, lanes] = jnp.concatenate([u, jnp.zeros((ROWS, LANES), f32)], axis=0).astype(bf16)
@@ -292,13 +312,13 @@
             lanes = tile_lanes(number)
             taps = chunk_taps(wide_scr, at, 0, number, count)
             halo = halo_buf[:, tile_lanes(at * TILES + number)].astype(f32)
-            column[pl.ds(0, ROWS), :] = halo[2 * ROWS :]
+            column[pl.ds(0, ROWS), :] = jnp.zeros((ROWS, LANES), f32)
+            column[pl.ds(ROWS, ROWS), :] = halo[2 * ROWS :]
             lay_column(column, query_buf.at[at], lanes)
+            found = fir(column, taps, 2 * ROWS, tokens // ROWS)
             for pair in range(tokens // (2 * ROWS)):
-                first = pair * 2 * ROWS + ROWS
-                found = [fir(column, taps, first), fir(column, taps, first + ROWS)]
                 rows = slice(pair * 2 * ROWS, (pair + 1) * 2 * ROWS)
-                gate_buf[at, rows, lanes] = jnp.concatenate(found, axis=0).astype(bf16)
+                gate_buf[at, rows, lanes] = jnp.concatenate(found[pair * 2 : pair * 2 + 2], axis=0).astype(bf16)
             return 0
 
         lax.fori_loop(0, TILES, tile, 0)
@@ -335,21 +355,25 @@
     lax.fori_loop(0, devices // 4, lap, jnp.zeros((piece_rows, LANES), f32))
 
 
-def local_kernel(u_ref, head_ref, rate_ref, coef_ref, skip_ref, y_ref, mid_ref, *scratches):
-    u_buf, y_buf, mid_buf, token_scr, vector_scr, part_scr, sum_scr, in_sem, out_sem, mid_sem = scratches
-    chunks, tokens = u_buf.shape[:2]
+def local_kernel(u_ref, head_ref, rate_ref, coef_ref, skip_ref, *rest, first, last):
+    y_ref, mid_ref, u_buf, y_buf, mid_buf, token_scr, sum_scr, in_sem, out_sem, mid_sem = rest[-10:]
+    tokens = u_buf.shape[1]
     modes = rate_ref.shape[0]
     half_groups = tokens // ROWS // 2
-    fetch = columns_in(((u_ref, u_buf),), in_sem)
-    begin(chunks, fetch)
-
-    def send(at):
-        return [
-            pltpu.make_async_copy(y_buf.at[at], y_ref.at[:, span(at)], out_sem.at[0, at]),
-            pltpu.make_async_copy(mid_buf.at[at], mid_ref.at[at], mid_sem.at[at]),
-        ]
-
-    def chunk(at):
+    take = columns_in(((u_ref, u_buf),), in_sem)
+    give = columns_out(y_ref, y_buf, out_sem)
+
+    def fetch(number):
+        return take(number + first)
+
+    def send(number):
+        at = number + first
+        return give(at) + [pltpu.make_async_copy(mid_buf.at[at], mid_ref.at[at], mid_sem.at[at])]
+
+    begin(last - first, fetch)
+
+    def chunk(number):
+        at = number + first
         front = u_buf[at, : 2 * ROWS].astype(f32) + head_ref[:, span(at)].astype(f32)
         u_buf[at, : 2 * ROWS] = front.astype(bf16)
         for pair in range(half_groups):
@@ -361,34 +385,21 @@
                     piece = lanes_of(block, tile)[part * ROWS : (part + 1) * ROWS]
                     put_tile(token_scr, within, half * TILES + tile, piece)
         (skip,) = spread_rows(skip_ref, at, range(1))
-        for first in range(0, modes, ROWS):
-            some = range(first, first + ROWS)
-            coef = spread_rows(coef_ref, at, some)
-            decay = [jnp.exp(-rate) for rate in spread_rows(rate_ref, at, some)]
-
-            def eight(group, state):
-                state = list(state)
-                for row in range(ROWS):
-                    strided = pl.ds(group * ROWS * ROWS + row, ROWS, stride=ROWS)
-                    dense = pl.ds(pl.multiple_of((group * ROWS + row) * ROWS, ROWS), ROWS)
-                    if first == 0:
-                        u = token_scr[strided, :]
-                        vector_scr[dense, :] = u
-                        so_far = skip * u
-                    else:
-                        u = vector_scr[dense, :]
-                        so_far = part_scr[dense, :]
-                    state = [factor * one + u for factor, one in zip(decay, state)]
-                    value = so_far + tree([factor * one for factor, one in zip(coef, state)])
-                    if first + ROWS < modes:
-                        part_scr[dense, :] = value
-                    else:
-                        sum_scr[strided, :] = value
-                return tuple(state)
-
-            state = lax.fori_loop(0, half_groups, eight, (jnp.zeros((ROWS, LANES), f32),) * ROWS)
-            for at_mode, factor, one in zip(some, coef, state):
-                mid_buf[at, at_mode] = factor * one
+        coef = spread_rows(coef_ref, at, range(modes))
+        decay = [jnp.exp(-rate) for rate in spread_rows(rate_ref, at, range(modes))]
+
+        def eight(group, state):
+            state = list(state)
+            for row in range(ROWS):
+                u = get_row(token_scr, group, row)
+                state = [factor * one + u for factor, one in zip(decay, state)]
+                terms = [factor * one for factor, one in zip([skip] + coef, [u] + state)]
+                sum_scr[pl.ds(group * ROWS * ROWS + row, ROWS, stride=ROWS), :] = tree(terms)
+            return tuple(state)
+
+        state = lax.fori_loop(0, half_groups, eight, (jnp.zeros((ROWS, LANES), f32),) * modes)
+        for mode, (factor, one) in enumerate(zip(coef, state)):
+            mid_buf[at, mode] = factor * one
         for group in range(2 * half_groups):
             half, within = group // half_groups, group % half_groups
             for tile in range(TILES):
@@ -396,7 +407,7 @@
                 rows = slice(group * ROWS, (group + 1) * ROWS)
                 y_buf[at, rows, tile * LANES : (tile + 1) * LANES] = sum_scr[pl.ds(slot, ROWS), :]
 
-    over_chunks(chunks, fetch, chunk, send)
+    over_chunks(last - first, fetch, chunk, send)
 
 
 def final_kernel(piece_ref, rate_ref, mid_ref, y_ref, gate_ref, out_ref, *scratches):
@@ -501,7 +512,7 @@
     halo = lax.ppermute(packed, axes, [(at, at + 1) for at in range(devices - 1)])
 
     feat = featurizer.reshape(members, taps, chunks, groups // chunks).transpose(2, 0, 1, 3)
-    column = vmem((ROWS + tokens, LANES), f32)
+    column = vmem((2 * ROWS + tokens, LANES), f32)
     half_buf, whole_buf = vmem((chunks, tokens, CHUNK), bf16), vmem((chunks, tokens, CHUNK), f32)
     u, wide_taps, state = call(
         signal_kernel,
@@ -519,12 +530,12 @@
         functools.partial(head_kernel, tokens=tokens, reach=taps - 1),
         (key_proj, value_proj, halo, rates, wide_taps, state),
         [near(pieces, bf16), near((2 * ROWS, width), bf16)],
-        [vmem((2, 2 * ROWS, width), bf16), vmem((modes * tiles, LANES), f32), vmem((TILES, 2, 2 * ROWS, LANES), f32)]
+        [vmem((2, 2 * ROWS, width), bf16), vmem((modes * tiles, LANES), f32), vmem((TILES, 2, 3 * ROWS, LANES), f32)]
         + [vmem((tiles * ROWS, LANES), f32), vmem((modes, tiles, LANES), f32), dma((2,))],
         "head",
         close=(2, 3, 4, 5),
     )
-    left, halo_late, rates_late, skip_late = lax.optimization_barrier((left, halo, rates, skip))
+    left, halo_late, rates_late, skip_late, u_late = lax.optimization_barrier((left, halo, rates, skip, u))
     coef = residues * jnp.sqrt(-jnp.expm1(-2.0 * rates_late) / modes)
     skip_row = skip_late[None, :]
     (gate,) = call(
@@ -538,12 +549,31 @@
         cost_estimate=cost(14 * elements, 4 * elements),
     )
 
+    stage = vmem((tokens // ROWS // 2 * ROWS * ROWS, LANES), f32)
+
+    def within(u, head, y, mid, first, last):
+        before = () if y is None else (y, mid)
+        return call(
+            functools.partial(local_kernel, first=first, last=last),
+            (u, head, rates, coef, skip_row, *before),
+            [far((tokens, width), f32), far((chunks, modes, ROWS, LANES), f32)],
+            [half_buf, whole_buf, vmem((chunks, modes, ROWS, LANES), f32), stage, stage]
+            + [dma((1, chunks)), dma((1, chunks)), dma((chunks,))],
+            "within",
+            close=(1, 2, 3, 4),
+            cost_estimate=cost(7 * (last - first) * tokens * CHUNK * 10, (last - first) * tokens * CHUNK * 8),
+            input_output_aliases={5 + at: at for at in range(len(before))},
+        )
+
+    early = chunks // 3
+    y, mid = within(u_late, head, None, None, 0, early)
+
     def swap(value):
         return lax.all_to_all(value, axes, split_axis=0, concat_axis=0, tiled=True)
 
     share = modes * width // devices
     theirs = swap(left if even else left.reshape(devices, share))
-    theirs, gate, coef, skip_row = lax.optimization_barrier((theirs, gate, coef, skip_row))
+    theirs, gate, coef, skip_row, y, mid = lax.optimization_barrier((theirs, gate, coef, skip_row, y, mid))
     if even:
         (entering,) = call(
             functools.partial(prefix_kernel, tokens=tokens, axes=axes),
@@ -565,17 +595,7 @@
 
     entering, u_late = lax.optimization_barrier((entering, u))
     entered = swap(entering).reshape(pieces)
-    stage = vmem((tokens // ROWS // 2 * ROWS * ROWS, LANES), f32)
-    y, mid = call(
-        local_kernel,
-        (u_late, head, rates, coef, skip_row),
-        [far((tokens, width), f32), far((chunks, modes, ROWS, LANES), f32)],
-        [half_buf, whole_buf, vmem((chunks, modes, ROWS, LANES), f32)] + [stage] * 4
-        + [dma((1, chunks)), dma((1, chunks)), dma((chunks,))],
-        "within",
-        close=(1, 2, 3, 4),
-        cost_estimate=cost(66 * elements, 8 * elements),
-    )
+    y, mid = within(u_late, head, y, mid, early, chunks)
 
     (out,) = call(
         final_kernel,

time: 49.7 us -> 52.7 us (1.060)
  starting transfers between devices: 12.4 us -> 15.1 us
  Pallas kernels: 31.9 us -> 33.7 us
  waiting for transfers between devices: 4.16 us -> 2.69 us
    all_to_all x2, starting transfers between devices: 8.46 us -> 11.1 us  [swap(): return lax.all_to_all(value, axes, split_axis=0, concat_axis=0, tiled=True)]
    pallas_call x7 -> x8, Pallas kernels: 31.9 us -> 33.7 us  [call(): pl.pallas_call(kernel, in_specs=[beside if at in close else there for at...]
    all_to_all x2, waiting for transfers between devices: 3.81 us -> 2.34 us  [swap(): return lax.all_to_all(value, axes, split_axis=0, concat_axis=0, tiled=True)]
  transfers between devices with their start and end apart: 3 -> 3, of which waited for: 2 -> 2; matrix products, arithmetic and copies ran while one was open for 1% -> 1% of each run, Pallas kernels for 44% -> 45%
where the time goes in v7:
time: 52.7 us; the launch traced here: 51.9 us
  Pallas kernels  33.7 us (64%)
  starting transfers between devices  15.1 us (29%)
  waiting for transfers between devices  2.69 us (5%)
    pallas_call x8, Pallas kernels, call(): pl.pallas_call(kernel, in_specs=[beside if at in close else there for at...  33.7 us
    all_to_all x2, starting transfers between devices, swap(): return lax.all_to_all(value, axes, split_axis=0, concat_axis=0, tiled=True)  11.1 us
    ppermute x1, starting transfers between devices, local(): lax.ppermute(packed, axes, [(at, at + 1) for at in range(devices - 1)])  3.95 us
    all_to_all x2, waiting for transfers between devices, swap(): return lax.all_to_all(value, axes, split_axis=0, concat_axis=0, tiled=True)  2.34 us
  transfers between devices with their start and end apart: 3, of which 2 were waited for; matrix products, arithmetic and copies ran while one was open for 1% of the time, Pallas kernels for 45%

profile of v7, /device:TPU:1, one launch (start us, length us, event | category | flops | bytes accessed | tf_op | source)
XLA Modules:
  0.0 51.9 jit_solution(4769086675530259066)
XLA Ops:
  0.0 0.0 copy-start.3
  0.0 0.0 copy-start
  0.0 1.1 %pack.1 = bf16[24,4608]{1,0:T(8,128)(2,1)S(1)} custom-call(bf16[128,4608]{1,0:T(8,128)(2,1)} %key_ref.5, bf16[128,4608]{1,0:T(8,128)(2,1)} %value_ref.5, bf16[128,4608]{1,0:T(8,128)(2,1)} %query_ref.3), custom_call_target="tpu_custom_call" | custom-call | tf_op jit(solution)/shard_map/pack/pallas_call | solution.py:494
  1.1 3.9 %collective-permute-start = (bf16[24,4608]{1,0:T(8,128)(2,1)S(1)}, bf16[24,4608]{1,0:T(8,128)(2,1)S(1)}, u32[]{:S(2)}, u32[]{:S(2)}) collective-permute-start(bf16[24,4608]{1,0:T(8,128)(2,1)S(1)} %pack.1), channel_id=1, source_target_pairs={{0,1},{1,2},{2,3},{3,4},{4,5},{5,6},{6,7},{7,8},{8,9},{9,10},{10,1... | collective-permute-start | bytes 663560 | tf_op jit(solution)/shard_map/ppermute | solution.py:512
  5.1 0.0 copy-done.3
  5.1 0.1 reshape.3
  5.3 0.0 copy-done
  5.3 8.6 %signal.1 = (bf16[128,4608]{1,0:T(8,128)(2,1)}, f32[9,2,8,512]{3,2,1,0:T(8,128)S(1)}, f32[16,36,128]{2,1,0:T(8,128)S(1)}) custom-call(bf16[128,4608]{1,0:T(8,128)(2,1)} %key_ref.5, bf16[128,4608]{1,0:T(8,128)(2,1)} %value_ref.5, f32[9,3,7,32]{3,2,1,0:T(8,128)S(1)} %bitcast.3, f32[16,4608]{1,0:T(8,128)S(1)} %copy-done), custom_call_target="tpu_custom_call" | custom-call | flops 35389440 | bytes 5898240 | tf_op jit(solution)/shard_map/signal/pallas_call | solution.py:494
  13.8 0.3 collective-permute-done.halo_ref
  14.2 2.5 %head.1 = (bf16[32,18,128]{2,1,0:T(8,128)(2,1)}, bf16[16,4608]{1,0:T(8,128)(2,1)S(1)}) custom-call(bf16[128,4608]{1,0:T(8,128)(2,1)} %key_ref.5, bf16[128,4608]{1,0:T(8,128)(2,1)} %value_ref.5, bf16[24,4608]{1,0:T(8,128)(2,1)S(1)} %collective-permute-done.halo_ref, f32[16,4608]{1,0:T(8,128)S(1)} %copy-done, f32[9,2,8,512]{3,2,1,0:T(8,128)S(1)} %get-tuple-element.27.wide_ref, ...), custom_call_target="tpu_custom_call" | custom-call | tf_op jit(solution)/shard_map/head/pallas_call | solution.py:494
  16.7 0.0 copy-done.1
  16.7 0.0 copy-start.4
  16.7 5.3 %all-to-all-start = ((bf16[32,18,128]{2,1,0:T(8,128)(2,1)}), bf16[32,18,128]{2,1,0:T(8,128)(2,1)S(1)}, u32[]{:S(2)}, u32[]{:S(2)}) async-start(bf16[32,18,128]{2,1,0:T(8,128)(2,1)} %get-tuple-element.31), calls=%async_computation | async-start | bytes 393216 | tf_op jit(solution)/shard_map/all_to_all | solution.py:572
  22.1 0.0 copy-done.2
  22.1 0.2 sqrt_multiply_fusion.coef_ref
  22.3 0.0 copy-done.4
  22.3 4.4 %gate.1.gate_ref = bf16[128,4608]{1,0:T(8,128)(2,1)} custom-call(bf16[128,4608]{1,0:T(8,128)(2,1)} %query_ref.3, bf16[24,4608]{1,0:T(8,128)(2,1)} %copy-done.1, f32[9,3,7,32]{3,2,1,0:T(8,128)S(1)} %bitcast.4), custom_call_target="tpu_custom_call" | custom-call | flops 8257536 | bytes 2359296 | tf_op jit(solution)/shard_map/gate/pallas_call | solution.py:494
  26.7 4.1 %within.2 = (f32[128,4608]{1,0:T(8,128)}, f32[9,16,8,128]{3,2,1,0:T(8,128)}) custom-call(bf16[128,4608]{1,0:T(8,128)(2,1)} %get-tuple-element.42.u_ref, bf16[16,4608]{1,0:T(8,128)(2,1)S(1)} %get-tuple-element.36.head_ref, f32[16,4608]{1,0:T(8,128)S(1)} %copy-done, f32[16,4608]{1,0:T(8,128)S(1)} %sqrt_multiply_fusion.coef_ref, ...), custom_call_target="tpu_custom_call" | custom-call | flops 13762560 | bytes 1572864 | tf_op jit(solution)/shard_map/within/pallas_call | solution.py:494
  30.8 0.0 all-to-all-done.piece_ref
  30.8 0.9 %prefix.1 = bf16[32,18,128]{2,1,0:T(8,128)(2,1)} custom-call(bf16[32,18,128]{2,1,0:T(8,128)(2,1)S(1)} %all-to-all-done.piece_ref, f32[16,4608]{1,0:T(8,128)S(1)} %copy-done, f32[16,4608]{1,0:T(8,128)S(1)} %sqrt_multiply_fusion.coef_ref), custom_call_target="tpu_custom_call" | custom-call | tf_op jit(solution)/shard_map/prefix/pallas_call | solution.py:494
  31.6 5.8 %all-to-all-start.1 = ((bf16[32,18,128]{2,1,0:T(8,128)(2,1)}), bf16[32,18,128]{2,1,0:T(8,128)(2,1)S(1)}, u32[]{:S(2)}, u32[]{:S(2)}) async-start(bf16[32,18,128]{2,1,0:T(8,128)(2,1)} %prefix.1), calls=%async_computation.1 | async-start | bytes 393216 | tf_op jit(solution)/shard_map/all_to_all | solution.py:572
  37.5 6.1 %within.3 = (f32[128,4608]{1,0:T(8,128)}, f32[9,16,8,128]{3,2,1,0:T(8,128)}) custom-call(bf16[128,4608]{1,0:T(8,128)(2,1)} %get-tuple-element.42.u_ref, bf16[16,4608]{1,0:T(8,128)(2,1)S(1)} %get-tuple-element.36.head_ref, f32[16,4608]{1,0:T(8,128)S(1)} %copy-done, ...), custom_call_target="tpu_custom_call", output_to_operand_aliasing={{0}: (5, {}), {1}: (6, {})} | custom-call | flops 27525120 | bytes 3145728 | tf_op jit(solution)/shard_map/within/pallas_call | solution.py:494
  43.6 2.3 %all-to-all-done.1.piece_ref = bf16[32,18,128]{2,1,0:T(8,128)(2,1)S(1)} async-done(((bf16[32,18,128]{2,1,0:T(8,128)(2,1)}), bf16[32,18,128]{2,1,0:T(8,128)(2,1)S(1)}, u32[]{:S(2)}, u32[]{:S(2)}) %all-to-all-start.1) | async-done | bytes 147488 | tf_op jit(solution)/shard_map/all_to_all | solution.py:572
  45.9 6.0 %final.1 = bf16[128,4608]{1,0:T(8,128)(2,1)} custom-call(bf16[32,18,128]{2,1,0:T(8,128)(2,1)S(1)} %all-to-all-done.1.piece_ref, f32[16,4608]{1,0:T(8,128)S(1)} %copy-done, f32[9,16,8,128]{3,2,1,0:T(8,128)} %get-tuple-element.46.mid_ref, f32[128,4608]{1,0:T(8,128)} %get-tuple-element.47.y_ref, bf16[128,4608]{1,0:T(8,128)(2,1)} %gate.1.gate_ref), custom_call_target="tpu_custom_call" | custom-call | flops 23592960 | bytes 5898240 | tf_op jit(solution)/shard_map/final/pallas_call | solution.py:494
  (4 shorter events, 0.1 us)
Async XLA Ops:
  0.0 5.1 %copy-start.3 = (f32[3,7,288]{2,1,0:T(8,128)S(1)}, f32[3,7,288]{2,1,0:T(8,128)}, u32[]{:S(2)}) copy-start(f32[3,7,288]{2,1,0:T(8,128)} %param.10) | copy-start | bytes 72580
  0.0 5.3 %copy-start = (f32[16,4608]{1,0:T(8,128)S(1)}, f32[16,4608]{1,0:T(8,128)}, u32[]{:S(2)}) copy-start(f32[16,4608]{1,0:T(8,128)} %rate_ref.11) | copy-start | bytes 884740
  1.1 13.0 %collective-permute-start = (bf16[24,4608]{1,0:T(8,128)(2,1)S(1)}, bf16[24,4608]{1,0:T(8,128)(2,1)S(1)}, u32[]{:S(2)}, u32[]{:S(2)}) collective-permute-start(bf16[24,4608]{1,0:T(8,128)(2,1)S(1)} %pack.1), channel_id=1, source_target_pairs={{0,1},{1,2},{2,3},{3,4},{4,5},{5,6},{6,7},{7,8},{8,9},{9,10},{10,1... | collective-permute-start | bytes 663560 | tf_op jit(solution)/shard_map/ppermute | solution.py:512
  14.2 2.5 %copy-start.1 = (bf16[24,4608]{1,0:T(8,128)(2,1)}, bf16[24,4608]{1,0:T(8,128)(2,1)S(1)}, u32[]{:S(2)}) copy-start(bf16[24,4608]{1,0:T(8,128)(2,1)S(1)} %collective-permute-done.halo_ref) | copy-start | bytes 663556
  14.2 7.9 %copy-start.2 = (f32[16,4608]{1,0:T(8,128)S(1)}, f32[16,4608]{1,0:T(8,128)}, u32[]{:S(2)}) copy-start(f32[16,4608]{1,0:T(8,128)} %param.12) | copy-start | bytes 884740
  16.7 5.5 %copy-start.4 = (f32[4608]{0:T(1024)S(1)}, f32[4608]{0:T(1024)}, u32[]{:S(2)}) copy-start(f32[4608]{0:T(1024)} %param.13) | copy-start | bytes 55300
  16.7 14.0 %all-to-all-start = ((bf16[32,18,128]{2,1,0:T(8,128)(2,1)}), bf16[32,18,128]{2,1,0:T(8,128)(2,1)S(1)}, u32[]{:S(2)}, u32[]{:S(2)}) async-start(bf16[32,18,128]{2,1,0:T(8,128)(2,1)} %get-tuple-element.31), calls=%async_computation | async-start | bytes 393216 | tf_op jit(solution)/shard_map/all_to_all | solution.py:572
  31.6 14.3 %all-to-all-start.1 = ((bf16[32,18,128]{2,1,0:T(8,128)(2,1)}), bf16[32,18,128]{2,1,0:T(8,128)(2,1)S(1)}, u32[]{:S(2)}, u32[]{:S(2)}) async-start(bf16[32,18,128]{2,1,0:T(8,128)(2,1)} %prefix.1), calls=%async_computation.1 | async-start | bytes 393216 | tf_op jit(solution)/shard_map/all_to_all | solution.py:572

commit v8 on v7

--- a/solution.py
+++ b/solution.py
@@ -12,7 +12,7 @@
 ROWS = 8
 TILES = 4
 CHUNK = TILES * LANES
-AHEAD = 3
+AHEAD = 2
 f32 = jnp.float32
 bf16 = jnp.bfloat16
 
@@ -69,36 +69,17 @@
     return [block[at : at + ROWS] for at in range(0, block.shape[0], ROWS)]
 
 
-def fir(column, taps, first, count):
-    half = ROWS // 2
-    top = sublane() < half
-
-    def seen(start, lags):
-        return [column[pl.ds(start - lag, ROWS), :] for lag in range(lags)]
-
-    def far_part(rows):
-        total = taps[half] * rows[0]
-        for lag in range(half + 1, len(taps)):
-            total = total + taps[lag] * rows[lag - half]
-        return pltpu.roll(total, half, 0)
-
-    before = far_part(seen(first - ROWS, len(taps) - half))
-    results = []
-    for start in range(first, first + count * ROWS, ROWS):
-        rows = seen(start, half)
-        now = far_part(rows)
-        total = taps[0] * rows[0]
-        for lag in range(1, half):
-            total = total + taps[lag] * rows[lag]
-        results.append(total + jnp.where(top, before, now))
-        before = now
-    return results
+def fir(column, taps, first):
+    total = taps[0] * column[pl.ds(first, ROWS), :]
+    for lag in range(1, len(taps)):
+        total = total + taps[lag] * column[pl.ds(first - lag, ROWS), :]
+    return total
 
 
 def lay_column(column, source, lanes):
     for pair in range(source.shape[0] // (2 * ROWS)):
         rows = slice(pair * 2 * ROWS, (pair + 1) * 2 * ROWS)
-        column[pl.ds((pair + 1) * 2 * ROWS, 2 * ROWS), :] = source[rows, lanes].astype(f32)
+        column[pl.ds(ROWS + pair * 2 * ROWS, 2 * ROWS), :] = source[rows, lanes].astype(f32)
 
 
 def chunk_taps(wide_ref, at, member, tile, count):
@@ -151,7 +132,7 @@
         start_all(fetch(at))
 
 
-def over_chunks(chunks, fetch, body, send):
+def over_chunks(chunks, fetch, body, send, last=True):
     def one(at, _):
         @pl.when(at + AHEAD < chunks)
         def _():
@@ -163,8 +144,9 @@
         return 0
 
     lax.fori_loop(0, chunks, one, 0)
-    for at in range(chunks):
-        wait_all(send(at))
+    if last:
+        for at in range(chunks):
+            wait_all(send(at))
 
 
 def columns_in(pairs, sem):
@@ -193,76 +175,71 @@
     out_ref[...] = jnp.concatenate(tails, axis=0).astype(bf16)
 
 
-def signal_kernel(key_ref, value_ref, feat_ref, rate_ref, u_ref, wide_ref, state_ref, *scratches):
-    key_buf, value_buf, u_buf, power_scr, *columns, in_sem, out_sem = scratches
-    chunks, tokens = u_buf.shape[:2]
+def signal_kernel(key_ref, value_ref, feat_ref, rate_ref, u_ref, wide_ref, state_ref, power_scr, last_scr, *columns):
+    tokens, tiles = u_ref.shape[0], state_ref.shape[1]
     modes = rate_ref.shape[0]
+    chunks = tiles // TILES
     count = feat_ref.shape[2]
-    fetch = columns_in(((key_ref, key_buf), (value_ref, value_buf)), in_sem)
-    begin(chunks, fetch)
     for member in range(2):
         widened(feat_ref, member + 1, wide_ref, member)
-
-    def chunk(at):
+    for column in columns:
+        column[pl.ds(0, ROWS), :] = jnp.zeros((ROWS, LANES), f32)
+    last_scr[...] = jnp.zeros(last_scr.shape, f32)
+
+    def powers(at, _):
         through = jnp.exp(-rate_ref[:, span(at)])
         for level in range(4):
-            power_scr[level] = through
+            power_scr[level, :, span(at)] = through
             through = through * through
-
-        def tile(number, _):
-            lanes = tile_lanes(number)
-            taps = [chunk_taps(wide_ref, at, member, number, count) for member in range(2)]
-            parts = []
-            for member, (column, buf) in enumerate(zip(columns, (key_buf, value_buf))):
-                column[pl.ds(0, 2 * ROWS), :] = jnp.zeros((2 * ROWS, LANES), f32)
-                lay_column(column, buf.at[at], lanes)
-                parts.append(fir(column, taps[member], 2 * ROWS, tokens // ROWS))
-            found = [one * other for one, other in zip(*parts)]
-            found[0] = jnp.where(sublane() < count - 1, 0.0, found[0])
-            for pair in range(tokens // (2 * ROWS)):
-                rows = slice(pair * 2 * ROWS, (pair + 1) * 2 * ROWS)
-                u_buf[at, rows, lanes] = jnp.concatenate(found[pair * 2 : pair * 2 + 2], axis=0).astype(bf16)
-            return 0
-
-        lax.fori_loop(0, TILES, tile, 0)
-
-        def gather(number, _):
-            lanes = tile_lanes(number)
-            decay = [wide(power_scr[3, mode : mode + 1, lanes]) for mode in range(modes)]
-            state = None
-            for pair in range(tokens // (2 * ROWS)):
-                for u in tiles_of(u_buf[at, pair * 2 * ROWS : (pair + 1) * 2 * ROWS, lanes]):
-                    if state is None:
-                        state = [u] * modes
-                    else:
-                        state = [decay[mode] * state[mode] + u for mode in range(modes)]
-            for mode in range(modes):
-                whole = state[mode]
-                for level in (2, 1, 0):
-                    factor = wide(power_scr[level, mode : mode + 1, lanes])
-                    whole = factor * whole + pltpu.roll(whole, ROWS - (1 << level), 0)
-                state_ref[mode, pl.ds(at * TILES + number, 1), :] = whole[:1]
-            return 0
-
-        lax.fori_loop(0, TILES, gather, 0)
-
-    over_chunks(chunks, fetch, chunk, columns_out(u_ref, u_buf, out_sem))
+        return 0
+
+    lax.fori_loop(0, chunks, powers, 0)
+
+    def reduce(number):
+        lanes = tile_lanes(number)
+        for mode in range(modes):
+            whole = last_scr[mode]
+            for level in (2, 1, 0):
+                factor = wide(power_scr[level, mode : mode + 1, lanes])
+                whole = factor * whole + pltpu.roll(whole, ROWS - (1 << level), 0)
+            state_ref[mode, pl.ds(number, 1), :] = whole[:1]
+
+    def tile(number, _):
+        lanes = tile_lanes(number)
+        reduce(jnp.maximum(number - 1, 0))
+        taps = [chunk_taps(wide_ref, number // TILES, member, number % TILES, count) for member in range(2)]
+        for column, ref in zip(columns, (key_ref, value_ref)):
+            lay_column(column, ref, lanes)
+        decay = [wide(power_scr[3, mode : mode + 1, lanes]) for mode in range(modes)]
+        state = None
+        for pair in range(tokens // (2 * ROWS)):
+            found = []
+            for first in (pair * 2 * ROWS + ROWS, pair * 2 * ROWS + 2 * ROWS):
+                u = fir(columns[0], taps[0], first) * fir(columns[1], taps[1], first)
+                found.append(jnp.where(sublane() < count - 1, 0.0, u) if first == ROWS else u)
+            both = jnp.concatenate(found, axis=0).astype(bf16)
+            u_ref[pair * 2 * ROWS : (pair + 1) * 2 * ROWS, lanes] = both
+            for u in tiles_of(both):
+                if state is None:
+                    state = [u] * modes
+                else:
+                    state = [factor * one + u for factor, one in zip(decay, state)]
+        for mode in range(modes):
+            last_scr[mode] = state[mode]
+        return 0
+
+    lax.fori_loop(0, tiles, tile, 0)
+    reduce(tiles - 1)
 
 
 def head_kernel(key_ref, value_ref, halo_ref, rate_ref, wide_ref, state_ref, out_ref, head_ref, *scratches, tokens, reach):
-    front_buf, rate_scr, column_scr, token_scr, total_scr, in_sem = scratches
+    rate_scr, column_scr, token_scr, total_scr = scratches
     modes, tiles = state_ref.shape[:2]
     pieces, piece_rows = out_ref.shape[:2]
-    copies = [
-        pltpu.make_async_copy(ref.at[pl.ds(0, 2 * ROWS)], front_buf.at[member], in_sem.at[member])
-        for member, ref in enumerate((key_ref, value_ref))
-    ]
-    start_all(copies)
     for group in range(modes // ROWS):
         for tile in range(tiles):
             rows = pl.ds((group * tiles + tile) * ROWS, ROWS)
             rate_scr[rows, :] = rate_ref[group * ROWS : (group + 1) * ROWS, tile * LANES : (tile + 1) * LANES]
-    wait_all(copies)
 
     def some(chunk, _):
         for number in range(TILES):
@@ -272,10 +249,10 @@
             for member in range(2):
                 taps = chunk_taps(wide_ref, chunk, member, number, reach + 1)
                 column = column_scr.at[number, member]
-                column[pl.ds(0, ROWS), :] = jnp.zeros((ROWS, LANES), f32)
-                column[pl.ds(ROWS, ROWS), :] = halo[member * ROWS : (member + 1) * ROWS]
-                column[pl.ds(2 * ROWS, ROWS), :] = front_buf[member, :, lanes].astype(f32)[:ROWS]
-                parts += fir(column, taps, 2 * ROWS, 1)
+                column[pl.ds(0, ROWS), :] = halo[member * ROWS : (member + 1) * ROWS]
+                source = (key_ref, value_ref)[member]
+                column[pl.ds(ROWS, ROWS), :] = source[: 2 * ROWS, lanes].astype(f32)[:ROWS]
+                parts.append(fir(column, taps, ROWS))
             u = jnp.where(sublane() < reach, rounded(parts[0] * parts[1]), 0.0)
             token_scr[pl.ds(pl.multiple_of((chunk * TILES + number) * ROWS, ROWS), ROWS), :] = u
             head_ref[:, lanes] = jnp.concatenate([u, jnp.zeros((ROWS, LANES), f32)], axis=0).astype(bf16)
@@ -296,14 +273,19 @@
             out_ref[mode * split + part] = rows.astype(out_ref.dtype)
 
 
-def gate_kernel(query_ref, halo_ref, feat_ref, gate_ref, *scratches):
-    query_buf, halo_buf, gate_buf, wide_scr, column, in_sem, small_sem, out_sem = scratches
+def gate_kernel(query_ref, halo_ref, feat_ref, u_ref, head_ref, rate_ref, coef_ref, skip_ref, gate_ref, *rest, early):
+    y_ref, mid_ref, query_buf, halo_buf, gate_buf, wide_scr, column, in_sem, small_sem, out_sem = rest[:10]
+    inner = rest[10:]
     chunks, tokens = gate_buf.shape[:2]
     count = feat_ref.shape[2]
     fetch = columns_in(((query_ref, query_buf),), in_sem)
     halo_copy = pltpu.make_async_copy(halo_ref, halo_buf, small_sem.at[0])
     halo_copy.start()
     begin(chunks, fetch)
+    local_fetch, local_chunk, local_send = local_parts(
+        u_ref, head_ref, rate_ref, coef_ref, skip_ref, y_ref, mid_ref, *inner, first=0
+    )
+    begin(early, local_fetch)
     widened(feat_ref, 0, wide_scr, 0)
     halo_copy.wait()
 
@@ -312,18 +294,22 @@
             lanes = tile_lanes(number)
             taps = chunk_taps(wide_scr, at, 0, number, count)
             halo = halo_buf[:, tile_lanes(at * TILES + number)].astype(f32)
-            column[pl.ds(0, ROWS), :] = jnp.zeros((ROWS, LANES), f32)
-            column[pl.ds(ROWS, ROWS), :] = halo[2 * ROWS :]
+            column[pl.ds(0, ROWS), :] = halo[2 * ROWS :]
             lay_column(column, query_buf.at[at], lanes)
-            found = fir(column, taps, 2 * ROWS, tokens // ROWS)
             for pair in range(tokens // (2 * ROWS)):
+                first = pair * 2 * ROWS + ROWS
+                found = [fir(column, taps, first), fir(column, taps, first + ROWS)]
                 rows = slice(pair * 2 * ROWS, (pair + 1) * 2 * ROWS)
-                gate_buf[at, rows, lanes] = jnp.concatenate(found[pair * 2 : pair * 2 + 2], axis=0).astype(bf16)
+                gate_buf[at, rows, lanes] = jnp.concatenate(found, axis=0).astype(bf16)
             return 0
 
         lax.fori_loop(0, TILES, tile, 0)
 
-    over_chunks(chunks, fetch, chunk, columns_out(gate_ref, gate_buf, out_sem))
+    give = columns_out(gate_ref, gate_buf, out_sem)
+    over_chunks(chunks, fetch, chunk, give, last=False)
+    over_chunks(early, local_fetch, local_chunk, local_send)
+    for at in range(chunks):
+        wait_all(give(at))
 
 
 def prefix_kernel(piece_ref, rate_ref, coef_ref, out_ref, table_scr, *, tokens, axes):
@@ -356,7 +342,13 @@
 
 
 def local_kernel(u_ref, head_ref, rate_ref, coef_ref, skip_ref, *rest, first, last):
-    y_ref, mid_ref, u_buf, y_buf, mid_buf, token_scr, sum_scr, in_sem, out_sem, mid_sem = rest[-10:]
+    fetch, chunk, send = local_parts(u_ref, head_ref, rate_ref, coef_ref, skip_ref, *rest[-10:], first=first)
+    begin(last - first, fetch)
+    over_chunks(last - first, fetch, chunk, send)
+
+
+def local_parts(u_ref, head_ref, rate_ref, coef_ref, skip_ref, y_ref, mid_ref, *scratches, first):
+    u_buf, y_buf, mid_buf, token_scr, sum_scr, in_sem, out_sem, mid_sem = scratches
     tokens = u_buf.shape[1]
     modes = rate_ref.shape[0]
     half_groups = tokens // ROWS // 2
@@ -369,8 +361,6 @@
     def send(number):
         at = number + first
         return give(at) + [pltpu.make_async_copy(mid_buf.at[at], mid_ref.at[at], mid_sem.at[at])]
-
-    begin(last - first, fetch)
 
     def chunk(number):
         at = number + first
@@ -407,7 +397,7 @@
                 rows = slice(group * ROWS, (group + 1) * ROWS)
                 y_buf[at, rows, tile * LANES : (tile + 1) * LANES] = sum_scr[pl.ds(slot, ROWS), :]
 
-    over_chunks(last - first, fetch, chunk, send)
+    return fetch, chunk, send
 
 
 def final_kernel(piece_ref, rate_ref, mid_ref, y_ref, gate_ref, out_ref, *scratches):
@@ -512,16 +502,15 @@
     halo = lax.ppermute(packed, axes, [(at, at + 1) for at in range(devices - 1)])
 
     feat = featurizer.reshape(members, taps, chunks, groups // chunks).transpose(2, 0, 1, 3)
-    column = vmem((2 * ROWS + tokens, LANES), f32)
+    column = vmem((ROWS + tokens, LANES), f32)
     half_buf, whole_buf = vmem((chunks, tokens, CHUNK), bf16), vmem((chunks, tokens, CHUNK), f32)
     u, wide_taps, state = call(
         signal_kernel,
         (key_proj, value_proj, feat, rates),
-        [far((tokens, width), bf16), near((chunks, 2, ROWS, CHUNK), f32), near((modes, tiles, LANES), f32)],
-        [half_buf, half_buf, half_buf, vmem((4, modes, CHUNK), f32), column, column]
-        + [dma((2, chunks)), dma((1, chunks))],
+        [near((tokens, width), bf16), near((chunks, 2, ROWS, CHUNK), f32), near((modes, tiles, LANES), f32)],
+        [vmem((4, modes, width), f32), vmem((modes, ROWS, LANES), f32), column, column],
         "signal",
-        close=(2, 3),
+        close=range(4),
         cost_estimate=cost(60 * elements, 10 * elements),
     )
 
@@ -530,43 +519,30 @@
         functools.partial(head_kernel, tokens=tokens, reach=taps - 1),
         (key_proj, value_proj, halo, rates, wide_taps, state),
         [near(pieces, bf16), near((2 * ROWS, width), bf16)],
-        [vmem((2, 2 * ROWS, width), bf16), vmem((modes * tiles, LANES), f32), vmem((TILES, 2, 3 * ROWS, LANES), f32)]
-        + [vmem((tiles * ROWS, LANES), f32), vmem((modes, tiles, LANES), f32), dma((2,))],
+        [vmem((modes * tiles, LANES), f32), vmem((TILES, 2, 2 * ROWS, LANES), f32)]
+        + [vmem((tiles * ROWS, LANES), f32), vmem((modes, tiles, LANES), f32)],
         "head",
-        close=(2, 3, 4, 5),
+        close=range(6),
     )
     left, halo_late, rates_late, skip_late, u_late = lax.optimization_barrier((left, halo, rates, skip, u))
     coef = residues * jnp.sqrt(-jnp.expm1(-2.0 * rates_late) / modes)
     skip_row = skip_late[None, :]
-    (gate,) = call(
-        gate_kernel,
-        (query, halo_late, feat),
-        [far((tokens, width), bf16)],
+    stage = vmem((tokens // ROWS // 2 * ROWS * ROWS, LANES), f32)
+    local_shapes = [far((tokens, width), f32), far((chunks, modes, ROWS, LANES), f32)]
+    local_scratches = [half_buf, whole_buf, vmem((chunks, modes, ROWS, LANES), f32), stage, stage]
+    local_scratches += [dma((1, chunks)), dma((1, chunks)), dma((chunks,))]
+    early = chunks * 2 // 9
+    gate, y, mid = call(
+        functools.partial(gate_kernel, early=early),
+        (query, halo_late, feat, u_late, head, rates, coef, skip_row),
+        [far((tokens, width), bf16)] + local_shapes,
         [half_buf, vmem((members * ROWS, width), bf16), half_buf, vmem((chunks, 1, ROWS, CHUNK), f32), column]
-        + [dma((1, chunks)), dma((1,)), dma((1, chunks))],
+        + [dma((1, chunks)), dma((1,)), dma((1, chunks))]
+        + local_scratches,
         "gate",
-        close=(2,),
-        cost_estimate=cost(14 * elements, 4 * elements),
-    )
-
-    stage = vmem((tokens // ROWS // 2 * ROWS * ROWS, LANES), f32)
-
-    def within(u, head, y, mid, first, last):
-        before = () if y is None else (y, mid)
-        return call(
-            functools.partial(local_kernel, first=first, last=last),
-            (u, head, rates, coef, skip_row, *before),
-            [far((tokens, width), f32), far((chunks, modes, ROWS, LANES), f32)],
-            [half_buf, whole_buf, vmem((chunks, modes, ROWS, LANES), f32), stage, stage]
-            + [dma((1, chunks)), dma((1, chunks)), dma((chunks,))],
-            "within",
-            close=(1, 2, 3, 4),
-            cost_estimate=cost(7 * (last - first) * tokens * CHUNK * 10, (last - first) * tokens * CHUNK * 8),
-            input_output_aliases={5 + at: at for at in range(len(before))},
-        )
-
-    early = chunks // 3
-    y, mid = within(u_late, head, None, None, 0, early)
+        close=(2, 4, 5, 6, 7),
+        cost_estimate=cost(28 * elements, 6 * elements),
+    )
 
     def swap(value):
         return lax.all_to_all(value, axes, split_axis=0, concat_axis=0, tiled=True)
@@ -595,7 +571,16 @@
 
     entering, u_late = lax.optimization_barrier((entering, u))
     entered = swap(entering).reshape(pieces)
-    y, mid = within(u_late, head, y, mid, early, chunks)
+    y, mid = call(
+        functools.partial(local_kernel, first=early, last=chunks),
+        (u_late, head, rates, coef, skip_row, y, mid),
+        local_shapes,
+        local_scratches,
+        "within",
+        close=(1, 2, 3, 4),
+        cost_estimate=cost(50 * elements, 8 * elements),
+        input_output_aliases={5: 0, 6: 1},
+    )
 
     (out,) = call(
         final_kernel,

time: 52.7 us -> 50.2 us (0.953)
  Pallas kernels: 33.7 us -> 30.8 us
  starting transfers between devices: 15.1 us -> 13.5 us
  local copies, waits for them, and re-layouts: 0.16 us -> 1.17 us
  waiting for transfers between devices: 2.69 us -> 3.54 us
    pallas_call x8 -> x7, Pallas kernels: 33.7 us -> 30.8 us  [call(): pl.pallas_call(kernel, in_specs=[beside if at in close else there for at...]
    all_to_all x2, starting transfers between devices: 11.1 us -> 9.53 us  [swap(): return lax.all_to_all(value, axes, split_axis=0, concat_axis=0, tiled=True)]
    unnamed x10 -> x16, local copies, waits for them, and re-layouts: 0.02 us -> 1.03 us
  transfers between devices with their start and end apart: 3 -> 3, of which waited for: 2 -> 3; matrix products, arithmetic and copies ran while one was open for 1% -> 1% of each run, Pallas kernels for 45% -> 42%
where the time goes in v8:
time: 50.2 us; the launch traced here: 49.4 us
  Pallas kernels  30.8 us (61%)
  starting transfers between devices  13.5 us (27%)
  waiting for transfers between devices  3.54 us (7%)
  local copies, waits for them, and re-layouts  1.17 us (2%)
    pallas_call x7, Pallas kernels, call(): pl.pallas_call(kernel, in_specs=[beside if at in close else there for at...  30.8 us
    all_to_all x2, starting transfers between devices, swap(): return lax.all_to_all(value, axes, split_axis=0, concat_axis=0, tiled=True)  9.53 us
    ppermute x1, starting transfers between devices, local(): lax.ppermute(packed, axes, [(at, at + 1) for at in range(devices - 1)])  3.95 us
    all_to_all x2, waiting for transfers between devices, swap(): return lax.all_to_all(value, axes, split_axis=0, concat_axis=0, tiled=True)  2.74 us
    unnamed x16, local copies, waits for them, and re-layouts  1.03 us
  transfers between devices with their start and end apart: 3, of which 3 were waited for; matrix products, arithmetic and copies ran while one was open for 1% of the time, Pallas kernels for 42%

profile of v8, /device:TPU:1, one launch (start us, length us, event | category | flops | bytes accessed | tf_op | source)
XLA Modules:
  0.0 49.4 jit_solution(8490516118021246942)
XLA Ops:
  0.0 0.0 copy-start.2
  0.0 1.2 %pack.1 = bf16[24,4608]{1,0:T(8,128)(2,1)S(1)} custom-call(bf16[128,4608]{1,0:T(8,128)(2,1)} %key_ref.5, bf16[128,4608]{1,0:T(8,128)(2,1)} %value_ref.5, bf16[128,4608]{1,0:T(8,128)(2,1)} %query_ref.3), custom_call_target="tpu_custom_call" | custom-call | tf_op jit(solution)/shard_map/pack/pallas_call | solution.py:484
  1.3 3.9 %collective-permute-start = (bf16[24,4608]{1,0:T(8,128)(2,1)S(1)}, bf16[24,4608]{1,0:T(8,128)(2,1)S(1)}, u32[]{:S(2)}, u32[]{:S(2)}) collective-permute-start(bf16[24,4608]{1,0:T(8,128)(2,1)S(1)} %pack.1), channel_id=1, source_target_pairs={{0,1},{1,2},{2,3},{3,4},{4,5},{5,6},{6,7},{7,8},{8,9},{9,10},{10,1... | collective-permute-start | bytes 663560 | tf_op jit(solution)/shard_map/ppermute | solution.py:502
  5.2 0.0 copy-done.6
  5.2 0.1 reshape.3
  5.4 0.0 copy-done
  5.4 0.0 copy-done.1
  5.4 0.0 copy-done.2
  5.4 7.1 %signal.1 = (bf16[128,4608]{1,0:T(8,128)(2,1)S(1)}, f32[9,2,8,512]{3,2,1,0:T(8,128)S(1)}, f32[16,36,128]{2,1,0:T(8,128)S(1)}) custom-call(bf16[128,4608]{1,0:T(8,128)(2,1)S(1)} %copy-done.1, bf16[128,4608]{1,0:T(8,128)(2,1)S(1)} %copy-done.2, f32[9,3,7,32]{3,2,1,0:T(8,128)S(1)} %bitcast.3, f32[16,4608]{1,0:T(8,128)S(1)} %copy-done), custom_call_target="tpu_custom_call" | custom-call | flops 35389440 | bytes 5898240 | tf_op jit(solution)/shard_map/signal/pallas_call | solution.py:484
  12.5 0.0 copy-start.3
  12.5 1.0 %copy-done.3 = bf16[128,4608]{1,0:T(8,128)(2,1)} copy-done((bf16[128,4608]{1,0:T(8,128)(2,1)}, bf16[128,4608]{1,0:T(8,128)(2,1)S(1)}, u32[]{:S(2)}) %copy-start.3) | copy-done | bytes 1179672
  13.5 0.8 %collective-permute-done.halo_ref = bf16[24,4608]{1,0:T(8,128)(2,1)S(1)} collective-permute-done((bf16[24,4608]{1,0:T(8,128)(2,1)S(1)}, bf16[24,4608]{1,0:T(8,128)(2,1)S(1)}, u32[]{:S(2)}, u32[]{:S(2)}) %collective-permute-start) | collective-permute-done | bytes 221216 | tf_op jit(solution)/shard_map/ppermute | solution.py:502
  14.3 1.4 %head.1 = (bf16[32,18,128]{2,1,0:T(8,128)(2,1)}, bf16[16,4608]{1,0:T(8,128)(2,1)S(1)}) custom-call(bf16[128,4608]{1,0:T(8,128)(2,1)S(1)} %copy-done.1, bf16[128,4608]{1,0:T(8,128)(2,1)S(1)} %copy-done.2, bf16[24,4608]{1,0:T(8,128)(2,1)S(1)} %collective-permute-done.halo_ref, f32[16,4608]{1,0:T(8,128)S(1)} %copy-done, ...), custom_call_target="tpu_custom_call" | custom-call | tf_op jit(solution)/shard_map/head/pallas_call | solution.py:484
  15.7 4.8 %all-to-all-start = ((bf16[32,18,128]{2,1,0:T(8,128)(2,1)}), bf16[32,18,128]{2,1,0:T(8,128)(2,1)S(1)}, u32[]{:S(2)}, u32[]{:S(2)}) async-start(bf16[32,18,128]{2,1,0:T(8,128)(2,1)} %get-tuple-element.32), calls=%async_computation | async-start | bytes 393216 | tf_op jit(solution)/shard_map/all_to_all | solution.py:548
  20.5 0.0 copy-done.5
  20.5 0.2 sqrt_multiply_fusion.coef_ref
  20.7 0.0 copy-done.7
  20.8 7.0 %gate.1 = (bf16[128,4608]{1,0:T(8,128)(2,1)}, f32[128,4608]{1,0:T(8,128)}, f32[9,16,8,128]{3,2,1,0:T(8,128)}) custom-call(bf16[128,4608]{1,0:T(8,128)(2,1)} %query_ref.3, bf16[24,4608]{1,0:T(8,128)(2,1)} %copy-done.4, f32[9,3,7,32]{3,2,1,0:T(8,128)S(1)} %bitcast.4, bf16[128,4608]{1,0:T(8,128)(2,1)} %copy-done.3, ...), custom_call_target="tpu_custom_call" | custom-call | flops 16515072 | bytes 3538944 | tf_op jit(solution)/shard_map/gate/pallas_call | solution.py:484
  27.8 1.2 %all-to-all-done.piece_ref = bf16[32,18,128]{2,1,0:T(8,128)(2,1)S(1)} async-done(((bf16[32,18,128]{2,1,0:T(8,128)(2,1)}), bf16[32,18,128]{2,1,0:T(8,128)(2,1)S(1)}, u32[]{:S(2)}, u32[]{:S(2)}) %all-to-all-start) | async-done | bytes 147488 | tf_op jit(solution)/shard_map/all_to_all | solution.py:548
  29.0 0.8 %prefix.1 = bf16[32,18,128]{2,1,0:T(8,128)(2,1)} custom-call(bf16[32,18,128]{2,1,0:T(8,128)(2,1)S(1)} %all-to-all-done.piece_ref, f32[16,4608]{1,0:T(8,128)S(1)} %copy-done, f32[16,4608]{1,0:T(8,128)S(1)} %sqrt_multiply_fusion.coef_ref), custom_call_target="tpu_custom_call" | custom-call | tf_op jit(solution)/shard_map/prefix/pallas_call | solution.py:484
  29.8 4.7 %all-to-all-start.1 = ((bf16[32,18,128]{2,1,0:T(8,128)(2,1)}), bf16[32,18,128]{2,1,0:T(8,128)(2,1)S(1)}, u32[]{:S(2)}, u32[]{:S(2)}) async-start(bf16[32,18,128]{2,1,0:T(8,128)(2,1)} %prefix.1), calls=%async_computation.1 | async-start | bytes 393216 | tf_op jit(solution)/shard_map/all_to_all | solution.py:548
  34.5 6.9 %within.1 = (f32[128,4608]{1,0:T(8,128)}, f32[9,16,8,128]{3,2,1,0:T(8,128)}) custom-call(bf16[128,4608]{1,0:T(8,128)(2,1)} %copy-done.3, bf16[16,4608]{1,0:T(8,128)(2,1)S(1)} %get-tuple-element.35.head_ref, f32[16,4608]{1,0:T(8,128)S(1)} %copy-done, f32[16,4608]{1,0:T(8,128)S(1)} %sqrt_multiply_fusion.coef_ref, ...), custom_call_target="tpu_custom_call", output_to_operand_aliasing={{0}: (5, {}), {1}: (6, {})} | custom-call | flops 29491200 | bytes 4718592 | tf_op jit(solution)/shard_map/within/pallas_call | solution.py:484
  41.4 1.6 %all-to-all-done.1.piece_ref = bf16[32,18,128]{2,1,0:T(8,128)(2,1)S(1)} async-done(((bf16[32,18,128]{2,1,0:T(8,128)(2,1)}), bf16[32,18,128]{2,1,0:T(8,128)(2,1)S(1)}, u32[]{:S(2)}, u32[]{:S(2)}) %all-to-all-start.1) | async-done | bytes 147488 | tf_op jit(solution)/shard_map/all_to_all | solution.py:548
  43.0 6.4 %final.1 = bf16[128,4608]{1,0:T(8,128)(2,1)} custom-call(bf16[32,18,128]{2,1,0:T(8,128)(2,1)S(1)} %all-to-all-done.1.piece_ref, f32[16,4608]{1,0:T(8,128)S(1)} %copy-done, f32[9,16,8,128]{3,2,1,0:T(8,128)} %get-tuple-element.48.mid_ref, f32[128,4608]{1,0:T(8,128)} %get-tuple-element.49.y_ref, bf16[128,4608]{1,0:T(8,128)(2,1)} %get-tuple-element.50.gate_ref), custom_call_target="tpu_custom_call" | custom-call | flops 23592960 | bytes 5898240 | tf_op jit(solution)/shard_map/final/pallas_call | solution.py:484
  (9 shorter events, 0.1 us)
Async XLA Ops:
  0.0 5.2 %copy-start.6 = (f32[3,7,288]{2,1,0:T(8,128)S(1)}, f32[3,7,288]{2,1,0:T(8,128)}, u32[]{:S(2)}) copy-start(f32[3,7,288]{2,1,0:T(8,128)} %param.10) | copy-start | bytes 72580
  0.0 5.4 %copy-start = (f32[16,4608]{1,0:T(8,128)S(1)}, f32[16,4608]{1,0:T(8,128)}, u32[]{:S(2)}) copy-start(f32[16,4608]{1,0:T(8,128)} %rate_ref.11) | copy-start | bytes 884740
  0.0 5.4 %copy-start.1 = (bf16[128,4608]{1,0:T(8,128)(2,1)S(1)}, bf16[128,4608]{1,0:T(8,128)(2,1)}, u32[]{:S(2)}) copy-start(bf16[128,4608]{1,0:T(8,128)(2,1)} %key_ref.5) | copy-start | bytes 3538948
  0.0 5.4 %copy-start.2 = (bf16[128,4608]{1,0:T(8,128)(2,1)S(1)}, bf16[128,4608]{1,0:T(8,128)(2,1)}, u32[]{:S(2)}) copy-start(bf16[128,4608]{1,0:T(8,128)(2,1)} %value_ref.5) | copy-start | bytes 3538948
  1.3 13.0 %collective-permute-start = (bf16[24,4608]{1,0:T(8,128)(2,1)S(1)}, bf16[24,4608]{1,0:T(8,128)(2,1)S(1)}, u32[]{:S(2)}, u32[]{:S(2)}) collective-permute-start(bf16[24,4608]{1,0:T(8,128)(2,1)S(1)} %pack.1), channel_id=1, source_target_pairs={{0,1},{1,2},{2,3},{3,4},{4,5},{5,6},{6,7},{7,8},{8,9},{9,10},{10,1... | collective-permute-start | bytes 663560 | tf_op jit(solution)/shard_map/ppermute | solution.py:502
  12.5 1.0 %copy-start.3 = (bf16[128,4608]{1,0:T(8,128)(2,1)}, bf16[128,4608]{1,0:T(8,128)(2,1)S(1)}, u32[]{:S(2)}) copy-start(bf16[128,4608]{1,0:T(8,128)(2,1)S(1)} %get-tuple-element.44.u_ref) | copy-start | bytes 3538948
  14.3 1.4 %copy-start.4 = (bf16[24,4608]{1,0:T(8,128)(2,1)}, bf16[24,4608]{1,0:T(8,128)(2,1)S(1)}, u32[]{:S(2)}) copy-start(bf16[24,4608]{1,0:T(8,128)(2,1)S(1)} %collective-permute-done.halo_ref) | copy-start | bytes 663556
  14.3 6.2 %copy-start.5 = (f32[16,4608]{1,0:T(8,128)S(1)}, f32[16,4608]{1,0:T(8,128)}, u32[]{:S(2)}) copy-start(f32[16,4608]{1,0:T(8,128)} %param.12) | copy-start | bytes 884740
  15.7 5.0 %copy-start.7 = (f32[4608]{0:T(1024)S(1)}, f32[4608]{0:T(1024)}, u32[]{:S(2)}) copy-start(f32[4608]{0:T(1024)} %param.13) | copy-start | bytes 55300
  15.7 13.3 %all-to-all-start = ((bf16[32,18,128]{2,1,0:T(8,128)(2,1)}), bf16[32,18,128]{2,1,0:T(8,128)(2,1)S(1)}, u32[]{:S(2)}, u32[]{:S(2)}) async-start(bf16[32,18,128]{2,1,0:T(8,128)(2,1)} %get-tuple-element.32), calls=%async_computation | async-start | bytes 393216 | tf_op jit(solution)/shard_map/all_to_all | solution.py:548
  29.8 13.2 %all-to-all-start.1 = ((bf16[32,18,128]{2,1,0:T(8,128)(2,1)}), bf16[32,18,128]{2,1,0:T(8,128)(2,1)S(1)}, u32[]{:S(2)}, u32[]{:S(2)}) async-start(bf16[32,18,128]{2,1,0:T(8,128)(2,1)} %prefix.1), calls=%async_computation.1 | async-start | bytes 393216 | tf_op jit(solution)/shard_map/all_to_all | solution.py:548

commit v9 on v8

--- a/solution.py
+++ b/solution.py
@@ -175,7 +175,8 @@
     out_ref[...] = jnp.concatenate(tails, axis=0).astype(bf16)
 
 
-def signal_kernel(key_ref, value_ref, feat_ref, rate_ref, u_ref, wide_ref, state_ref, power_scr, last_scr, *columns):
+def signal_kernel(key_ref, value_ref, feat_ref, rate_ref, u_ref, wide_ref, state_ref, *scratches):
+    u_buf, power_scr, last_scr, *columns, out_sem = scratches
     tokens, tiles = u_ref.shape[0], state_ref.shape[1]
     modes = rate_ref.shape[0]
     chunks = tiles // TILES
@@ -218,7 +219,7 @@
                 u = fir(columns[0], taps[0], first) * fir(columns[1], taps[1], first)
                 found.append(jnp.where(sublane() < count - 1, 0.0, u) if first == ROWS else u)
             both = jnp.concatenate(found, axis=0).astype(bf16)
-            u_ref[pair * 2 * ROWS : (pair + 1) * 2 * ROWS, lanes] = both
+            u_buf[pair * 2 * ROWS : (pair + 1) * 2 * ROWS, lanes] = both
             for u in tiles_of(both):
                 if state is None:
                     state = [u] * modes
@@ -228,14 +229,23 @@
             last_scr[mode] = state[mode]
         return 0
 
-    lax.fori_loop(0, tiles, tile, 0)
+    def send(at):
+        return pltpu.make_async_copy(u_buf.at[:, span(at)], u_ref.at[:, span(at)], out_sem.at[at])
+
+    def chunk(at, _):
+        lax.fori_loop(at * TILES, (at + 1) * TILES, tile, 0)
+        send(at).start()
+        return 0
+
+    lax.fori_loop(0, chunks, chunk, 0)
     reduce(tiles - 1)
+    for at in range(chunks):
+        send(at).wait()
 
 
 def head_kernel(key_ref, value_ref, halo_ref, rate_ref, wide_ref, state_ref, out_ref, head_ref, *scratches, tokens, reach):
     rate_scr, column_scr, token_scr, total_scr = scratches
     modes, tiles = state_ref.shape[:2]
-    pieces, piece_rows = out_ref.shape[:2]
     for group in range(modes // ROWS):
         for tile in range(tiles):
             rows = pl.ds((group * tiles + tile) * ROWS, ROWS)
@@ -260,17 +270,14 @@
 
     lax.fori_loop(0, tiles // TILES, some, 0)
     signals = [token_scr[pl.ds(row, tiles, stride=ROWS), :] for row in range(reach)]
-    split = pieces // modes
     for mode in range(modes):
         start = mode // ROWS * tiles * ROWS + mode % ROWS
         decay = jnp.exp(-rate_scr[pl.ds(start, tiles, stride=ROWS), :])
         head = signals[0]
         for row in range(1, reach):
             head = decay * head + signals[row]
-        total_scr[mode] = state_ref[mode] + power(decay, tokens - reach) * head
-        for part in range(split):
-            rows = total_scr[mode, part * piece_rows : (part + 1) * piece_rows, :]
-            out_ref[mode * split + part] = rows.astype(out_ref.dtype)
+        total_scr[mode * tiles : (mode + 1) * tiles, :] = state_ref[mode] + power(decay, tokens - reach) * head
+    out_ref[...] = total_scr[...].astype(bf16)
 
 
 def gate_kernel(query_ref, halo_ref, feat_ref, u_ref, head_ref, rate_ref, coef_ref, skip_ref, gate_ref, *rest, early):
@@ -312,39 +319,45 @@
         wait_all(give(at))
 
 
-def prefix_kernel(piece_ref, rate_ref, coef_ref, out_ref, table_scr, *, tokens, axes):
-    devices, piece_rows = piece_ref.shape[:2]
-    split = devices // rate_ref.shape[0]
+def carry_kernel(state_ref, rate_ref, coef_ref, out_ref, state_buf, rate_scr, through_scr, total_scr, sem, *, tokens, axes):
+    devices, rows = state_buf.shape[:2]
+    modes = rate_ref.shape[0]
+    tiles = rows // modes
     mine = lax.axis_index(axes)
-    mode, part = mine // split, mine % split
-    group = pl.multiple_of(mode // ROWS * ROWS, ROWS)
-    first = pl.multiple_of(part * piece_rows * LANES, LANES)
-
-    def mine_of(ref):
-        rows = ref[pl.ds(group, ROWS), pl.ds(first, piece_rows * LANES)]
-        here = lax.broadcasted_iota(jnp.int32, rows.shape, 0) == mode - group
-        row = jnp.sum(jnp.where(here, rows, 0.0), axis=0, keepdims=True)
-        for number in range(piece_rows):
-            table_scr[number : number + 1, :] = lanes_of(row, number)
-        return table_scr[:piece_rows, :]
-
-    coef = mine_of(coef_ref)
-    through = jnp.exp(-float(tokens) * mine_of(rate_ref))
-
-    def lap(number, entering):
-        for step in range(4):
-            source = number * 4 + step
-            out_ref[source] = (coef * entering).astype(out_ref.dtype)
-            entering = through * entering + piece_ref[source].astype(f32)
-        return entering
-
-    lax.fori_loop(0, devices // 4, lap, jnp.zeros((piece_rows, LANES), f32))
-
-
-def local_kernel(u_ref, head_ref, rate_ref, coef_ref, skip_ref, *rest, first, last):
-    fetch, chunk, send = local_parts(u_ref, head_ref, rate_ref, coef_ref, skip_ref, *rest[-10:], first=first)
-    begin(last - first, fetch)
-    over_chunks(last - first, fetch, chunk, send)
+
+    def fetch(source):
+        return pltpu.make_async_copy(state_ref.at[source], state_buf.at[source], sem.at[source])
+
+    def begin_one(source, _):
+        fetch(source).start()
+        return 0
+
+    lax.fori_loop(0, mine, begin_one, 0)
+
+    def by_row(ref):
+        for group in range(modes // ROWS):
+            for tile in range(tiles):
+                place = pl.ds((group * tiles + tile) * ROWS, ROWS)
+                rate_scr[place, :] = ref[group * ROWS : (group + 1) * ROWS, tile * LANES : (tile + 1) * LANES]
+        return [
+            rate_scr[pl.ds(mode // ROWS * tiles * ROWS + mode % ROWS, tiles, stride=ROWS), :] for mode in range(modes)
+        ]
+
+    for mode, rate in enumerate(by_row(rate_ref)):
+        through_scr[mode * tiles : (mode + 1) * tiles, :] = jnp.exp(-float(tokens) * rate)
+    total_scr[...] = jnp.zeros(total_scr.shape, f32)
+
+    def lap(source, _):
+        fetch(source).wait()
+        for first in range(0, rows, 2 * ROWS):
+            part = slice(first, first + 2 * ROWS)
+            total_scr[part, :] = through_scr[part, :] * total_scr[part, :] + state_buf[source, part, :].astype(f32)
+        return 0
+
+    lax.fori_loop(0, mine, lap, 0)
+    for mode, coef in enumerate(by_row(coef_ref)):
+        part = slice(mode * tiles, (mode + 1) * tiles)
+        out_ref[part, :] = coef * total_scr[part, :]
 
 
 def local_parts(u_ref, head_ref, rate_ref, coef_ref, skip_ref, y_ref, mid_ref, *scratches, first):
@@ -401,7 +414,7 @@
 
 
 def final_kernel(piece_ref, rate_ref, mid_ref, y_ref, gate_ref, out_ref, *scratches):
-    mid_buf, y_buf, gate_buf, out_buf, total_scr, power_scr, lead_scr, in_sem, mid_sem, out_sem = scratches
+    mid_buf, y_buf, gate_buf, out_buf, power_scr, lead_scr, in_sem, mid_sem, out_sem = scratches
     chunks, modes = mid_buf.shape[:2]
     tokens = y_buf.shape[1]
     columns = columns_in(((y_ref, y_buf), (gate_ref, gate_buf)), in_sem)
@@ -410,12 +423,7 @@
         return columns(at) + [pltpu.make_async_copy(mid_ref.at[at], mid_buf.at[at], mid_sem.at[at])]
 
     begin(chunks, fetch)
-    pieces, piece_rows = piece_ref.shape[:2]
-    split = pieces // modes
-    for mode in range(modes):
-        for part in range(split):
-            rows = piece_ref[mode * split + part].astype(f32)
-            total_scr[mode, part * piece_rows : (part + 1) * piece_rows, :] = rows
+    tiles = piece_ref.shape[0] // modes
     bits = [(sublane() >> level) % 2 == 1 for level in range(3)]
 
     def chunk(at):
@@ -433,7 +441,7 @@
                 for bit, row in zip(bits, rows):
                     lead = lead * jnp.where(bit, row, 1.0)
                 lead_scr[mode] = lead
-                state.append(lead * wide(total_scr[mode, pl.ds(at * TILES + number, 1), :]))
+                state.append(lead * wide(piece_ref[pl.ds(mode * tiles + at * TILES + number, 1), :]))
             decay = [wide(power_scr[3, mode : mode + 1, lanes]) for mode in range(modes)]
             for pair in range(tokens // (2 * ROWS)):
                 rows = slice(pair * 2 * ROWS, (pair + 1) * 2 * ROWS)
@@ -467,8 +475,6 @@
     devices = math.prod(lax.axis_size(axis) for axis in axes)
     chunks = width // CHUNK
     tiles = width // LANES
-    split = devices // modes
-    even = devices % modes == 0 and tiles % split == 0
     vmem = pltpu.VMEM
     far = pltpu.HBM
     near = jax.ShapeDtypeStruct
@@ -507,34 +513,34 @@
     u, wide_taps, state = call(
         signal_kernel,
         (key_proj, value_proj, feat, rates),
-        [near((tokens, width), bf16), near((chunks, 2, ROWS, CHUNK), f32), near((modes, tiles, LANES), f32)],
-        [vmem((4, modes, width), f32), vmem((modes, ROWS, LANES), f32), column, column],
+        [far((tokens, width), bf16), near((chunks, 2, ROWS, CHUNK), f32), near((modes, tiles, LANES), f32)],
+        [vmem((tokens, width), bf16), vmem((4, modes, width), f32), vmem((modes, ROWS, LANES), f32)]
+        + [column, column, dma((chunks,))],
         "signal",
         close=range(4),
         cost_estimate=cost(60 * elements, 10 * elements),
     )
 
-    pieces = (modes * split, tiles // split, LANES) if even else (modes, tiles, LANES)
+    flat = (modes * tiles, LANES)
     left, head = call(
         functools.partial(head_kernel, tokens=tokens, reach=taps - 1),
         (key_proj, value_proj, halo, rates, wide_taps, state),
-        [near(pieces, bf16), near((2 * ROWS, width), bf16)],
+        [near(flat, bf16), near((2 * ROWS, width), bf16)],
         [vmem((modes * tiles, LANES), f32), vmem((TILES, 2, 2 * ROWS, LANES), f32)]
-        + [vmem((tiles * ROWS, LANES), f32), vmem((modes, tiles, LANES), f32)],
+        + [vmem((tiles * ROWS, LANES), f32), vmem(flat, f32)],
         "head",
         close=range(6),
     )
-    left, halo_late, rates_late, skip_late, u_late = lax.optimization_barrier((left, halo, rates, skip, u))
+    left, halo_late, rates_late, skip_late = lax.optimization_barrier((left, halo, rates, skip))
     coef = residues * jnp.sqrt(-jnp.expm1(-2.0 * rates_late) / modes)
     skip_row = skip_late[None, :]
     stage = vmem((tokens // ROWS // 2 * ROWS * ROWS, LANES), f32)
     local_shapes = [far((tokens, width), f32), far((chunks, modes, ROWS, LANES), f32)]
     local_scratches = [half_buf, whole_buf, vmem((chunks, modes, ROWS, LANES), f32), stage, stage]
     local_scratches += [dma((1, chunks)), dma((1, chunks)), dma((chunks,))]
-    early = chunks * 2 // 9
     gate, y, mid = call(
-        functools.partial(gate_kernel, early=early),
-        (query, halo_late, feat, u_late, head, rates, coef, skip_row),
+        functools.partial(gate_kernel, early=chunks),
+        (query, halo_late, feat, u, head, rates, coef, skip_row),
         [far((tokens, width), bf16)] + local_shapes,
         [half_buf, vmem((members * ROWS, width), bf16), half_buf, vmem((chunks, 1, ROWS, CHUNK), f32), column]
         + [dma((1, chunks)), dma((1,)), dma((1, chunks))]
@@ -544,50 +550,40 @@
         cost_estimate=cost(28 * elements, 6 * elements),
     )
 
-    def swap(value):
-        return lax.all_to_all(value, axes, split_axis=0, concat_axis=0, tiled=True)
-
-    share = modes * width // devices
-    theirs = swap(left if even else left.reshape(devices, share))
-    theirs, gate, coef, skip_row, y, mid = lax.optimization_barrier((theirs, gate, coef, skip_row, y, mid))
-    if even:
-        (entering,) = call(
-            functools.partial(prefix_kernel, tokens=tokens, axes=axes),
-            (theirs, rates, coef),
-            [near(pieces, bf16)],
-            [vmem((-(-pieces[1] // ROWS) * ROWS, LANES), f32)],
-            "prefix",
-            close=(0, 1, 2),
+    if devices * flat[0] * LANES * 2 <= 8 * 2**20:
+        gathered = lax.all_gather(left, axes)
+        gathered, gate, y, mid = lax.optimization_barrier((gathered, gate, y, mid))
+        (entered,) = call(
+            functools.partial(carry_kernel, tokens=tokens, axes=axes),
+            (gathered, rates, coef),
+            [near(flat, f32)],
+            [vmem((devices, *flat), bf16)] + [vmem(flat, f32)] * 3 + [dma((devices,))],
+            "carry",
+            close=(1, 2),
         )
     else:
-        mine = lax.axis_index(axes)
-        through = jnp.exp(-float(tokens) * lax.dynamic_slice_in_dim(rates.reshape(-1), mine * share, share))
-        factor = lax.dynamic_slice_in_dim(coef.reshape(-1), mine * share, share)
+        share = modes * width // devices
+        first = lax.axis_index(axes) * share
+
+        def swap(value):
+            return lax.all_to_all(value, axes, split_axis=0, concat_axis=0, tiled=True)
+
+        theirs = swap(left.reshape(devices, share))
+        through = jnp.exp(-float(tokens) * lax.dynamic_slice_in_dim(rates.reshape(-1), first, share))
+        factor = lax.dynamic_slice_in_dim(coef.reshape(-1), first, share)
         _, entering = lax.scan(
             lambda so_far, piece: (through * so_far + piece.astype(f32), (factor * so_far).astype(bf16)),
             jnp.zeros((share,), f32),
             theirs,
         )
-
-    entering, u_late = lax.optimization_barrier((entering, u))
-    entered = swap(entering).reshape(pieces)
-    y, mid = call(
-        functools.partial(local_kernel, first=early, last=chunks),
-        (u_late, head, rates, coef, skip_row, y, mid),
-        local_shapes,
-        local_scratches,
-        "within",
-        close=(1, 2, 3, 4),
-        cost_estimate=cost(50 * elements, 8 * elements),
-        input_output_aliases={5: 0, 6: 1},
-    )
+        entered = swap(entering).reshape(flat).astype(f32)
 
     (out,) = call(
         final_kernel,
         (entered, rates, mid, y, gate),
         [far((tokens, width), bf16)],
         [vmem((chunks, modes, ROWS, LANES), f32), whole_buf, half_buf, half_buf]
-        + [vmem((modes, tiles, LANES), f32), vmem((4, modes, CHUNK), f32), vmem((modes, ROWS, LANES), f32)]
+        + [vmem((4, modes, CHUNK), f32), vmem((modes, ROWS, LANES), f32)]
         + [dma((2, chunks)), dma((chunks,)), dma((1, chunks))],
         "final",
         close=(0, 1),

time: 50.2 us -> 102 us (2.03)
  waiting for transfers between devices: 3.54 us -> 52.7 us
  between operations: 0.15 us -> 13.5 us
  starting transfers between devices: 13.5 us -> 3.95 us
    all_gather x0 -> x1, waiting for transfers between devices: none -> 51.7 us  [local(): gathered = lax.all_gather(left, axes)]
    all_to_all x2 -> x0, starting transfers between devices: 9.53 us -> none  [swap(): return lax.all_to_all(value, axes, split_axis=0, concat_axis=0, tiled=True)]
    all_to_all x2 -> x0, waiting for transfers between devices: 2.74 us -> none  [swap(): return lax.all_to_all(value, axes, split_axis=0, concat_axis=0, tiled=True)]
    pallas_call x7 -> x6, Pallas kernels: 30.8 us -> 30.5 us  [call(): pl.pallas_call(kernel, in_specs=[beside if at in close else there for at...]
  transfers between devices with their start and end apart: 3 -> 2, of which waited for: 3 -> 2; matrix products, arithmetic and copies ran while one was open for 1% -> 0% of each run, Pallas kernels for 42% -> 20%
where the time goes in v9:
time: 102 us; the launch traced here: 101 us
  waiting for transfers between devices  52.7 us (52%)
  Pallas kernels  30.5 us (30%)
  between operations  13.5 us (13%)
  starting transfers between devices  3.95 us (4%)
    all_gather x1, waiting for transfers between devices, local(): gathered = lax.all_gather(left, axes)  51.7 us
    pallas_call x6, Pallas kernels, call(): pl.pallas_call(kernel, in_specs=[beside if at in close else there for at...  30.5 us
    ppermute x1, starting transfers between devices, local(): lax.ppermute(packed, axes, [(at, at + 1) for at in range(devices - 1)])  3.95 us
  transfers between devices with their start and end apart: 2, of which 2 were waited for; matrix products, arithmetic and copies ran while one was open for 0% of the time, Pallas kernels for 20%

profile of v9, /device:TPU:1, one launch (start us, length us, event | category | flops | bytes accessed | tf_op | source)
XLA Modules:
  0.0 101.0 jit_solution(16805729613937635301)
XLA Ops:
  6.5 0.0 copy-start.5
  6.5 0.0 copy-start
  6.5 0.0 all-gather.3.cloned.1.call-start
  6.5 0.0 copy-start.1
  6.5 0.0 copy-start.2
  6.5 1.2 %pack.1 = bf16[24,4608]{1,0:T(8,128)(2,1)S(1)} custom-call(bf16[128,4608]{1,0:T(8,128)(2,1)} %key_ref.5, bf16[128,4608]{1,0:T(8,128)(2,1)} %value_ref.5, bf16[128,4608]{1,0:T(8,128)(2,1)} %query_ref.3), custom_call_target="tpu_custom_call" | custom-call | tf_op jit(solution)/shard_map/pack/pallas_call | solution.py:490
  7.8 3.9 %collective-permute-start = (bf16[24,4608]{1,0:T(8,128)(2,1)S(1)}, bf16[24,4608]{1,0:T(8,128)(2,1)S(1)}, u32[]{:S(2)}, u32[]{:S(2)}) collective-permute-start(bf16[24,4608]{1,0:T(8,128)(2,1)S(1)} %pack.1), channel_id=1, source_target_pairs={{0,1},{1,2},{2,3},{3,4},{4,5},{5,6},{6,7},{7,8},{8,9},{9,10},{10,1... | collective-permute-start | bytes 663560 | tf_op jit(solution)/shard_map/ppermute | solution.py:508
  11.8 0.0 copy-done.5
  11.8 0.1 reshape.3
  11.9 0.0 copy-done
  11.9 0.0 copy-done.1
  11.9 0.0 copy-done.2
  11.9 7.8 %signal.1 = (bf16[128,4608]{1,0:T(8,128)(2,1)}, f32[9,2,8,512]{3,2,1,0:T(8,128)S(1)}, f32[16,36,128]{2,1,0:T(8,128)S(1)}) custom-call(bf16[128,4608]{1,0:T(8,128)(2,1)S(1)} %copy-done.1, bf16[128,4608]{1,0:T(8,128)(2,1)S(1)} %copy-done.2, f32[9,3,7,32]{3,2,1,0:T(8,128)S(1)} %bitcast.4, f32[16,4608]{1,0:T(8,128)S(1)} %copy-done), custom_call_target="tpu_custom_call" | custom-call | flops 35389440 | bytes 5898240 | tf_op jit(solution)/shard_map/signal/pallas_call | solution.py:490
  19.8 1.1 %collective-permute-done.halo_ref = bf16[24,4608]{1,0:T(8,128)(2,1)S(1)} collective-permute-done((bf16[24,4608]{1,0:T(8,128)(2,1)S(1)}, bf16[24,4608]{1,0:T(8,128)(2,1)S(1)}, u32[]{:S(2)}, u32[]{:S(2)}) %collective-permute-start) | collective-permute-done | bytes 221216 | tf_op jit(solution)/shard_map/ppermute | solution.py:508
  20.8 1.3 %head.1 = (bf16[576,128]{1,0:T(8,128)(2,1)}, bf16[16,4608]{1,0:T(8,128)(2,1)S(1)}) custom-call(bf16[128,4608]{1,0:T(8,128)(2,1)S(1)} %copy-done.1, bf16[128,4608]{1,0:T(8,128)(2,1)S(1)} %copy-done.2, bf16[24,4608]{1,0:T(8,128)(2,1)S(1)} %collective-permute-done.halo_ref, f32[16,4608]{1,0:T(8,128)S(1)} %copy-done, ...), custom_call_target="tpu_custom_call" | custom-call | tf_op jit(solution)/shard_map/head/pallas_call | solution.py:490
  22.2 0.0 copy-done.3
  22.2 0.0 all-gather.3.cloned.1.call-update
  22.2 0.0 copy-done.6
  22.2 0.0 copy-done.4
  22.2 0.2 sqrt_multiply_fusion.coef_ref
  22.4 11.9 %gate.1 = (bf16[128,4608]{1,0:T(8,128)(2,1)}, f32[128,4608]{1,0:T(8,128)}, f32[9,16,8,128]{3,2,1,0:T(8,128)}) custom-call(bf16[128,4608]{1,0:T(8,128)(2,1)} %query_ref.3, bf16[24,4608]{1,0:T(8,128)(2,1)} %copy-done.3, f32[9,3,7,32]{3,2,1,0:T(8,128)S(1)} %bitcast.5, bf16[128,4608]{1,0:T(8,128)(2,1)} %get-tuple-element.26.u_ref, ...), custom_call_target="tpu_custom_call" | custom-call | flops 16515072 | bytes 3538944 | tf_op jit(solution)/shard_map/gate/pallas_call | solution.py:490
  34.4 51.7 %all-gather.3.cloned.1.call-done = bf16[18432,128]{1,0:T(8,128)(2,1)} async-done(((bf16[576,128]{1,0:T(8,128)(2,1)}), bf16[18432,128]{1,0:T(8,128)(2,1)}) %all-gather.3.cloned.1.call-update) | async-done | bytes 4718608 | tf_op jit(solution)/shard_map/all_gather | solution.py:554
  86.0 1.7 %carry.1.piece_ref = f32[576,128]{1,0:T(8,128)S(1)} custom-call(bf16[32,576,128]{2,1,0:T(8,128)(2,1)} %bitcast.6, f32[16,4608]{1,0:T(8,128)S(1)} %copy-done, f32[16,4608]{1,0:T(8,128)S(1)} %sqrt_multiply_fusion.coef_ref), custom_call_target="tpu_custom_call" | custom-call | tf_op jit(solution)/shard_map/carry/pallas_call | solution.py:490
  87.8 6.4 %final.1 = bf16[128,4608]{1,0:T(8,128)(2,1)} custom-call(f32[576,128]{1,0:T(8,128)S(1)} %carry.1.piece_ref, f32[16,4608]{1,0:T(8,128)S(1)} %copy-done, f32[9,16,8,128]{3,2,1,0:T(8,128)} %get-tuple-element.34.mid_ref, f32[128,4608]{1,0:T(8,128)} %get-tuple-element.35.y_ref, bf16[128,4608]{1,0:T(8,128)(2,1)} %get-tuple-element.36.gate_ref), custom_call_target="tpu_custom_call" | custom-call | flops 23592960 | bytes 5898240 | tf_op jit(solution)/shard_map/final/pallas_call | solution.py:490
  (5 shorter events, 0.1 us)
Async XLA Ops:
  6.5 5.2 %copy-start.5 = (f32[3,7,288]{2,1,0:T(8,128)S(1)}, f32[3,7,288]{2,1,0:T(8,128)}, u32[]{:S(2)}) copy-start(f32[3,7,288]{2,1,0:T(8,128)} %param.10) | copy-start | bytes 72580
  6.5 5.4 %copy-start = (f32[16,4608]{1,0:T(8,128)S(1)}, f32[16,4608]{1,0:T(8,128)}, u32[]{:S(2)}) copy-start(f32[16,4608]{1,0:T(8,128)} %rate_ref.9) | copy-start | bytes 884740
  6.5 79.5 %all-gather.3.cloned.1.call-start = ((), (), s32[]{:S(2)}) async-start(), calls=%async_computation | async-start | bytes 4866048 | tf_op jit(solution)/shard_map/all_gather | solution.py:554
  6.5 5.4 %copy-start.1 = (bf16[128,4608]{1,0:T(8,128)(2,1)S(1)}, bf16[128,4608]{1,0:T(8,128)(2,1)}, u32[]{:S(2)}) copy-start(bf16[128,4608]{1,0:T(8,128)(2,1)} %key_ref.5) | copy-start | bytes 3538948
  6.5 5.4 %copy-start.2 = (bf16[128,4608]{1,0:T(8,128)(2,1)S(1)}, bf16[128,4608]{1,0:T(8,128)(2,1)}, u32[]{:S(2)}) copy-start(bf16[128,4608]{1,0:T(8,128)(2,1)} %value_ref.5) | copy-start | bytes 3538948
  7.8 13.0 %collective-permute-start = (bf16[24,4608]{1,0:T(8,128)(2,1)S(1)}, bf16[24,4608]{1,0:T(8,128)(2,1)S(1)}, u32[]{:S(2)}, u32[]{:S(2)}) collective-permute-start(bf16[24,4608]{1,0:T(8,128)(2,1)S(1)} %pack.1), channel_id=1, source_target_pairs={{0,1},{1,2},{2,3},{3,4},{4,5},{5,6},{6,7},{7,8},{8,9},{9,10},{10,1... | collective-permute-start | bytes 663560 | tf_op jit(solution)/shard_map/ppermute | solution.py:508
  20.8 1.3 %copy-start.3 = (bf16[24,4608]{1,0:T(8,128)(2,1)}, bf16[24,4608]{1,0:T(8,128)(2,1)S(1)}, u32[]{:S(2)}) copy-start(bf16[24,4608]{1,0:T(8,128)(2,1)S(1)} %collective-permute-done.halo_ref) | copy-start | bytes 663556
  20.8 1.4 %copy-start.6 = (f32[4608]{0:T(1024)S(1)}, f32[4608]{0:T(1024)}, u32[]{:S(2)}) copy-start(f32[4608]{0:T(1024)} %param.13) | copy-start | bytes 55300
  20.8 1.4 %copy-start.4 = (f32[16,4608]{1,0:T(8,128)S(1)}, f32[16,4608]{1,0:T(8,128)}, u32[]{:S(2)}) copy-start(f32[16,4608]{1,0:T(8,128)} %param.12) | copy-start | bytes 884740
Sparse Core Ops, SparseCore 0:
  22.3 63.6 all-gather.2

commit v10 on v8

--- a/solution.py
+++ b/solution.py
@@ -69,17 +69,34 @@
     return [block[at : at + ROWS] for at in range(0, block.shape[0], ROWS)]
 
 
-def fir(column, taps, first):
-    total = taps[0] * column[pl.ds(first, ROWS), :]
-    for lag in range(1, len(taps)):
-        total = total + taps[lag] * column[pl.ds(first - lag, ROWS), :]
-    return total
+def fir(column, taps, first, count):
+    half = ROWS // 2
+    top = sublane() < half
+
+    def seen(start, lags):
+        return [column[pl.ds(start - lag, ROWS), :] for lag in range(lags)]
+
+    def far_part(rows):
+        total = taps[half] * rows[0]
+        for lag in range(half + 1, len(taps)):
+            total = total + taps[lag] * rows[lag - half]
+        return pltpu.roll(total, half, 0)
+
+    before = far_part(seen(first - ROWS, len(taps) - half))
+    for start in range(first, first + count * ROWS, ROWS):
+        rows = seen(start, half)
+        now = far_part(rows)
+        total = taps[0] * rows[0]
+        for lag in range(1, half):
+            total = total + taps[lag] * rows[lag]
+        yield total + jnp.where(top, before, now)
+        before = now
 
 
 def lay_column(column, source, lanes):
     for pair in range(source.shape[0] // (2 * ROWS)):
         rows = slice(pair * 2 * ROWS, (pair + 1) * 2 * ROWS)
-        column[pl.ds(ROWS + pair * 2 * ROWS, 2 * ROWS), :] = source[rows, lanes].astype(f32)
+        column[pl.ds((pair + 1) * 2 * ROWS, 2 * ROWS), :] = source[rows, lanes].astype(f32)
 
 
 def chunk_taps(wide_ref, at, member, tile, count):
@@ -132,21 +149,25 @@
         start_all(fetch(at))
 
 
-def over_chunks(chunks, fetch, body, send, last=True):
+def over_chunks(first, last, body, send):
     def one(at, _):
+        body(at)
+        start_all(send(at))
+        return 0
+
+    lax.fori_loop(first, last, one, 0)
+
+
+def with_fetch(chunks, fetch, body):
+    def one(at):
         @pl.when(at + AHEAD < chunks)
         def _():
             start_all(fetch(at + AHEAD))
 
         wait_all(fetch(at))
         body(at)
-        start_all(send(at))
-        return 0
-
-    lax.fori_loop(0, chunks, one, 0)
-    if last:
-        for at in range(chunks):
-            wait_all(send(at))
+
+    return one
 
 
 def columns_in(pairs, sem):
@@ -183,7 +204,7 @@
     for member in range(2):
         widened(feat_ref, member + 1, wide_ref, member)
     for column in columns:
-        column[pl.ds(0, ROWS), :] = jnp.zeros((ROWS, LANES), f32)
+        column[pl.ds(0, 2 * ROWS), :] = jnp.zeros((2 * ROWS, LANES), f32)
     last_scr[...] = jnp.zeros(last_scr.shape, f32)
 
     def powers(at, _):
@@ -212,11 +233,11 @@
             lay_column(column, ref, lanes)
         decay = [wide(power_scr[3, mode : mode + 1, lanes]) for mode in range(modes)]
         state = None
+        parts = [fir(column, some, 2 * ROWS, tokens // ROWS) for column, some in zip(columns, taps)]
         for pair in range(tokens // (2 * ROWS)):
-            found = []
-            for first in (pair * 2 * ROWS + ROWS, pair * 2 * ROWS + 2 * ROWS):
-                u = fir(columns[0], taps[0], first) * fir(columns[1], taps[1], first)
-                found.append(jnp.where(sublane() < count - 1, 0.0, u) if first == ROWS else u)
+            found = [next(parts[0]) * next(parts[1]) for _ in range(2)]
+            if pair == 0:
+                found[0] = jnp.where(sublane() < count - 1, 0.0, found[0])
             both = jnp.concatenate(found, axis=0).astype(bf16)
             u_ref[pair * 2 * ROWS : (pair + 1) * 2 * ROWS, lanes] = both
             for u in tiles_of(both):
@@ -249,10 +270,11 @@
             for member in range(2):
                 taps = chunk_taps(wide_ref, chunk, member, number, reach + 1)
                 column = column_scr.at[number, member]
-                column[pl.ds(0, ROWS), :] = halo[member * ROWS : (member + 1) * ROWS]
+                column[pl.ds(0, ROWS), :] = jnp.zeros((ROWS, LANES), f32)
+                column[pl.ds(ROWS, ROWS), :] = halo[member * ROWS : (member + 1) * ROWS]
                 source = (key_ref, value_ref)[member]
-                column[pl.ds(ROWS, ROWS), :] = source[: 2 * ROWS, lanes].astype(f32)[:ROWS]
-                parts.append(fir(column, taps, ROWS))
+                column[pl.ds(2 * ROWS, ROWS), :] = source[: 2 * ROWS, lanes].astype(f32)[:ROWS]
+                parts += fir(column, taps, 2 * ROWS, 1)
             u = jnp.where(sublane() < reach, rounded(parts[0] * parts[1]), 0.0)
             token_scr[pl.ds(pl.multiple_of((chunk * TILES + number) * ROWS, ROWS), ROWS), :] = u
             head_ref[:, lanes] = jnp.concatenate([u, jnp.zeros((ROWS, LANES), f32)], axis=0).astype(bf16)
@@ -274,40 +296,37 @@
 
 
 def gate_kernel(query_ref, halo_ref, feat_ref, u_ref, head_ref, rate_ref, coef_ref, skip_ref, gate_ref, *rest, early):
-    y_ref, mid_ref, query_buf, halo_buf, gate_buf, wide_scr, column, in_sem, small_sem, out_sem = rest[:10]
-    inner = rest[10:]
+    y_ref, mid_ref, halo_buf, gate_buf, wide_scr, column, small_sem, out_sem = rest[:8]
+    inner = rest[8:]
     chunks, tokens = gate_buf.shape[:2]
     count = feat_ref.shape[2]
-    fetch = columns_in(((query_ref, query_buf),), in_sem)
     halo_copy = pltpu.make_async_copy(halo_ref, halo_buf, small_sem.at[0])
     halo_copy.start()
-    begin(chunks, fetch)
-    local_fetch, local_chunk, local_send = local_parts(
-        u_ref, head_ref, rate_ref, coef_ref, skip_ref, y_ref, mid_ref, *inner, first=0
-    )
-    begin(early, local_fetch)
     widened(feat_ref, 0, wide_scr, 0)
+    local_chunk, local_send = local_parts(u_ref, head_ref, rate_ref, coef_ref, skip_ref, y_ref, mid_ref, *inner)
+    over_chunks(0, early, local_chunk, local_send)
     halo_copy.wait()
+    column[pl.ds(0, ROWS), :] = jnp.zeros((ROWS, LANES), f32)
 
     def chunk(at):
         def tile(number, _):
             lanes = tile_lanes(number)
+            all_lanes = tile_lanes(at * TILES + number)
             taps = chunk_taps(wide_scr, at, 0, number, count)
-            halo = halo_buf[:, tile_lanes(at * TILES + number)].astype(f32)
-            column[pl.ds(0, ROWS), :] = halo[2 * ROWS :]
-            lay_column(column, query_buf.at[at], lanes)
+            column[pl.ds(ROWS, ROWS), :] = halo_buf[:, all_lanes].astype(f32)[2 * ROWS :]
+            lay_column(column, query_ref, all_lanes)
+            found = list(fir(column, taps, 2 * ROWS, tokens // ROWS))
             for pair in range(tokens // (2 * ROWS)):
-                first = pair * 2 * ROWS + ROWS
-                found = [fir(column, taps, first), fir(column, taps, first + ROWS)]
                 rows = slice(pair * 2 * ROWS, (pair + 1) * 2 * ROWS)
-                gate_buf[at, rows, lanes] = jnp.concatenate(found, axis=0).astype(bf16)
+                gate_buf[at, rows, lanes] = jnp.concatenate(found[pair * 2 : pair * 2 + 2], axis=0).astype(bf16)
             return 0
 
         lax.fori_loop(0, TILES, tile, 0)
 
     give = columns_out(gate_ref, gate_buf, out_sem)
-    over_chunks(chunks, fetch, chunk, give, last=False)
-    over_chunks(early, local_fetch, local_chunk, local_send)
+    over_chunks(0, chunks, chunk, give)
+    for at in range(early):
+        wait_all(local_send(at))
     for at in range(chunks):
         wait_all(give(at))
 
@@ -342,32 +361,27 @@
 
 
 def local_kernel(u_ref, head_ref, rate_ref, coef_ref, skip_ref, *rest, first, last):
-    fetch, chunk, send = local_parts(u_ref, head_ref, rate_ref, coef_ref, skip_ref, *rest[-10:], first=first)
-    begin(last - first, fetch)
-    over_chunks(last - first, fetch, chunk, send)
-
-
-def local_parts(u_ref, head_ref, rate_ref, coef_ref, skip_ref, y_ref, mid_ref, *scratches, first):
-    u_buf, y_buf, mid_buf, token_scr, sum_scr, in_sem, out_sem, mid_sem = scratches
-    tokens = u_buf.shape[1]
+    chunk, send = local_parts(u_ref, head_ref, rate_ref, coef_ref, skip_ref, *rest[-8:])
+    over_chunks(first, last, chunk, send)
+    for at in range(first, last):
+        wait_all(send(at))
+
+
+def local_parts(u_ref, head_ref, rate_ref, coef_ref, skip_ref, y_ref, mid_ref, *scratches):
+    y_buf, mid_buf, token_scr, sum_scr, out_sem, mid_sem = scratches
+    tokens = u_ref.shape[0]
     modes = rate_ref.shape[0]
     half_groups = tokens // ROWS // 2
-    take = columns_in(((u_ref, u_buf),), in_sem)
     give = columns_out(y_ref, y_buf, out_sem)
 
-    def fetch(number):
-        return take(number + first)
-
-    def send(number):
-        at = number + first
+    def send(at):
         return give(at) + [pltpu.make_async_copy(mid_buf.at[at], mid_ref.at[at], mid_sem.at[at])]
 
-    def chunk(number):
-        at = number + first
-        front = u_buf[at, : 2 * ROWS].astype(f32) + head_ref[:, span(at)].astype(f32)
-        u_buf[at, : 2 * ROWS] = front.astype(bf16)
+    def chunk(at):
         for pair in range(half_groups):
-            block = u_buf[at, pair * 2 * ROWS : (pair + 1) * 2 * ROWS, :].astype(f32)
+            block = u_ref[pair * 2 * ROWS : (pair + 1) * 2 * ROWS, span(at)].astype(f32)
+            if pair == 0:
+                block = block + head_ref[:, span(at)].astype(f32)
             for part in range(2):
                 group = pair * 2 + part
                 half, within = group // half_groups, group % half_groups
@@ -397,7 +411,7 @@
                 rows = slice(group * ROWS, (group + 1) * ROWS)
                 y_buf[at, rows, tile * LANES : (tile + 1) * LANES] = sum_scr[pl.ds(slot, ROWS), :]
 
-    return fetch, chunk, send
+    return chunk, send
 
 
 def final_kernel(piece_ref, rate_ref, mid_ref, y_ref, gate_ref, out_ref, *scratches):
@@ -453,7 +467,10 @@
 
         lax.fori_loop(0, TILES, tile, 0)
 
-    over_chunks(chunks, fetch, chunk, columns_out(out_ref, out_buf, out_sem))
+    give = columns_out(out_ref, out_buf, out_sem)
+    over_chunks(0, chunks, with_fetch(chunks, fetch, chunk), give)
+    for at in range(chunks):
+        wait_all(give(at))
 
 
 def cost(flops, moved):
@@ -502,7 +519,7 @@
     halo = lax.ppermute(packed, axes, [(at, at + 1) for at in range(devices - 1)])
 
     feat = featurizer.reshape(members, taps, chunks, groups // chunks).transpose(2, 0, 1, 3)
-    column = vmem((ROWS + tokens, LANES), f32)
+    column = vmem((2 * ROWS + tokens, LANES), f32)
     half_buf, whole_buf = vmem((chunks, tokens, CHUNK), bf16), vmem((chunks, tokens, CHUNK), f32)
     u, wide_taps, state = call(
         signal_kernel,
@@ -519,28 +536,28 @@
         functools.partial(head_kernel, tokens=tokens, reach=taps - 1),
         (key_proj, value_proj, halo, rates, wide_taps, state),
         [near(pieces, bf16), near((2 * ROWS, width), bf16)],
-        [vmem((modes * tiles, LANES), f32), vmem((TILES, 2, 2 * ROWS, LANES), f32)]
+        [vmem((modes * tiles, LANES), f32), vmem((TILES, 2, 3 * ROWS, LANES), f32)]
         + [vmem((tiles * ROWS, LANES), f32), vmem((modes, tiles, LANES), f32)],
         "head",
         close=range(6),
     )
-    left, halo_late, rates_late, skip_late, u_late = lax.optimization_barrier((left, halo, rates, skip, u))
+    left, halo_late, rates_late, skip_late = lax.optimization_barrier((left, halo, rates, skip))
     coef = residues * jnp.sqrt(-jnp.expm1(-2.0 * rates_late) / modes)
     skip_row = skip_late[None, :]
     stage = vmem((tokens // ROWS // 2 * ROWS * ROWS, LANES), f32)
     local_shapes = [far((tokens, width), f32), far((chunks, modes, ROWS, LANES), f32)]
-    local_scratches = [half_buf, whole_buf, vmem((chunks, modes, ROWS, LANES), f32), stage, stage]
-    local_scratches += [dma((1, chunks)), dma((1, chunks)), dma((chunks,))]
+    local_scratches = [whole_buf, vmem((chunks, modes, ROWS, LANES), f32), stage, stage]
+    local_scratches += [dma((1, chunks)), dma((chunks,))]
     early = chunks * 2 // 9
     gate, y, mid = call(
         functools.partial(gate_kernel, early=early),
-        (query, halo_late, feat, u_late, head, rates, coef, skip_row),
+        (query, halo_late, feat, u, head, rates, coef, skip_row),
         [far((tokens, width), bf16)] + local_shapes,
-        [half_buf, vmem((members * ROWS, width), bf16), half_buf, vmem((chunks, 1, ROWS, CHUNK), f32), column]
-        + [dma((1, chunks)), dma((1,)), dma((1, chunks))]
+        [vmem((members * ROWS, width), bf16), half_buf, vmem((chunks, 1, ROWS, CHUNK), f32), column]
+        + [dma((1,)), dma((1, chunks))]
         + local_scratches,
         "gate",
-        close=(2, 4, 5, 6, 7),
+        close=(0, 2, 3, 4, 5, 6, 7),
         cost_estimate=cost(28 * elements, 6 * elements),
     )
 
@@ -569,15 +586,15 @@
             theirs,
         )
 
-    entering, u_late = lax.optimization_barrier((entering, u))
+    entering, y = lax.optimization_barrier((entering, y))
     entered = swap(entering).reshape(pieces)
     y, mid = call(
         functools.partial(local_kernel, first=early, last=chunks),
-        (u_late, head, rates, coef, skip_row, y, mid),
+        (u, head, rates, coef, skip_row, y, mid),
         local_shapes,
         local_scratches,
         "within",
-        close=(1, 2, 3, 4),
+        close=range(5),
         cost_estimate=cost(50 * elements, 8 * elements),
         input_output_aliases={5: 0, 6: 1},
     )

time: 50.2 us -> 48.7 us (0.970)
  Pallas kernels: 30.8 us -> 27.1 us
  waiting for transfers between devices: 3.54 us -> 5.99 us
  starting transfers between devices: 13.5 us -> 12.1 us
  local copies, waits for them, and re-layouts: 1.17 us -> 2.45 us
    pallas_call x7, Pallas kernels: 30.8 us -> 27.1 us  [call(): pl.pallas_call(kernel, in_specs=[beside if at in close else there for at...]
    all_to_all x2, waiting for transfers between devices: 2.74 us -> 5.35 us  [swap(): return lax.all_to_all(value, axes, split_axis=0, concat_axis=0, tiled=True)]
    all_to_all x2, starting transfers between devices: 9.53 us -> 8.13 us  [swap(): return lax.all_to_all(value, axes, split_axis=0, concat_axis=0, tiled=True)]
    unnamed x16 -> x22, local copies, waits for them, and re-layouts: 1.03 us -> 2.31 us
  transfers between devices with their start and end apart: 3 -> 3, of which waited for: 3 -> 3; matrix products, arithmetic and copies ran while one was open for 1% -> 1% of each run, Pallas kernels for 42% -> 36%
where the time goes in v10:
time: 48.7 us; the launch traced here: 48 us
  Pallas kernels  27.1 us (56%)
  starting transfers between devices  12.1 us (25%)
  waiting for transfers between devices  5.99 us (12%)
  local copies, waits for them, and re-layouts  2.45 us (5%)
    pallas_call x7, Pallas kernels, call(): pl.pallas_call(kernel, in_specs=[beside if at in close else there for at...  27.1 us
    all_to_all x2, starting transfers between devices, swap(): return lax.all_to_all(value, axes, split_axis=0, concat_axis=0, tiled=True)  8.13 us
    all_to_all x2, waiting for transfers between devices, swap(): return lax.all_to_all(value, axes, split_axis=0, concat_axis=0, tiled=True)  5.35 us
    ppermute x1, starting transfers between devices, local(): lax.ppermute(packed, axes, [(at, at + 1) for at in range(devices - 1)])  3.95 us
    unnamed x22, local copies, waits for them, and re-layouts  2.31 us
  transfers between devices with their start and end apart: 3, of which 3 were waited for; matrix products, arithmetic and copies ran while one was open for 1% of the time, Pallas kernels for 36%

profile of v10, /device:TPU:1, one launch (start us, length us, event | category | flops | bytes accessed | tf_op | source)
XLA Modules:
  0.0 48.0 jit_solution(15673475881656784740)
XLA Ops:
  0.0 0.0 copy-start.2
  0.0 1.2 %pack.1 = bf16[24,4608]{1,0:T(8,128)(2,1)S(1)} custom-call(bf16[128,4608]{1,0:T(8,128)(2,1)} %key_ref.5, bf16[128,4608]{1,0:T(8,128)(2,1)} %value_ref.5, bf16[128,4608]{1,0:T(8,128)(2,1)} %query_ref.3), custom_call_target="tpu_custom_call" | custom-call | tf_op jit(solution)/shard_map/pack/pallas_call | solution.py:501
  1.3 3.9 %collective-permute-start = (bf16[24,4608]{1,0:T(8,128)(2,1)S(1)}, bf16[24,4608]{1,0:T(8,128)(2,1)S(1)}, u32[]{:S(2)}, u32[]{:S(2)}) collective-permute-start(bf16[24,4608]{1,0:T(8,128)(2,1)S(1)} %pack.1), channel_id=1, source_target_pairs={{0,1},{1,2},{2,3},{3,4},{4,5},{5,6},{6,7},{7,8},{8,9},{9,10},{10,1... | collective-permute-start | bytes 663560 | tf_op jit(solution)/shard_map/ppermute | solution.py:519
  5.2 0.0 copy-done.9
  5.2 0.1 reshape.3
  5.4 7.2 %signal.1 = (bf16[128,4608]{1,0:T(8,128)(2,1)S(1)}, f32[9,2,8,512]{3,2,1,0:T(8,128)S(1)}, f32[16,36,128]{2,1,0:T(8,128)S(1)}) custom-call(bf16[128,4608]{1,0:T(8,128)(2,1)S(1)} %copy-done.1, bf16[128,4608]{1,0:T(8,128)(2,1)S(1)} %copy-done.2, f32[9,3,7,32]{3,2,1,0:T(8,128)S(1)} %bitcast.3, f32[16,4608]{1,0:T(8,128)S(1)} %copy-done), custom_call_target="tpu_custom_call" | custom-call | flops 35389440 | bytes 5898240 | tf_op jit(solution)/shard_map/signal/pallas_call | solution.py:501
  12.6 0.0 copy-start.4
  12.7 1.0 %copy-done.4 = bf16[128,4608]{1,0:T(8,128)(2,1)} copy-done((bf16[128,4608]{1,0:T(8,128)(2,1)}, bf16[128,4608]{1,0:T(8,128)(2,1)S(1)}, u32[]{:S(2)}) %copy-start.4) | copy-done | bytes 1179672
  13.7 0.6 %collective-permute-done.halo_ref = bf16[24,4608]{1,0:T(8,128)(2,1)S(1)} collective-permute-done((bf16[24,4608]{1,0:T(8,128)(2,1)S(1)}, bf16[24,4608]{1,0:T(8,128)(2,1)S(1)}, u32[]{:S(2)}, u32[]{:S(2)}) %collective-permute-start) | collective-permute-done | bytes 221216 | tf_op jit(solution)/shard_map/ppermute | solution.py:519
  14.3 1.5 %head.1 = (bf16[32,18,128]{2,1,0:T(8,128)(2,1)}, bf16[16,4608]{1,0:T(8,128)(2,1)S(1)}) custom-call(bf16[128,4608]{1,0:T(8,128)(2,1)S(1)} %copy-done.1, bf16[128,4608]{1,0:T(8,128)(2,1)S(1)} %copy-done.2, bf16[24,4608]{1,0:T(8,128)(2,1)S(1)} %collective-permute-done.halo_ref, f32[16,4608]{1,0:T(8,128)S(1)} %copy-done, ...), custom_call_target="tpu_custom_call" | custom-call | tf_op jit(solution)/shard_map/head/pallas_call | solution.py:501
  15.8 5.0 %all-to-all-start = ((bf16[32,18,128]{2,1,0:T(8,128)(2,1)}), bf16[32,18,128]{2,1,0:T(8,128)(2,1)S(1)}, u32[]{:S(2)}, u32[]{:S(2)}) async-start(bf16[32,18,128]{2,1,0:T(8,128)(2,1)} %get-tuple-element.30), calls=%async_computation | async-start | bytes 393216 | tf_op jit(solution)/shard_map/all_to_all | solution.py:565
  20.8 0.0 copy-done.8
  20.8 0.2 sqrt_multiply_fusion.coef_ref
  21.0 0.0 copy-done.10
  21.0 0.0 copy-start.5
  21.0 1.3 %copy-done.5 = bf16[128,4608]{1,0:T(8,128)(2,1)S(1)} copy-done((bf16[128,4608]{1,0:T(8,128)(2,1)S(1)}, bf16[128,4608]{1,0:T(8,128)(2,1)}, u32[]{:S(2)}) %copy-start.5) | copy-done | bytes 1179672
  22.3 4.2 %gate.1 = (bf16[128,4608]{1,0:T(8,128)(2,1)}, f32[128,4608]{1,0:T(8,128)}, f32[9,16,8,128]{3,2,1,0:T(8,128)}) custom-call(bf16[128,4608]{1,0:T(8,128)(2,1)S(1)} %copy-done.3, bf16[24,4608]{1,0:T(8,128)(2,1)} %copy-done.7, f32[9,3,7,32]{3,2,1,0:T(8,128)S(1)} %bitcast.4, bf16[128,4608]{1,0:T(8,128)(2,1)S(1)} %copy-done.5, ...), custom_call_target="tpu_custom_call" | custom-call | flops 16515072 | bytes 3538944 | tf_op jit(solution)/shard_map/gate/pallas_call | solution.py:501
  26.4 0.0 copy-start.6
  26.5 2.7 %all-to-all-done.piece_ref = bf16[32,18,128]{2,1,0:T(8,128)(2,1)S(1)} async-done(((bf16[32,18,128]{2,1,0:T(8,128)(2,1)}), bf16[32,18,128]{2,1,0:T(8,128)(2,1)S(1)}, u32[]{:S(2)}, u32[]{:S(2)}) %all-to-all-start) | async-done | bytes 147488 | tf_op jit(solution)/shard_map/all_to_all | solution.py:565
  29.2 0.8 %prefix.1 = bf16[32,18,128]{2,1,0:T(8,128)(2,1)} custom-call(bf16[32,18,128]{2,1,0:T(8,128)(2,1)S(1)} %all-to-all-done.piece_ref, f32[16,4608]{1,0:T(8,128)S(1)} %copy-done, f32[16,4608]{1,0:T(8,128)S(1)} %sqrt_multiply_fusion.coef_ref), custom_call_target="tpu_custom_call" | custom-call | tf_op jit(solution)/shard_map/prefix/pallas_call | solution.py:501
  30.0 3.1 %all-to-all-start.1 = ((bf16[32,18,128]{2,1,0:T(8,128)(2,1)}), bf16[32,18,128]{2,1,0:T(8,128)(2,1)S(1)}, u32[]{:S(2)}, u32[]{:S(2)}) async-start(bf16[32,18,128]{2,1,0:T(8,128)(2,1)} %prefix.1), calls=%async_computation.1 | async-start | bytes 393216 | tf_op jit(solution)/shard_map/all_to_all | solution.py:565
  33.2 5.8 %within.1 = (f32[128,4608]{1,0:T(8,128)}, f32[9,16,8,128]{3,2,1,0:T(8,128)}) custom-call(bf16[128,4608]{1,0:T(8,128)(2,1)S(1)} %copy-done.6, bf16[16,4608]{1,0:T(8,128)(2,1)S(1)} %get-tuple-element.33.head_ref, f32[16,4608]{1,0:T(8,128)S(1)} %copy-done, f32[16,4608]{1,0:T(8,128)S(1)} %sqrt_multiply_fusion.coef_ref, ...), custom_call_target="tpu_custom_call", output_to_operand_aliasing={{0}: (5, {}), {1}: (6, {})} | custom-call | flops 29491200 | bytes 4718592 | tf_op jit(solution)/shard_map/within/pallas_call | solution.py:501
  39.0 2.6 %all-to-all-done.1.piece_ref = bf16[32,18,128]{2,1,0:T(8,128)(2,1)S(1)} async-done(((bf16[32,18,128]{2,1,0:T(8,128)(2,1)}), bf16[32,18,128]{2,1,0:T(8,128)(2,1)S(1)}, u32[]{:S(2)}, u32[]{:S(2)}) %all-to-all-start.1) | async-done | bytes 147488 | tf_op jit(solution)/shard_map/all_to_all | solution.py:565
  41.6 6.4 %final.1 = bf16[128,4608]{1,0:T(8,128)(2,1)} custom-call(bf16[32,18,128]{2,1,0:T(8,128)(2,1)S(1)} %all-to-all-done.1.piece_ref, f32[16,4608]{1,0:T(8,128)S(1)} %copy-done, f32[9,16,8,128]{3,2,1,0:T(8,128)} %get-tuple-element.46.mid_ref, f32[128,4608]{1,0:T(8,128)} %get-tuple-element.47.y_ref, bf16[128,4608]{1,0:T(8,128)(2,1)} %get-tuple-element.48.gate_ref), custom_call_target="tpu_custom_call" | custom-call | flops 23592960 | bytes 5898240 | tf_op jit(solution)/shard_map/final/pallas_call | solution.py:501
  (15 shorter events, 0.1 us)
Async XLA Ops:
  0.0 5.2 %copy-start.9 = (f32[3,7,288]{2,1,0:T(8,128)S(1)}, f32[3,7,288]{2,1,0:T(8,128)}, u32[]{:S(2)}) copy-start(f32[3,7,288]{2,1,0:T(8,128)} %param.10) | copy-start | bytes 72580
  0.0 5.4 %copy-start = (f32[16,4608]{1,0:T(8,128)S(1)}, f32[16,4608]{1,0:T(8,128)}, u32[]{:S(2)}) copy-start(f32[16,4608]{1,0:T(8,128)} %rate_ref.11) | copy-start | bytes 884740
  0.0 5.4 %copy-start.1 = (bf16[128,4608]{1,0:T(8,128)(2,1)S(1)}, bf16[128,4608]{1,0:T(8,128)(2,1)}, u32[]{:S(2)}) copy-start(bf16[128,4608]{1,0:T(8,128)(2,1)} %key_ref.5) | copy-start | bytes 3538948
  0.0 5.4 %copy-start.2 = (bf16[128,4608]{1,0:T(8,128)(2,1)S(1)}, bf16[128,4608]{1,0:T(8,128)(2,1)}, u32[]{:S(2)}) copy-start(bf16[128,4608]{1,0:T(8,128)(2,1)} %value_ref.5) | copy-start | bytes 3538948
  1.3 13.0 %collective-permute-start = (bf16[24,4608]{1,0:T(8,128)(2,1)S(1)}, bf16[24,4608]{1,0:T(8,128)(2,1)S(1)}, u32[]{:S(2)}, u32[]{:S(2)}) collective-permute-start(bf16[24,4608]{1,0:T(8,128)(2,1)S(1)} %pack.1), channel_id=1, source_target_pairs={{0,1},{1,2},{2,3},{3,4},{4,5},{5,6},{6,7},{7,8},{8,9},{9,10},{10,1... | collective-permute-start | bytes 663560 | tf_op jit(solution)/shard_map/ppermute | solution.py:519
  12.6 1.0 %copy-start.4 = (bf16[128,4608]{1,0:T(8,128)(2,1)}, bf16[128,4608]{1,0:T(8,128)(2,1)S(1)}, u32[]{:S(2)}) copy-start(bf16[128,4608]{1,0:T(8,128)(2,1)S(1)} %get-tuple-element.32.u_ref) | copy-start | bytes 3538948
  14.3 1.5 %copy-start.7 = (bf16[24,4608]{1,0:T(8,128)(2,1)}, bf16[24,4608]{1,0:T(8,128)(2,1)S(1)}, u32[]{:S(2)}) copy-start(bf16[24,4608]{1,0:T(8,128)(2,1)S(1)} %collective-permute-done.halo_ref) | copy-start | bytes 663556
  14.3 6.5 %copy-start.8 = (f32[16,4608]{1,0:T(8,128)S(1)}, f32[16,4608]{1,0:T(8,128)}, u32[]{:S(2)}) copy-start(f32[16,4608]{1,0:T(8,128)} %param.12) | copy-start | bytes 884740
  15.8 5.2 %copy-start.10 = (f32[4608]{0:T(1024)S(1)}, f32[4608]{0:T(1024)}, u32[]{:S(2)}) copy-start(f32[4608]{0:T(1024)} %param.13) | copy-start | bytes 55300
  15.8 5.2 %copy-start.3 = (bf16[128,4608]{1,0:T(8,128)(2,1)S(1)}, bf16[128,4608]{1,0:T(8,128)(2,1)}, u32[]{:S(2)}) copy-start(bf16[128,4608]{1,0:T(8,128)(2,1)} %query_ref.3) | copy-start | bytes 3538948
  15.8 13.4 %all-to-all-start = ((bf16[32,18,128]{2,1,0:T(8,128)(2,1)}), bf16[32,18,128]{2,1,0:T(8,128)(2,1)S(1)}, u32[]{:S(2)}, u32[]{:S(2)}) async-start(bf16[32,18,128]{2,1,0:T(8,128)(2,1)} %get-tuple-element.30), calls=%async_computation | async-start | bytes 393216 | tf_op jit(solution)/shard_map/all_to_all | solution.py:565
  21.0 1.3 %copy-start.5 = (bf16[128,4608]{1,0:T(8,128)(2,1)S(1)}, bf16[128,4608]{1,0:T(8,128)(2,1)}, u32[]{:S(2)}) copy-start(bf16[128,4608]{1,0:T(8,128)(2,1)} %copy-done.4) | copy-start | bytes 3538948
  26.4 6.8 %copy-start.6 = (bf16[128,4608]{1,0:T(8,128)(2,1)S(1)}, bf16[128,4608]{1,0:T(8,128)(2,1)}, u32[]{:S(2)}) copy-start(bf16[128,4608]{1,0:T(8,128)(2,1)} %copy-done.4) | copy-start | bytes 3538948
  30.0 11.6 %all-to-all-start.1 = ((bf16[32,18,128]{2,1,0:T(8,128)(2,1)}), bf16[32,18,128]{2,1,0:T(8,128)(2,1)S(1)}, u32[]{:S(2)}, u32[]{:S(2)}) async-start(bf16[32,18,128]{2,1,0:T(8,128)(2,1)} %prefix.1), calls=%async_computation.1 | async-start | bytes 393216 | tf_op jit(solution)/shard_map/all_to_all | solution.py:565

commit v11 on v10

--- a/solution.py
+++ b/solution.py
@@ -12,7 +12,7 @@
 ROWS = 8
 TILES = 4
 CHUNK = TILES * LANES
-AHEAD = 2
+AHEAD = 4
 f32 = jnp.float32
 bf16 = jnp.bfloat16
 
@@ -253,8 +253,10 @@
     reduce(tiles - 1)
 
 
-def head_kernel(key_ref, value_ref, halo_ref, rate_ref, wide_ref, state_ref, out_ref, head_ref, *scratches, tokens, reach):
-    rate_scr, column_scr, token_scr, total_scr = scratches
+def head_kernel(key_ref, value_ref, halo_ref, rate_ref, wide_ref, state_ref, u_ref, *rest, tokens, reach):
+    out_ref, head_ref, u_out_ref, rate_scr, column_scr, token_scr, total_scr, sem = rest
+    move = pltpu.make_async_copy(u_ref, u_out_ref, sem.at[0])
+    move.start()
     modes, tiles = state_ref.shape[:2]
     pieces, piece_rows = out_ref.shape[:2]
     for group in range(modes // ROWS):
@@ -293,6 +295,7 @@
         for part in range(split):
             rows = total_scr[mode, part * piece_rows : (part + 1) * piece_rows, :]
             out_ref[mode * split + part] = rows.astype(out_ref.dtype)
+    move.wait()
 
 
 def gate_kernel(query_ref, halo_ref, feat_ref, u_ref, head_ref, rate_ref, coef_ref, skip_ref, gate_ref, *rest, early):
@@ -532,14 +535,14 @@
     )
 
     pieces = (modes * split, tiles // split, LANES) if even else (modes, tiles, LANES)
-    left, head = call(
+    left, head, u = call(
         functools.partial(head_kernel, tokens=tokens, reach=taps - 1),
-        (key_proj, value_proj, halo, rates, wide_taps, state),
-        [near(pieces, bf16), near((2 * ROWS, width), bf16)],
+        (key_proj, value_proj, halo, rates, wide_taps, state, u),
+        [near(pieces, bf16), near((2 * ROWS, width), bf16), far((tokens, width), bf16)],
         [vmem((modes * tiles, LANES), f32), vmem((TILES, 2, 3 * ROWS, LANES), f32)]
-        + [vmem((tiles * ROWS, LANES), f32), vmem((modes, tiles, LANES), f32)],
+        + [vmem((tiles * ROWS, LANES), f32), vmem((modes, tiles, LANES), f32), dma((1,))],
         "head",
-        close=range(6),
+        close=range(7),
     )
     left, halo_late, rates_late, skip_late = lax.optimization_barrier((left, halo, rates, skip))
     coef = residues * jnp.sqrt(-jnp.expm1(-2.0 * rates_late) / modes)
@@ -548,7 +551,7 @@
     local_shapes = [far((tokens, width), f32), far((chunks, modes, ROWS, LANES), f32)]
     local_scratches = [whole_buf, vmem((chunks, modes, ROWS, LANES), f32), stage, stage]
     local_scratches += [dma((1, chunks)), dma((chunks,))]
-    early = chunks * 2 // 9
+    early = chunks * 5 // 9
     gate, y, mid = call(
         functools.partial(gate_kernel, early=early),
         (query, halo_late, feat, u, head, rates, coef, skip_row),

time: 48.7 us -> 49.8 us (1.023)
  starting transfers between devices: 12.1 us -> 13.2 us
  waiting for transfers between devices: 5.99 us -> 7.02 us
  local copies, waits for them, and re-layouts: 2.45 us -> 1.45 us
    all_to_all x2, starting transfers between devices: 8.13 us -> 9.23 us  [swap(): return lax.all_to_all(value, axes, split_axis=0, concat_axis=0, tiled=True)]
    ppermute x1, waiting for transfers between devices: 0.63 us -> 1.65 us  [local(): lax.ppermute(packed, axes, [(at, at + 1) for at in range(devices - 1)])]
    unnamed x22 -> x20, local copies, waits for them, and re-layouts: 2.31 us -> 1.31 us
  transfers between devices with their start and end apart: 3 -> 3, of which waited for: 3 -> 3; matrix products, arithmetic and copies ran while one was open for 1% -> 1% of each run, Pallas kernels for 36% -> 35%
where the time goes in v11:
time: 49.8 us; the launch traced here: 49.2 us
  Pallas kernels  27.1 us (54%)
  starting transfers between devices  13.2 us (27%)
  waiting for transfers between devices  7.02 us (14%)
  local copies, waits for them, and re-layouts  1.45 us (3%)
    pallas_call x7, Pallas kernels, call(): pl.pallas_call(kernel, in_specs=[beside if at in close else there for at...  27.1 us
    all_to_all x2, starting transfers between devices, swap(): return lax.all_to_all(value, axes, split_axis=0, concat_axis=0, tiled=True)  9.23 us
    all_to_all x2, waiting for transfers between devices, swap(): return lax.all_to_all(value, axes, split_axis=0, concat_axis=0, tiled=True)  5.37 us
    ppermute x1, starting transfers between devices, local(): lax.ppermute(packed, axes, [(at, at + 1) for at in range(devices - 1)])  3.95 us
    ppermute x1, waiting for transfers between devices, local(): lax.ppermute(packed, axes, [(at, at + 1) for at in range(devices - 1)])  1.65 us
    unnamed x20, local copies, waits for them, and re-layouts  1.31 us
  transfers between devices with their start and end apart: 3, of which 3 were waited for; matrix products, arithmetic and copies ran while one was open for 1% of the time, Pallas kernels for 35%

profile of v11, /device:TPU:1, one launch (start us, length us, event | category | flops | bytes accessed | tf_op | source)
XLA Modules:
  0.0 49.2 jit_solution(3829569406959774569)
XLA Ops:
  0.0 0.0 copy-start.2
  0.0 1.2 %pack.1 = bf16[24,4608]{1,0:T(8,128)(2,1)S(1)} custom-call(bf16[128,4608]{1,0:T(8,128)(2,1)} %key_ref.5, bf16[128,4608]{1,0:T(8,128)(2,1)} %value_ref.5, bf16[128,4608]{1,0:T(8,128)(2,1)} %query_ref.3), custom_call_target="tpu_custom_call" | custom-call | tf_op jit(solution)/shard_map/pack/pallas_call | solution.py:504
  1.3 3.9 %collective-permute-start = (bf16[24,4608]{1,0:T(8,128)(2,1)S(1)}, bf16[24,4608]{1,0:T(8,128)(2,1)S(1)}, u32[]{:S(2)}, u32[]{:S(2)}) collective-permute-start(bf16[24,4608]{1,0:T(8,128)(2,1)S(1)} %pack.1), channel_id=1, source_target_pairs={{0,1},{1,2},{2,3},{3,4},{4,5},{5,6},{6,7},{7,8},{8,9},{9,10},{10,1... | collective-permute-start | bytes 663560 | tf_op jit(solution)/shard_map/ppermute | solution.py:522
  5.2 0.0 copy-done.8
  5.2 0.1 reshape.3
  5.4 0.0 copy-done
  5.4 0.0 copy-done.1
  5.4 7.2 %signal.1 = (bf16[128,4608]{1,0:T(8,128)(2,1)S(1)}, f32[9,2,8,512]{3,2,1,0:T(8,128)S(1)}, f32[16,36,128]{2,1,0:T(8,128)S(1)}) custom-call(bf16[128,4608]{1,0:T(8,128)(2,1)S(1)} %copy-done.1, bf16[128,4608]{1,0:T(8,128)(2,1)S(1)} %copy-done.2, f32[9,3,7,32]{3,2,1,0:T(8,128)S(1)} %bitcast.3, f32[16,4608]{1,0:T(8,128)S(1)} %copy-done), custom_call_target="tpu_custom_call" | custom-call | flops 35389440 | bytes 5898240 | tf_op jit(solution)/shard_map/signal/pallas_call | solution.py:504
  12.6 1.6 %collective-permute-done.halo_ref = bf16[24,4608]{1,0:T(8,128)(2,1)S(1)} collective-permute-done((bf16[24,4608]{1,0:T(8,128)(2,1)S(1)}, bf16[24,4608]{1,0:T(8,128)(2,1)S(1)}, u32[]{:S(2)}, u32[]{:S(2)}) %collective-permute-start) | collective-permute-done | bytes 221216 | tf_op jit(solution)/shard_map/ppermute | solution.py:522
  14.3 1.7 %head.1 = (bf16[32,18,128]{2,1,0:T(8,128)(2,1)}, bf16[16,4608]{1,0:T(8,128)(2,1)S(1)}, bf16[128,4608]{1,0:T(8,128)(2,1)}) custom-call(bf16[128,4608]{1,0:T(8,128)(2,1)S(1)} %copy-done.1, bf16[128,4608]{1,0:T(8,128)(2,1)S(1)} %copy-done.2, bf16[24,4608]{1,0:T(8,128)(2,1)S(1)} %collective-permute-done.halo_ref, f32[16,4608]{1,0:T(8,128)S(1)} %copy-done, ...), custom_call_target="tpu_custom_call" | custom-call | tf_op jit(solution)/shard_map/head/pallas_call | solution.py:504
  16.0 0.0 copy-start.9
  16.1 0.0 copy-start.3
  16.1 4.0 %all-to-all-start = ((bf16[32,18,128]{2,1,0:T(8,128)(2,1)}), bf16[32,18,128]{2,1,0:T(8,128)(2,1)S(1)}, u32[]{:S(2)}, u32[]{:S(2)}) async-start(bf16[32,18,128]{2,1,0:T(8,128)(2,1)} %get-tuple-element.32), calls=%async_computation | async-start | bytes 393216 | tf_op jit(solution)/shard_map/all_to_all | solution.py:568
  20.1 0.2 sqrt_multiply_fusion.coef_ref
  20.3 0.0 copy-start.4
  20.3 1.3 %copy-done.4 = bf16[128,4608]{1,0:T(8,128)(2,1)S(1)} copy-done((bf16[128,4608]{1,0:T(8,128)(2,1)S(1)}, bf16[128,4608]{1,0:T(8,128)(2,1)}, u32[]{:S(2)}) %copy-start.4) | copy-done | bytes 1179672
  21.6 6.3 %gate.1 = (bf16[128,4608]{1,0:T(8,128)(2,1)}, f32[128,4608]{1,0:T(8,128)}, f32[9,16,8,128]{3,2,1,0:T(8,128)}) custom-call(bf16[128,4608]{1,0:T(8,128)(2,1)S(1)} %copy-done.3, bf16[24,4608]{1,0:T(8,128)(2,1)} %copy-done.6, f32[9,3,7,32]{3,2,1,0:T(8,128)S(1)} %bitcast.4, bf16[128,4608]{1,0:T(8,128)(2,1)S(1)} %copy-done.4, ...), custom_call_target="tpu_custom_call" | custom-call | flops 16515072 | bytes 3538944 | tf_op jit(solution)/shard_map/gate/pallas_call | solution.py:504
  27.9 0.0 copy-start.5
  27.9 0.6 %all-to-all-done.piece_ref = bf16[32,18,128]{2,1,0:T(8,128)(2,1)S(1)} async-done(((bf16[32,18,128]{2,1,0:T(8,128)(2,1)}), bf16[32,18,128]{2,1,0:T(8,128)(2,1)S(1)}, u32[]{:S(2)}, u32[]{:S(2)}) %all-to-all-start) | async-done | bytes 147488 | tf_op jit(solution)/shard_map/all_to_all | solution.py:568
  28.5 0.8 %prefix.1 = bf16[32,18,128]{2,1,0:T(8,128)(2,1)} custom-call(bf16[32,18,128]{2,1,0:T(8,128)(2,1)S(1)} %all-to-all-done.piece_ref, f32[16,4608]{1,0:T(8,128)S(1)} %copy-done, f32[16,4608]{1,0:T(8,128)S(1)} %sqrt_multiply_fusion.coef_ref), custom_call_target="tpu_custom_call" | custom-call | tf_op jit(solution)/shard_map/prefix/pallas_call | solution.py:504
  29.4 5.2 %all-to-all-start.1 = ((bf16[32,18,128]{2,1,0:T(8,128)(2,1)}), bf16[32,18,128]{2,1,0:T(8,128)(2,1)S(1)}, u32[]{:S(2)}, u32[]{:S(2)}) async-start(bf16[32,18,128]{2,1,0:T(8,128)(2,1)} %prefix.1), calls=%async_computation.1 | async-start | bytes 393216 | tf_op jit(solution)/shard_map/all_to_all | solution.py:568
  34.6 3.7 %within.1 = (f32[128,4608]{1,0:T(8,128)}, f32[9,16,8,128]{3,2,1,0:T(8,128)}) custom-call(bf16[128,4608]{1,0:T(8,128)(2,1)S(1)} %copy-done.5, bf16[16,4608]{1,0:T(8,128)(2,1)S(1)} %get-tuple-element.35.head_ref, f32[16,4608]{1,0:T(8,128)S(1)} %copy-done, f32[16,4608]{1,0:T(8,128)S(1)} %sqrt_multiply_fusion.coef_ref, ...), custom_call_target="tpu_custom_call", output_to_operand_aliasing={{0}: (5, {}), {1}: (6, {})} | custom-call | flops 29491200 | bytes 4718592 | tf_op jit(solution)/shard_map/within/pallas_call | solution.py:504
  38.3 4.7 %all-to-all-done.1.piece_ref = bf16[32,18,128]{2,1,0:T(8,128)(2,1)S(1)} async-done(((bf16[32,18,128]{2,1,0:T(8,128)(2,1)}), bf16[32,18,128]{2,1,0:T(8,128)(2,1)S(1)}, u32[]{:S(2)}, u32[]{:S(2)}) %all-to-all-start.1) | async-done | bytes 147488 | tf_op jit(solution)/shard_map/all_to_all | solution.py:568
  43.0 6.1 %final.1 = bf16[128,4608]{1,0:T(8,128)(2,1)} custom-call(bf16[32,18,128]{2,1,0:T(8,128)(2,1)S(1)} %all-to-all-done.1.piece_ref, f32[16,4608]{1,0:T(8,128)S(1)} %copy-done, f32[9,16,8,128]{3,2,1,0:T(8,128)} %get-tuple-element.48.mid_ref, f32[128,4608]{1,0:T(8,128)} %get-tuple-element.49.y_ref, bf16[128,4608]{1,0:T(8,128)(2,1)} %get-tuple-element.50.gate_ref), custom_call_target="tpu_custom_call" | custom-call | flops 23592960 | bytes 5898240 | tf_op jit(solution)/shard_map/final/pallas_call | solution.py:504
  (13 shorter events, 0.1 us)
Async XLA Ops:
  0.0 5.2 %copy-start.8 = (f32[3,7,288]{2,1,0:T(8,128)S(1)}, f32[3,7,288]{2,1,0:T(8,128)}, u32[]{:S(2)}) copy-start(f32[3,7,288]{2,1,0:T(8,128)} %param.10) | copy-start | bytes 72580
  0.0 5.4 %copy-start = (f32[16,4608]{1,0:T(8,128)S(1)}, f32[16,4608]{1,0:T(8,128)}, u32[]{:S(2)}) copy-start(f32[16,4608]{1,0:T(8,128)} %rate_ref.11) | copy-start | bytes 884740
  0.0 5.4 %copy-start.1 = (bf16[128,4608]{1,0:T(8,128)(2,1)S(1)}, bf16[128,4608]{1,0:T(8,128)(2,1)}, u32[]{:S(2)}) copy-start(bf16[128,4608]{1,0:T(8,128)(2,1)} %key_ref.5) | copy-start | bytes 3538948
  0.0 5.4 %copy-start.2 = (bf16[128,4608]{1,0:T(8,128)(2,1)S(1)}, bf16[128,4608]{1,0:T(8,128)(2,1)}, u32[]{:S(2)}) copy-start(bf16[128,4608]{1,0:T(8,128)(2,1)} %value_ref.5) | copy-start | bytes 3538948
  1.3 13.0 %collective-permute-start = (bf16[24,4608]{1,0:T(8,128)(2,1)S(1)}, bf16[24,4608]{1,0:T(8,128)(2,1)S(1)}, u32[]{:S(2)}, u32[]{:S(2)}) collective-permute-start(bf16[24,4608]{1,0:T(8,128)(2,1)S(1)} %pack.1), channel_id=1, source_target_pairs={{0,1},{1,2},{2,3},{3,4},{4,5},{5,6},{6,7},{7,8},{8,9},{9,10},{10,1... | collective-permute-start | bytes 663560 | tf_op jit(solution)/shard_map/ppermute | solution.py:522
  14.3 1.7 %copy-start.6 = (bf16[24,4608]{1,0:T(8,128)(2,1)}, bf16[24,4608]{1,0:T(8,128)(2,1)S(1)}, u32[]{:S(2)}) copy-start(bf16[24,4608]{1,0:T(8,128)(2,1)S(1)} %collective-permute-done.halo_ref) | copy-start | bytes 663556
  14.3 5.8 %copy-start.7 = (f32[16,4608]{1,0:T(8,128)S(1)}, f32[16,4608]{1,0:T(8,128)}, u32[]{:S(2)}) copy-start(f32[16,4608]{1,0:T(8,128)} %param.12) | copy-start | bytes 884740
  16.0 4.2 %copy-start.9 = (f32[4608]{0:T(1024)S(1)}, f32[4608]{0:T(1024)}, u32[]{:S(2)}) copy-start(f32[4608]{0:T(1024)} %param.13) | copy-start | bytes 55300
  16.1 4.3 %copy-start.3 = (bf16[128,4608]{1,0:T(8,128)(2,1)S(1)}, bf16[128,4608]{1,0:T(8,128)(2,1)}, u32[]{:S(2)}) copy-start(bf16[128,4608]{1,0:T(8,128)(2,1)} %query_ref.3) | copy-start | bytes 3538948
  16.1 12.5 %all-to-all-start = ((bf16[32,18,128]{2,1,0:T(8,128)(2,1)}), bf16[32,18,128]{2,1,0:T(8,128)(2,1)S(1)}, u32[]{:S(2)}, u32[]{:S(2)}) async-start(bf16[32,18,128]{2,1,0:T(8,128)(2,1)} %get-tuple-element.32), calls=%async_computation | async-start | bytes 393216 | tf_op jit(solution)/shard_map/all_to_all | solution.py:568
  20.3 1.3 %copy-start.4 = (bf16[128,4608]{1,0:T(8,128)(2,1)S(1)}, bf16[128,4608]{1,0:T(8,128)(2,1)}, u32[]{:S(2)}) copy-start(bf16[128,4608]{1,0:T(8,128)(2,1)} %get-tuple-element.34.u_ref) | copy-start | bytes 3538948
  27.9 6.7 %copy-start.5 = (bf16[128,4608]{1,0:T(8,128)(2,1)S(1)}, bf16[128,4608]{1,0:T(8,128)(2,1)}, u32[]{:S(2)}) copy-start(bf16[128,4608]{1,0:T(8,128)(2,1)} %get-tuple-element.34.u_ref) | copy-start | bytes 3538948
  29.4 13.7 %all-to-all-start.1 = ((bf16[32,18,128]{2,1,0:T(8,128)(2,1)}), bf16[32,18,128]{2,1,0:T(8,128)(2,1)S(1)}, u32[]{:S(2)}, u32[]{:S(2)}) async-start(bf16[32,18,128]{2,1,0:T(8,128)(2,1)} %prefix.1), calls=%async_computation.1 | async-start | bytes 393216 | tf_op jit(solution)/shard_map/all_to_all | solution.py:568

commit v12 on v11

--- a/solution.py
+++ b/solution.py
@@ -197,7 +197,7 @@
 
 
 def signal_kernel(key_ref, value_ref, feat_ref, rate_ref, u_ref, wide_ref, state_ref, power_scr, last_scr, *columns):
-    tokens, tiles = u_ref.shape[0], state_ref.shape[1]
+    tokens, tiles = u_ref.shape[0], u_ref.shape[1] // LANES
     modes = rate_ref.shape[0]
     chunks = tiles // TILES
     count = feat_ref.shape[2]
@@ -223,7 +223,7 @@
             for level in (2, 1, 0):
                 factor = wide(power_scr[level, mode : mode + 1, lanes])
                 whole = factor * whole + pltpu.roll(whole, ROWS - (1 << level), 0)
-            state_ref[mode, pl.ds(number, 1), :] = whole[:1]
+            state_ref[mode : mode + 1, lanes] = whole[:1]
 
     def tile(number, _):
         lanes = tile_lanes(number)
@@ -254,15 +254,11 @@
 
 
 def head_kernel(key_ref, value_ref, halo_ref, rate_ref, wide_ref, state_ref, u_ref, *rest, tokens, reach):
-    out_ref, head_ref, u_out_ref, rate_scr, column_scr, token_scr, total_scr, sem = rest
+    out_ref, head_ref, u_out_ref, column_scr, token_scr, total_scr, sem = rest
     move = pltpu.make_async_copy(u_ref, u_out_ref, sem.at[0])
     move.start()
-    modes, tiles = state_ref.shape[:2]
-    pieces, piece_rows = out_ref.shape[:2]
-    for group in range(modes // ROWS):
-        for tile in range(tiles):
-            rows = pl.ds((group * tiles + tile) * ROWS, ROWS)
-            rate_scr[rows, :] = rate_ref[group * ROWS : (group + 1) * ROWS, tile * LANES : (tile + 1) * LANES]
+    modes, tiles = state_ref.shape[0], state_ref.shape[1] // LANES
+    pieces, piece_modes, piece_width = out_ref.shape
 
     def some(chunk, _):
         for number in range(TILES):
@@ -278,23 +274,23 @@
                 column[pl.ds(2 * ROWS, ROWS), :] = source[: 2 * ROWS, lanes].astype(f32)[:ROWS]
                 parts += fir(column, taps, 2 * ROWS, 1)
             u = jnp.where(sublane() < reach, rounded(parts[0] * parts[1]), 0.0)
-            token_scr[pl.ds(pl.multiple_of((chunk * TILES + number) * ROWS, ROWS), ROWS), :] = u
+            token_scr[number] = u
+            for group in range(0, modes, ROWS):
+                decay = jnp.exp(-rate_ref[group : group + ROWS, lanes])
+                head = wide(token_scr[number, :1, :])
+                for row in range(1, reach):
+                    head = decay * head + wide(token_scr[number, row : row + 1, :])
+                total = state_ref[group : group + ROWS, lanes] + power(decay, tokens - reach) * head
+                total_scr[group : group + ROWS, lanes] = total
             head_ref[:, lanes] = jnp.concatenate([u, jnp.zeros((ROWS, LANES), f32)], axis=0).astype(bf16)
         return 0
 
     lax.fori_loop(0, tiles // TILES, some, 0)
-    signals = [token_scr[pl.ds(row, tiles, stride=ROWS), :] for row in range(reach)]
-    split = pieces // modes
-    for mode in range(modes):
-        start = mode // ROWS * tiles * ROWS + mode % ROWS
-        decay = jnp.exp(-rate_scr[pl.ds(start, tiles, stride=ROWS), :])
-        head = signals[0]
-        for row in range(1, reach):
-            head = decay * head + signals[row]
-        total_scr[mode] = state_ref[mode] + power(decay, tokens - reach) * head
-        for part in range(split):
-            rows = total_scr[mode, part * piece_rows : (part + 1) * piece_rows, :]
-            out_ref[mode * split + part] = rows.astype(out_ref.dtype)
+    split = pieces * piece_modes // modes
+    for piece in range(pieces):
+        first, part = piece // split * piece_modes, piece % split
+        rows = total_scr[first : first + piece_modes, part * piece_width : (part + 1) * piece_width]
+        out_ref[piece] = rows.astype(out_ref.dtype)
     move.wait()
 
 
@@ -334,21 +330,22 @@
         wait_all(give(at))
 
 
-def prefix_kernel(piece_ref, rate_ref, coef_ref, out_ref, table_scr, *, tokens, axes):
-    devices, piece_rows = piece_ref.shape[:2]
-    split = devices // rate_ref.shape[0]
+def prefix_kernel(piece_ref, rate_ref, coef_ref, out_ref, *, tokens, axes):
+    devices, piece_modes, piece_width = piece_ref.shape
+    split = devices * piece_modes // rate_ref.shape[0]
     mine = lax.axis_index(axes)
-    mode, part = mine // split, mine % split
+    mode, part = mine // split * piece_modes, mine % split
     group = pl.multiple_of(mode // ROWS * ROWS, ROWS)
-    first = pl.multiple_of(part * piece_rows * LANES, LANES)
+    first = pl.multiple_of(part * piece_width, LANES)
 
     def mine_of(ref):
-        rows = ref[pl.ds(group, ROWS), pl.ds(first, piece_rows * LANES)]
-        here = lax.broadcasted_iota(jnp.int32, rows.shape, 0) == mode - group
-        row = jnp.sum(jnp.where(here, rows, 0.0), axis=0, keepdims=True)
-        for number in range(piece_rows):
-            table_scr[number : number + 1, :] = lanes_of(row, number)
-        return table_scr[:piece_rows, :]
+        rows = ref[pl.ds(group, ROWS), pl.ds(first, piece_width)]
+        place = lax.broadcasted_iota(jnp.int32, rows.shape, 0)
+        found = [
+            jnp.sum(jnp.where(place == mode - group + row, rows, 0.0), axis=0, keepdims=True)
+            for row in range(piece_modes)
+        ]
+        return jnp.concatenate(found, axis=0)
 
     coef = mine_of(coef_ref)
     through = jnp.exp(-float(tokens) * mine_of(rate_ref))
@@ -360,7 +357,7 @@
             entering = through * entering + piece_ref[source].astype(f32)
         return entering
 
-    lax.fori_loop(0, devices // 4, lap, jnp.zeros((piece_rows, LANES), f32))
+    lax.fori_loop(0, devices // 4, lap, jnp.zeros((piece_modes, piece_width), f32))
 
 
 def local_kernel(u_ref, head_ref, rate_ref, coef_ref, skip_ref, *rest, first, last):
@@ -427,12 +424,12 @@
         return columns(at) + [pltpu.make_async_copy(mid_ref.at[at], mid_buf.at[at], mid_sem.at[at])]
 
     begin(chunks, fetch)
-    pieces, piece_rows = piece_ref.shape[:2]
-    split = pieces // modes
-    for mode in range(modes):
-        for part in range(split):
-            rows = piece_ref[mode * split + part].astype(f32)
-            total_scr[mode, part * piece_rows : (part + 1) * piece_rows, :] = rows
+    pieces, piece_modes, piece_width = piece_ref.shape
+    split = pieces * piece_modes // modes
+    for piece in range(pieces):
+        first, part = piece // split * piece_modes, piece % split
+        lanes = slice(part * piece_width, (part + 1) * piece_width)
+        total_scr[first : first + piece_modes, lanes] = piece_ref[piece].astype(f32)
     bits = [(sublane() >> level) % 2 == 1 for level in range(3)]
 
     def chunk(at):
@@ -450,7 +447,7 @@
                 for bit, row in zip(bits, rows):
                     lead = lead * jnp.where(bit, row, 1.0)
                 lead_scr[mode] = lead
-                state.append(lead * wide(total_scr[mode, pl.ds(at * TILES + number, 1), :]))
+                state.append(lead * wide(total_scr[mode : mode + 1, tile_lanes(at * TILES + number)]))
             decay = [wide(power_scr[3, mode : mode + 1, lanes]) for mode in range(modes)]
             for pair in range(tokens // (2 * ROWS)):
                 rows = slice(pair * 2 * ROWS, (pair + 1) * 2 * ROWS)
@@ -487,8 +484,8 @@
     devices = math.prod(lax.axis_size(axis) for axis in axes)
     chunks = width // CHUNK
     tiles = width // LANES
-    split = devices // modes
-    even = devices % modes == 0 and tiles % split == 0
+    split = devices * 2 // modes
+    even = devices * 2 % modes == 0 and tiles % split == 0
     vmem = pltpu.VMEM
     far = pltpu.HBM
     near = jax.ShapeDtypeStruct
@@ -527,20 +524,20 @@
     u, wide_taps, state = call(
         signal_kernel,
         (key_proj, value_proj, feat, rates),
-        [near((tokens, width), bf16), near((chunks, 2, ROWS, CHUNK), f32), near((modes, tiles, LANES), f32)],
+        [near((tokens, width), bf16), near((chunks, 2, ROWS, CHUNK), f32), near((modes, width), f32)],
         [vmem((4, modes, width), f32), vmem((modes, ROWS, LANES), f32), column, column],
         "signal",
         close=range(4),
         cost_estimate=cost(60 * elements, 10 * elements),
     )
 
-    pieces = (modes * split, tiles // split, LANES) if even else (modes, tiles, LANES)
+    pieces = (devices, 2, width // split) if even else (modes // 2, 2, width)
     left, head, u = call(
         functools.partial(head_kernel, tokens=tokens, reach=taps - 1),
         (key_proj, value_proj, halo, rates, wide_taps, state, u),
         [near(pieces, bf16), near((2 * ROWS, width), bf16), far((tokens, width), bf16)],
-        [vmem((modes * tiles, LANES), f32), vmem((TILES, 2, 3 * ROWS, LANES), f32)]
-        + [vmem((tiles * ROWS, LANES), f32), vmem((modes, tiles, LANES), f32), dma((1,))],
+        [vmem((TILES, 2, 3 * ROWS, LANES), f32), vmem((TILES, ROWS, LANES), f32)]
+        + [vmem((modes, width), f32), dma((1,))],
         "head",
         close=range(7),
     )
@@ -551,7 +548,7 @@
     local_shapes = [far((tokens, width), f32), far((chunks, modes, ROWS, LANES), f32)]
     local_scratches = [whole_buf, vmem((chunks, modes, ROWS, LANES), f32), stage, stage]
     local_scratches += [dma((1, chunks)), dma((chunks,))]
-    early = chunks * 5 // 9
+    early = chunks // 3
     gate, y, mid = call(
         functools.partial(gate_kernel, early=early),
         (query, halo_late, feat, u, head, rates, coef, skip_row),
@@ -575,7 +572,7 @@
             functools.partial(prefix_kernel, tokens=tokens, axes=axes),
             (theirs, rates, coef),
             [near(pieces, bf16)],
-            [vmem((-(-pieces[1] // ROWS) * ROWS, LANES), f32)],
+            [],
             "prefix",
             close=(0, 1, 2),
         )
@@ -607,7 +604,7 @@
         (entered, rates, mid, y, gate),
         [far((tokens, width), bf16)],
         [vmem((chunks, modes, ROWS, LANES), f32), whole_buf, half_buf, half_buf]
-        + [vmem((modes, tiles, LANES), f32), vmem((4, modes, CHUNK), f32), vmem((modes, ROWS, LANES), f32)]
+        + [vmem((modes, width), f32), vmem((4, modes, CHUNK), f32), vmem((modes, ROWS, LANES), f32)]
         + [dma((2, chunks)), dma((chunks,)), dma((1, chunks))],
         "final",
         close=(0, 1),

time: 49.8 us -> 47.8 us (0.960)
  waiting for transfers between devices: 7.02 us -> 5.5 us
  starting transfers between devices: 13.2 us -> 12.5 us
    all_to_all x2, waiting for transfers between devices: 5.37 us -> 3.85 us  [swap(): return lax.all_to_all(value, axes, split_axis=0, concat_axis=0, tiled=True)]
    all_to_all x2, starting transfers between devices: 9.23 us -> 8.58 us  [swap(): return lax.all_to_all(value, axes, split_axis=0, concat_axis=0, tiled=True)]
  transfers between devices with their start and end apart: 3 -> 3, of which waited for: 3 -> 3; matrix products, arithmetic and copies ran while one was open for 1% -> 1% of each run, Pallas kernels for 35% -> 37%
where the time goes in v12:
time: 47.8 us; the launch traced here: 47.1 us
  Pallas kernels  27.3 us (57%)
  starting transfers between devices  12.5 us (26%)
  waiting for transfers between devices  5.5 us (12%)
  local copies, waits for them, and re-layouts  1.44 us (3%)
    pallas_call x7, Pallas kernels, call(): pl.pallas_call(kernel, in_specs=[beside if at in close else there for at...  27.3 us
    all_to_all x2, starting transfers between devices, swap(): return lax.all_to_all(value, axes, split_axis=0, concat_axis=0, tiled=True)  8.58 us
    ppermute x1, starting transfers between devices, local(): lax.ppermute(packed, axes, [(at, at + 1) for at in range(devices - 1)])  3.95 us
    all_to_all x2, waiting for transfers between devices, swap(): return lax.all_to_all(value, axes, split_axis=0, concat_axis=0, tiled=True)  3.85 us
    ppermute x1, waiting for transfers between devices, local(): lax.ppermute(packed, axes, [(at, at + 1) for at in range(devices - 1)])  1.65 us
    unnamed x20, local copies, waits for them, and re-layouts  1.3 us
  transfers between devices with their start and end apart: 3, of which 3 were waited for; matrix products, arithmetic and copies ran while one was open for 1% of the time, Pallas kernels for 37%

profile of v12, /device:TPU:1, one launch (start us, length us, event | category | flops | bytes accessed | tf_op | source)
XLA Modules:
  0.0 47.1 jit_solution(14963140715095934668)
XLA Ops:
  0.0 0.0 copy-start.2
  0.0 1.2 %pack.1 = bf16[24,4608]{1,0:T(8,128)(2,1)S(1)} custom-call(bf16[128,4608]{1,0:T(8,128)(2,1)} %key_ref.5, bf16[128,4608]{1,0:T(8,128)(2,1)} %value_ref.5, bf16[128,4608]{1,0:T(8,128)(2,1)} %query_ref.3), custom_call_target="tpu_custom_call" | custom-call | tf_op jit(solution)/shard_map/pack/pallas_call | solution.py:501
  1.3 3.9 %collective-permute-start = (bf16[24,4608]{1,0:T(8,128)(2,1)S(1)}, bf16[24,4608]{1,0:T(8,128)(2,1)S(1)}, u32[]{:S(2)}, u32[]{:S(2)}) collective-permute-start(bf16[24,4608]{1,0:T(8,128)(2,1)S(1)} %pack.1), channel_id=1, source_target_pairs={{0,1},{1,2},{2,3},{3,4},{4,5},{5,6},{6,7},{7,8},{8,9},{9,10},{10,1... | collective-permute-start | bytes 663560 | tf_op jit(solution)/shard_map/ppermute | solution.py:519
  5.2 0.0 copy-done.8
  5.2 0.1 reshape.3
  5.4 0.0 copy-done
  5.4 7.2 %signal.1 = (bf16[128,4608]{1,0:T(8,128)(2,1)S(1)}, f32[9,2,8,512]{3,2,1,0:T(8,128)S(1)}, f32[16,4608]{1,0:T(8,128)S(1)}) custom-call(bf16[128,4608]{1,0:T(8,128)(2,1)S(1)} %copy-done.1, bf16[128,4608]{1,0:T(8,128)(2,1)S(1)} %copy-done.2, f32[9,3,7,32]{3,2,1,0:T(8,128)S(1)} %bitcast.3, f32[16,4608]{1,0:T(8,128)S(1)} %copy-done), custom_call_target="tpu_custom_call" | custom-call | flops 35389440 | bytes 5898240 | tf_op jit(solution)/shard_map/signal/pallas_call | solution.py:501
  12.6 1.6 %collective-permute-done.halo_ref = bf16[24,4608]{1,0:T(8,128)(2,1)S(1)} collective-permute-done((bf16[24,4608]{1,0:T(8,128)(2,1)S(1)}, bf16[24,4608]{1,0:T(8,128)(2,1)S(1)}, u32[]{:S(2)}, u32[]{:S(2)}) %collective-permute-start) | collective-permute-done | bytes 221216 | tf_op jit(solution)/shard_map/ppermute | solution.py:519
  14.3 1.7 %head.1 = (bf16[32,2,1152]{2,1,0:T(2,128)(2,1)}, bf16[16,4608]{1,0:T(8,128)(2,1)S(1)}, bf16[128,4608]{1,0:T(8,128)(2,1)}) custom-call(bf16[128,4608]{1,0:T(8,128)(2,1)S(1)} %copy-done.1, bf16[128,4608]{1,0:T(8,128)(2,1)S(1)} %copy-done.2, bf16[24,4608]{1,0:T(8,128)(2,1)S(1)} %collective-permute-done.halo_ref, f32[16,4608]{1,0:T(8,128)S(1)} %copy-done, ...), custom_call_target="tpu_custom_call" | custom-call | tf_op jit(solution)/shard_map/head/pallas_call | solution.py:501
  16.0 0.0 copy-start.3
  16.0 4.0 %all-to-all-start = ((bf16[32,2,1152]{2,1,0:T(2,128)(2,1)}), bf16[32,2,1152]{2,1,0:T(2,128)(2,1)S(1)}, u32[]{:S(2)}, u32[]{:S(2)}) async-start(bf16[32,2,1152]{2,1,0:T(2,128)(2,1)} %get-tuple-element.32), calls=%async_computation | async-start | bytes 294912 | tf_op jit(solution)/shard_map/all_to_all | solution.py:565
  20.0 0.0 copy-done.7
  20.1 0.2 sqrt_multiply_fusion.coef_ref
  20.2 0.0 copy-done.9
  20.3 0.0 copy-start.4
  20.3 1.3 %copy-done.4 = bf16[128,4608]{1,0:T(8,128)(2,1)S(1)} copy-done((bf16[128,4608]{1,0:T(8,128)(2,1)S(1)}, bf16[128,4608]{1,0:T(8,128)(2,1)}, u32[]{:S(2)}) %copy-start.4) | copy-done | bytes 1179672
  21.6 4.9 %gate.1 = (bf16[128,4608]{1,0:T(8,128)(2,1)}, f32[128,4608]{1,0:T(8,128)}, f32[9,16,8,128]{3,2,1,0:T(8,128)}) custom-call(bf16[128,4608]{1,0:T(8,128)(2,1)S(1)} %copy-done.3, bf16[24,4608]{1,0:T(8,128)(2,1)} %copy-done.6, f32[9,3,7,32]{3,2,1,0:T(8,128)S(1)} %bitcast.4, bf16[128,4608]{1,0:T(8,128)(2,1)S(1)} %copy-done.4, ...), custom_call_target="tpu_custom_call" | custom-call | flops 16515072 | bytes 3538944 | tf_op jit(solution)/shard_map/gate/pallas_call | solution.py:501
  26.4 0.0 copy-start.5
  26.4 1.3 %all-to-all-done.piece_ref = bf16[32,2,1152]{2,1,0:T(2,128)(2,1)S(1)} async-done(((bf16[32,2,1152]{2,1,0:T(2,128)(2,1)}), bf16[32,2,1152]{2,1,0:T(2,128)(2,1)S(1)}, u32[]{:S(2)}, u32[]{:S(2)}) %all-to-all-start) | async-done | bytes 147488 | tf_op jit(solution)/shard_map/all_to_all | solution.py:565
  27.7 1.0 %prefix.1 = bf16[32,2,1152]{2,1,0:T(2,128)(2,1)} custom-call(bf16[32,2,1152]{2,1,0:T(2,128)(2,1)S(1)} %all-to-all-done.piece_ref, f32[16,4608]{1,0:T(8,128)S(1)} %copy-done, f32[16,4608]{1,0:T(8,128)S(1)} %sqrt_multiply_fusion.coef_ref), custom_call_target="tpu_custom_call" | custom-call | tf_op jit(solution)/shard_map/prefix/pallas_call | solution.py:501
  28.7 4.6 %all-to-all-start.1 = ((bf16[32,2,1152]{2,1,0:T(2,128)(2,1)}), bf16[32,2,1152]{2,1,0:T(2,128)(2,1)S(1)}, u32[]{:S(2)}, u32[]{:S(2)}) async-start(bf16[32,2,1152]{2,1,0:T(2,128)(2,1)} %prefix.1), calls=%async_computation.1 | async-start | bytes 294912 | tf_op jit(solution)/shard_map/all_to_all | solution.py:565
  33.3 5.1 %within.1 = (f32[128,4608]{1,0:T(8,128)}, f32[9,16,8,128]{3,2,1,0:T(8,128)}) custom-call(bf16[128,4608]{1,0:T(8,128)(2,1)S(1)} %copy-done.5, bf16[16,4608]{1,0:T(8,128)(2,1)S(1)} %get-tuple-element.35.head_ref, f32[16,4608]{1,0:T(8,128)S(1)} %copy-done, f32[16,4608]{1,0:T(8,128)S(1)} %sqrt_multiply_fusion.coef_ref, ...), custom_call_target="tpu_custom_call", output_to_operand_aliasing={{0}: (5, {}), {1}: (6, {})} | custom-call | flops 29491200 | bytes 4718592 | tf_op jit(solution)/shard_map/within/pallas_call | solution.py:501
  38.4 2.6 %all-to-all-done.1.piece_ref = bf16[32,2,1152]{2,1,0:T(2,128)(2,1)S(1)} async-done(((bf16[32,2,1152]{2,1,0:T(2,128)(2,1)}), bf16[32,2,1152]{2,1,0:T(2,128)(2,1)S(1)}, u32[]{:S(2)}, u32[]{:S(2)}) %all-to-all-start.1) | async-done | bytes 147488 | tf_op jit(solution)/shard_map/all_to_all | solution.py:565
  41.0 6.1 %final.1 = bf16[128,4608]{1,0:T(8,128)(2,1)} custom-call(bf16[32,2,1152]{2,1,0:T(2,128)(2,1)S(1)} %all-to-all-done.1.piece_ref, f32[16,4608]{1,0:T(8,128)S(1)} %copy-done, f32[9,16,8,128]{3,2,1,0:T(8,128)} %get-tuple-element.48.mid_ref, f32[128,4608]{1,0:T(8,128)} %get-tuple-element.49.y_ref, bf16[128,4608]{1,0:T(8,128)(2,1)} %get-tuple-element.50.gate_ref), custom_call_target="tpu_custom_call" | custom-call | flops 23592960 | bytes 5898240 | tf_op jit(solution)/shard_map/final/pallas_call | solution.py:501
  (13 shorter events, 0.1 us)
Async XLA Ops:
  0.0 5.2 %copy-start.8 = (f32[3,7,288]{2,1,0:T(8,128)S(1)}, f32[3,7,288]{2,1,0:T(8,128)}, u32[]{:S(2)}) copy-start(f32[3,7,288]{2,1,0:T(8,128)} %param.10) | copy-start | bytes 72580
  0.0 5.4 %copy-start = (f32[16,4608]{1,0:T(8,128)S(1)}, f32[16,4608]{1,0:T(8,128)}, u32[]{:S(2)}) copy-start(f32[16,4608]{1,0:T(8,128)} %rate_ref.11) | copy-start | bytes 884740
  0.0 5.4 %copy-start.1 = (bf16[128,4608]{1,0:T(8,128)(2,1)S(1)}, bf16[128,4608]{1,0:T(8,128)(2,1)}, u32[]{:S(2)}) copy-start(bf16[128,4608]{1,0:T(8,128)(2,1)} %key_ref.5) | copy-start | bytes 3538948
  0.0 5.4 %copy-start.2 = (bf16[128,4608]{1,0:T(8,128)(2,1)S(1)}, bf16[128,4608]{1,0:T(8,128)(2,1)}, u32[]{:S(2)}) copy-start(bf16[128,4608]{1,0:T(8,128)(2,1)} %value_ref.5) | copy-start | bytes 3538948
  1.3 13.0 %collective-permute-start = (bf16[24,4608]{1,0:T(8,128)(2,1)S(1)}, bf16[24,4608]{1,0:T(8,128)(2,1)S(1)}, u32[]{:S(2)}, u32[]{:S(2)}) collective-permute-start(bf16[24,4608]{1,0:T(8,128)(2,1)S(1)} %pack.1), channel_id=1, source_target_pairs={{0,1},{1,2},{2,3},{3,4},{4,5},{5,6},{6,7},{7,8},{8,9},{9,10},{10,1... | collective-permute-start | bytes 663560 | tf_op jit(solution)/shard_map/ppermute | solution.py:519
  14.3 1.7 %copy-start.6 = (bf16[24,4608]{1,0:T(8,128)(2,1)}, bf16[24,4608]{1,0:T(8,128)(2,1)S(1)}, u32[]{:S(2)}) copy-start(bf16[24,4608]{1,0:T(8,128)(2,1)S(1)} %collective-permute-done.halo_ref) | copy-start | bytes 663556
  14.3 5.7 %copy-start.7 = (f32[16,4608]{1,0:T(8,128)S(1)}, f32[16,4608]{1,0:T(8,128)}, u32[]{:S(2)}) copy-start(f32[16,4608]{1,0:T(8,128)} %param.12) | copy-start | bytes 884740
  14.3 5.9 %copy-start.9 = (f32[4608]{0:T(1024)S(1)}, f32[4608]{0:T(1024)}, u32[]{:S(2)}) copy-start(f32[4608]{0:T(1024)} %param.13) | copy-start | bytes 55300
  16.0 4.3 %copy-start.3 = (bf16[128,4608]{1,0:T(8,128)(2,1)S(1)}, bf16[128,4608]{1,0:T(8,128)(2,1)}, u32[]{:S(2)}) copy-start(bf16[128,4608]{1,0:T(8,128)(2,1)} %query_ref.3) | copy-start | bytes 3538948
  16.0 11.7 %all-to-all-start = ((bf16[32,2,1152]{2,1,0:T(2,128)(2,1)}), bf16[32,2,1152]{2,1,0:T(2,128)(2,1)S(1)}, u32[]{:S(2)}, u32[]{:S(2)}) async-start(bf16[32,2,1152]{2,1,0:T(2,128)(2,1)} %get-tuple-element.32), calls=%async_computation | async-start | bytes 294912 | tf_op jit(solution)/shard_map/all_to_all | solution.py:565
  20.3 1.3 %copy-start.4 = (bf16[128,4608]{1,0:T(8,128)(2,1)S(1)}, bf16[128,4608]{1,0:T(8,128)(2,1)}, u32[]{:S(2)}) copy-start(bf16[128,4608]{1,0:T(8,128)(2,1)} %get-tuple-element.34.u_ref) | copy-start | bytes 3538948
  26.4 6.9 %copy-start.5 = (bf16[128,4608]{1,0:T(8,128)(2,1)S(1)}, bf16[128,4608]{1,0:T(8,128)(2,1)}, u32[]{:S(2)}) copy-start(bf16[128,4608]{1,0:T(8,128)(2,1)} %get-tuple-element.34.u_ref) | copy-start | bytes 3538948
  28.7 12.3 %all-to-all-start.1 = ((bf16[32,2,1152]{2,1,0:T(2,128)(2,1)}), bf16[32,2,1152]{2,1,0:T(2,128)(2,1)S(1)}, u32[]{:S(2)}, u32[]{:S(2)}) async-start(bf16[32,2,1152]{2,1,0:T(2,128)(2,1)} %prefix.1), calls=%async_computation.1 | async-start | bytes 294912 | tf_op jit(solution)/shard_map/all_to_all | solution.py:565

commit v13 on v12

--- a/solution.py
+++ b/solution.py
@@ -184,6 +184,12 @@
     return lambda at: [pltpu.make_async_copy(buf.at[at], ref.at[:, span(at)], sem.at[0, at])]
 
 
+def lay_halo(column, halo, member, lanes):
+    pairs = halo.shape[0] // 3
+    for pair in range(pairs):
+        column[pl.ds(2 * ROWS - 2 * pairs + 2 * pair, 2), :] = halo[member * pairs + pair, :, lanes].astype(f32)
+
+
 def pack_kernel(key_ref, value_ref, query_ref, out_ref, in_buf, in_sem):
     tokens = key_ref.shape[0]
     copies = [
@@ -192,8 +198,11 @@
     ]
     start_all(copies)
     wait_all(copies)
-    tails = [in_buf[at].astype(f32)[ROWS:] for at in range(len(copies))]
-    out_ref[...] = jnp.concatenate(tails, axis=0).astype(bf16)
+    pairs = out_ref.shape[0] // len(copies)
+    for at in range(len(copies)):
+        tail = in_buf[at].astype(f32)[2 * ROWS - 2 * pairs :]
+        for pair in range(pairs):
+            out_ref[at * pairs + pair] = tail[2 * pair : 2 * pair + 2].astype(bf16)
 
 
 def signal_kernel(key_ref, value_ref, feat_ref, rate_ref, u_ref, wide_ref, state_ref, power_scr, last_scr, *columns):
@@ -225,7 +234,7 @@
                 whole = factor * whole + pltpu.roll(whole, ROWS - (1 << level), 0)
             state_ref[mode : mode + 1, lanes] = whole[:1]
 
-    def tile(number, _):
+    def tile(number, columns):
         lanes = tile_lanes(number)
         reduce(jnp.maximum(number - 1, 0))
         taps = [chunk_taps(wide_ref, number // TILES, member, number % TILES, count) for member in range(2)]
@@ -247,9 +256,13 @@
                     state = [factor * one + u for factor, one in zip(decay, state)]
         for mode in range(modes):
             last_scr[mode] = state[mode]
+
+    def two(number, _):
+        tile(2 * number, columns[:2])
+        tile(2 * number + 1, columns[2:])
         return 0
 
-    lax.fori_loop(0, tiles, tile, 0)
+    lax.fori_loop(0, tiles // 2, two, 0)
     reduce(tiles - 1)
 
 
@@ -263,13 +276,12 @@
     def some(chunk, _):
         for number in range(TILES):
             lanes = tile_lanes(chunk * TILES + number)
-            halo = halo_ref[:, lanes].astype(f32)
             parts = []
             for member in range(2):
                 taps = chunk_taps(wide_ref, chunk, member, number, reach + 1)
                 column = column_scr.at[number, member]
-                column[pl.ds(0, ROWS), :] = jnp.zeros((ROWS, LANES), f32)
-                column[pl.ds(ROWS, ROWS), :] = halo[member * ROWS : (member + 1) * ROWS]
+                column[pl.ds(0, 2 * ROWS), :] = jnp.zeros((2 * ROWS, LANES), f32)
+                lay_halo(column, halo_ref, member, lanes)
                 source = (key_ref, value_ref)[member]
                 column[pl.ds(2 * ROWS, ROWS), :] = source[: 2 * ROWS, lanes].astype(f32)[:ROWS]
                 parts += fir(column, taps, 2 * ROWS, 1)
@@ -295,24 +307,25 @@
 
 
 def gate_kernel(query_ref, halo_ref, feat_ref, u_ref, head_ref, rate_ref, coef_ref, skip_ref, gate_ref, *rest, early):
-    y_ref, mid_ref, halo_buf, gate_buf, wide_scr, column, small_sem, out_sem = rest[:8]
-    inner = rest[8:]
+    y_ref, mid_ref, halo_buf, u_buf, gate_buf, wide_scr, column, small_sem, out_sem = rest[:9]
+    inner = rest[9:]
     chunks, tokens = gate_buf.shape[:2]
     count = feat_ref.shape[2]
     halo_copy = pltpu.make_async_copy(halo_ref, halo_buf, small_sem.at[0])
     halo_copy.start()
+    u_copy = pltpu.make_async_copy(u_ref.at[:, pl.ds(0, early * CHUNK)], u_buf, small_sem.at[1])
+    u_copy.start()
     widened(feat_ref, 0, wide_scr, 0)
-    local_chunk, local_send = local_parts(u_ref, head_ref, rate_ref, coef_ref, skip_ref, y_ref, mid_ref, *inner)
-    over_chunks(0, early, local_chunk, local_send)
+    local_chunk, local_send = local_parts(u_buf, head_ref, rate_ref, coef_ref, skip_ref, y_ref, mid_ref, *inner)
     halo_copy.wait()
-    column[pl.ds(0, ROWS), :] = jnp.zeros((ROWS, LANES), f32)
+    column[pl.ds(0, 2 * ROWS), :] = jnp.zeros((2 * ROWS, LANES), f32)
 
     def chunk(at):
         def tile(number, _):
             lanes = tile_lanes(number)
             all_lanes = tile_lanes(at * TILES + number)
             taps = chunk_taps(wide_scr, at, 0, number, count)
-            column[pl.ds(ROWS, ROWS), :] = halo_buf[:, all_lanes].astype(f32)[2 * ROWS :]
+            lay_halo(column, halo_buf, 2, all_lanes)
             lay_column(column, query_ref, all_lanes)
             found = list(fir(column, taps, 2 * ROWS, tokens // ROWS))
             for pair in range(tokens // (2 * ROWS)):
@@ -324,6 +337,8 @@
 
     give = columns_out(gate_ref, gate_buf, out_sem)
     over_chunks(0, chunks, chunk, give)
+    u_copy.wait()
+    over_chunks(0, early, local_chunk, local_send)
     for at in range(early):
         wait_all(local_send(at))
     for at in range(chunks):
@@ -333,7 +348,7 @@
 def prefix_kernel(piece_ref, rate_ref, coef_ref, out_ref, *, tokens, axes):
     devices, piece_modes, piece_width = piece_ref.shape
     split = devices * piece_modes // rate_ref.shape[0]
-    mine = lax.axis_index(axes)
+    mine = devices - 1 - lax.axis_index(axes)
     mode, part = mine // split * piece_modes, mine % split
     group = pl.multiple_of(mode // ROWS * ROWS, ROWS)
     first = pl.multiple_of(part * piece_width, LANES)
@@ -352,7 +367,7 @@
 
     def lap(number, entering):
         for step in range(4):
-            source = number * 4 + step
+            source = devices - 1 - (number * 4 + step)
             out_ref[source] = (coef * entering).astype(out_ref.dtype)
             entering = through * entering + piece_ref[source].astype(f32)
         return entering
@@ -438,13 +453,13 @@
             power_scr[level] = through
             through = through * through
 
-        def tile(number, _):
+        def tile(number, lead_scr):
             lanes = tile_lanes(number)
             state = []
             for mode in range(modes):
                 rows = [wide(power_scr[level, mode : mode + 1, lanes]) for level in range(3)]
-                lead = rows[0]
-                for bit, row in zip(bits, rows):
+                lead = jnp.where(bits[0], rows[1], rows[0])
+                for bit, row in zip(bits[1:], rows[1:]):
                     lead = lead * jnp.where(bit, row, 1.0)
                 lead_scr[mode] = lead
                 state.append(lead * wide(total_scr[mode : mode + 1, tile_lanes(at * TILES + number)]))
@@ -463,9 +478,13 @@
                     sums.append(y_buf[at, here, lanes] + tree(state))
                     state = [factor * one for factor, one in zip(decay, state)]
                 out_buf[at, rows, lanes] = (gates * rounded(jnp.concatenate(sums, axis=0))).astype(bf16)
+
+        def two(number, _):
+            tile(2 * number, lead_scr.at[0])
+            tile(2 * number + 1, lead_scr.at[1])
             return 0
 
-        lax.fori_loop(0, TILES, tile, 0)
+        lax.fori_loop(0, TILES // 2, two, 0)
 
     give = columns_out(out_ref, out_buf, out_sem)
     over_chunks(0, chunks, with_fetch(chunks, fetch, chunk), give)
@@ -509,10 +528,11 @@
             **more,
         )(*inputs)
 
+    halo_shape = (members * (taps - 1) // 2, 2, width)
     (packed,) = call(
         pack_kernel,
         (key_proj, value_proj, query),
-        [near((members * ROWS, width), bf16)],
+        [near(halo_shape, bf16)],
         [vmem((members, 2 * ROWS, width), bf16), dma((members,))],
         "pack",
     )
@@ -525,7 +545,7 @@
         signal_kernel,
         (key_proj, value_proj, feat, rates),
         [near((tokens, width), bf16), near((chunks, 2, ROWS, CHUNK), f32), near((modes, width), f32)],
-        [vmem((4, modes, width), f32), vmem((modes, ROWS, LANES), f32), column, column],
+        [vmem((4, modes, width), f32), vmem((modes, ROWS, LANES), f32)] + [column] * 4,
         "signal",
         close=range(4),
         cost_estimate=cost(60 * elements, 10 * elements),
@@ -548,21 +568,22 @@
     local_shapes = [far((tokens, width), f32), far((chunks, modes, ROWS, LANES), f32)]
     local_scratches = [whole_buf, vmem((chunks, modes, ROWS, LANES), f32), stage, stage]
     local_scratches += [dma((1, chunks)), dma((chunks,))]
-    early = chunks // 3
+    early = chunks * 4 // 9
     gate, y, mid = call(
         functools.partial(gate_kernel, early=early),
         (query, halo_late, feat, u, head, rates, coef, skip_row),
         [far((tokens, width), bf16)] + local_shapes,
-        [vmem((members * ROWS, width), bf16), half_buf, vmem((chunks, 1, ROWS, CHUNK), f32), column]
-        + [dma((1,)), dma((1, chunks))]
+        [vmem(halo_shape, bf16), vmem((tokens, early * CHUNK), bf16), half_buf]
+        + [vmem((chunks, 1, ROWS, CHUNK), f32), column, dma((2,)), dma((1, chunks))]
         + local_scratches,
         "gate",
-        close=(0, 2, 3, 4, 5, 6, 7),
+        close=(0, 2, 4, 5, 6, 7),
         cost_estimate=cost(28 * elements, 6 * elements),
     )
 
     def swap(value):
-        return lax.all_to_all(value, axes, split_axis=0, concat_axis=0, tiled=True)
+        order = [list(range(devices))[::-1]]
+        return lax.all_to_all(value, axes, split_axis=0, concat_axis=0, axis_index_groups=order, tiled=True)
 
     share = modes * width // devices
     theirs = swap(left if even else left.reshape(devices, share))
@@ -577,13 +598,14 @@
             close=(0, 1, 2),
         )
     else:
-        mine = lax.axis_index(axes)
+        mine = devices - 1 - lax.axis_index(axes)
         through = jnp.exp(-float(tokens) * lax.dynamic_slice_in_dim(rates.reshape(-1), mine * share, share))
         factor = lax.dynamic_slice_in_dim(coef.reshape(-1), mine * share, share)
         _, entering = lax.scan(
             lambda so_far, piece: (through * so_far + piece.astype(f32), (factor * so_far).astype(bf16)),
             jnp.zeros((share,), f32),
             theirs,
+            reverse=True,
         )
 
     entering, y = lax.optimization_barrier((entering, y))
@@ -604,7 +626,7 @@
         (entered, rates, mid, y, gate),
         [far((tokens, width), bf16)],
         [vmem((chunks, modes, ROWS, LANES), f32), whole_buf, half_buf, half_buf]
-        + [vmem((modes, width), f32), vmem((4, modes, CHUNK), f32), vmem((modes, ROWS, LANES), f32)]
+        + [vmem((modes, width), f32), vmem((4, modes, CHUNK), f32), vmem((2, modes, ROWS, LANES), f32)]
         + [dma((2, chunks)), dma((chunks,)), dma((1, chunks))],
         "final",
         close=(0, 1),

time: 47.8 us -> 48.1 us (level)
  the two profiles are of different devices: /device:TPU:1 before, /device:TPU:0 now
where the time goes in v13:
time: 48.1 us; the launch traced here: 47.9 us
  Pallas kernels  27.5 us (57%)
  starting transfers between devices  13.7 us (28%)
  waiting for transfers between devices  6.09 us (13%)
    pallas_call x7, Pallas kernels, call(): pl.pallas_call(kernel, in_specs=[beside if at in close else there for at...  27.5 us
    all_to_all x2, starting transfers between devices, swap(): lax.all_to_all(value, axes, split_axis=0, concat_axis=0, axis_index_group...  8.86 us
    all_to_all x2, waiting for transfers between devices, swap(): lax.all_to_all(value, axes, split_axis=0, concat_axis=0, axis_index_group...  6.09 us
    ppermute x1, starting transfers between devices, local(): lax.ppermute(packed, axes, [(at, at + 1) for at in range(devices - 1)])  4.85 us
  transfers between devices with their start and end apart: 3, of which 2 were waited for; matrix products, arithmetic and copies ran while one was open for 1% of the time, Pallas kernels for 37%

profile of v13, /device:TPU:0, one launch (start us, length us, event | category | flops | bytes accessed | tf_op | source)
XLA Modules:
  0.0 47.9 jit_solution(12108905125593716170)
XLA Ops:
  0.0 1.3 %pack.1 = bf16[9,2,4608]{2,1,0:T(2,128)(2,1)S(1)} custom-call(bf16[128,4608]{1,0:T(8,128)(2,1)} %key_ref.5, bf16[128,4608]{1,0:T(8,128)(2,1)} %value_ref.5, bf16[128,4608]{1,0:T(8,128)(2,1)} %query_ref.3), custom_call_target="tpu_custom_call" | custom-call | tf_op jit(solution)/shard_map/pack/pallas_call | solution.py:520
  1.3 4.9 %collective-permute-start = (bf16[9,2,4608]{2,1,0:T(2,128)(2,1)S(1)}, bf16[9,2,4608]{2,1,0:T(2,128)(2,1)S(1)}, u32[]{:S(2)}, u32[]{:S(2)}) collective-permute-start(bf16[9,2,4608]{2,1,0:T(2,128)(2,1)S(1)} %pack.1), channel_id=1, source_target_pairs={{0,1},{1,2},{2,3},{3,4},{4,5},{5,6},{6,7},{7,8},{8,9},{9,10},{10,1... | collective-permute-start | bytes 497672 | tf_op jit(solution)/shard_map/ppermute | solution.py:539
  6.1 0.0 copy-done.7
  6.2 0.1 reshape.3
  6.3 0.0 copy-done.2
  6.3 0.0 copy-done.1
  6.3 6.8 %signal.1 = (bf16[128,4608]{1,0:T(8,128)(2,1)S(1)}, f32[9,2,8,512]{3,2,1,0:T(8,128)S(1)}, f32[16,4608]{1,0:T(8,128)S(1)}) custom-call(bf16[128,4608]{1,0:T(8,128)(2,1)S(1)} %copy-done.1, bf16[128,4608]{1,0:T(8,128)(2,1)S(1)} %copy-done.2, f32[9,3,7,32]{3,2,1,0:T(8,128)S(1)} %bitcast.3, f32[16,4608]{1,0:T(8,128)S(1)} %copy-done), custom_call_target="tpu_custom_call" | custom-call | flops 35389440 | bytes 5898240 | tf_op jit(solution)/shard_map/signal/pallas_call | solution.py:520
  13.1 0.0 collective-permute-done.halo_ref
  13.1 0.0 copy-start.6
  13.2 0.0 copy-start.8
  13.2 1.7 %head.1 = (bf16[32,2,1152]{2,1,0:T(2,128)(2,1)}, bf16[16,4608]{1,0:T(8,128)(2,1)S(1)}, bf16[128,4608]{1,0:T(8,128)(2,1)}) custom-call(bf16[128,4608]{1,0:T(8,128)(2,1)S(1)} %copy-done.1, bf16[128,4608]{1,0:T(8,128)(2,1)S(1)} %copy-done.2, bf16[9,2,4608]{2,1,0:T(2,128)(2,1)S(1)} %collective-permute-done.halo_ref, f32[16,4608]{1,0:T(8,128)S(1)} %copy-done, ...), custom_call_target="tpu_custom_call" | custom-call | tf_op jit(solution)/shard_map/head/pallas_call | solution.py:520
  14.9 0.0 copy-start.3
  14.9 4.9 %all-to-all-start = ((bf16[32,2,1152]{2,1,0:T(2,128)(2,1)}), bf16[32,2,1152]{2,1,0:T(2,128)(2,1)S(1)}, u32[]{:S(2)}, u32[]{:S(2)}) async-start(bf16[32,2,1152]{2,1,0:T(2,128)(2,1)} %get-tuple-element.32), calls=%async_computation | async-start | bytes 294912 | tf_op jit(solution)/shard_map/all_to_all | solution.py:586
  19.8 0.0 copy-done.6
  19.8 0.2 sqrt_multiply_fusion.coef_ref
  20.0 0.0 copy-done.8
  20.1 6.4 %gate.1 = (bf16[128,4608]{1,0:T(8,128)(2,1)}, f32[128,4608]{1,0:T(8,128)}, f32[9,16,8,128]{3,2,1,0:T(8,128)}) custom-call(bf16[128,4608]{1,0:T(8,128)(2,1)S(1)} %copy-done.3, bf16[9,2,4608]{2,1,0:T(2,128)(2,1)} %copy-done.5, f32[9,3,7,32]{3,2,1,0:T(8,128)S(1)} %bitcast.4, bf16[128,4608]{1,0:T(8,128)(2,1)} %get-tuple-element.34.u_ref, ...), custom_call_target="tpu_custom_call" | custom-call | flops 16515072 | bytes 3538944 | tf_op jit(solution)/shard_map/gate/pallas_call | solution.py:520
  26.5 0.0 copy-start.4
  26.5 1.9 %all-to-all-done.piece_ref = bf16[32,2,1152]{2,1,0:T(2,128)(2,1)S(1)} async-done(((bf16[32,2,1152]{2,1,0:T(2,128)(2,1)}), bf16[32,2,1152]{2,1,0:T(2,128)(2,1)S(1)}, u32[]{:S(2)}, u32[]{:S(2)}) %all-to-all-start) | async-done | bytes 147488 | tf_op jit(solution)/shard_map/all_to_all | solution.py:586
  28.4 1.0 %prefix.1 = bf16[32,2,1152]{2,1,0:T(2,128)(2,1)} custom-call(bf16[32,2,1152]{2,1,0:T(2,128)(2,1)S(1)} %all-to-all-done.piece_ref, f32[16,4608]{1,0:T(8,128)S(1)} %copy-done, f32[16,4608]{1,0:T(8,128)S(1)} %sqrt_multiply_fusion.coef_ref), custom_call_target="tpu_custom_call" | custom-call | tf_op jit(solution)/shard_map/prefix/pallas_call | solution.py:520
  29.4 3.9 %all-to-all-start.1 = ((bf16[32,2,1152]{2,1,0:T(2,128)(2,1)}), bf16[32,2,1152]{2,1,0:T(2,128)(2,1)S(1)}, u32[]{:S(2)}, u32[]{:S(2)}) async-start(bf16[32,2,1152]{2,1,0:T(2,128)(2,1)} %prefix.1), calls=%async_computation.1 | async-start | bytes 294912 | tf_op jit(solution)/shard_map/all_to_all | solution.py:586
  33.3 4.4 %within.1 = (f32[128,4608]{1,0:T(8,128)}, f32[9,16,8,128]{3,2,1,0:T(8,128)}) custom-call(bf16[128,4608]{1,0:T(8,128)(2,1)S(1)} %copy-done.4, bf16[16,4608]{1,0:T(8,128)(2,1)S(1)} %get-tuple-element.35.head_ref, f32[16,4608]{1,0:T(8,128)S(1)} %copy-done, f32[16,4608]{1,0:T(8,128)S(1)} %sqrt_multiply_fusion.coef_ref, ...), custom_call_target="tpu_custom_call", output_to_operand_aliasing={{0}: (5, {}), {1}: (6, {})} | custom-call | flops 29491200 | bytes 4718592 | tf_op jit(solution)/shard_map/within/pallas_call | solution.py:520
  37.7 4.2 %all-to-all-done.1.piece_ref = bf16[32,2,1152]{2,1,0:T(2,128)(2,1)S(1)} async-done(((bf16[32,2,1152]{2,1,0:T(2,128)(2,1)}), bf16[32,2,1152]{2,1,0:T(2,128)(2,1)S(1)}, u32[]{:S(2)}, u32[]{:S(2)}) %all-to-all-start.1) | async-done | bytes 147488 | tf_op jit(solution)/shard_map/all_to_all | solution.py:586
  41.9 5.9 %final.1 = bf16[128,4608]{1,0:T(8,128)(2,1)} custom-call(bf16[32,2,1152]{2,1,0:T(2,128)(2,1)S(1)} %all-to-all-done.1.piece_ref, f32[16,4608]{1,0:T(8,128)S(1)} %copy-done, f32[9,16,8,128]{3,2,1,0:T(8,128)} %get-tuple-element.48.mid_ref, f32[128,4608]{1,0:T(8,128)} %get-tuple-element.49.y_ref, bf16[128,4608]{1,0:T(8,128)(2,1)} %get-tuple-element.50.gate_ref), custom_call_target="tpu_custom_call" | custom-call | flops 23592960 | bytes 5898240 | tf_op jit(solution)/shard_map/final/pallas_call | solution.py:520
  (11 shorter events, 0.1 us)
Async XLA Ops:
  0.0 6.3 %copy-start.2 = (bf16[128,4608]{1,0:T(8,128)(2,1)S(1)}, bf16[128,4608]{1,0:T(8,128)(2,1)}, u32[]{:S(2)}) copy-start(bf16[128,4608]{1,0:T(8,128)(2,1)} %value_ref.5) | copy-start | bytes 3538948
  0.0 6.3 %copy-start.1 = (bf16[128,4608]{1,0:T(8,128)(2,1)S(1)}, bf16[128,4608]{1,0:T(8,128)(2,1)}, u32[]{:S(2)}) copy-start(bf16[128,4608]{1,0:T(8,128)(2,1)} %key_ref.5) | copy-start | bytes 3538948
  0.0 6.1 %copy-start.7 = (f32[3,7,288]{2,1,0:T(8,128)S(1)}, f32[3,7,288]{2,1,0:T(8,128)}, u32[]{:S(2)}) copy-start(f32[3,7,288]{2,1,0:T(8,128)} %param.10) | copy-start | bytes 72580
  0.0 6.3 %copy-start = (f32[16,4608]{1,0:T(8,128)S(1)}, f32[16,4608]{1,0:T(8,128)}, u32[]{:S(2)}) copy-start(f32[16,4608]{1,0:T(8,128)} %rate_ref.11) | copy-start | bytes 884740
  1.3 11.8 %collective-permute-start = (bf16[9,2,4608]{2,1,0:T(2,128)(2,1)S(1)}, bf16[9,2,4608]{2,1,0:T(2,128)(2,1)S(1)}, u32[]{:S(2)}, u32[]{:S(2)}) collective-permute-start(bf16[9,2,4608]{2,1,0:T(2,128)(2,1)S(1)} %pack.1), channel_id=1, source_target_pairs={{0,1},{1,2},{2,3},{3,4},{4,5},{5,6},{6,7},{7,8},{8,9},{9,10},{10,1... | collective-permute-start | bytes 497672 | tf_op jit(solution)/shard_map/ppermute | solution.py:539
  13.1 1.7 %copy-start.5 = (bf16[9,2,4608]{2,1,0:T(2,128)(2,1)}, bf16[9,2,4608]{2,1,0:T(2,128)(2,1)S(1)}, u32[]{:S(2)}) copy-start(bf16[9,2,4608]{2,1,0:T(2,128)(2,1)S(1)} %collective-permute-done.halo_ref) | copy-start | bytes 497668
  13.1 6.7 %copy-start.6 = (f32[16,4608]{1,0:T(8,128)S(1)}, f32[16,4608]{1,0:T(8,128)}, u32[]{:S(2)}) copy-start(f32[16,4608]{1,0:T(8,128)} %param.12) | copy-start | bytes 884740
  13.2 6.9 %copy-start.8 = (f32[4608]{0:T(1024)S(1)}, f32[4608]{0:T(1024)}, u32[]{:S(2)}) copy-start(f32[4608]{0:T(1024)} %param.13) | copy-start | bytes 55300
  14.9 5.2 %copy-start.3 = (bf16[128,4608]{1,0:T(8,128)(2,1)S(1)}, bf16[128,4608]{1,0:T(8,128)(2,1)}, u32[]{:S(2)}) copy-start(bf16[128,4608]{1,0:T(8,128)(2,1)} %query_ref.3) | copy-start | bytes 3538948
  14.9 13.5 %all-to-all-start = ((bf16[32,2,1152]{2,1,0:T(2,128)(2,1)}), bf16[32,2,1152]{2,1,0:T(2,128)(2,1)S(1)}, u32[]{:S(2)}, u32[]{:S(2)}) async-start(bf16[32,2,1152]{2,1,0:T(2,128)(2,1)} %get-tuple-element.32), calls=%async_computation | async-start | bytes 294912 | tf_op jit(solution)/shard_map/all_to_all | solution.py:586
  26.5 6.9 %copy-start.4 = (bf16[128,4608]{1,0:T(8,128)(2,1)S(1)}, bf16[128,4608]{1,0:T(8,128)(2,1)}, u32[]{:S(2)}) copy-start(bf16[128,4608]{1,0:T(8,128)(2,1)} %get-tuple-element.34.u_ref) | copy-start | bytes 3538948
  29.4 12.5 %all-to-all-start.1 = ((bf16[32,2,1152]{2,1,0:T(2,128)(2,1)}), bf16[32,2,1152]{2,1,0:T(2,128)(2,1)S(1)}, u32[]{:S(2)}, u32[]{:S(2)}) async-start(bf16[32,2,1152]{2,1,0:T(2,128)(2,1)} %prefix.1), calls=%async_computation.1 | async-start | bytes 294912 | tf_op jit(solution)/shard_map/all_to_all | solution.py:586

commit v14 on v13

--- a/solution.py
+++ b/solution.py
@@ -13,6 +13,7 @@
 TILES = 4
 CHUNK = TILES * LANES
 AHEAD = 4
+LAP = 4
 f32 = jnp.float32
 bf16 = jnp.bfloat16
 
@@ -39,6 +40,10 @@
 
 def wide(row):
     return jnp.broadcast_to(row, (ROWS, LANES))
+
+
+def first_half():
+    return lax.broadcasted_iota(jnp.int32, (ROWS, LANES), 0) < TILES
 
 
 def sublane():
@@ -104,8 +109,9 @@
 
 
 def widened(feat_ref, member, out_ref, position):
-    chunks, _, taps, count = feat_ref.shape
-    rows = [feat_ref[at, member] for at in range(chunks)]
+    chunks, taps = out_ref.shape[0], feat_ref.shape[1]
+    count = feat_ref.shape[2] // chunks
+    rows = [feat_ref[member, :, at * count : (at + 1) * count] for at in range(chunks)]
     rows = [jnp.concatenate([row, jnp.zeros((ROWS - taps, count), f32)], axis=0) for row in rows]
     group = lax.broadcasted_iota(jnp.int32, (count, CHUNK), 0)
     lane = lax.broadcasted_iota(jnp.int32, (count, CHUNK), 1)
@@ -209,7 +215,7 @@
     tokens, tiles = u_ref.shape[0], u_ref.shape[1] // LANES
     modes = rate_ref.shape[0]
     chunks = tiles // TILES
-    count = feat_ref.shape[2]
+    count = feat_ref.shape[1]
     for member in range(2):
         widened(feat_ref, member + 1, wide_ref, member)
     for column in columns:
@@ -257,12 +263,12 @@
         for mode in range(modes):
             last_scr[mode] = state[mode]
 
-    def two(number, _):
-        tile(2 * number, columns[:2])
-        tile(2 * number + 1, columns[2:])
+    def some(number, _):
+        for part in range(TILES):
+            tile(TILES * number + part, columns[2 * part : 2 * part + 2])
         return 0
 
-    lax.fori_loop(0, tiles // 2, two, 0)
+    lax.fori_loop(0, tiles // TILES, some, 0)
     reduce(tiles - 1)
 
 
@@ -307,16 +313,16 @@
 
 
 def gate_kernel(query_ref, halo_ref, feat_ref, u_ref, head_ref, rate_ref, coef_ref, skip_ref, gate_ref, *rest, early):
-    y_ref, mid_ref, halo_buf, u_buf, gate_buf, wide_scr, column, small_sem, out_sem = rest[:9]
-    inner = rest[9:]
+    y_ref, halo_buf, u_buf, gate_buf, wide_scr, column, small_sem, out_sem = rest[:8]
+    inner = rest[8:]
     chunks, tokens = gate_buf.shape[:2]
-    count = feat_ref.shape[2]
+    count = feat_ref.shape[1]
     halo_copy = pltpu.make_async_copy(halo_ref, halo_buf, small_sem.at[0])
     halo_copy.start()
     u_copy = pltpu.make_async_copy(u_ref.at[:, pl.ds(0, early * CHUNK)], u_buf, small_sem.at[1])
     u_copy.start()
     widened(feat_ref, 0, wide_scr, 0)
-    local_chunk, local_send = local_parts(u_buf, head_ref, rate_ref, coef_ref, skip_ref, y_ref, mid_ref, *inner)
+    local_chunk, local_send = local_parts(u_buf, head_ref, rate_ref, coef_ref, skip_ref, y_ref, *inner)
     halo_copy.wait()
     column[pl.ds(0, 2 * ROWS), :] = jnp.zeros((2 * ROWS, LANES), f32)
 
@@ -376,21 +382,18 @@
 
 
 def local_kernel(u_ref, head_ref, rate_ref, coef_ref, skip_ref, *rest, first, last):
-    chunk, send = local_parts(u_ref, head_ref, rate_ref, coef_ref, skip_ref, *rest[-8:])
+    chunk, send = local_parts(u_ref, head_ref, rate_ref, coef_ref, skip_ref, *rest[-5:])
     over_chunks(first, last, chunk, send)
     for at in range(first, last):
         wait_all(send(at))
 
 
-def local_parts(u_ref, head_ref, rate_ref, coef_ref, skip_ref, y_ref, mid_ref, *scratches):
-    y_buf, mid_buf, token_scr, sum_scr, out_sem, mid_sem = scratches
+def local_parts(u_ref, head_ref, rate_ref, coef_ref, skip_ref, y_ref, *scratches):
+    y_buf, token_scr, sum_scr, out_sem = scratches
     tokens = u_ref.shape[0]
     modes = rate_ref.shape[0]
     half_groups = tokens // ROWS // 2
-    give = columns_out(y_ref, y_buf, out_sem)
-
-    def send(at):
-        return give(at) + [pltpu.make_async_copy(mid_buf.at[at], mid_ref.at[at], mid_sem.at[at])]
+    top = first_half()
 
     def chunk(at):
         for pair in range(half_groups):
@@ -417,8 +420,18 @@
             return tuple(state)
 
         state = lax.fori_loop(0, half_groups, eight, (jnp.zeros((ROWS, LANES), f32),) * modes)
-        for mode, (factor, one) in enumerate(zip(coef, state)):
-            mid_buf[at, mode] = factor * one
+        carried = tuple(
+            jnp.where(top, 0.0, pltpu.roll(factor * one, TILES, 0)) for factor, one in zip(coef, state)
+        )
+
+        def eight_more(group, carried):
+            for row in range(ROWS):
+                carried = [factor * one for factor, one in zip(decay, carried)]
+                place = pl.ds(group * ROWS * ROWS + row, ROWS, stride=ROWS)
+                sum_scr[place, :] = sum_scr[place, :] + tree(carried)
+            return tuple(carried)
+
+        lax.fori_loop(0, half_groups, eight_more, carried)
         for group in range(2 * half_groups):
             half, within = group // half_groups, group % half_groups
             for tile in range(TILES):
@@ -426,26 +439,22 @@
                 rows = slice(group * ROWS, (group + 1) * ROWS)
                 y_buf[at, rows, tile * LANES : (tile + 1) * LANES] = sum_scr[pl.ds(slot, ROWS), :]
 
-    return chunk, send
-
-
-def final_kernel(piece_ref, rate_ref, mid_ref, y_ref, gate_ref, out_ref, *scratches):
-    mid_buf, y_buf, gate_buf, out_buf, total_scr, power_scr, lead_scr, in_sem, mid_sem, out_sem = scratches
-    chunks, modes = mid_buf.shape[:2]
-    tokens = y_buf.shape[1]
-    columns = columns_in(((y_ref, y_buf), (gate_ref, gate_buf)), in_sem)
-
-    def fetch(at):
-        return columns(at) + [pltpu.make_async_copy(mid_ref.at[at], mid_buf.at[at], mid_sem.at[at])]
-
-    begin(chunks, fetch)
-    pieces, piece_modes, piece_width = piece_ref.shape
-    split = pieces * piece_modes // modes
-    for piece in range(pieces):
-        first, part = piece // split * piece_modes, piece % split
-        lanes = slice(part * piece_width, (part + 1) * piece_width)
-        total_scr[first : first + piece_modes, lanes] = piece_ref[piece].astype(f32)
+    return chunk, columns_out(y_ref, y_buf, out_sem)
+
+
+def final_kernel(piece_ref, rate_ref, y_ref, gate_ref, out_ref, *scratches, axes):
+    y_buf, gate_buf, out_buf, total_scr, power_scr, in_sem, out_sem = scratches
+    chunks, tokens = y_buf.shape[:2]
+    modes = rate_ref.shape[0]
+    fetch = columns_in(((y_ref, y_buf), (gate_ref, gate_buf)), in_sem)
+    give = columns_out(out_ref, out_buf, out_sem)
+    start_all(fetch(0))
     bits = [(sublane() >> level) % 2 == 1 for level in range(3)]
+    pairs = [slice(first, first + 2 * ROWS) for first in range(0, tokens, 2 * ROWS)]
+
+    def finish(at, rows, lanes, sums):
+        gates = gate_buf[at, rows, lanes].astype(f32)
+        out_buf[at, rows, lanes] = (gates * rounded(sums)).astype(bf16)
 
     def chunk(at):
         through = jnp.exp(-rate_ref[:, span(at)])
@@ -453,7 +462,7 @@
             power_scr[level] = through
             through = through * through
 
-        def tile(number, lead_scr):
+        def tile(number):
             lanes = tile_lanes(number)
             state = []
             for mode in range(modes):
@@ -461,33 +470,53 @@
                 lead = jnp.where(bits[0], rows[1], rows[0])
                 for bit, row in zip(bits[1:], rows[1:]):
                     lead = lead * jnp.where(bit, row, 1.0)
-                lead_scr[mode] = lead
                 state.append(lead * wide(total_scr[mode : mode + 1, tile_lanes(at * TILES + number)]))
             decay = [wide(power_scr[3, mode : mode + 1, lanes]) for mode in range(modes)]
-            for pair in range(tokens // (2 * ROWS)):
-                rows = slice(pair * 2 * ROWS, (pair + 1) * 2 * ROWS)
-                gates = gate_buf[at, rows, lanes].astype(f32)
+            for rows in pairs:
                 sums = []
-                for part in range(2):
-                    if pair == tokens // (4 * ROWS) and part == 0:
-                        state = [
-                            one + lead_scr[mode] * wide(mid_buf[at, mode, pl.ds(number, 1), :])
-                            for mode, one in enumerate(state)
-                        ]
-                    here = slice((pair * 2 + part) * ROWS, (pair * 2 + part + 1) * ROWS)
-                    sums.append(y_buf[at, here, lanes] + tree(state))
+                for first in (rows.start, rows.start + ROWS):
+                    sums.append(y_buf[at, first : first + ROWS, lanes] + tree(state))
                     state = [factor * one for factor, one in zip(decay, state)]
-                out_buf[at, rows, lanes] = (gates * rounded(jnp.concatenate(sums, axis=0))).astype(bf16)
-
-        def two(number, _):
-            tile(2 * number, lead_scr.at[0])
-            tile(2 * number + 1, lead_scr.at[1])
+                finish(at, rows, lanes, jnp.concatenate(sums, axis=0))
+
+        def some(number, _):
+            for part in range(LAP):
+                tile(number * LAP + part)
             return 0
 
-        lax.fori_loop(0, TILES // 2, two, 0)
-
-    give = columns_out(out_ref, out_buf, out_sem)
-    over_chunks(0, chunks, with_fetch(chunks, fetch, chunk), give)
+        lax.fori_loop(0, TILES // LAP, some, 0)
+
+    def chunk_alone(at):
+        def tile(number, _):
+            lanes = tile_lanes(number)
+            for rows in pairs:
+                finish(at, rows, lanes, y_buf[at, rows, lanes])
+            return 0
+
+        lax.fori_loop(0, TILES, tile, 0)
+
+    def begin_others():
+        for at in range(1, min(AHEAD, chunks)):
+            start_all(fetch(at))
+
+    first = lax.axis_index(axes) == 0
+
+    @pl.when(first)
+    def _():
+        begin_others()
+        over_chunks(0, chunks, with_fetch(chunks, fetch, chunk_alone), give)
+
+    @pl.when(jnp.logical_not(first))
+    def _():
+        pieces, piece_modes, piece_width = piece_ref.shape
+        split = pieces * piece_modes // modes
+        for piece in range(pieces):
+            row, part = piece // split * piece_modes, piece % split
+            lanes = slice(part * piece_width, (part + 1) * piece_width)
+            total_scr[row : row + piece_modes, lanes] = piece_ref[piece].astype(f32)
+        begin_others()
+        over_chunks(0, chunks, with_fetch(chunks, fetch, chunk), give)
+
     for at in range(chunks):
         wait_all(give(at))
 
@@ -538,14 +567,13 @@
     )
     halo = lax.ppermute(packed, axes, [(at, at + 1) for at in range(devices - 1)])
 
-    feat = featurizer.reshape(members, taps, chunks, groups // chunks).transpose(2, 0, 1, 3)
     column = vmem((2 * ROWS + tokens, LANES), f32)
     half_buf, whole_buf = vmem((chunks, tokens, CHUNK), bf16), vmem((chunks, tokens, CHUNK), f32)
     u, wide_taps, state = call(
         signal_kernel,
-        (key_proj, value_proj, feat, rates),
+        (key_proj, value_proj, featurizer, rates),
         [near((tokens, width), bf16), near((chunks, 2, ROWS, CHUNK), f32), near((modes, width), f32)],
-        [vmem((4, modes, width), f32), vmem((modes, ROWS, LANES), f32)] + [column] * 4,
+        [vmem((4, modes, width), f32), vmem((modes, ROWS, LANES), f32)] + [column] * (2 * TILES),
         "signal",
         close=range(4),
         cost_estimate=cost(60 * elements, 10 * elements),
@@ -565,13 +593,12 @@
     coef = residues * jnp.sqrt(-jnp.expm1(-2.0 * rates_late) / modes)
     skip_row = skip_late[None, :]
     stage = vmem((tokens // ROWS // 2 * ROWS * ROWS, LANES), f32)
-    local_shapes = [far((tokens, width), f32), far((chunks, modes, ROWS, LANES), f32)]
-    local_scratches = [whole_buf, vmem((chunks, modes, ROWS, LANES), f32), stage, stage]
-    local_scratches += [dma((1, chunks)), dma((chunks,))]
+    local_shapes = [far((tokens, width), f32)]
+    local_scratches = [whole_buf, stage, stage, dma((1, chunks))]
     early = chunks * 4 // 9
-    gate, y, mid = call(
+    gate, y = call(
         functools.partial(gate_kernel, early=early),
-        (query, halo_late, feat, u, head, rates, coef, skip_row),
+        (query, halo_late, featurizer, u, head, rates, coef, skip_row),
         [far((tokens, width), bf16)] + local_shapes,
         [vmem(halo_shape, bf16), vmem((tokens, early * CHUNK), bf16), half_buf]
         + [vmem((chunks, 1, ROWS, CHUNK), f32), column, dma((2,)), dma((1, chunks))]
@@ -587,7 +614,7 @@
 
     share = modes * width // devices
     theirs = swap(left if even else left.reshape(devices, share))
-    theirs, gate, coef, skip_row, y, mid = lax.optimization_barrier((theirs, gate, coef, skip_row, y, mid))
+    theirs, gate, coef, skip_row, y = lax.optimization_barrier((theirs, gate, coef, skip_row, y))
     if even:
         (entering,) = call(
             functools.partial(prefix_kernel, tokens=tokens, axes=axes),
@@ -610,24 +637,23 @@
 
     entering, y = lax.optimization_barrier((entering, y))
     entered = swap(entering).reshape(pieces)
-    y, mid = call(
+    (y,) = call(
         functools.partial(local_kernel, first=early, last=chunks),
-        (u, head, rates, coef, skip_row, y, mid),
+        (u, head, rates, coef, skip_row, y),
         local_shapes,
         local_scratches,
         "within",
         close=range(5),
         cost_estimate=cost(50 * elements, 8 * elements),
-        input_output_aliases={5: 0, 6: 1},
+        input_output_aliases={5: 0},
     )
 
     (out,) = call(
-        final_kernel,
-        (entered, rates, mid, y, gate),
+        functools.partial(final_kernel, axes=axes),
+        (entered, rates, y, gate),
         [far((tokens, width), bf16)],
-        [vmem((chunks, modes, ROWS, LANES), f32), whole_buf, half_buf, half_buf]
-        + [vmem((modes, width), f32), vmem((4, modes, CHUNK), f32), vmem((2, modes, ROWS, LANES), f32)]
-        + [dma((2, chunks)), dma((chunks,)), dma((1, chunks))],
+        [whole_buf, half_buf, half_buf, vmem((modes, width), f32), vmem((4, modes, CHUNK), f32)]
+        + [dma((2, chunks)), dma((1, chunks))],
         "final",
         close=(0, 1),
         cost_estimate=cost(40 * elements, 10 * elements),

time: 48.1 us -> 47.9 us (level)
  the two profiles are of different devices: /device:TPU:0 before, /device:TPU:1 now
where the time goes in v14:
time: 47.9 us; the launch traced here: 47.5 us
  Pallas kernels  29.6 us (62%)
  starting transfers between devices  14.2 us (30%)
  waiting for transfers between devices  3.31 us (7%)
    pallas_call x7, Pallas kernels, call(): pl.pallas_call(kernel, in_specs=[beside if at in close else there for at...  29.6 us
    all_to_all x2, starting transfers between devices, swap(): lax.all_to_all(value, axes, split_axis=0, concat_axis=0, axis_index_group...  10.3 us
    ppermute x1, starting transfers between devices, local(): lax.ppermute(packed, axes, [(at, at + 1) for at in range(devices - 1)])  3.95 us
    all_to_all x2, waiting for transfers between devices, swap(): lax.all_to_all(value, axes, split_axis=0, concat_axis=0, axis_index_group...  2.26 us
    ppermute x1, waiting for transfers between devices, local(): lax.ppermute(packed, axes, [(at, at + 1) for at in range(devices - 1)])  1.05 us
  transfers between devices with their start and end apart: 3, of which 3 were waited for; matrix products, arithmetic and copies ran while one was open for 0% of the time, Pallas kernels for 43%

profile of v14, /device:TPU:1, one launch (start us, length us, event | category | flops | bytes accessed | tf_op | source)
XLA Modules:
  0.0 47.5 jit_solution(2642662090541981307)
XLA Ops:
  0.0 0.0 copy-start.6
  0.0 1.3 %pack.1 = bf16[9,2,4608]{2,1,0:T(2,128)(2,1)S(1)} custom-call(bf16[128,4608]{1,0:T(8,128)(2,1)} %key_ref.5, bf16[128,4608]{1,0:T(8,128)(2,1)} %value_ref.5, bf16[128,4608]{1,0:T(8,128)(2,1)} %query_ref.3), custom_call_target="tpu_custom_call" | custom-call | tf_op jit(solution)/shard_map/pack/pallas_call | solution.py:549
  1.3 3.9 %collective-permute-start = (bf16[9,2,4608]{2,1,0:T(2,128)(2,1)S(1)}, bf16[9,2,4608]{2,1,0:T(2,128)(2,1)S(1)}, u32[]{:S(2)}, u32[]{:S(2)}) collective-permute-start(bf16[9,2,4608]{2,1,0:T(2,128)(2,1)S(1)} %pack.1), channel_id=1, source_target_pairs={{0,1},{1,2},{2,3},{3,4},{4,5},{5,6},{6,7},{7,8},{8,9},{9,10},{10,1... | collective-permute-start | bytes 497672 | tf_op jit(solution)/shard_map/ppermute | solution.py:568
  5.2 0.0 copy-done.2
  5.2 0.0 copy-done.1
  5.3 0.0 copy-done
  5.3 0.0 copy-done.6
  5.3 6.8 %signal.1 = (bf16[128,4608]{1,0:T(8,128)(2,1)S(1)}, f32[9,2,8,512]{3,2,1,0:T(8,128)S(1)}, f32[16,4608]{1,0:T(8,128)S(1)}) custom-call(bf16[128,4608]{1,0:T(8,128)(2,1)S(1)} %copy-done.1, bf16[128,4608]{1,0:T(8,128)(2,1)S(1)} %copy-done.2, f32[3,7,288]{2,1,0:T(8,128)S(1)} %copy-done.6, f32[16,4608]{1,0:T(8,128)S(1)} %copy-done), custom_call_target="tpu_custom_call" | custom-call | flops 35389440 | bytes 5898240 | tf_op jit(solution)/shard_map/signal/pallas_call | solution.py:549
  12.1 1.1 %collective-permute-done.halo_ref = bf16[9,2,4608]{2,1,0:T(2,128)(2,1)S(1)} collective-permute-done((bf16[9,2,4608]{2,1,0:T(2,128)(2,1)S(1)}, bf16[9,2,4608]{2,1,0:T(2,128)(2,1)S(1)}, u32[]{:S(2)}, u32[]{:S(2)}) %collective-permute-start) | collective-permute-done | bytes 165920 | tf_op jit(solution)/shard_map/ppermute | solution.py:568
  13.1 1.7 %head.1 = (bf16[32,2,1152]{2,1,0:T(2,128)(2,1)}, bf16[16,4608]{1,0:T(8,128)(2,1)S(1)}, bf16[128,4608]{1,0:T(8,128)(2,1)}) custom-call(bf16[128,4608]{1,0:T(8,128)(2,1)S(1)} %copy-done.1, bf16[128,4608]{1,0:T(8,128)(2,1)S(1)} %copy-done.2, bf16[9,2,4608]{2,1,0:T(2,128)(2,1)S(1)} %collective-permute-done.halo_ref, f32[16,4608]{1,0:T(8,128)S(1)} %copy-done, ...), custom_call_target="tpu_custom_call" | custom-call | tf_op jit(solution)/shard_map/head/pallas_call | solution.py:549
  14.8 0.0 copy-done.5
  14.8 0.0 copy-start.3
  14.9 4.6 %all-to-all-start = ((bf16[32,2,1152]{2,1,0:T(2,128)(2,1)}), bf16[32,2,1152]{2,1,0:T(2,128)(2,1)S(1)}, u32[]{:S(2)}, u32[]{:S(2)}) async-start(bf16[32,2,1152]{2,1,0:T(2,128)(2,1)} %get-tuple-element.28), calls=%async_computation | async-start | bytes 294912 | tf_op jit(solution)/shard_map/all_to_all | solution.py:613
  19.5 0.0 copy-done.7
  19.5 0.2 sqrt_multiply_fusion.coef_ref
  19.7 0.0 copy-done.8
  19.7 7.6 %gate.1 = (bf16[128,4608]{1,0:T(8,128)(2,1)}, f32[128,4608]{1,0:T(8,128)}) custom-call(bf16[128,4608]{1,0:T(8,128)(2,1)S(1)} %copy-done.3, bf16[9,2,4608]{2,1,0:T(2,128)(2,1)} %copy-done.5, f32[3,7,288]{2,1,0:T(8,128)S(1)} %copy-done.6, bf16[128,4608]{1,0:T(8,128)(2,1)} %get-tuple-element.30.u_ref, bf16[16,4608]{1,0:T(8,128)(2,1)S(1)} %get-tuple-element.31.head_ref, ...), custom_call_target="tpu_custom_call" | custom-call | flops 16515072 | bytes 3538944 | tf_op jit(solution)/shard_map/gate/pallas_call | solution.py:549
  27.3 0.0 copy-start.4
  27.3 0.2 all-to-all-done.piece_ref
  27.5 1.0 %prefix.1 = bf16[32,2,1152]{2,1,0:T(2,128)(2,1)} custom-call(bf16[32,2,1152]{2,1,0:T(2,128)(2,1)S(1)} %all-to-all-done.piece_ref, f32[16,4608]{1,0:T(8,128)S(1)} %copy-done, f32[16,4608]{1,0:T(8,128)S(1)} %sqrt_multiply_fusion.coef_ref), custom_call_target="tpu_custom_call" | custom-call | tf_op jit(solution)/shard_map/prefix/pallas_call | solution.py:549
  28.5 5.6 %all-to-all-start.1 = ((bf16[32,2,1152]{2,1,0:T(2,128)(2,1)}), bf16[32,2,1152]{2,1,0:T(2,128)(2,1)S(1)}, u32[]{:S(2)}, u32[]{:S(2)}) async-start(bf16[32,2,1152]{2,1,0:T(2,128)(2,1)} %prefix.1), calls=%async_computation.1 | async-start | bytes 294912 | tf_op jit(solution)/shard_map/all_to_all | solution.py:613
  34.2 6.0 %within.1.y_ref = f32[128,4608]{1,0:T(8,128)} custom-call(bf16[128,4608]{1,0:T(8,128)(2,1)S(1)} %copy-done.4, bf16[16,4608]{1,0:T(8,128)(2,1)S(1)} %get-tuple-element.31.head_ref, f32[16,4608]{1,0:T(8,128)S(1)} %copy-done, f32[16,4608]{1,0:T(8,128)S(1)} %sqrt_multiply_fusion.coef_ref, ...), custom_call_target="tpu_custom_call", output_to_operand_aliasing={{}: (5, {})} | custom-call | flops 29491200 | bytes 4718592 | tf_op jit(solution)/shard_map/within/pallas_call | solution.py:549
  40.2 2.0 %all-to-all-done.1.piece_ref = bf16[32,2,1152]{2,1,0:T(2,128)(2,1)S(1)} async-done(((bf16[32,2,1152]{2,1,0:T(2,128)(2,1)}), bf16[32,2,1152]{2,1,0:T(2,128)(2,1)S(1)}, u32[]{:S(2)}, u32[]{:S(2)}) %all-to-all-start.1) | async-done | bytes 147488 | tf_op jit(solution)/shard_map/all_to_all | solution.py:613
  42.2 5.3 %final.1 = bf16[128,4608]{1,0:T(8,128)(2,1)} custom-call(bf16[32,2,1152]{2,1,0:T(2,128)(2,1)S(1)} %all-to-all-done.1.piece_ref, f32[16,4608]{1,0:T(8,128)S(1)} %copy-done, f32[128,4608]{1,0:T(8,128)} %within.1.y_ref, bf16[128,4608]{1,0:T(8,128)(2,1)} %get-tuple-element.42.gate_ref), custom_call_target="tpu_custom_call" | custom-call | flops 23592960 | bytes 5898240 | tf_op jit(solution)/shard_map/final/pallas_call | solution.py:549
  (9 shorter events, 0.0 us)
Async XLA Ops:
  0.0 5.2 %copy-start.2 = (bf16[128,4608]{1,0:T(8,128)(2,1)S(1)}, bf16[128,4608]{1,0:T(8,128)(2,1)}, u32[]{:S(2)}) copy-start(bf16[128,4608]{1,0:T(8,128)(2,1)} %value_ref.5) | copy-start | bytes 3538948
  0.0 5.2 %copy-start.1 = (bf16[128,4608]{1,0:T(8,128)(2,1)S(1)}, bf16[128,4608]{1,0:T(8,128)(2,1)}, u32[]{:S(2)}) copy-start(bf16[128,4608]{1,0:T(8,128)(2,1)} %key_ref.5) | copy-start | bytes 3538948
  0.0 5.3 %copy-start = (f32[16,4608]{1,0:T(8,128)S(1)}, f32[16,4608]{1,0:T(8,128)}, u32[]{:S(2)}) copy-start(f32[16,4608]{1,0:T(8,128)} %rate_ref.11) | copy-start | bytes 884740
  0.0 5.3 %copy-start.6 = (f32[3,7,288]{2,1,0:T(8,128)S(1)}, f32[3,7,288]{2,1,0:T(8,128)}, u32[]{:S(2)}) copy-start(f32[3,7,288]{2,1,0:T(8,128)} %feat_ref.3) | copy-start | bytes 72580
  1.3 11.8 %collective-permute-start = (bf16[9,2,4608]{2,1,0:T(2,128)(2,1)S(1)}, bf16[9,2,4608]{2,1,0:T(2,128)(2,1)S(1)}, u32[]{:S(2)}, u32[]{:S(2)}) collective-permute-start(bf16[9,2,4608]{2,1,0:T(2,128)(2,1)S(1)} %pack.1), channel_id=1, source_target_pairs={{0,1},{1,2},{2,3},{3,4},{4,5},{5,6},{6,7},{7,8},{8,9},{9,10},{10,1... | collective-permute-start | bytes 497672 | tf_op jit(solution)/shard_map/ppermute | solution.py:568
  13.1 1.7 %copy-start.5 = (bf16[9,2,4608]{2,1,0:T(2,128)(2,1)}, bf16[9,2,4608]{2,1,0:T(2,128)(2,1)S(1)}, u32[]{:S(2)}) copy-start(bf16[9,2,4608]{2,1,0:T(2,128)(2,1)S(1)} %collective-permute-done.halo_ref) | copy-start | bytes 497668
  13.1 6.4 %copy-start.7 = (f32[16,4608]{1,0:T(8,128)S(1)}, f32[16,4608]{1,0:T(8,128)}, u32[]{:S(2)}) copy-start(f32[16,4608]{1,0:T(8,128)} %param.12) | copy-start | bytes 884740
  13.1 6.6 %copy-start.8 = (f32[4608]{0:T(1024)S(1)}, f32[4608]{0:T(1024)}, u32[]{:S(2)}) copy-start(f32[4608]{0:T(1024)} %param.13) | copy-start | bytes 55300
  14.8 4.9 %copy-start.3 = (bf16[128,4608]{1,0:T(8,128)(2,1)S(1)}, bf16[128,4608]{1,0:T(8,128)(2,1)}, u32[]{:S(2)}) copy-start(bf16[128,4608]{1,0:T(8,128)(2,1)} %query_ref.3) | copy-start | bytes 3538948
  14.9 12.7 %all-to-all-start = ((bf16[32,2,1152]{2,1,0:T(2,128)(2,1)}), bf16[32,2,1152]{2,1,0:T(2,128)(2,1)S(1)}, u32[]{:S(2)}, u32[]{:S(2)}) async-start(bf16[32,2,1152]{2,1,0:T(2,128)(2,1)} %get-tuple-element.28), calls=%async_computation | async-start | bytes 294912 | tf_op jit(solution)/shard_map/all_to_all | solution.py:613
  27.3 6.9 %copy-start.4 = (bf16[128,4608]{1,0:T(8,128)(2,1)S(1)}, bf16[128,4608]{1,0:T(8,128)(2,1)}, u32[]{:S(2)}) copy-start(bf16[128,4608]{1,0:T(8,128)(2,1)} %get-tuple-element.30.u_ref) | copy-start | bytes 3538948
  28.5 13.7 %all-to-all-start.1 = ((bf16[32,2,1152]{2,1,0:T(2,128)(2,1)}), bf16[32,2,1152]{2,1,0:T(2,128)(2,1)S(1)}, u32[]{:S(2)}, u32[]{:S(2)}) async-start(bf16[32,2,1152]{2,1,0:T(2,128)(2,1)} %prefix.1), calls=%async_computation.1 | async-start | bytes 294912 | tf_op jit(solution)/shard_map/all_to_all | solution.py:613

commit v15 on v14

--- a/solution.py
+++ b/solution.py
@@ -595,7 +595,7 @@
     stage = vmem((tokens // ROWS // 2 * ROWS * ROWS, LANES), f32)
     local_shapes = [far((tokens, width), f32)]
     local_scratches = [whole_buf, stage, stage, dma((1, chunks))]
-    early = chunks * 4 // 9
+    early = chunks * 2 // 9
     gate, y = call(
         functools.partial(gate_kernel, early=early),
         (query, halo_late, featurizer, u, head, rates, coef, skip_row),

time: 47.9 us -> 45.9 us (0.958)
  starting transfers between devices: 14.2 us -> 12.2 us
    all_to_all x2, starting transfers between devices: 10.3 us -> 8.23 us  [swap(): lax.all_to_all(value, axes, split_axis=0, concat_axis=0, axis_index_group...]
  transfers between devices with their start and end apart: 3 -> 3, of which waited for: 3 -> 2; matrix products, arithmetic and copies ran while one was open for 0% -> 0% of each run, Pallas kernels for 43% -> 45%
where the time goes in v15:
time: 45.9 us; the launch traced here: 45.5 us
  Pallas kernels  29.6 us (64%)
  starting transfers between devices  12.2 us (27%)
  waiting for transfers between devices  3.31 us (7%)
    pallas_call x7, Pallas kernels, call(): pl.pallas_call(kernel, in_specs=[beside if at in close else there for at...  29.6 us
    all_to_all x2, starting transfers between devices, swap(): lax.all_to_all(value, axes, split_axis=0, concat_axis=0, axis_index_group...  8.23 us
    ppermute x1, starting transfers between devices, local(): lax.ppermute(packed, axes, [(at, at + 1) for at in range(devices - 1)])  3.95 us
    all_to_all x2, waiting for transfers between devices, swap(): lax.all_to_all(value, axes, split_axis=0, concat_axis=0, axis_index_group...  2.26 us
    ppermute x1, waiting for transfers between devices, local(): lax.ppermute(packed, axes, [(at, at + 1) for at in range(devices - 1)])  1.05 us
  transfers between devices with their start and end apart: 3, of which 2 were waited for; matrix products, arithmetic and copies ran while one was open for 0% of the time, Pallas kernels for 45%

profile of v15, /device:TPU:1, one launch (start us, length us, event | category | flops | bytes accessed | tf_op | source)
XLA Modules:
  0.0 45.5 jit_solution(12917527688549664419)
XLA Ops:
  0.0 0.0 copy-start.6
  0.0 1.3 %pack.1 = bf16[9,2,4608]{2,1,0:T(2,128)(2,1)S(1)} custom-call(bf16[128,4608]{1,0:T(8,128)(2,1)} %key_ref.5, bf16[128,4608]{1,0:T(8,128)(2,1)} %value_ref.5, bf16[128,4608]{1,0:T(8,128)(2,1)} %query_ref.3), custom_call_target="tpu_custom_call" | custom-call | tf_op jit(solution)/shard_map/pack/pallas_call | solution.py:549
  1.3 3.9 %collective-permute-start = (bf16[9,2,4608]{2,1,0:T(2,128)(2,1)S(1)}, bf16[9,2,4608]{2,1,0:T(2,128)(2,1)S(1)}, u32[]{:S(2)}, u32[]{:S(2)}) collective-permute-start(bf16[9,2,4608]{2,1,0:T(2,128)(2,1)S(1)} %pack.1), channel_id=1, source_target_pairs={{0,1},{1,2},{2,3},{3,4},{4,5},{5,6},{6,7},{7,8},{8,9},{9,10},{10,1... | collective-permute-start | bytes 497672 | tf_op jit(solution)/shard_map/ppermute | solution.py:568
  5.2 0.0 copy-done.2
  5.2 0.0 copy-done.1
  5.3 0.0 copy-done
  5.3 0.0 copy-done.6
  5.3 6.8 %signal.1 = (bf16[128,4608]{1,0:T(8,128)(2,1)S(1)}, f32[9,2,8,512]{3,2,1,0:T(8,128)S(1)}, f32[16,4608]{1,0:T(8,128)S(1)}) custom-call(bf16[128,4608]{1,0:T(8,128)(2,1)S(1)} %copy-done.1, bf16[128,4608]{1,0:T(8,128)(2,1)S(1)} %copy-done.2, f32[3,7,288]{2,1,0:T(8,128)S(1)} %copy-done.6, f32[16,4608]{1,0:T(8,128)S(1)} %copy-done), custom_call_target="tpu_custom_call" | custom-call | flops 35389440 | bytes 5898240 | tf_op jit(solution)/shard_map/signal/pallas_call | solution.py:549
  12.1 1.1 %collective-permute-done.halo_ref = bf16[9,2,4608]{2,1,0:T(2,128)(2,1)S(1)} collective-permute-done((bf16[9,2,4608]{2,1,0:T(2,128)(2,1)S(1)}, bf16[9,2,4608]{2,1,0:T(2,128)(2,1)S(1)}, u32[]{:S(2)}, u32[]{:S(2)}) %collective-permute-start) | collective-permute-done | bytes 165920 | tf_op jit(solution)/shard_map/ppermute | solution.py:568
  13.1 1.7 %head.1 = (bf16[32,2,1152]{2,1,0:T(2,128)(2,1)}, bf16[16,4608]{1,0:T(8,128)(2,1)S(1)}, bf16[128,4608]{1,0:T(8,128)(2,1)}) custom-call(bf16[128,4608]{1,0:T(8,128)(2,1)S(1)} %copy-done.1, bf16[128,4608]{1,0:T(8,128)(2,1)S(1)} %copy-done.2, bf16[9,2,4608]{2,1,0:T(2,128)(2,1)S(1)} %collective-permute-done.halo_ref, f32[16,4608]{1,0:T(8,128)S(1)} %copy-done, ...), custom_call_target="tpu_custom_call" | custom-call | tf_op jit(solution)/shard_map/head/pallas_call | solution.py:549
  14.8 0.0 copy-start.3
  14.9 4.6 %all-to-all-start = ((bf16[32,2,1152]{2,1,0:T(2,128)(2,1)}), bf16[32,2,1152]{2,1,0:T(2,128)(2,1)S(1)}, u32[]{:S(2)}, u32[]{:S(2)}) async-start(bf16[32,2,1152]{2,1,0:T(2,128)(2,1)} %get-tuple-element.28), calls=%async_computation | async-start | bytes 294912 | tf_op jit(solution)/shard_map/all_to_all | solution.py:613
  19.5 0.0 copy-done.7
  19.5 0.2 sqrt_multiply_fusion.coef_ref
  19.7 0.0 copy-done.8
  19.7 5.5 %gate.1 = (bf16[128,4608]{1,0:T(8,128)(2,1)}, f32[128,4608]{1,0:T(8,128)}) custom-call(bf16[128,4608]{1,0:T(8,128)(2,1)S(1)} %copy-done.3, bf16[9,2,4608]{2,1,0:T(2,128)(2,1)} %copy-done.5, f32[3,7,288]{2,1,0:T(8,128)S(1)} %copy-done.6, bf16[128,4608]{1,0:T(8,128)(2,1)} %get-tuple-element.30.u_ref, bf16[16,4608]{1,0:T(8,128)(2,1)S(1)} %get-tuple-element.31.head_ref, ...), custom_call_target="tpu_custom_call" | custom-call | flops 16515072 | bytes 3538944 | tf_op jit(solution)/shard_map/gate/pallas_call | solution.py:549
  25.3 0.0 copy-start.4
  25.3 2.3 %all-to-all-done.piece_ref = bf16[32,2,1152]{2,1,0:T(2,128)(2,1)S(1)} async-done(((bf16[32,2,1152]{2,1,0:T(2,128)(2,1)}), bf16[32,2,1152]{2,1,0:T(2,128)(2,1)S(1)}, u32[]{:S(2)}, u32[]{:S(2)}) %all-to-all-start) | async-done | bytes 147488 | tf_op jit(solution)/shard_map/all_to_all | solution.py:613
  27.5 1.0 %prefix.1 = bf16[32,2,1152]{2,1,0:T(2,128)(2,1)} custom-call(bf16[32,2,1152]{2,1,0:T(2,128)(2,1)S(1)} %all-to-all-done.piece_ref, f32[16,4608]{1,0:T(8,128)S(1)} %copy-done, f32[16,4608]{1,0:T(8,128)S(1)} %sqrt_multiply_fusion.coef_ref), custom_call_target="tpu_custom_call" | custom-call | tf_op jit(solution)/shard_map/prefix/pallas_call | solution.py:549
  28.5 3.6 %all-to-all-start.1 = ((bf16[32,2,1152]{2,1,0:T(2,128)(2,1)}), bf16[32,2,1152]{2,1,0:T(2,128)(2,1)S(1)}, u32[]{:S(2)}, u32[]{:S(2)}) async-start(bf16[32,2,1152]{2,1,0:T(2,128)(2,1)} %prefix.1), calls=%async_computation.1 | async-start | bytes 294912 | tf_op jit(solution)/shard_map/all_to_all | solution.py:613
  32.1 0.0 copy-done.4
  32.1 8.1 %within.1.y_ref = f32[128,4608]{1,0:T(8,128)} custom-call(bf16[128,4608]{1,0:T(8,128)(2,1)S(1)} %copy-done.4, bf16[16,4608]{1,0:T(8,128)(2,1)S(1)} %get-tuple-element.31.head_ref, f32[16,4608]{1,0:T(8,128)S(1)} %copy-done, f32[16,4608]{1,0:T(8,128)S(1)} %sqrt_multiply_fusion.coef_ref, ...), custom_call_target="tpu_custom_call", output_to_operand_aliasing={{}: (5, {})} | custom-call | flops 29491200 | bytes 4718592 | tf_op jit(solution)/shard_map/within/pallas_call | solution.py:549
  40.2 0.0 all-to-all-done.1.piece_ref
  40.2 5.3 %final.1 = bf16[128,4608]{1,0:T(8,128)(2,1)} custom-call(bf16[32,2,1152]{2,1,0:T(2,128)(2,1)S(1)} %all-to-all-done.1.piece_ref, f32[16,4608]{1,0:T(8,128)S(1)} %copy-done, f32[128,4608]{1,0:T(8,128)} %within.1.y_ref, bf16[128,4608]{1,0:T(8,128)(2,1)} %get-tuple-element.42.gate_ref), custom_call_target="tpu_custom_call" | custom-call | flops 23592960 | bytes 5898240 | tf_op jit(solution)/shard_map/final/pallas_call | solution.py:549
  (9 shorter events, 0.0 us)
Async XLA Ops:
  0.0 5.2 %copy-start.2 = (bf16[128,4608]{1,0:T(8,128)(2,1)S(1)}, bf16[128,4608]{1,0:T(8,128)(2,1)}, u32[]{:S(2)}) copy-start(bf16[128,4608]{1,0:T(8,128)(2,1)} %value_ref.5) | copy-start | bytes 3538948
  0.0 5.2 %copy-start.1 = (bf16[128,4608]{1,0:T(8,128)(2,1)S(1)}, bf16[128,4608]{1,0:T(8,128)(2,1)}, u32[]{:S(2)}) copy-start(bf16[128,4608]{1,0:T(8,128)(2,1)} %key_ref.5) | copy-start | bytes 3538948
  0.0 5.3 %copy-start = (f32[16,4608]{1,0:T(8,128)S(1)}, f32[16,4608]{1,0:T(8,128)}, u32[]{:S(2)}) copy-start(f32[16,4608]{1,0:T(8,128)} %rate_ref.11) | copy-start | bytes 884740
  0.0 5.3 %copy-start.6 = (f32[3,7,288]{2,1,0:T(8,128)S(1)}, f32[3,7,288]{2,1,0:T(8,128)}, u32[]{:S(2)}) copy-start(f32[3,7,288]{2,1,0:T(8,128)} %feat_ref.3) | copy-start | bytes 72580
  1.3 11.8 %collective-permute-start = (bf16[9,2,4608]{2,1,0:T(2,128)(2,1)S(1)}, bf16[9,2,4608]{2,1,0:T(2,128)(2,1)S(1)}, u32[]{:S(2)}, u32[]{:S(2)}) collective-permute-start(bf16[9,2,4608]{2,1,0:T(2,128)(2,1)S(1)} %pack.1), channel_id=1, source_target_pairs={{0,1},{1,2},{2,3},{3,4},{4,5},{5,6},{6,7},{7,8},{8,9},{9,10},{10,1... | collective-permute-start | bytes 497672 | tf_op jit(solution)/shard_map/ppermute | solution.py:568
  13.1 1.7 %copy-start.5 = (bf16[9,2,4608]{2,1,0:T(2,128)(2,1)}, bf16[9,2,4608]{2,1,0:T(2,128)(2,1)S(1)}, u32[]{:S(2)}) copy-start(bf16[9,2,4608]{2,1,0:T(2,128)(2,1)S(1)} %collective-permute-done.halo_ref) | copy-start | bytes 497668
  13.1 6.4 %copy-start.7 = (f32[16,4608]{1,0:T(8,128)S(1)}, f32[16,4608]{1,0:T(8,128)}, u32[]{:S(2)}) copy-start(f32[16,4608]{1,0:T(8,128)} %param.12) | copy-start | bytes 884740
  13.1 6.6 %copy-start.8 = (f32[4608]{0:T(1024)S(1)}, f32[4608]{0:T(1024)}, u32[]{:S(2)}) copy-start(f32[4608]{0:T(1024)} %param.13) | copy-start | bytes 55300
  14.8 4.9 %copy-start.3 = (bf16[128,4608]{1,0:T(8,128)(2,1)S(1)}, bf16[128,4608]{1,0:T(8,128)(2,1)}, u32[]{:S(2)}) copy-start(bf16[128,4608]{1,0:T(8,128)(2,1)} %query_ref.3) | copy-start | bytes 3538948
  14.9 12.7 %all-to-all-start = ((bf16[32,2,1152]{2,1,0:T(2,128)(2,1)}), bf16[32,2,1152]{2,1,0:T(2,128)(2,1)S(1)}, u32[]{:S(2)}, u32[]{:S(2)}) async-start(bf16[32,2,1152]{2,1,0:T(2,128)(2,1)} %get-tuple-element.28), calls=%async_computation | async-start | bytes 294912 | tf_op jit(solution)/shard_map/all_to_all | solution.py:613
  25.3 6.9 %copy-start.4 = (bf16[128,4608]{1,0:T(8,128)(2,1)S(1)}, bf16[128,4608]{1,0:T(8,128)(2,1)}, u32[]{:S(2)}) copy-start(bf16[128,4608]{1,0:T(8,128)(2,1)} %get-tuple-element.30.u_ref) | copy-start | bytes 3538948
  28.5 11.7 %all-to-all-start.1 = ((bf16[32,2,1152]{2,1,0:T(2,128)(2,1)}), bf16[32,2,1152]{2,1,0:T(2,128)(2,1)S(1)}, u32[]{:S(2)}, u32[]{:S(2)}) async-start(bf16[32,2,1152]{2,1,0:T(2,128)(2,1)} %prefix.1), calls=%async_computation.1 | async-start | bytes 294912 | tf_op jit(solution)/shard_map/all_to_all | solution.py:613

commit v16 on v15

--- a/solution.py
+++ b/solution.py
@@ -96,6 +96,13 @@
             total = total + taps[lag] * rows[lag]
         yield total + jnp.where(top, before, now)
         before = now
+
+
+def fir_loads(column, taps, first):
+    total = taps[0] * column[pl.ds(first, ROWS), :]
+    for lag in range(1, len(taps)):
+        total = total + taps[lag] * column[pl.ds(first - lag, ROWS), :]
+    return total
 
 
 def lay_column(column, source, lanes):
@@ -211,7 +218,8 @@
             out_ref[at * pairs + pair] = tail[2 * pair : 2 * pair + 2].astype(bf16)
 
 
-def signal_kernel(key_ref, value_ref, feat_ref, rate_ref, u_ref, wide_ref, state_ref, power_scr, last_scr, *columns):
+def signal_kernel(key_ref, value_ref, feat_ref, rate_ref, u_ref, u_out_ref, wide_ref, state_ref, *scratches):
+    power_scr, last_scr, *columns, out_sem = scratches
     tokens, tiles = u_ref.shape[0], u_ref.shape[1] // LANES
     modes = rate_ref.shape[0]
     chunks = tiles // TILES
@@ -248,9 +256,10 @@
             lay_column(column, ref, lanes)
         decay = [wide(power_scr[3, mode : mode + 1, lanes]) for mode in range(modes)]
         state = None
-        parts = [fir(column, some, 2 * ROWS, tokens // ROWS) for column, some in zip(columns, taps)]
         for pair in range(tokens // (2 * ROWS)):
-            found = [next(parts[0]) * next(parts[1]) for _ in range(2)]
+            found = []
+            for first in (pair * 2 * ROWS + 2 * ROWS, pair * 2 * ROWS + 3 * ROWS):
+                found.append(fir_loads(columns[0], taps[0], first) * fir_loads(columns[1], taps[1], first))
             if pair == 0:
                 found[0] = jnp.where(sublane() < count - 1, 0.0, found[0])
             both = jnp.concatenate(found, axis=0).astype(bf16)
@@ -263,20 +272,31 @@
         for mode in range(modes):
             last_scr[mode] = state[mode]
 
-    def some(number, _):
+    def send(at):
+        return pltpu.make_async_copy(u_ref.at[:, span(at)], u_out_ref.at[:, span(at)], out_sem.at[at])
+
+    def chunk(at, _):
         for part in range(TILES):
-            tile(TILES * number + part, columns[2 * part : 2 * part + 2])
+            tile(TILES * at + part, columns[2 * part : 2 * part + 2])
+
+        @pl.when(at < chunks - 1)
+        def _():
+            send(at).start()
+
         return 0
 
-    lax.fori_loop(0, tiles // TILES, some, 0)
+    lax.fori_loop(0, chunks, chunk, 0)
     reduce(tiles - 1)
-
-
-def head_kernel(key_ref, value_ref, halo_ref, rate_ref, wide_ref, state_ref, u_ref, *rest, tokens, reach):
+    for at in range(chunks - 1):
+        send(at).wait()
+
+
+def head_kernel(key_ref, value_ref, halo_ref, rate_ref, wide_ref, state_ref, u_ref, _, *rest, tokens, reach):
     out_ref, head_ref, u_out_ref, column_scr, token_scr, total_scr, sem = rest
-    move = pltpu.make_async_copy(u_ref, u_out_ref, sem.at[0])
+    modes, tiles = state_ref.shape[0], state_ref.shape[1] // LANES
+    last = span(tiles // TILES - 1)
+    move = pltpu.make_async_copy(u_ref.at[:, last], u_out_ref.at[:, last], sem.at[0])
     move.start()
-    modes, tiles = state_ref.shape[0], state_ref.shape[1] // LANES
     pieces, piece_modes, piece_width = out_ref.shape
 
     def some(chunk, _):
@@ -569,11 +589,13 @@
 
     column = vmem((2 * ROWS + tokens, LANES), f32)
     half_buf, whole_buf = vmem((chunks, tokens, CHUNK), bf16), vmem((chunks, tokens, CHUNK), f32)
-    u, wide_taps, state = call(
+    u, u_far, wide_taps, state = call(
         signal_kernel,
         (key_proj, value_proj, featurizer, rates),
-        [near((tokens, width), bf16), near((chunks, 2, ROWS, CHUNK), f32), near((modes, width), f32)],
-        [vmem((4, modes, width), f32), vmem((modes, ROWS, LANES), f32)] + [column] * (2 * TILES),
+        [near((tokens, width), bf16), far((tokens, width), bf16)]
+        + [near((chunks, 2, ROWS, CHUNK), f32), near((modes, width), f32)],
+        [vmem((4, modes, width), f32), vmem((modes, ROWS, LANES), f32)] + [column] * (2 * TILES)
+        + [dma((chunks,))],
         "signal",
         close=range(4),
         cost_estimate=cost(60 * elements, 10 * elements),
@@ -582,12 +604,13 @@
     pieces = (devices, 2, width // split) if even else (modes // 2, 2, width)
     left, head, u = call(
         functools.partial(head_kernel, tokens=tokens, reach=taps - 1),
-        (key_proj, value_proj, halo, rates, wide_taps, state, u),
+        (key_proj, value_proj, halo, rates, wide_taps, state, u, u_far),
         [near(pieces, bf16), near((2 * ROWS, width), bf16), far((tokens, width), bf16)],
         [vmem((TILES, 2, 3 * ROWS, LANES), f32), vmem((TILES, ROWS, LANES), f32)]
         + [vmem((modes, width), f32), dma((1,))],
         "head",
         close=range(7),
+        input_output_aliases={7: 2},
     )
     left, halo_late, rates_late, skip_late = lax.optimization_barrier((left, halo, rates, skip))
     coef = residues * jnp.sqrt(-jnp.expm1(-2.0 * rates_late) / modes)

time: 45.9 us -> 45.7 us (level)
  no operation moved by 1% of the time
where the time goes in v16:
time: 45.7 us; the launch traced here: 45.3 us
  Pallas kernels  29.4 us (64%)
  starting transfers between devices  12.1 us (26%)
  waiting for transfers between devices  3.44 us (8%)
    pallas_call x7, Pallas kernels, call(): pl.pallas_call(kernel, in_specs=[beside if at in close else there for at...  29.4 us
    all_to_all x2, starting transfers between devices, swap(): lax.all_to_all(value, axes, split_axis=0, concat_axis=0, axis_index_group...  8.11 us
    ppermute x1, starting transfers between devices, local(): lax.ppermute(packed, axes, [(at, at + 1) for at in range(devices - 1)])  3.95 us
    all_to_all x2, waiting for transfers between devices, swap(): lax.all_to_all(value, axes, split_axis=0, concat_axis=0, axis_index_group...  2.26 us
    ppermute x1, waiting for transfers between devices, local(): lax.ppermute(packed, axes, [(at, at + 1) for at in range(devices - 1)])  1.18 us
  transfers between devices with their start and end apart: 3, of which 2 were waited for; matrix products, arithmetic and copies ran while one was open for 0% of the time, Pallas kernels for 45%

profile of v16, /device:TPU:1, one launch (start us, length us, event | category | flops | bytes accessed | tf_op | source)
XLA Modules:
  0.0 45.3 jit_solution(254094115728492097)
XLA Ops:
  0.0 1.3 %pack.1 = bf16[9,2,4608]{2,1,0:T(2,128)(2,1)S(1)} custom-call(bf16[128,4608]{1,0:T(8,128)(2,1)} %key_ref.5, bf16[128,4608]{1,0:T(8,128)(2,1)} %value_ref.5, bf16[128,4608]{1,0:T(8,128)(2,1)} %query_ref.3), custom_call_target="tpu_custom_call" | custom-call | tf_op jit(solution)/shard_map/pack/pallas_call | solution.py:569
  1.3 3.9 %collective-permute-start = (bf16[9,2,4608]{2,1,0:T(2,128)(2,1)S(1)}, bf16[9,2,4608]{2,1,0:T(2,128)(2,1)S(1)}, u32[]{:S(2)}, u32[]{:S(2)}) collective-permute-start(bf16[9,2,4608]{2,1,0:T(2,128)(2,1)S(1)} %pack.1), channel_id=1, source_target_pairs={{0,1},{1,2},{2,3},{3,4},{4,5},{5,6},{6,7},{7,8},{8,9},{9,10},{10,1... | collective-permute-start | bytes 497672 | tf_op jit(solution)/shard_map/ppermute | solution.py:588
  5.2 0.0 copy-done.2
  5.2 0.0 copy-done.1
  5.3 0.0 copy-done
  5.3 0.0 copy-done.6
  5.3 6.7 %signal.1 = (bf16[128,4608]{1,0:T(8,128)(2,1)S(1)}, bf16[128,4608]{1,0:T(8,128)(2,1)}, f32[9,2,8,512]{3,2,1,0:T(8,128)S(1)}, f32[16,4608]{1,0:T(8,128)S(1)}) custom-call(bf16[128,4608]{1,0:T(8,128)(2,1)S(1)} %copy-done.1, bf16[128,4608]{1,0:T(8,128)(2,1)S(1)} %copy-done.2, f32[3,7,288]{2,1,0:T(8,128)S(1)} %copy-done.6, f32[16,4608]{1,0:T(8,128)S(1)} %copy-done), custom_call_target="tpu_custom_call" | custom-call | flops 35389440 | bytes 5898240 | tf_op jit(solution)/shard_map/signal/pallas_call | solution.py:569
  11.9 1.2 %collective-permute-done.halo_ref = bf16[9,2,4608]{2,1,0:T(2,128)(2,1)S(1)} collective-permute-done((bf16[9,2,4608]{2,1,0:T(2,128)(2,1)S(1)}, bf16[9,2,4608]{2,1,0:T(2,128)(2,1)S(1)}, u32[]{:S(2)}, u32[]{:S(2)}) %collective-permute-start) | collective-permute-done | bytes 165920 | tf_op jit(solution)/shard_map/ppermute | solution.py:588
  13.1 1.6 %head.1 = (bf16[32,2,1152]{2,1,0:T(2,128)(2,1)}, bf16[16,4608]{1,0:T(8,128)(2,1)S(1)}, bf16[128,4608]{1,0:T(8,128)(2,1)}) custom-call(bf16[128,4608]{1,0:T(8,128)(2,1)S(1)} %copy-done.1, bf16[128,4608]{1,0:T(8,128)(2,1)S(1)} %copy-done.2, bf16[9,2,4608]{2,1,0:T(2,128)(2,1)S(1)} %collective-permute-done.halo_ref, ...), custom_call_target="tpu_custom_call", output_to_operand_aliasing={{2}: (7, {})} | custom-call | tf_op jit(solution)/shard_map/head/pallas_call | solution.py:569
  14.7 0.0 copy-done.5
  14.8 0.0 copy-start.4
  14.8 4.5 %all-to-all-start = ((bf16[32,2,1152]{2,1,0:T(2,128)(2,1)}), bf16[32,2,1152]{2,1,0:T(2,128)(2,1)S(1)}, u32[]{:S(2)}, u32[]{:S(2)}) async-start(bf16[32,2,1152]{2,1,0:T(2,128)(2,1)} %get-tuple-element.30), calls=%async_computation | async-start | bytes 294912 | tf_op jit(solution)/shard_map/all_to_all | solution.py:636
  19.3 0.0 copy-done.7
  19.3 0.2 sqrt_multiply_fusion.coef_ref
  19.5 0.0 copy-done.8
  19.5 5.5 %gate.1 = (bf16[128,4608]{1,0:T(8,128)(2,1)}, f32[128,4608]{1,0:T(8,128)}) custom-call(bf16[128,4608]{1,0:T(8,128)(2,1)S(1)} %copy-done.4, bf16[9,2,4608]{2,1,0:T(2,128)(2,1)} %copy-done.5, f32[3,7,288]{2,1,0:T(8,128)S(1)} %copy-done.6, bf16[128,4608]{1,0:T(8,128)(2,1)} %get-tuple-element.32.u_ref, bf16[16,4608]{1,0:T(8,128)(2,1)S(1)} %get-tuple-element.33.head_ref, ...), custom_call_target="tpu_custom_call" | custom-call | flops 16515072 | bytes 3538944 | tf_op jit(solution)/shard_map/gate/pallas_call | solution.py:569
  25.1 0.0 copy-start.3
  25.1 2.3 %all-to-all-done.piece_ref = bf16[32,2,1152]{2,1,0:T(2,128)(2,1)S(1)} async-done(((bf16[32,2,1152]{2,1,0:T(2,128)(2,1)}), bf16[32,2,1152]{2,1,0:T(2,128)(2,1)S(1)}, u32[]{:S(2)}, u32[]{:S(2)}) %all-to-all-start) | async-done | bytes 147488 | tf_op jit(solution)/shard_map/all_to_all | solution.py:636
  27.3 1.0 %prefix.1 = bf16[32,2,1152]{2,1,0:T(2,128)(2,1)} custom-call(bf16[32,2,1152]{2,1,0:T(2,128)(2,1)S(1)} %all-to-all-done.piece_ref, f32[16,4608]{1,0:T(8,128)S(1)} %copy-done, f32[16,4608]{1,0:T(8,128)S(1)} %sqrt_multiply_fusion.coef_ref), custom_call_target="tpu_custom_call" | custom-call | tf_op jit(solution)/shard_map/prefix/pallas_call | solution.py:569
  28.3 3.6 %all-to-all-start.1 = ((bf16[32,2,1152]{2,1,0:T(2,128)(2,1)}), bf16[32,2,1152]{2,1,0:T(2,128)(2,1)S(1)}, u32[]{:S(2)}, u32[]{:S(2)}) async-start(bf16[32,2,1152]{2,1,0:T(2,128)(2,1)} %prefix.1), calls=%async_computation.1 | async-start | bytes 294912 | tf_op jit(solution)/shard_map/all_to_all | solution.py:636
  31.9 0.0 copy-done.3
  31.9 8.1 %within.1.y_ref = f32[128,4608]{1,0:T(8,128)} custom-call(bf16[128,4608]{1,0:T(8,128)(2,1)S(1)} %copy-done.3, bf16[16,4608]{1,0:T(8,128)(2,1)S(1)} %get-tuple-element.33.head_ref, f32[16,4608]{1,0:T(8,128)S(1)} %copy-done, f32[16,4608]{1,0:T(8,128)S(1)} %sqrt_multiply_fusion.coef_ref, ...), custom_call_target="tpu_custom_call", output_to_operand_aliasing={{}: (5, {})} | custom-call | flops 29491200 | bytes 4718592 | tf_op jit(solution)/shard_map/within/pallas_call | solution.py:569
  40.0 0.0 all-to-all-done.1.piece_ref
  40.0 5.3 %final.1 = bf16[128,4608]{1,0:T(8,128)(2,1)} custom-call(bf16[32,2,1152]{2,1,0:T(2,128)(2,1)S(1)} %all-to-all-done.1.piece_ref, f32[16,4608]{1,0:T(8,128)S(1)} %copy-done, f32[128,4608]{1,0:T(8,128)} %within.1.y_ref, bf16[128,4608]{1,0:T(8,128)(2,1)} %get-tuple-element.44.gate_ref), custom_call_target="tpu_custom_call" | custom-call | flops 23592960 | bytes 5898240 | tf_op jit(solution)/shard_map/final/pallas_call | solution.py:569
  (9 shorter events, 0.0 us)
Async XLA Ops:
  0.0 5.2 %copy-start.2 = (bf16[128,4608]{1,0:T(8,128)(2,1)S(1)}, bf16[128,4608]{1,0:T(8,128)(2,1)}, u32[]{:S(2)}) copy-start(bf16[128,4608]{1,0:T(8,128)(2,1)} %value_ref.5) | copy-start | bytes 3538948
  0.0 5.2 %copy-start.1 = (bf16[128,4608]{1,0:T(8,128)(2,1)S(1)}, bf16[128,4608]{1,0:T(8,128)(2,1)}, u32[]{:S(2)}) copy-start(bf16[128,4608]{1,0:T(8,128)(2,1)} %key_ref.5) | copy-start | bytes 3538948
  0.0 5.3 %copy-start = (f32[16,4608]{1,0:T(8,128)S(1)}, f32[16,4608]{1,0:T(8,128)}, u32[]{:S(2)}) copy-start(f32[16,4608]{1,0:T(8,128)} %rate_ref.11) | copy-start | bytes 884740
  0.0 5.3 %copy-start.6 = (f32[3,7,288]{2,1,0:T(8,128)S(1)}, f32[3,7,288]{2,1,0:T(8,128)}, u32[]{:S(2)}) copy-start(f32[3,7,288]{2,1,0:T(8,128)} %feat_ref.3) | copy-start | bytes 72580
  1.3 11.8 %collective-permute-start = (bf16[9,2,4608]{2,1,0:T(2,128)(2,1)S(1)}, bf16[9,2,4608]{2,1,0:T(2,128)(2,1)S(1)}, u32[]{:S(2)}, u32[]{:S(2)}) collective-permute-start(bf16[9,2,4608]{2,1,0:T(2,128)(2,1)S(1)} %pack.1), channel_id=1, source_target_pairs={{0,1},{1,2},{2,3},{3,4},{4,5},{5,6},{6,7},{7,8},{8,9},{9,10},{10,1... | collective-permute-start | bytes 497672 | tf_op jit(solution)/shard_map/ppermute | solution.py:588
  13.1 1.6 %copy-start.5 = (bf16[9,2,4608]{2,1,0:T(2,128)(2,1)}, bf16[9,2,4608]{2,1,0:T(2,128)(2,1)S(1)}, u32[]{:S(2)}) copy-start(bf16[9,2,4608]{2,1,0:T(2,128)(2,1)S(1)} %collective-permute-done.halo_ref) | copy-start | bytes 497668
  13.1 6.1 %copy-start.7 = (f32[16,4608]{1,0:T(8,128)S(1)}, f32[16,4608]{1,0:T(8,128)}, u32[]{:S(2)}) copy-start(f32[16,4608]{1,0:T(8,128)} %param.12) | copy-start | bytes 884740
  13.1 6.3 %copy-start.8 = (f32[4608]{0:T(1024)S(1)}, f32[4608]{0:T(1024)}, u32[]{:S(2)}) copy-start(f32[4608]{0:T(1024)} %param.13) | copy-start | bytes 55300
  14.8 4.8 %copy-start.4 = (bf16[128,4608]{1,0:T(8,128)(2,1)S(1)}, bf16[128,4608]{1,0:T(8,128)(2,1)}, u32[]{:S(2)}) copy-start(bf16[128,4608]{1,0:T(8,128)(2,1)} %query_ref.3) | copy-start | bytes 3538948
  14.8 12.6 %all-to-all-start = ((bf16[32,2,1152]{2,1,0:T(2,128)(2,1)}), bf16[32,2,1152]{2,1,0:T(2,128)(2,1)S(1)}, u32[]{:S(2)}, u32[]{:S(2)}) async-start(bf16[32,2,1152]{2,1,0:T(2,128)(2,1)} %get-tuple-element.30), calls=%async_computation | async-start | bytes 294912 | tf_op jit(solution)/shard_map/all_to_all | solution.py:636
  25.1 6.9 %copy-start.3 = (bf16[128,4608]{1,0:T(8,128)(2,1)S(1)}, bf16[128,4608]{1,0:T(8,128)(2,1)}, u32[]{:S(2)}) copy-start(bf16[128,4608]{1,0:T(8,128)(2,1)} %get-tuple-element.32.u_ref) | copy-start | bytes 3538948
  28.3 11.7 %all-to-all-start.1 = ((bf16[32,2,1152]{2,1,0:T(2,128)(2,1)}), bf16[32,2,1152]{2,1,0:T(2,128)(2,1)S(1)}, u32[]{:S(2)}, u32[]{:S(2)}) async-start(bf16[32,2,1152]{2,1,0:T(2,128)(2,1)} %prefix.1), calls=%async_computation.1 | async-start | bytes 294912 | tf_op jit(solution)/shard_map/all_to_all | solution.py:636

commit v17 on v16

--- a/solution.py
+++ b/solution.py
@@ -310,7 +310,7 @@
                 lay_halo(column, halo_ref, member, lanes)
                 source = (key_ref, value_ref)[member]
                 column[pl.ds(2 * ROWS, ROWS), :] = source[: 2 * ROWS, lanes].astype(f32)[:ROWS]
-                parts += fir(column, taps, 2 * ROWS, 1)
+                parts.append(fir_loads(column, taps, 2 * ROWS))
             u = jnp.where(sublane() < reach, rounded(parts[0] * parts[1]), 0.0)
             token_scr[number] = u
             for group in range(0, modes, ROWS):
@@ -381,12 +381,7 @@
 
     def mine_of(ref):
         rows = ref[pl.ds(group, ROWS), pl.ds(first, piece_width)]
-        place = lax.broadcasted_iota(jnp.int32, rows.shape, 0)
-        found = [
-            jnp.sum(jnp.where(place == mode - group + row, rows, 0.0), axis=0, keepdims=True)
-            for row in range(piece_modes)
-        ]
-        return jnp.concatenate(found, axis=0)
+        return pltpu.roll(rows, lax.rem(ROWS - (mode - group), ROWS), 0)[:piece_modes]
 
     coef = mine_of(coef_ref)
     through = jnp.exp(-float(tokens) * mine_of(rate_ref))
@@ -401,11 +396,18 @@
     lax.fori_loop(0, devices // 4, lap, jnp.zeros((piece_modes, piece_width), f32))
 
 
-def local_kernel(u_ref, head_ref, rate_ref, coef_ref, skip_ref, *rest, first, last):
-    chunk, send = local_parts(u_ref, head_ref, rate_ref, coef_ref, skip_ref, *rest[-5:])
+def local_kernel(u_ref, head_ref, rate_ref, coef_ref, skip_ref, gate_ref, _, y_ref, y_last_ref, gate_last_ref, *scratches, first):
+    *inner, sem = scratches
+    last = u_ref.shape[1] // CHUNK - 1
+    take = pltpu.make_async_copy(gate_ref.at[:, span(last)], gate_last_ref, sem.at[0])
+    take.start()
+    chunk, send = local_parts(u_ref, head_ref, rate_ref, coef_ref, skip_ref, y_ref, *inner)
     over_chunks(first, last, chunk, send)
+    chunk(last)
+    y_last_ref[...] = inner[0][last]
     for at in range(first, last):
         wait_all(send(at))
+    take.wait()
 
 
 def local_parts(u_ref, head_ref, rate_ref, coef_ref, skip_ref, y_ref, *scratches):
@@ -462,13 +464,13 @@
     return chunk, columns_out(y_ref, y_buf, out_sem)
 
 
-def final_kernel(piece_ref, rate_ref, y_ref, gate_ref, out_ref, *scratches, axes):
+def final_kernel(piece_ref, rate_ref, y_last_ref, gate_last_ref, y_ref, gate_ref, out_ref, *scratches, axes):
     y_buf, gate_buf, out_buf, total_scr, power_scr, in_sem, out_sem = scratches
     chunks, tokens = y_buf.shape[:2]
     modes = rate_ref.shape[0]
     fetch = columns_in(((y_ref, y_buf), (gate_ref, gate_buf)), in_sem)
     give = columns_out(out_ref, out_buf, out_sem)
-    start_all(fetch(0))
+    begin(chunks - 1, fetch)
     bits = [(sublane() >> level) % 2 == 1 for level in range(3)]
     pairs = [slice(first, first + 2 * ROWS) for first in range(0, tokens, 2 * ROWS)]
 
@@ -515,16 +517,19 @@
 
         lax.fori_loop(0, TILES, tile, 0)
 
-    def begin_others():
-        for at in range(1, min(AHEAD, chunks)):
-            start_all(fetch(at))
+    def all_chunks(body):
+        last = chunks - 1
+        y_buf[last] = y_last_ref[...]
+        gate_buf[last] = gate_last_ref[...]
+        body(last)
+        start_all(give(last))
+        over_chunks(0, last, with_fetch(last, fetch, body), give)
 
     first = lax.axis_index(axes) == 0
 
     @pl.when(first)
     def _():
-        begin_others()
-        over_chunks(0, chunks, with_fetch(chunks, fetch, chunk_alone), give)
+        all_chunks(chunk_alone)
 
     @pl.when(jnp.logical_not(first))
     def _():
@@ -534,8 +539,7 @@
             row, part = piece // split * piece_modes, piece % split
             lanes = slice(part * piece_width, (part + 1) * piece_width)
             total_scr[row : row + piece_modes, lanes] = piece_ref[piece].astype(f32)
-        begin_others()
-        over_chunks(0, chunks, with_fetch(chunks, fetch, chunk), give)
+        all_chunks(chunk)
 
     for at in range(chunks):
         wait_all(give(at))
@@ -660,25 +664,25 @@
 
     entering, y = lax.optimization_barrier((entering, y))
     entered = swap(entering).reshape(pieces)
-    (y,) = call(
-        functools.partial(local_kernel, first=early, last=chunks),
-        (u, head, rates, coef, skip_row, y),
-        local_shapes,
-        local_scratches,
+    y, y_last, gate_last = call(
+        functools.partial(local_kernel, first=early),
+        (u, head, rates, coef, skip_row, gate, y),
+        local_shapes + [near((tokens, CHUNK), f32), near((tokens, CHUNK), bf16)],
+        local_scratches + [dma((1,))],
         "within",
         close=range(5),
         cost_estimate=cost(50 * elements, 8 * elements),
-        input_output_aliases={5: 0},
+        input_output_aliases={6: 0},
     )
 
     (out,) = call(
         functools.partial(final_kernel, axes=axes),
-        (entered, rates, y, gate),
+        (entered, rates, y_last, gate_last, y, gate),
         [far((tokens, width), bf16)],
         [whole_buf, half_buf, half_buf, vmem((modes, width), f32), vmem((4, modes, CHUNK), f32)]
         + [dma((2, chunks)), dma((1, chunks))],
         "final",
-        close=(0, 1),
+        close=range(4),
         cost_estimate=cost(40 * elements, 10 * elements),
     )
     return out

time: 45.7 us -> 45.1 us (0.987)
  Pallas kernels: 29.4 us -> 28.1 us
  waiting for transfers between devices: 3.44 us -> 4.2 us
    pallas_call x7, Pallas kernels: 29.4 us -> 28.1 us  [call(): pl.pallas_call(kernel, in_specs=[beside if at in close else there for at...]
    all_to_all x2, waiting for transfers between devices: 2.26 us -> 3.02 us  [swap(): lax.all_to_all(value, axes, split_axis=0, concat_axis=0, axis_index_group...]
  transfers between devices with their start and end apart: 3 -> 3, of which waited for: 2 -> 3; matrix products, arithmetic and copies ran while one was open for 0% -> 0% of each run, Pallas kernels for 45% -> 43%
where the time goes in v17:
time: 45.1 us; the launch traced here: 44.8 us
  Pallas kernels  28.1 us (62%)
  starting transfers between devices  12 us (27%)
  waiting for transfers between devices  4.2 us (9%)
    pallas_call x7, Pallas kernels, call(): pl.pallas_call(kernel, in_specs=[beside if at in close else there for at...  28.1 us
    all_to_all x2, starting transfers between devices, swap(): lax.all_to_all(value, axes, split_axis=0, concat_axis=0, axis_index_group...  8.08 us
    ppermute x1, starting transfers between devices, local(): lax.ppermute(packed, axes, [(at, at + 1) for at in range(devices - 1)])  3.95 us
    all_to_all x2, waiting for transfers between devices, swap(): lax.all_to_all(value, axes, split_axis=0, concat_axis=0, axis_index_group...  3.02 us
    ppermute x1, waiting for transfers between devices, local(): lax.ppermute(packed, axes, [(at, at + 1) for at in range(devices - 1)])  1.18 us
  transfers between devices with their start and end apart: 3, of which 3 were waited for; matrix products, arithmetic and copies ran while one was open for 0% of the time, Pallas kernels for 43%

profile of v17, /device:TPU:1, one launch (start us, length us, event | category | flops | bytes accessed | tf_op | source)
XLA Modules:
  0.0 44.8 jit_solution(3609647092927697985)
XLA Ops:
  0.0 0.0 copy-start.6
  0.0 1.3 %pack.1 = bf16[9,2,4608]{2,1,0:T(2,128)(2,1)S(1)} custom-call(bf16[128,4608]{1,0:T(8,128)(2,1)} %key_ref.5, bf16[128,4608]{1,0:T(8,128)(2,1)} %value_ref.5, bf16[128,4608]{1,0:T(8,128)(2,1)} %query_ref.3), custom_call_target="tpu_custom_call" | custom-call | tf_op jit(solution)/shard_map/pack/pallas_call | solution.py:573
  1.3 3.9 %collective-permute-start = (bf16[9,2,4608]{2,1,0:T(2,128)(2,1)S(1)}, bf16[9,2,4608]{2,1,0:T(2,128)(2,1)S(1)}, u32[]{:S(2)}, u32[]{:S(2)}) collective-permute-start(bf16[9,2,4608]{2,1,0:T(2,128)(2,1)S(1)} %pack.1), channel_id=1, source_target_pairs={{0,1},{1,2},{2,3},{3,4},{4,5},{5,6},{6,7},{7,8},{8,9},{9,10},{10,1... | collective-permute-start | bytes 497672 | tf_op jit(solution)/shard_map/ppermute | solution.py:592
  5.2 0.0 copy-done.3
  5.2 0.0 copy-done.2
  5.3 0.0 copy-done
  5.3 0.0 copy-done.6
  5.3 6.7 %signal.1 = (bf16[128,4608]{1,0:T(8,128)(2,1)S(1)}, bf16[128,4608]{1,0:T(8,128)(2,1)}, f32[9,2,8,512]{3,2,1,0:T(8,128)S(1)}, f32[16,4608]{1,0:T(8,128)S(1)}) custom-call(bf16[128,4608]{1,0:T(8,128)(2,1)S(1)} %copy-done.2, bf16[128,4608]{1,0:T(8,128)(2,1)S(1)} %copy-done.3, f32[3,7,288]{2,1,0:T(8,128)S(1)} %copy-done.6, f32[16,4608]{1,0:T(8,128)S(1)} %copy-done), custom_call_target="tpu_custom_call" | custom-call | flops 35389440 | bytes 5898240 | tf_op jit(solution)/shard_map/signal/pallas_call | solution.py:573
  11.9 1.2 %collective-permute-done.halo_ref = bf16[9,2,4608]{2,1,0:T(2,128)(2,1)S(1)} collective-permute-done((bf16[9,2,4608]{2,1,0:T(2,128)(2,1)S(1)}, bf16[9,2,4608]{2,1,0:T(2,128)(2,1)S(1)}, u32[]{:S(2)}, u32[]{:S(2)}) %collective-permute-start) | collective-permute-done | bytes 165920 | tf_op jit(solution)/shard_map/ppermute | solution.py:592
  13.1 1.5 %head.1 = (bf16[32,2,1152]{2,1,0:T(2,128)(2,1)}, bf16[16,4608]{1,0:T(8,128)(2,1)S(1)}, bf16[128,4608]{1,0:T(8,128)(2,1)}) custom-call(bf16[128,4608]{1,0:T(8,128)(2,1)S(1)} %copy-done.2, bf16[128,4608]{1,0:T(8,128)(2,1)S(1)} %copy-done.3, bf16[9,2,4608]{2,1,0:T(2,128)(2,1)S(1)} %collective-permute-done.halo_ref, ...), custom_call_target="tpu_custom_call", output_to_operand_aliasing={{2}: (7, {})} | custom-call | tf_op jit(solution)/shard_map/head/pallas_call | solution.py:573
  14.6 0.0 copy-done.5
  14.6 0.0 copy-start.4
  14.7 4.5 %all-to-all-start = ((bf16[32,2,1152]{2,1,0:T(2,128)(2,1)}), bf16[32,2,1152]{2,1,0:T(2,128)(2,1)S(1)}, u32[]{:S(2)}, u32[]{:S(2)}) async-start(bf16[32,2,1152]{2,1,0:T(2,128)(2,1)} %get-tuple-element.33), calls=%async_computation | async-start | bytes 294912 | tf_op jit(solution)/shard_map/all_to_all | solution.py:640
  19.2 0.0 copy-done.7
  19.2 0.2 sqrt_multiply_fusion.coef_ref
  19.4 0.0 copy-done.8
  19.4 5.5 %gate.1 = (bf16[128,4608]{1,0:T(8,128)(2,1)}, f32[128,4608]{1,0:T(8,128)}) custom-call(bf16[128,4608]{1,0:T(8,128)(2,1)S(1)} %copy-done.4, bf16[9,2,4608]{2,1,0:T(2,128)(2,1)} %copy-done.5, f32[3,7,288]{2,1,0:T(8,128)S(1)} %copy-done.6, bf16[128,4608]{1,0:T(8,128)(2,1)} %get-tuple-element.35.u_ref, bf16[16,4608]{1,0:T(8,128)(2,1)S(1)} %get-tuple-element.36.head_ref, ...), custom_call_target="tpu_custom_call" | custom-call | flops 16515072 | bytes 3538944 | tf_op jit(solution)/shard_map/gate/pallas_call | solution.py:573
  24.9 0.0 copy-start.1
  24.9 2.3 %all-to-all-done.piece_ref = bf16[32,2,1152]{2,1,0:T(2,128)(2,1)S(1)} async-done(((bf16[32,2,1152]{2,1,0:T(2,128)(2,1)}), bf16[32,2,1152]{2,1,0:T(2,128)(2,1)S(1)}, u32[]{:S(2)}, u32[]{:S(2)}) %all-to-all-start) | async-done | bytes 147488 | tf_op jit(solution)/shard_map/all_to_all | solution.py:640
  27.2 0.9 %prefix.1 = bf16[32,2,1152]{2,1,0:T(2,128)(2,1)} custom-call(bf16[32,2,1152]{2,1,0:T(2,128)(2,1)S(1)} %all-to-all-done.piece_ref, f32[16,4608]{1,0:T(8,128)S(1)} %copy-done, f32[16,4608]{1,0:T(8,128)S(1)} %sqrt_multiply_fusion.coef_ref), custom_call_target="tpu_custom_call" | custom-call | tf_op jit(solution)/shard_map/prefix/pallas_call | solution.py:573
  28.2 3.6 %all-to-all-start.1 = ((bf16[32,2,1152]{2,1,0:T(2,128)(2,1)}), bf16[32,2,1152]{2,1,0:T(2,128)(2,1)S(1)}, u32[]{:S(2)}, u32[]{:S(2)}) async-start(bf16[32,2,1152]{2,1,0:T(2,128)(2,1)} %prefix.1), calls=%async_computation.1 | async-start | bytes 294912 | tf_op jit(solution)/shard_map/all_to_all | solution.py:640
  31.8 7.3 %within.1 = (f32[128,4608]{1,0:T(8,128)}, f32[128,512]{1,0:T(8,128)S(1)}, bf16[128,512]{1,0:T(8,128)(2,1)S(1)}) custom-call(bf16[128,4608]{1,0:T(8,128)(2,1)S(1)} %copy-done.1, bf16[16,4608]{1,0:T(8,128)(2,1)S(1)} %get-tuple-element.36.head_ref, f32[16,4608]{1,0:T(8,128)S(1)} %copy-done, ...), custom_call_target="tpu_custom_call", output_to_operand_aliasing={{0}: (6, {})} | custom-call | flops 29491200 | bytes 4718592 | tf_op jit(solution)/shard_map/within/pallas_call | solution.py:573
  39.1 0.7 %all-to-all-done.1.piece_ref = bf16[32,2,1152]{2,1,0:T(2,128)(2,1)S(1)} async-done(((bf16[32,2,1152]{2,1,0:T(2,128)(2,1)}), bf16[32,2,1152]{2,1,0:T(2,128)(2,1)S(1)}, u32[]{:S(2)}, u32[]{:S(2)}) %all-to-all-start.1) | async-done | bytes 147488 | tf_op jit(solution)/shard_map/all_to_all | solution.py:640
  39.8 4.9 %final.1 = bf16[128,4608]{1,0:T(8,128)(2,1)} custom-call(bf16[32,2,1152]{2,1,0:T(2,128)(2,1)S(1)} %all-to-all-done.1.piece_ref, f32[16,4608]{1,0:T(8,128)S(1)} %copy-done, f32[128,512]{1,0:T(8,128)S(1)} %get-tuple-element.48.y_last_ref, bf16[128,512]{1,0:T(8,128)(2,1)S(1)} %get-tuple-element.49.gate_last_ref, f32[128,4608]{1,0:T(8,128)} %get-tuple-element.50.y_ref, ...), custom_call_target="tpu_custom_call" | custom-call | flops 23592960 | bytes 5898240 | tf_op jit(solution)/shard_map/final/pallas_call | solution.py:573
  (9 shorter events, 0.0 us)
Async XLA Ops:
  0.0 5.2 %copy-start.3 = (bf16[128,4608]{1,0:T(8,128)(2,1)S(1)}, bf16[128,4608]{1,0:T(8,128)(2,1)}, u32[]{:S(2)}) copy-start(bf16[128,4608]{1,0:T(8,128)(2,1)} %value_ref.5) | copy-start | bytes 3538948
  0.0 5.2 %copy-start.2 = (bf16[128,4608]{1,0:T(8,128)(2,1)S(1)}, bf16[128,4608]{1,0:T(8,128)(2,1)}, u32[]{:S(2)}) copy-start(bf16[128,4608]{1,0:T(8,128)(2,1)} %key_ref.5) | copy-start | bytes 3538948
  0.0 5.3 %copy-start = (f32[16,4608]{1,0:T(8,128)S(1)}, f32[16,4608]{1,0:T(8,128)}, u32[]{:S(2)}) copy-start(f32[16,4608]{1,0:T(8,128)} %rate_ref.11) | copy-start | bytes 884740
  0.0 5.3 %copy-start.6 = (f32[3,7,288]{2,1,0:T(8,128)S(1)}, f32[3,7,288]{2,1,0:T(8,128)}, u32[]{:S(2)}) copy-start(f32[3,7,288]{2,1,0:T(8,128)} %feat_ref.3) | copy-start | bytes 72580
  1.3 11.8 %collective-permute-start = (bf16[9,2,4608]{2,1,0:T(2,128)(2,1)S(1)}, bf16[9,2,4608]{2,1,0:T(2,128)(2,1)S(1)}, u32[]{:S(2)}, u32[]{:S(2)}) collective-permute-start(bf16[9,2,4608]{2,1,0:T(2,128)(2,1)S(1)} %pack.1), channel_id=1, source_target_pairs={{0,1},{1,2},{2,3},{3,4},{4,5},{5,6},{6,7},{7,8},{8,9},{9,10},{10,1... | collective-permute-start | bytes 497672 | tf_op jit(solution)/shard_map/ppermute | solution.py:592
  13.1 1.5 %copy-start.5 = (bf16[9,2,4608]{2,1,0:T(2,128)(2,1)}, bf16[9,2,4608]{2,1,0:T(2,128)(2,1)S(1)}, u32[]{:S(2)}) copy-start(bf16[9,2,4608]{2,1,0:T(2,128)(2,1)S(1)} %collective-permute-done.halo_ref) | copy-start | bytes 497668
  13.1 6.0 %copy-start.7 = (f32[16,4608]{1,0:T(8,128)S(1)}, f32[16,4608]{1,0:T(8,128)}, u32[]{:S(2)}) copy-start(f32[16,4608]{1,0:T(8,128)} %param.12) | copy-start | bytes 884740
  13.1 6.2 %copy-start.8 = (f32[4608]{0:T(1024)S(1)}, f32[4608]{0:T(1024)}, u32[]{:S(2)}) copy-start(f32[4608]{0:T(1024)} %param.13) | copy-start | bytes 55300
  14.6 4.8 %copy-start.4 = (bf16[128,4608]{1,0:T(8,128)(2,1)S(1)}, bf16[128,4608]{1,0:T(8,128)(2,1)}, u32[]{:S(2)}) copy-start(bf16[128,4608]{1,0:T(8,128)(2,1)} %query_ref.3) | copy-start | bytes 3538948
  14.7 12.6 %all-to-all-start = ((bf16[32,2,1152]{2,1,0:T(2,128)(2,1)}), bf16[32,2,1152]{2,1,0:T(2,128)(2,1)S(1)}, u32[]{:S(2)}, u32[]{:S(2)}) async-start(bf16[32,2,1152]{2,1,0:T(2,128)(2,1)} %get-tuple-element.33), calls=%async_computation | async-start | bytes 294912 | tf_op jit(solution)/shard_map/all_to_all | solution.py:640
  24.9 6.8 %copy-start.1 = (bf16[128,4608]{1,0:T(8,128)(2,1)S(1)}, bf16[128,4608]{1,0:T(8,128)(2,1)}, u32[]{:S(2)}) copy-start(bf16[128,4608]{1,0:T(8,128)(2,1)} %get-tuple-element.35.u_ref) | copy-start | bytes 3538948
  28.2 11.7 %all-to-all-start.1 = ((bf16[32,2,1152]{2,1,0:T(2,128)(2,1)}), bf16[32,2,1152]{2,1,0:T(2,128)(2,1)S(1)}, u32[]{:S(2)}, u32[]{:S(2)}) async-start(bf16[32,2,1152]{2,1,0:T(2,128)(2,1)} %prefix.1), calls=%async_computation.1 | async-start | bytes 294912 | tf_op jit(solution)/shard_map/all_to_all | solution.py:640

commit v18 on v17

--- a/solution.py
+++ b/solution.py
@@ -299,12 +299,15 @@
     move.start()
     pieces, piece_modes, piece_width = out_ref.shape
 
+    lap = column_scr.shape[0]
+
     def some(chunk, _):
-        for number in range(TILES):
-            lanes = tile_lanes(chunk * TILES + number)
+        for number in range(lap):
+            lanes = tile_lanes(chunk * lap + number)
             parts = []
             for member in range(2):
-                taps = chunk_taps(wide_ref, chunk, member, number, reach + 1)
+                place = chunk * (lap // TILES) + number // TILES
+                taps = chunk_taps(wide_ref, place, member, number % TILES, reach + 1)
                 column = column_scr.at[number, member]
                 column[pl.ds(0, 2 * ROWS), :] = jnp.zeros((2 * ROWS, LANES), f32)
                 lay_halo(column, halo_ref, member, lanes)
@@ -323,7 +326,7 @@
             head_ref[:, lanes] = jnp.concatenate([u, jnp.zeros((ROWS, LANES), f32)], axis=0).astype(bf16)
         return 0
 
-    lax.fori_loop(0, tiles // TILES, some, 0)
+    lax.fori_loop(0, tiles // lap, some, 0)
     split = pieces * piece_modes // modes
     for piece in range(pieces):
         first, part = piece // split * piece_modes, piece % split
@@ -386,14 +389,10 @@
     coef = mine_of(coef_ref)
     through = jnp.exp(-float(tokens) * mine_of(rate_ref))
 
-    def lap(number, entering):
-        for step in range(4):
-            source = devices - 1 - (number * 4 + step)
-            out_ref[source] = (coef * entering).astype(out_ref.dtype)
-            entering = through * entering + piece_ref[source].astype(f32)
-        return entering
-
-    lax.fori_loop(0, devices // 4, lap, jnp.zeros((piece_modes, piece_width), f32))
+    entering = jnp.zeros((piece_modes, piece_width), f32)
+    for source in reversed(range(devices)):
+        out_ref[source] = (coef * entering).astype(out_ref.dtype)
+        entering = through * entering + piece_ref[source].astype(f32)
 
 
 def local_kernel(u_ref, head_ref, rate_ref, coef_ref, skip_ref, gate_ref, _, y_ref, y_last_ref, gate_last_ref, *scratches, first):
@@ -466,11 +465,13 @@
 
 def final_kernel(piece_ref, rate_ref, y_last_ref, gate_last_ref, y_ref, gate_ref, out_ref, *scratches, axes):
     y_buf, gate_buf, out_buf, total_scr, power_scr, in_sem, out_sem = scratches
+    pieces, piece_modes, piece_width = piece_ref.shape
     chunks, tokens = y_buf.shape[:2]
     modes = rate_ref.shape[0]
     fetch = columns_in(((y_ref, y_buf), (gate_ref, gate_buf)), in_sem)
     give = columns_out(out_ref, out_buf, out_sem)
     begin(chunks - 1, fetch)
+    split, piece_tiles = pieces * piece_modes // modes, piece_width // LANES
     bits = [(sublane() >> level) % 2 == 1 for level in range(3)]
     pairs = [slice(first, first + 2 * ROWS) for first in range(0, tokens, 2 * ROWS)]
 
@@ -486,13 +487,15 @@
 
         def tile(number):
             lanes = tile_lanes(number)
+            part, within = (at * TILES + number) // piece_tiles, (at * TILES + number) % piece_tiles
             state = []
             for mode in range(modes):
                 rows = [wide(power_scr[level, mode : mode + 1, lanes]) for level in range(3)]
                 lead = jnp.where(bits[0], rows[1], rows[0])
                 for bit, row in zip(bits[1:], rows[1:]):
                     lead = lead * jnp.where(bit, row, 1.0)
-                state.append(lead * wide(total_scr[mode : mode + 1, tile_lanes(at * TILES + number)]))
+                piece, row = mode // piece_modes * split + part, mode % piece_modes
+                state.append(lead * wide(total_scr[piece, row : row + 1, tile_lanes(within)]))
             decay = [wide(power_scr[3, mode : mode + 1, lanes]) for mode in range(modes)]
             for rows in pairs:
                 sums = []
@@ -533,12 +536,7 @@
 
     @pl.when(jnp.logical_not(first))
     def _():
-        pieces, piece_modes, piece_width = piece_ref.shape
-        split = pieces * piece_modes // modes
-        for piece in range(pieces):
-            row, part = piece // split * piece_modes, piece % split
-            lanes = slice(part * piece_width, (part + 1) * piece_width)
-            total_scr[row : row + piece_modes, lanes] = piece_ref[piece].astype(f32)
+        total_scr[...] = piece_ref[...].astype(f32)
         all_chunks(chunk)
 
     for at in range(chunks):
@@ -606,11 +604,12 @@
     )
 
     pieces = (devices, 2, width // split) if even else (modes // 2, 2, width)
+    lap = TILES * (3 if chunks % 3 == 0 else 1)
     left, head, u = call(
         functools.partial(head_kernel, tokens=tokens, reach=taps - 1),
         (key_proj, value_proj, halo, rates, wide_taps, state, u, u_far),
         [near(pieces, bf16), near((2 * ROWS, width), bf16), far((tokens, width), bf16)],
-        [vmem((TILES, 2, 3 * ROWS, LANES), f32), vmem((TILES, ROWS, LANES), f32)]
+        [vmem((lap, 2, 3 * ROWS, LANES), f32), vmem((lap, ROWS, LANES), f32)]
         + [vmem((modes, width), f32), dma((1,))],
         "head",
         close=range(7),
@@ -622,7 +621,7 @@
     stage = vmem((tokens // ROWS // 2 * ROWS * ROWS, LANES), f32)
     local_shapes = [far((tokens, width), f32)]
     local_scratches = [whole_buf, stage, stage, dma((1, chunks))]
-    early = chunks * 2 // 9
+    early = chunks // 9
     gate, y = call(
         functools.partial(gate_kernel, early=early),
         (query, halo_late, featurizer, u, head, rates, coef, skip_row),
@@ -679,7 +678,7 @@
         functools.partial(final_kernel, axes=axes),
         (entered, rates, y_last, gate_last, y, gate),
         [far((tokens, width), bf16)],
-        [whole_buf, half_buf, half_buf, vmem((modes, width), f32), vmem((4, modes, CHUNK), f32)]
+        [whole_buf, half_buf, half_buf, vmem(pieces, f32), vmem((4, modes, CHUNK), f32)]
         + [dma((2, chunks)), dma((1, chunks))],
         "final",
         close=range(4),

time: 45.1 us -> 44.6 us (0.989)
  starting transfers between devices: 12 us -> 11.4 us
    all_to_all x2, starting transfers between devices: 8.08 us -> 7.46 us  [swap(): lax.all_to_all(value, axes, split_axis=0, concat_axis=0, axis_index_group...]
  transfers between devices with their start and end apart: 3 -> 3, of which waited for: 3 -> 2; matrix products, arithmetic and copies ran while one was open for 0% -> 0% of each run, Pallas kernels for 43% -> 44%
where the time goes in v18:
time: 44.6 us; the launch traced here: 44.3 us
  Pallas kernels  28 us (63%)
  starting transfers between devices  11.4 us (26%)
  waiting for transfers between devices  4.46 us (10%)
    pallas_call x7, Pallas kernels, call(): pl.pallas_call(kernel, in_specs=[beside if at in close else there for at...  28 us
    all_to_all x2, starting transfers between devices, swap(): lax.all_to_all(value, axes, split_axis=0, concat_axis=0, axis_index_group...  7.46 us
    ppermute x1, starting transfers between devices, local(): lax.ppermute(packed, axes, [(at, at + 1) for at in range(devices - 1)])  3.95 us
    all_to_all x2, waiting for transfers between devices, swap(): lax.all_to_all(value, axes, split_axis=0, concat_axis=0, axis_index_group...  3.28 us
    ppermute x1, waiting for transfers between devices, local(): lax.ppermute(packed, axes, [(at, at + 1) for at in range(devices - 1)])  1.18 us
  transfers between devices with their start and end apart: 3, of which 2 were waited for; matrix products, arithmetic and copies ran while one was open for 0% of the time, Pallas kernels for 44%

profile of v18, /device:TPU:1, one launch (start us, length us, event | category | flops | bytes accessed | tf_op | source)
XLA Modules:
  0.0 44.3 jit_solution(2763426250677418737)
XLA Ops:
  0.0 0.0 copy-start.6
  0.0 1.3 %pack.1 = bf16[9,2,4608]{2,1,0:T(2,128)(2,1)S(1)} custom-call(bf16[128,4608]{1,0:T(8,128)(2,1)} %key_ref.5, bf16[128,4608]{1,0:T(8,128)(2,1)} %value_ref.5, bf16[128,4608]{1,0:T(8,128)(2,1)} %query_ref.3), custom_call_target="tpu_custom_call" | custom-call | tf_op jit(solution)/shard_map/pack/pallas_call | solution.py:571
  1.3 3.9 %collective-permute-start = (bf16[9,2,4608]{2,1,0:T(2,128)(2,1)S(1)}, bf16[9,2,4608]{2,1,0:T(2,128)(2,1)S(1)}, u32[]{:S(2)}, u32[]{:S(2)}) collective-permute-start(bf16[9,2,4608]{2,1,0:T(2,128)(2,1)S(1)} %pack.1), channel_id=1, source_target_pairs={{0,1},{1,2},{2,3},{3,4},{4,5},{5,6},{6,7},{7,8},{8,9},{9,10},{10,1... | collective-permute-start | bytes 497672 | tf_op jit(solution)/shard_map/ppermute | solution.py:590
  5.2 0.0 copy-done.3
  5.2 0.0 copy-done.2
  5.3 0.0 copy-done
  5.3 0.0 copy-done.6
  5.3 6.7 %signal.1 = (bf16[128,4608]{1,0:T(8,128)(2,1)S(1)}, bf16[128,4608]{1,0:T(8,128)(2,1)}, f32[9,2,8,512]{3,2,1,0:T(8,128)S(1)}, f32[16,4608]{1,0:T(8,128)S(1)}) custom-call(bf16[128,4608]{1,0:T(8,128)(2,1)S(1)} %copy-done.2, bf16[128,4608]{1,0:T(8,128)(2,1)S(1)} %copy-done.3, f32[3,7,288]{2,1,0:T(8,128)S(1)} %copy-done.6, f32[16,4608]{1,0:T(8,128)S(1)} %copy-done), custom_call_target="tpu_custom_call" | custom-call | flops 35389440 | bytes 5898240 | tf_op jit(solution)/shard_map/signal/pallas_call | solution.py:571
  11.9 1.2 %collective-permute-done.halo_ref = bf16[9,2,4608]{2,1,0:T(2,128)(2,1)S(1)} collective-permute-done((bf16[9,2,4608]{2,1,0:T(2,128)(2,1)S(1)}, bf16[9,2,4608]{2,1,0:T(2,128)(2,1)S(1)}, u32[]{:S(2)}, u32[]{:S(2)}) %collective-permute-start) | collective-permute-done | bytes 165920 | tf_op jit(solution)/shard_map/ppermute | solution.py:590
  13.1 1.4 %head.1 = (bf16[32,2,1152]{2,1,0:T(2,128)(2,1)}, bf16[16,4608]{1,0:T(8,128)(2,1)S(1)}, bf16[128,4608]{1,0:T(8,128)(2,1)}) custom-call(bf16[128,4608]{1,0:T(8,128)(2,1)S(1)} %copy-done.2, bf16[128,4608]{1,0:T(8,128)(2,1)S(1)} %copy-done.3, bf16[9,2,4608]{2,1,0:T(2,128)(2,1)S(1)} %collective-permute-done.halo_ref, ...), custom_call_target="tpu_custom_call", output_to_operand_aliasing={{2}: (7, {})} | custom-call | tf_op jit(solution)/shard_map/head/pallas_call | solution.py:571
  14.5 0.0 copy-done.5
  14.5 0.0 copy-start.4
  14.5 4.5 %all-to-all-start = ((bf16[32,2,1152]{2,1,0:T(2,128)(2,1)}), bf16[32,2,1152]{2,1,0:T(2,128)(2,1)S(1)}, u32[]{:S(2)}, u32[]{:S(2)}) async-start(bf16[32,2,1152]{2,1,0:T(2,128)(2,1)} %get-tuple-element.33), calls=%async_computation | async-start | bytes 294912 | tf_op jit(solution)/shard_map/all_to_all | solution.py:639
  19.1 0.0 copy-done.7
  19.1 0.2 sqrt_multiply_fusion.coef_ref
  19.3 0.0 copy-done.4
  19.3 4.5 %gate.1 = (bf16[128,4608]{1,0:T(8,128)(2,1)}, f32[128,4608]{1,0:T(8,128)}) custom-call(bf16[128,4608]{1,0:T(8,128)(2,1)S(1)} %copy-done.4, bf16[9,2,4608]{2,1,0:T(2,128)(2,1)} %copy-done.5, f32[3,7,288]{2,1,0:T(8,128)S(1)} %copy-done.6, bf16[128,4608]{1,0:T(8,128)(2,1)} %get-tuple-element.35.u_ref, bf16[16,4608]{1,0:T(8,128)(2,1)S(1)} %get-tuple-element.36.head_ref, ...), custom_call_target="tpu_custom_call" | custom-call | flops 16515072 | bytes 3538944 | tf_op jit(solution)/shard_map/gate/pallas_call | solution.py:571
  23.8 0.0 copy-start.1
  23.8 3.3 %all-to-all-done.piece_ref = bf16[32,2,1152]{2,1,0:T(2,128)(2,1)S(1)} async-done(((bf16[32,2,1152]{2,1,0:T(2,128)(2,1)}), bf16[32,2,1152]{2,1,0:T(2,128)(2,1)S(1)}, u32[]{:S(2)}, u32[]{:S(2)}) %all-to-all-start) | async-done | bytes 147488 | tf_op jit(solution)/shard_map/all_to_all | solution.py:639
  27.1 0.9 %prefix.1 = bf16[32,2,1152]{2,1,0:T(2,128)(2,1)} custom-call(bf16[32,2,1152]{2,1,0:T(2,128)(2,1)S(1)} %all-to-all-done.piece_ref, f32[16,4608]{1,0:T(8,128)S(1)} %copy-done, f32[16,4608]{1,0:T(8,128)S(1)} %sqrt_multiply_fusion.coef_ref), custom_call_target="tpu_custom_call" | custom-call | tf_op jit(solution)/shard_map/prefix/pallas_call | solution.py:571
  28.0 3.0 %all-to-all-start.1 = ((bf16[32,2,1152]{2,1,0:T(2,128)(2,1)}), bf16[32,2,1152]{2,1,0:T(2,128)(2,1)S(1)}, u32[]{:S(2)}, u32[]{:S(2)}) async-start(bf16[32,2,1152]{2,1,0:T(2,128)(2,1)} %prefix.1), calls=%async_computation.1 | async-start | bytes 294912 | tf_op jit(solution)/shard_map/all_to_all | solution.py:639
  31.0 8.3 %within.1 = (f32[128,4608]{1,0:T(8,128)}, f32[128,512]{1,0:T(8,128)S(1)}, bf16[128,512]{1,0:T(8,128)(2,1)S(1)}) custom-call(bf16[128,4608]{1,0:T(8,128)(2,1)S(1)} %copy-done.1, bf16[16,4608]{1,0:T(8,128)(2,1)S(1)} %get-tuple-element.36.head_ref, f32[16,4608]{1,0:T(8,128)S(1)} %copy-done, ...), custom_call_target="tpu_custom_call", output_to_operand_aliasing={{0}: (6, {})} | custom-call | flops 29491200 | bytes 4718592 | tf_op jit(solution)/shard_map/within/pallas_call | solution.py:571
  39.3 0.0 all-to-all-done.1.piece_ref
  39.4 5.0 %final.1 = bf16[128,4608]{1,0:T(8,128)(2,1)} custom-call(bf16[32,2,1152]{2,1,0:T(2,128)(2,1)S(1)} %all-to-all-done.1.piece_ref, f32[16,4608]{1,0:T(8,128)S(1)} %copy-done, f32[128,512]{1,0:T(8,128)S(1)} %get-tuple-element.48.y_last_ref, bf16[128,512]{1,0:T(8,128)(2,1)S(1)} %get-tuple-element.49.gate_last_ref, f32[128,4608]{1,0:T(8,128)} %get-tuple-element.50.y_ref, ...), custom_call_target="tpu_custom_call" | custom-call | flops 23592960 | bytes 5898240 | tf_op jit(solution)/shard_map/final/pallas_call | solution.py:571
  (9 shorter events, 0.0 us)
Async XLA Ops:
  0.0 5.2 %copy-start.3 = (bf16[128,4608]{1,0:T(8,128)(2,1)S(1)}, bf16[128,4608]{1,0:T(8,128)(2,1)}, u32[]{:S(2)}) copy-start(bf16[128,4608]{1,0:T(8,128)(2,1)} %value_ref.5) | copy-start | bytes 3538948
  0.0 5.2 %copy-start.2 = (bf16[128,4608]{1,0:T(8,128)(2,1)S(1)}, bf16[128,4608]{1,0:T(8,128)(2,1)}, u32[]{:S(2)}) copy-start(bf16[128,4608]{1,0:T(8,128)(2,1)} %key_ref.5) | copy-start | bytes 3538948
  0.0 5.3 %copy-start = (f32[16,4608]{1,0:T(8,128)S(1)}, f32[16,4608]{1,0:T(8,128)}, u32[]{:S(2)}) copy-start(f32[16,4608]{1,0:T(8,128)} %rate_ref.11) | copy-start | bytes 884740
  0.0 5.3 %copy-start.6 = (f32[3,7,288]{2,1,0:T(8,128)S(1)}, f32[3,7,288]{2,1,0:T(8,128)}, u32[]{:S(2)}) copy-start(f32[3,7,288]{2,1,0:T(8,128)} %feat_ref.3) | copy-start | bytes 72580
  1.3 11.8 %collective-permute-start = (bf16[9,2,4608]{2,1,0:T(2,128)(2,1)S(1)}, bf16[9,2,4608]{2,1,0:T(2,128)(2,1)S(1)}, u32[]{:S(2)}, u32[]{:S(2)}) collective-permute-start(bf16[9,2,4608]{2,1,0:T(2,128)(2,1)S(1)} %pack.1), channel_id=1, source_target_pairs={{0,1},{1,2},{2,3},{3,4},{4,5},{5,6},{6,7},{7,8},{8,9},{9,10},{10,1... | collective-permute-start | bytes 497672 | tf_op jit(solution)/shard_map/ppermute | solution.py:590
  13.1 1.4 %copy-start.5 = (bf16[9,2,4608]{2,1,0:T(2,128)(2,1)}, bf16[9,2,4608]{2,1,0:T(2,128)(2,1)S(1)}, u32[]{:S(2)}) copy-start(bf16[9,2,4608]{2,1,0:T(2,128)(2,1)S(1)} %collective-permute-done.halo_ref) | copy-start | bytes 497668
  13.1 5.9 %copy-start.7 = (f32[16,4608]{1,0:T(8,128)S(1)}, f32[16,4608]{1,0:T(8,128)}, u32[]{:S(2)}) copy-start(f32[16,4608]{1,0:T(8,128)} %param.12) | copy-start | bytes 884740
  13.1 6.1 %copy-start.8 = (f32[4608]{0:T(1024)S(1)}, f32[4608]{0:T(1024)}, u32[]{:S(2)}) copy-start(f32[4608]{0:T(1024)} %param.13) | copy-start | bytes 55300
  14.5 4.8 %copy-start.4 = (bf16[128,4608]{1,0:T(8,128)(2,1)S(1)}, bf16[128,4608]{1,0:T(8,128)(2,1)}, u32[]{:S(2)}) copy-start(bf16[128,4608]{1,0:T(8,128)(2,1)} %query_ref.3) | copy-start | bytes 3538948
  14.5 12.6 %all-to-all-start = ((bf16[32,2,1152]{2,1,0:T(2,128)(2,1)}), bf16[32,2,1152]{2,1,0:T(2,128)(2,1)S(1)}, u32[]{:S(2)}, u32[]{:S(2)}) async-start(bf16[32,2,1152]{2,1,0:T(2,128)(2,1)} %get-tuple-element.33), calls=%async_computation | async-start | bytes 294912 | tf_op jit(solution)/shard_map/all_to_all | solution.py:639
  23.8 7.2 %copy-start.1 = (bf16[128,4608]{1,0:T(8,128)(2,1)S(1)}, bf16[128,4608]{1,0:T(8,128)(2,1)}, u32[]{:S(2)}) copy-start(bf16[128,4608]{1,0:T(8,128)(2,1)} %get-tuple-element.35.u_ref) | copy-start | bytes 3538948
  28.0 11.3 %all-to-all-start.1 = ((bf16[32,2,1152]{2,1,0:T(2,128)(2,1)}), bf16[32,2,1152]{2,1,0:T(2,128)(2,1)S(1)}, u32[]{:S(2)}, u32[]{:S(2)}) async-start(bf16[32,2,1152]{2,1,0:T(2,128)(2,1)} %prefix.1), calls=%async_computation.1 | async-start | bytes 294912 | tf_op jit(solution)/shard_map/all_to_all | solution.py:639

commit v19 on v18

--- a/solution.py
+++ b/solution.py
@@ -475,11 +475,10 @@
     bits = [(sublane() >> level) % 2 == 1 for level in range(3)]
     pairs = [slice(first, first + 2 * ROWS) for first in range(0, tokens, 2 * ROWS)]
 
-    def finish(at, rows, lanes, sums):
-        gates = gate_buf[at, rows, lanes].astype(f32)
-        out_buf[at, rows, lanes] = (gates * rounded(sums)).astype(bf16)
-
-    def chunk(at):
+    def finish(at, gates, rows, lanes, sums):
+        out_buf[at, rows, lanes] = gates[rows, lanes] * sums.astype(bf16)
+
+    def chunk(at, y, gates):
         through = jnp.exp(-rate_ref[:, span(at)])
         for level in range(4):
             power_scr[level] = through
@@ -500,9 +499,9 @@
             for rows in pairs:
                 sums = []
                 for first in (rows.start, rows.start + ROWS):
-                    sums.append(y_buf[at, first : first + ROWS, lanes] + tree(state))
+                    sums.append(y[first : first + ROWS, lanes] + tree(state))
                     state = [factor * one for factor, one in zip(decay, state)]
-                finish(at, rows, lanes, jnp.concatenate(sums, axis=0))
+                finish(at, gates, rows, lanes, jnp.concatenate(sums, axis=0))
 
         def some(number, _):
             for part in range(LAP):
@@ -511,22 +510,20 @@
 
         lax.fori_loop(0, TILES // LAP, some, 0)
 
-    def chunk_alone(at):
+    def chunk_alone(at, y, gates):
         def tile(number, _):
             lanes = tile_lanes(number)
             for rows in pairs:
-                finish(at, rows, lanes, y_buf[at, rows, lanes])
+                finish(at, gates, rows, lanes, y[rows, lanes])
             return 0
 
         lax.fori_loop(0, TILES, tile, 0)
 
     def all_chunks(body):
         last = chunks - 1
-        y_buf[last] = y_last_ref[...]
-        gate_buf[last] = gate_last_ref[...]
-        body(last)
+        body(last, y_last_ref, gate_last_ref)
         start_all(give(last))
-        over_chunks(0, last, with_fetch(last, fetch, body), give)
+        over_chunks(0, last, with_fetch(last, fetch, lambda at: body(at, y_buf.at[at], gate_buf.at[at])), give)
 
     first = lax.axis_index(axes) == 0
 

time: 44.6 us -> 44.5 us (level)
  no operation moved by 1% of the time
where the time goes in v19:
time: 44.5 us; the launch traced here: 44.1 us
  Pallas kernels  27.8 us (62%)
  starting transfers between devices  11.4 us (26%)
  waiting for transfers between devices  4.46 us (10%)
    pallas_call x7, Pallas kernels, call(): pl.pallas_call(kernel, in_specs=[beside if at in close else there for at...  27.8 us
    all_to_all x2, starting transfers between devices, swap(): lax.all_to_all(value, axes, split_axis=0, concat_axis=0, axis_index_group...  7.46 us
    ppermute x1, starting transfers between devices, local(): lax.ppermute(packed, axes, [(at, at + 1) for at in range(devices - 1)])  3.95 us
    all_to_all x2, waiting for transfers between devices, swap(): lax.all_to_all(value, axes, split_axis=0, concat_axis=0, axis_index_group...  3.28 us
    ppermute x1, waiting for transfers between devices, local(): lax.ppermute(packed, axes, [(at, at + 1) for at in range(devices - 1)])  1.18 us
  transfers between devices with their start and end apart: 3, of which 2 were waited for; matrix products, arithmetic and copies ran while one was open for 0% of the time, Pallas kernels for 44%

profile of v19, /device:TPU:1, one launch (start us, length us, event | category | flops | bytes accessed | tf_op | source)
XLA Modules:
  0.0 44.1 jit_solution(492922233715250323)
XLA Ops:
  0.0 0.0 copy-start.6
  0.0 1.3 %pack.1 = bf16[9,2,4608]{2,1,0:T(2,128)(2,1)S(1)} custom-call(bf16[128,4608]{1,0:T(8,128)(2,1)} %key_ref.5, bf16[128,4608]{1,0:T(8,128)(2,1)} %value_ref.5, bf16[128,4608]{1,0:T(8,128)(2,1)} %query_ref.3), custom_call_target="tpu_custom_call" | custom-call | tf_op jit(solution)/shard_map/pack/pallas_call | solution.py:568
  1.3 3.9 %collective-permute-start = (bf16[9,2,4608]{2,1,0:T(2,128)(2,1)S(1)}, bf16[9,2,4608]{2,1,0:T(2,128)(2,1)S(1)}, u32[]{:S(2)}, u32[]{:S(2)}) collective-permute-start(bf16[9,2,4608]{2,1,0:T(2,128)(2,1)S(1)} %pack.1), channel_id=1, source_target_pairs={{0,1},{1,2},{2,3},{3,4},{4,5},{5,6},{6,7},{7,8},{8,9},{9,10},{10,1... | collective-permute-start | bytes 497672 | tf_op jit(solution)/shard_map/ppermute | solution.py:587
  5.2 0.0 copy-done.3
  5.2 0.0 copy-done.2
  5.3 0.0 copy-done
  5.3 0.0 copy-done.6
  5.3 6.7 %signal.1 = (bf16[128,4608]{1,0:T(8,128)(2,1)S(1)}, bf16[128,4608]{1,0:T(8,128)(2,1)}, f32[9,2,8,512]{3,2,1,0:T(8,128)S(1)}, f32[16,4608]{1,0:T(8,128)S(1)}) custom-call(bf16[128,4608]{1,0:T(8,128)(2,1)S(1)} %copy-done.2, bf16[128,4608]{1,0:T(8,128)(2,1)S(1)} %copy-done.3, f32[3,7,288]{2,1,0:T(8,128)S(1)} %copy-done.6, f32[16,4608]{1,0:T(8,128)S(1)} %copy-done), custom_call_target="tpu_custom_call" | custom-call | flops 35389440 | bytes 5898240 | tf_op jit(solution)/shard_map/signal/pallas_call | solution.py:568
  11.9 1.2 %collective-permute-done.halo_ref = bf16[9,2,4608]{2,1,0:T(2,128)(2,1)S(1)} collective-permute-done((bf16[9,2,4608]{2,1,0:T(2,128)(2,1)S(1)}, bf16[9,2,4608]{2,1,0:T(2,128)(2,1)S(1)}, u32[]{:S(2)}, u32[]{:S(2)}) %collective-permute-start) | collective-permute-done | bytes 165920 | tf_op jit(solution)/shard_map/ppermute | solution.py:587
  13.1 1.4 %head.1 = (bf16[32,2,1152]{2,1,0:T(2,128)(2,1)}, bf16[16,4608]{1,0:T(8,128)(2,1)S(1)}, bf16[128,4608]{1,0:T(8,128)(2,1)}) custom-call(bf16[128,4608]{1,0:T(8,128)(2,1)S(1)} %copy-done.2, bf16[128,4608]{1,0:T(8,128)(2,1)S(1)} %copy-done.3, bf16[9,2,4608]{2,1,0:T(2,128)(2,1)S(1)} %collective-permute-done.halo_ref, ...), custom_call_target="tpu_custom_call", output_to_operand_aliasing={{2}: (7, {})} | custom-call | tf_op jit(solution)/shard_map/head/pallas_call | solution.py:568
  14.5 0.0 copy-done.5
  14.5 0.0 copy-start.4
  14.5 4.5 %all-to-all-start = ((bf16[32,2,1152]{2,1,0:T(2,128)(2,1)}), bf16[32,2,1152]{2,1,0:T(2,128)(2,1)S(1)}, u32[]{:S(2)}, u32[]{:S(2)}) async-start(bf16[32,2,1152]{2,1,0:T(2,128)(2,1)} %get-tuple-element.33), calls=%async_computation | async-start | bytes 294912 | tf_op jit(solution)/shard_map/all_to_all | solution.py:636
  19.1 0.0 copy-done.7
  19.1 0.2 sqrt_multiply_fusion.coef_ref
  19.3 0.0 copy-done.4
  19.3 4.5 %gate.1 = (bf16[128,4608]{1,0:T(8,128)(2,1)}, f32[128,4608]{1,0:T(8,128)}) custom-call(bf16[128,4608]{1,0:T(8,128)(2,1)S(1)} %copy-done.4, bf16[9,2,4608]{2,1,0:T(2,128)(2,1)} %copy-done.5, f32[3,7,288]{2,1,0:T(8,128)S(1)} %copy-done.6, bf16[128,4608]{1,0:T(8,128)(2,1)} %get-tuple-element.35.u_ref, bf16[16,4608]{1,0:T(8,128)(2,1)S(1)} %get-tuple-element.36.head_ref, ...), custom_call_target="tpu_custom_call" | custom-call | flops 16515072 | bytes 3538944 | tf_op jit(solution)/shard_map/gate/pallas_call | solution.py:568
  23.8 0.0 copy-start.1
  23.8 3.3 %all-to-all-done.piece_ref = bf16[32,2,1152]{2,1,0:T(2,128)(2,1)S(1)} async-done(((bf16[32,2,1152]{2,1,0:T(2,128)(2,1)}), bf16[32,2,1152]{2,1,0:T(2,128)(2,1)S(1)}, u32[]{:S(2)}, u32[]{:S(2)}) %all-to-all-start) | async-done | bytes 147488 | tf_op jit(solution)/shard_map/all_to_all | solution.py:636
  27.1 0.9 %prefix.1 = bf16[32,2,1152]{2,1,0:T(2,128)(2,1)} custom-call(bf16[32,2,1152]{2,1,0:T(2,128)(2,1)S(1)} %all-to-all-done.piece_ref, f32[16,4608]{1,0:T(8,128)S(1)} %copy-done, f32[16,4608]{1,0:T(8,128)S(1)} %sqrt_multiply_fusion.coef_ref), custom_call_target="tpu_custom_call" | custom-call | tf_op jit(solution)/shard_map/prefix/pallas_call | solution.py:568
  28.0 3.0 %all-to-all-start.1 = ((bf16[32,2,1152]{2,1,0:T(2,128)(2,1)}), bf16[32,2,1152]{2,1,0:T(2,128)(2,1)S(1)}, u32[]{:S(2)}, u32[]{:S(2)}) async-start(bf16[32,2,1152]{2,1,0:T(2,128)(2,1)} %prefix.1), calls=%async_computation.1 | async-start | bytes 294912 | tf_op jit(solution)/shard_map/all_to_all | solution.py:636
  31.0 8.3 %within.1 = (f32[128,4608]{1,0:T(8,128)}, f32[128,512]{1,0:T(8,128)S(1)}, bf16[128,512]{1,0:T(8,128)(2,1)S(1)}) custom-call(bf16[128,4608]{1,0:T(8,128)(2,1)S(1)} %copy-done.1, bf16[16,4608]{1,0:T(8,128)(2,1)S(1)} %get-tuple-element.36.head_ref, f32[16,4608]{1,0:T(8,128)S(1)} %copy-done, ...), custom_call_target="tpu_custom_call", output_to_operand_aliasing={{0}: (6, {})} | custom-call | flops 29491200 | bytes 4718592 | tf_op jit(solution)/shard_map/within/pallas_call | solution.py:568
  39.3 0.0 all-to-all-done.1.piece_ref
  39.4 4.8 %final.1 = bf16[128,4608]{1,0:T(8,128)(2,1)} custom-call(bf16[32,2,1152]{2,1,0:T(2,128)(2,1)S(1)} %all-to-all-done.1.piece_ref, f32[16,4608]{1,0:T(8,128)S(1)} %copy-done, f32[128,512]{1,0:T(8,128)S(1)} %get-tuple-element.48.y_last_ref, bf16[128,512]{1,0:T(8,128)(2,1)S(1)} %get-tuple-element.49.gate_last_ref, f32[128,4608]{1,0:T(8,128)} %get-tuple-element.50.y_ref, ...), custom_call_target="tpu_custom_call" | custom-call | flops 23592960 | bytes 5898240 | tf_op jit(solution)/shard_map/final/pallas_call | solution.py:568
  (9 shorter events, 0.0 us)
Async XLA Ops:
  0.0 5.2 %copy-start.3 = (bf16[128,4608]{1,0:T(8,128)(2,1)S(1)}, bf16[128,4608]{1,0:T(8,128)(2,1)}, u32[]{:S(2)}) copy-start(bf16[128,4608]{1,0:T(8,128)(2,1)} %value_ref.5) | copy-start | bytes 3538948
  0.0 5.2 %copy-start.2 = (bf16[128,4608]{1,0:T(8,128)(2,1)S(1)}, bf16[128,4608]{1,0:T(8,128)(2,1)}, u32[]{:S(2)}) copy-start(bf16[128,4608]{1,0:T(8,128)(2,1)} %key_ref.5) | copy-start | bytes 3538948
  0.0 5.3 %copy-start = (f32[16,4608]{1,0:T(8,128)S(1)}, f32[16,4608]{1,0:T(8,128)}, u32[]{:S(2)}) copy-start(f32[16,4608]{1,0:T(8,128)} %rate_ref.11) | copy-start | bytes 884740
  0.0 5.3 %copy-start.6 = (f32[3,7,288]{2,1,0:T(8,128)S(1)}, f32[3,7,288]{2,1,0:T(8,128)}, u32[]{:S(2)}) copy-start(f32[3,7,288]{2,1,0:T(8,128)} %feat_ref.3) | copy-start | bytes 72580
  1.3 11.8 %collective-permute-start = (bf16[9,2,4608]{2,1,0:T(2,128)(2,1)S(1)}, bf16[9,2,4608]{2,1,0:T(2,128)(2,1)S(1)}, u32[]{:S(2)}, u32[]{:S(2)}) collective-permute-start(bf16[9,2,4608]{2,1,0:T(2,128)(2,1)S(1)} %pack.1), channel_id=1, source_target_pairs={{0,1},{1,2},{2,3},{3,4},{4,5},{5,6},{6,7},{7,8},{8,9},{9,10},{10,1... | collective-permute-start | bytes 497672 | tf_op jit(solution)/shard_map/ppermute | solution.py:587
  13.1 1.4 %copy-start.5 = (bf16[9,2,4608]{2,1,0:T(2,128)(2,1)}, bf16[9,2,4608]{2,1,0:T(2,128)(2,1)S(1)}, u32[]{:S(2)}) copy-start(bf16[9,2,4608]{2,1,0:T(2,128)(2,1)S(1)} %collective-permute-done.halo_ref) | copy-start | bytes 497668
  13.1 5.9 %copy-start.7 = (f32[16,4608]{1,0:T(8,128)S(1)}, f32[16,4608]{1,0:T(8,128)}, u32[]{:S(2)}) copy-start(f32[16,4608]{1,0:T(8,128)} %param.12) | copy-start | bytes 884740
  13.1 6.1 %copy-start.8 = (f32[4608]{0:T(1024)S(1)}, f32[4608]{0:T(1024)}, u32[]{:S(2)}) copy-start(f32[4608]{0:T(1024)} %param.13) | copy-start | bytes 55300
  14.5 4.8 %copy-start.4 = (bf16[128,4608]{1,0:T(8,128)(2,1)S(1)}, bf16[128,4608]{1,0:T(8,128)(2,1)}, u32[]{:S(2)}) copy-start(bf16[128,4608]{1,0:T(8,128)(2,1)} %query_ref.3) | copy-start | bytes 3538948
  14.5 12.6 %all-to-all-start = ((bf16[32,2,1152]{2,1,0:T(2,128)(2,1)}), bf16[32,2,1152]{2,1,0:T(2,128)(2,1)S(1)}, u32[]{:S(2)}, u32[]{:S(2)}) async-start(bf16[32,2,1152]{2,1,0:T(2,128)(2,1)} %get-tuple-element.33), calls=%async_computation | async-start | bytes 294912 | tf_op jit(solution)/shard_map/all_to_all | solution.py:636
  23.8 7.2 %copy-start.1 = (bf16[128,4608]{1,0:T(8,128)(2,1)S(1)}, bf16[128,4608]{1,0:T(8,128)(2,1)}, u32[]{:S(2)}) copy-start(bf16[128,4608]{1,0:T(8,128)(2,1)} %get-tuple-element.35.u_ref) | copy-start | bytes 3538948
  28.0 11.3 %all-to-all-start.1 = ((bf16[32,2,1152]{2,1,0:T(2,128)(2,1)}), bf16[32,2,1152]{2,1,0:T(2,128)(2,1)S(1)}, u32[]{:S(2)}, u32[]{:S(2)}) async-start(bf16[32,2,1152]{2,1,0:T(2,128)(2,1)} %prefix.1), calls=%async_computation.1 | async-start | bytes 294912 | tf_op jit(solution)/shard_map/all_to_all | solution.py:636

commit v20 on v19

--- a/solution.py
+++ b/solution.py
@@ -203,6 +203,15 @@
         column[pl.ds(2 * ROWS - 2 * pairs + 2 * pair, 2), :] = halo[member * pairs + pair, :, lanes].astype(f32)
 
 
+def decay_powers(rate_ref, power_scr):
+    for first in range(0, rate_ref.shape[1], CHUNK):
+        lanes = slice(first, first + CHUNK)
+        through = jnp.exp(-rate_ref[:, lanes])
+        for level in range(power_scr.shape[0]):
+            power_scr[level, :, lanes] = through
+            through = through * through
+
+
 def pack_kernel(key_ref, value_ref, query_ref, out_ref, in_buf, in_sem):
     tokens = key_ref.shape[0]
     copies = [
@@ -230,14 +239,7 @@
         column[pl.ds(0, 2 * ROWS), :] = jnp.zeros((2 * ROWS, LANES), f32)
     last_scr[...] = jnp.zeros(last_scr.shape, f32)
 
-    def powers(at, _):
-        through = jnp.exp(-rate_ref[:, span(at)])
-        for level in range(4):
-            power_scr[level, :, span(at)] = through
-            through = through * through
-        return 0
-
-    lax.fori_loop(0, chunks, powers, 0)
+    decay_powers(rate_ref, power_scr)
 
     def reduce(number):
         lanes = tile_lanes(number)
@@ -479,23 +481,18 @@
         out_buf[at, rows, lanes] = gates[rows, lanes] * sums.astype(bf16)
 
     def chunk(at, y, gates):
-        through = jnp.exp(-rate_ref[:, span(at)])
-        for level in range(4):
-            power_scr[level] = through
-            through = through * through
-
         def tile(number):
-            lanes = tile_lanes(number)
+            lanes, all_lanes = tile_lanes(number), tile_lanes(at * TILES + number)
             part, within = (at * TILES + number) // piece_tiles, (at * TILES + number) % piece_tiles
             state = []
             for mode in range(modes):
-                rows = [wide(power_scr[level, mode : mode + 1, lanes]) for level in range(3)]
+                rows = [wide(power_scr[level, mode : mode + 1, all_lanes]) for level in range(3)]
                 lead = jnp.where(bits[0], rows[1], rows[0])
                 for bit, row in zip(bits[1:], rows[1:]):
                     lead = lead * jnp.where(bit, row, 1.0)
                 piece, row = mode // piece_modes * split + part, mode % piece_modes
                 state.append(lead * wide(total_scr[piece, row : row + 1, tile_lanes(within)]))
-            decay = [wide(power_scr[3, mode : mode + 1, lanes]) for mode in range(modes)]
+            decay = [wide(power_scr[3, mode : mode + 1, all_lanes]) for mode in range(modes)]
             for rows in pairs:
                 sums = []
                 for first in (rows.start, rows.start + ROWS):
@@ -533,6 +530,7 @@
 
     @pl.when(jnp.logical_not(first))
     def _():
+        decay_powers(rate_ref, power_scr)
         total_scr[...] = piece_ref[...].astype(f32)
         all_chunks(chunk)
 
@@ -675,7 +673,7 @@
         functools.partial(final_kernel, axes=axes),
         (entered, rates, y_last, gate_last, y, gate),
         [far((tokens, width), bf16)],
-        [whole_buf, half_buf, half_buf, vmem(pieces, f32), vmem((4, modes, CHUNK), f32)]
+        [whole_buf, half_buf, half_buf, vmem(pieces, f32), vmem((4, modes, width), f32)]
         + [dma((2, chunks)), dma((1, chunks))],
         "final",
         close=range(4),

time: 44.5 us -> 44.2 us (level)
  no operation moved by 1% of the time
where the time goes in v20:
time: 44.2 us; the launch traced here: 43.9 us
  Pallas kernels  27.6 us (62%)
  starting transfers between devices  11.3 us (26%)
  waiting for transfers between devices  4.62 us (10%)
    pallas_call x7, Pallas kernels, call(): pl.pallas_call(kernel, in_specs=[beside if at in close else there for at...  27.6 us
    all_to_all x2, starting transfers between devices, swap(): lax.all_to_all(value, axes, split_axis=0, concat_axis=0, axis_index_group...  7.31 us
    ppermute x1, starting transfers between devices, local(): lax.ppermute(packed, axes, [(at, at + 1) for at in range(devices - 1)])  3.95 us
    all_to_all x2, waiting for transfers between devices, swap(): lax.all_to_all(value, axes, split_axis=0, concat_axis=0, axis_index_group...  3.28 us
    ppermute x1, waiting for transfers between devices, local(): lax.ppermute(packed, axes, [(at, at + 1) for at in range(devices - 1)])  1.33 us
  transfers between devices with their start and end apart: 3, of which 2 were waited for; matrix products, arithmetic and copies ran while one was open for 0% of the time, Pallas kernels for 44%

profile of v20, /device:TPU:1, one launch (start us, length us, event | category | flops | bytes accessed | tf_op | source)
XLA Modules:
  0.0 43.9 jit_solution(3452592676648908673)
XLA Ops:
  0.0 0.0 copy-start.6
  0.0 1.3 %pack.1 = bf16[9,2,4608]{2,1,0:T(2,128)(2,1)S(1)} custom-call(bf16[128,4608]{1,0:T(8,128)(2,1)} %key_ref.5, bf16[128,4608]{1,0:T(8,128)(2,1)} %value_ref.5, bf16[128,4608]{1,0:T(8,128)(2,1)} %query_ref.3), custom_call_target="tpu_custom_call" | custom-call | tf_op jit(solution)/shard_map/pack/pallas_call | solution.py:566
  1.3 3.9 %collective-permute-start = (bf16[9,2,4608]{2,1,0:T(2,128)(2,1)S(1)}, bf16[9,2,4608]{2,1,0:T(2,128)(2,1)S(1)}, u32[]{:S(2)}, u32[]{:S(2)}) collective-permute-start(bf16[9,2,4608]{2,1,0:T(2,128)(2,1)S(1)} %pack.1), channel_id=1, source_target_pairs={{0,1},{1,2},{2,3},{3,4},{4,5},{5,6},{6,7},{7,8},{8,9},{9,10},{10,1... | collective-permute-start | bytes 497672 | tf_op jit(solution)/shard_map/ppermute | solution.py:585
  5.2 0.0 copy-done.3
  5.2 0.0 copy-done.2
  5.3 0.0 copy-done
  5.3 0.0 copy-done.6
  5.3 6.5 %signal.1 = (bf16[128,4608]{1,0:T(8,128)(2,1)S(1)}, bf16[128,4608]{1,0:T(8,128)(2,1)}, f32[9,2,8,512]{3,2,1,0:T(8,128)S(1)}, f32[16,4608]{1,0:T(8,128)S(1)}) custom-call(bf16[128,4608]{1,0:T(8,128)(2,1)S(1)} %copy-done.2, bf16[128,4608]{1,0:T(8,128)(2,1)S(1)} %copy-done.3, f32[3,7,288]{2,1,0:T(8,128)S(1)} %copy-done.6, f32[16,4608]{1,0:T(8,128)S(1)} %copy-done), custom_call_target="tpu_custom_call" | custom-call | flops 35389440 | bytes 5898240 | tf_op jit(solution)/shard_map/signal/pallas_call | solution.py:566
  11.8 1.3 %collective-permute-done.halo_ref = bf16[9,2,4608]{2,1,0:T(2,128)(2,1)S(1)} collective-permute-done((bf16[9,2,4608]{2,1,0:T(2,128)(2,1)S(1)}, bf16[9,2,4608]{2,1,0:T(2,128)(2,1)S(1)}, u32[]{:S(2)}, u32[]{:S(2)}) %collective-permute-start) | collective-permute-done | bytes 165920 | tf_op jit(solution)/shard_map/ppermute | solution.py:585
  13.1 1.4 %head.1 = (bf16[32,2,1152]{2,1,0:T(2,128)(2,1)}, bf16[16,4608]{1,0:T(8,128)(2,1)S(1)}, bf16[128,4608]{1,0:T(8,128)(2,1)}) custom-call(bf16[128,4608]{1,0:T(8,128)(2,1)S(1)} %copy-done.2, bf16[128,4608]{1,0:T(8,128)(2,1)S(1)} %copy-done.3, bf16[9,2,4608]{2,1,0:T(2,128)(2,1)S(1)} %collective-permute-done.halo_ref, ...), custom_call_target="tpu_custom_call", output_to_operand_aliasing={{2}: (7, {})} | custom-call | tf_op jit(solution)/shard_map/head/pallas_call | solution.py:566
  14.5 0.0 copy-done.5
  14.5 0.0 copy-start.4
  14.5 4.3 %all-to-all-start = ((bf16[32,2,1152]{2,1,0:T(2,128)(2,1)}), bf16[32,2,1152]{2,1,0:T(2,128)(2,1)S(1)}, u32[]{:S(2)}, u32[]{:S(2)}) async-start(bf16[32,2,1152]{2,1,0:T(2,128)(2,1)} %get-tuple-element.33), calls=%async_computation | async-start | bytes 294912 | tf_op jit(solution)/shard_map/all_to_all | solution.py:634
  18.9 0.0 copy-done.7
  18.9 0.2 sqrt_multiply_fusion.coef_ref
  19.1 0.0 copy-done.4
  19.1 4.5 %gate.1 = (bf16[128,4608]{1,0:T(8,128)(2,1)}, f32[128,4608]{1,0:T(8,128)}) custom-call(bf16[128,4608]{1,0:T(8,128)(2,1)S(1)} %copy-done.4, bf16[9,2,4608]{2,1,0:T(2,128)(2,1)} %copy-done.5, f32[3,7,288]{2,1,0:T(8,128)S(1)} %copy-done.6, bf16[128,4608]{1,0:T(8,128)(2,1)} %get-tuple-element.35.u_ref, bf16[16,4608]{1,0:T(8,128)(2,1)S(1)} %get-tuple-element.36.head_ref, ...), custom_call_target="tpu_custom_call" | custom-call | flops 16515072 | bytes 3538944 | tf_op jit(solution)/shard_map/gate/pallas_call | solution.py:566
  23.7 0.0 copy-start.1
  23.7 3.3 %all-to-all-done.piece_ref = bf16[32,2,1152]{2,1,0:T(2,128)(2,1)S(1)} async-done(((bf16[32,2,1152]{2,1,0:T(2,128)(2,1)}), bf16[32,2,1152]{2,1,0:T(2,128)(2,1)S(1)}, u32[]{:S(2)}, u32[]{:S(2)}) %all-to-all-start) | async-done | bytes 147488 | tf_op jit(solution)/shard_map/all_to_all | solution.py:634
  27.0 0.9 %prefix.1 = bf16[32,2,1152]{2,1,0:T(2,128)(2,1)} custom-call(bf16[32,2,1152]{2,1,0:T(2,128)(2,1)S(1)} %all-to-all-done.piece_ref, f32[16,4608]{1,0:T(8,128)S(1)} %copy-done, f32[16,4608]{1,0:T(8,128)S(1)} %sqrt_multiply_fusion.coef_ref), custom_call_target="tpu_custom_call" | custom-call | tf_op jit(solution)/shard_map/prefix/pallas_call | solution.py:566
  27.9 3.0 %all-to-all-start.1 = ((bf16[32,2,1152]{2,1,0:T(2,128)(2,1)}), bf16[32,2,1152]{2,1,0:T(2,128)(2,1)S(1)}, u32[]{:S(2)}, u32[]{:S(2)}) async-start(bf16[32,2,1152]{2,1,0:T(2,128)(2,1)} %prefix.1), calls=%async_computation.1 | async-start | bytes 294912 | tf_op jit(solution)/shard_map/all_to_all | solution.py:634
  30.8 8.3 %within.1 = (f32[128,4608]{1,0:T(8,128)}, f32[128,512]{1,0:T(8,128)S(1)}, bf16[128,512]{1,0:T(8,128)(2,1)S(1)}) custom-call(bf16[128,4608]{1,0:T(8,128)(2,1)S(1)} %copy-done.1, bf16[16,4608]{1,0:T(8,128)(2,1)S(1)} %get-tuple-element.36.head_ref, f32[16,4608]{1,0:T(8,128)S(1)} %copy-done, ...), custom_call_target="tpu_custom_call", output_to_operand_aliasing={{0}: (6, {})} | custom-call | flops 29491200 | bytes 4718592 | tf_op jit(solution)/shard_map/within/pallas_call | solution.py:566
  39.2 0.0 all-to-all-done.1.piece_ref
  39.2 4.7 %final.1 = bf16[128,4608]{1,0:T(8,128)(2,1)} custom-call(bf16[32,2,1152]{2,1,0:T(2,128)(2,1)S(1)} %all-to-all-done.1.piece_ref, f32[16,4608]{1,0:T(8,128)S(1)} %copy-done, f32[128,512]{1,0:T(8,128)S(1)} %get-tuple-element.48.y_last_ref, bf16[128,512]{1,0:T(8,128)(2,1)S(1)} %get-tuple-element.49.gate_last_ref, f32[128,4608]{1,0:T(8,128)} %get-tuple-element.50.y_ref, ...), custom_call_target="tpu_custom_call" | custom-call | flops 23592960 | bytes 5898240 | tf_op jit(solution)/shard_map/final/pallas_call | solution.py:566
  (9 shorter events, 0.0 us)
Async XLA Ops:
  0.0 5.2 %copy-start.3 = (bf16[128,4608]{1,0:T(8,128)(2,1)S(1)}, bf16[128,4608]{1,0:T(8,128)(2,1)}, u32[]{:S(2)}) copy-start(bf16[128,4608]{1,0:T(8,128)(2,1)} %value_ref.5) | copy-start | bytes 3538948
  0.0 5.2 %copy-start.2 = (bf16[128,4608]{1,0:T(8,128)(2,1)S(1)}, bf16[128,4608]{1,0:T(8,128)(2,1)}, u32[]{:S(2)}) copy-start(bf16[128,4608]{1,0:T(8,128)(2,1)} %key_ref.5) | copy-start | bytes 3538948
  0.0 5.3 %copy-start = (f32[16,4608]{1,0:T(8,128)S(1)}, f32[16,4608]{1,0:T(8,128)}, u32[]{:S(2)}) copy-start(f32[16,4608]{1,0:T(8,128)} %rate_ref.11) | copy-start | bytes 884740
  0.0 5.3 %copy-start.6 = (f32[3,7,288]{2,1,0:T(8,128)S(1)}, f32[3,7,288]{2,1,0:T(8,128)}, u32[]{:S(2)}) copy-start(f32[3,7,288]{2,1,0:T(8,128)} %feat_ref.3) | copy-start | bytes 72580
  1.3 11.8 %collective-permute-start = (bf16[9,2,4608]{2,1,0:T(2,128)(2,1)S(1)}, bf16[9,2,4608]{2,1,0:T(2,128)(2,1)S(1)}, u32[]{:S(2)}, u32[]{:S(2)}) collective-permute-start(bf16[9,2,4608]{2,1,0:T(2,128)(2,1)S(1)} %pack.1), channel_id=1, source_target_pairs={{0,1},{1,2},{2,3},{3,4},{4,5},{5,6},{6,7},{7,8},{8,9},{9,10},{10,1... | collective-permute-start | bytes 497672 | tf_op jit(solution)/shard_map/ppermute | solution.py:585
  13.1 1.4 %copy-start.5 = (bf16[9,2,4608]{2,1,0:T(2,128)(2,1)}, bf16[9,2,4608]{2,1,0:T(2,128)(2,1)S(1)}, u32[]{:S(2)}) copy-start(bf16[9,2,4608]{2,1,0:T(2,128)(2,1)S(1)} %collective-permute-done.halo_ref) | copy-start | bytes 497668
  13.1 5.8 %copy-start.7 = (f32[16,4608]{1,0:T(8,128)S(1)}, f32[16,4608]{1,0:T(8,128)}, u32[]{:S(2)}) copy-start(f32[16,4608]{1,0:T(8,128)} %param.12) | copy-start | bytes 884740
  13.1 6.0 %copy-start.8 = (f32[4608]{0:T(1024)S(1)}, f32[4608]{0:T(1024)}, u32[]{:S(2)}) copy-start(f32[4608]{0:T(1024)} %param.13) | copy-start | bytes 55300
  14.5 4.6 %copy-start.4 = (bf16[128,4608]{1,0:T(8,128)(2,1)S(1)}, bf16[128,4608]{1,0:T(8,128)(2,1)}, u32[]{:S(2)}) copy-start(bf16[128,4608]{1,0:T(8,128)(2,1)} %query_ref.3) | copy-start | bytes 3538948
  14.5 12.4 %all-to-all-start = ((bf16[32,2,1152]{2,1,0:T(2,128)(2,1)}), bf16[32,2,1152]{2,1,0:T(2,128)(2,1)S(1)}, u32[]{:S(2)}, u32[]{:S(2)}) async-start(bf16[32,2,1152]{2,1,0:T(2,128)(2,1)} %get-tuple-element.33), calls=%async_computation | async-start | bytes 294912 | tf_op jit(solution)/shard_map/all_to_all | solution.py:634
  23.7 7.2 %copy-start.1 = (bf16[128,4608]{1,0:T(8,128)(2,1)S(1)}, bf16[128,4608]{1,0:T(8,128)(2,1)}, u32[]{:S(2)}) copy-start(bf16[128,4608]{1,0:T(8,128)(2,1)} %get-tuple-element.35.u_ref) | copy-start | bytes 3538948
  27.9 11.3 %all-to-all-start.1 = ((bf16[32,2,1152]{2,1,0:T(2,128)(2,1)}), bf16[32,2,1152]{2,1,0:T(2,128)(2,1)S(1)}, u32[]{:S(2)}, u32[]{:S(2)}) async-start(bf16[32,2,1152]{2,1,0:T(2,128)(2,1)} %prefix.1), calls=%async_computation.1 | async-start | bytes 294912 | tf_op jit(solution)/shard_map/all_to_all | solution.py:634

commit v21 on v20

--- a/solution.py
+++ b/solution.py
@@ -613,7 +613,7 @@
     left, halo_late, rates_late, skip_late = lax.optimization_barrier((left, halo, rates, skip))
     coef = residues * jnp.sqrt(-jnp.expm1(-2.0 * rates_late) / modes)
     skip_row = skip_late[None, :]
-    stage = vmem((tokens // ROWS // 2 * ROWS * ROWS, LANES), f32)
+    stage = vmem((tokens // ROWS // 2 * ROWS * ROWS + ROWS, LANES), f32)
     local_shapes = [far((tokens, width), f32)]
     local_scratches = [whole_buf, stage, stage, dma((1, chunks))]
     early = chunks // 9

time: 44.2 us -> 44.2 us (level)
  no operation moved by 1% of the time
where the time goes in v21:
time: 44.2 us; the launch traced here: 43.9 us
  Pallas kernels  27.6 us (62%)
  starting transfers between devices  11.3 us (26%)
  waiting for transfers between devices  4.62 us (10%)
    pallas_call x7, Pallas kernels, call(): pl.pallas_call(kernel, in_specs=[beside if at in close else there for at...  27.6 us
    all_to_all x2, starting transfers between devices, swap(): lax.all_to_all(value, axes, split_axis=0, concat_axis=0, axis_index_group...  7.31 us
    ppermute x1, starting transfers between devices, local(): lax.ppermute(packed, axes, [(at, at + 1) for at in range(devices - 1)])  3.95 us
    all_to_all x2, waiting for transfers between devices, swap(): lax.all_to_all(value, axes, split_axis=0, concat_axis=0, axis_index_group...  3.28 us
    ppermute x1, waiting for transfers between devices, local(): lax.ppermute(packed, axes, [(at, at + 1) for at in range(devices - 1)])  1.33 us
  transfers between devices with their start and end apart: 3, of which 2 were waited for; matrix products, arithmetic and copies ran while one was open for 0% of the time, Pallas kernels for 44%

profile of v21, /device:TPU:1, one launch (start us, length us, event | category | flops | bytes accessed | tf_op | source)
XLA Modules:
  0.0 43.9 jit_solution(14944831755178671418)
XLA Ops:
  0.0 0.0 copy-start.6
  0.0 1.3 %pack.1 = bf16[9,2,4608]{2,1,0:T(2,128)(2,1)S(1)} custom-call(bf16[128,4608]{1,0:T(8,128)(2,1)} %key_ref.5, bf16[128,4608]{1,0:T(8,128)(2,1)} %value_ref.5, bf16[128,4608]{1,0:T(8,128)(2,1)} %query_ref.3), custom_call_target="tpu_custom_call" | custom-call | tf_op jit(solution)/shard_map/pack/pallas_call | solution.py:566
  1.3 3.9 %collective-permute-start = (bf16[9,2,4608]{2,1,0:T(2,128)(2,1)S(1)}, bf16[9,2,4608]{2,1,0:T(2,128)(2,1)S(1)}, u32[]{:S(2)}, u32[]{:S(2)}) collective-permute-start(bf16[9,2,4608]{2,1,0:T(2,128)(2,1)S(1)} %pack.1), channel_id=1, source_target_pairs={{0,1},{1,2},{2,3},{3,4},{4,5},{5,6},{6,7},{7,8},{8,9},{9,10},{10,1... | collective-permute-start | bytes 497672 | tf_op jit(solution)/shard_map/ppermute | solution.py:585
  5.2 0.0 copy-done.3
  5.2 0.0 copy-done.2
  5.3 0.0 copy-done
  5.3 0.0 copy-done.6
  5.3 6.5 %signal.1 = (bf16[128,4608]{1,0:T(8,128)(2,1)S(1)}, bf16[128,4608]{1,0:T(8,128)(2,1)}, f32[9,2,8,512]{3,2,1,0:T(8,128)S(1)}, f32[16,4608]{1,0:T(8,128)S(1)}) custom-call(bf16[128,4608]{1,0:T(8,128)(2,1)S(1)} %copy-done.2, bf16[128,4608]{1,0:T(8,128)(2,1)S(1)} %copy-done.3, f32[3,7,288]{2,1,0:T(8,128)S(1)} %copy-done.6, f32[16,4608]{1,0:T(8,128)S(1)} %copy-done), custom_call_target="tpu_custom_call" | custom-call | flops 35389440 | bytes 5898240 | tf_op jit(solution)/shard_map/signal/pallas_call | solution.py:566
  11.8 1.3 %collective-permute-done.halo_ref = bf16[9,2,4608]{2,1,0:T(2,128)(2,1)S(1)} collective-permute-done((bf16[9,2,4608]{2,1,0:T(2,128)(2,1)S(1)}, bf16[9,2,4608]{2,1,0:T(2,128)(2,1)S(1)}, u32[]{:S(2)}, u32[]{:S(2)}) %collective-permute-start) | collective-permute-done | bytes 165920 | tf_op jit(solution)/shard_map/ppermute | solution.py:585
  13.1 1.4 %head.1 = (bf16[32,2,1152]{2,1,0:T(2,128)(2,1)}, bf16[16,4608]{1,0:T(8,128)(2,1)S(1)}, bf16[128,4608]{1,0:T(8,128)(2,1)}) custom-call(bf16[128,4608]{1,0:T(8,128)(2,1)S(1)} %copy-done.2, bf16[128,4608]{1,0:T(8,128)(2,1)S(1)} %copy-done.3, bf16[9,2,4608]{2,1,0:T(2,128)(2,1)S(1)} %collective-permute-done.halo_ref, ...), custom_call_target="tpu_custom_call", output_to_operand_aliasing={{2}: (7, {})} | custom-call | tf_op jit(solution)/shard_map/head/pallas_call | solution.py:566
  14.5 0.0 copy-done.5
  14.5 0.0 copy-start.4
  14.5 4.3 %all-to-all-start = ((bf16[32,2,1152]{2,1,0:T(2,128)(2,1)}), bf16[32,2,1152]{2,1,0:T(2,128)(2,1)S(1)}, u32[]{:S(2)}, u32[]{:S(2)}) async-start(bf16[32,2,1152]{2,1,0:T(2,128)(2,1)} %get-tuple-element.33), calls=%async_computation | async-start | bytes 294912 | tf_op jit(solution)/shard_map/all_to_all | solution.py:634
  18.9 0.0 copy-done.7
  18.9 0.2 sqrt_multiply_fusion.coef_ref
  19.1 0.0 copy-done.4
  19.1 4.5 %gate.1 = (bf16[128,4608]{1,0:T(8,128)(2,1)}, f32[128,4608]{1,0:T(8,128)}) custom-call(bf16[128,4608]{1,0:T(8,128)(2,1)S(1)} %copy-done.4, bf16[9,2,4608]{2,1,0:T(2,128)(2,1)} %copy-done.5, f32[3,7,288]{2,1,0:T(8,128)S(1)} %copy-done.6, bf16[128,4608]{1,0:T(8,128)(2,1)} %get-tuple-element.35.u_ref, bf16[16,4608]{1,0:T(8,128)(2,1)S(1)} %get-tuple-element.36.head_ref, ...), custom_call_target="tpu_custom_call" | custom-call | flops 16515072 | bytes 3538944 | tf_op jit(solution)/shard_map/gate/pallas_call | solution.py:566
  23.7 0.0 copy-start.1
  23.7 3.3 %all-to-all-done.piece_ref = bf16[32,2,1152]{2,1,0:T(2,128)(2,1)S(1)} async-done(((bf16[32,2,1152]{2,1,0:T(2,128)(2,1)}), bf16[32,2,1152]{2,1,0:T(2,128)(2,1)S(1)}, u32[]{:S(2)}, u32[]{:S(2)}) %all-to-all-start) | async-done | bytes 147488 | tf_op jit(solution)/shard_map/all_to_all | solution.py:634
  27.0 0.9 %prefix.1 = bf16[32,2,1152]{2,1,0:T(2,128)(2,1)} custom-call(bf16[32,2,1152]{2,1,0:T(2,128)(2,1)S(1)} %all-to-all-done.piece_ref, f32[16,4608]{1,0:T(8,128)S(1)} %copy-done, f32[16,4608]{1,0:T(8,128)S(1)} %sqrt_multiply_fusion.coef_ref), custom_call_target="tpu_custom_call" | custom-call | tf_op jit(solution)/shard_map/prefix/pallas_call | solution.py:566
  27.9 3.0 %all-to-all-start.1 = ((bf16[32,2,1152]{2,1,0:T(2,128)(2,1)}), bf16[32,2,1152]{2,1,0:T(2,128)(2,1)S(1)}, u32[]{:S(2)}, u32[]{:S(2)}) async-start(bf16[32,2,1152]{2,1,0:T(2,128)(2,1)} %prefix.1), calls=%async_computation.1 | async-start | bytes 294912 | tf_op jit(solution)/shard_map/all_to_all | solution.py:634
  30.8 8.3 %within.1 = (f32[128,4608]{1,0:T(8,128)}, f32[128,512]{1,0:T(8,128)S(1)}, bf16[128,512]{1,0:T(8,128)(2,1)S(1)}) custom-call(bf16[128,4608]{1,0:T(8,128)(2,1)S(1)} %copy-done.1, bf16[16,4608]{1,0:T(8,128)(2,1)S(1)} %get-tuple-element.36.head_ref, f32[16,4608]{1,0:T(8,128)S(1)} %copy-done, ...), custom_call_target="tpu_custom_call", output_to_operand_aliasing={{0}: (6, {})} | custom-call | flops 29491200 | bytes 4718592 | tf_op jit(solution)/shard_map/within/pallas_call | solution.py:566
  39.2 0.0 all-to-all-done.1.piece_ref
  39.2 4.7 %final.1 = bf16[128,4608]{1,0:T(8,128)(2,1)} custom-call(bf16[32,2,1152]{2,1,0:T(2,128)(2,1)S(1)} %all-to-all-done.1.piece_ref, f32[16,4608]{1,0:T(8,128)S(1)} %copy-done, f32[128,512]{1,0:T(8,128)S(1)} %get-tuple-element.48.y_last_ref, bf16[128,512]{1,0:T(8,128)(2,1)S(1)} %get-tuple-element.49.gate_last_ref, f32[128,4608]{1,0:T(8,128)} %get-tuple-element.50.y_ref, ...), custom_call_target="tpu_custom_call" | custom-call | flops 23592960 | bytes 5898240 | tf_op jit(solution)/shard_map/final/pallas_call | solution.py:566
  (9 shorter events, 0.0 us)
Async XLA Ops:
  0.0 5.2 %copy-start.3 = (bf16[128,4608]{1,0:T(8,128)(2,1)S(1)}, bf16[128,4608]{1,0:T(8,128)(2,1)}, u32[]{:S(2)}) copy-start(bf16[128,4608]{1,0:T(8,128)(2,1)} %value_ref.5) | copy-start | bytes 3538948
  0.0 5.2 %copy-start.2 = (bf16[128,4608]{1,0:T(8,128)(2,1)S(1)}, bf16[128,4608]{1,0:T(8,128)(2,1)}, u32[]{:S(2)}) copy-start(bf16[128,4608]{1,0:T(8,128)(2,1)} %key_ref.5) | copy-start | bytes 3538948
  0.0 5.3 %copy-start = (f32[16,4608]{1,0:T(8,128)S(1)}, f32[16,4608]{1,0:T(8,128)}, u32[]{:S(2)}) copy-start(f32[16,4608]{1,0:T(8,128)} %rate_ref.11) | copy-start | bytes 884740
  0.0 5.3 %copy-start.6 = (f32[3,7,288]{2,1,0:T(8,128)S(1)}, f32[3,7,288]{2,1,0:T(8,128)}, u32[]{:S(2)}) copy-start(f32[3,7,288]{2,1,0:T(8,128)} %feat_ref.3) | copy-start | bytes 72580
  1.3 11.8 %collective-permute-start = (bf16[9,2,4608]{2,1,0:T(2,128)(2,1)S(1)}, bf16[9,2,4608]{2,1,0:T(2,128)(2,1)S(1)}, u32[]{:S(2)}, u32[]{:S(2)}) collective-permute-start(bf16[9,2,4608]{2,1,0:T(2,128)(2,1)S(1)} %pack.1), channel_id=1, source_target_pairs={{0,1},{1,2},{2,3},{3,4},{4,5},{5,6},{6,7},{7,8},{8,9},{9,10},{10,1... | collective-permute-start | bytes 497672 | tf_op jit(solution)/shard_map/ppermute | solution.py:585
  13.1 1.4 %copy-start.5 = (bf16[9,2,4608]{2,1,0:T(2,128)(2,1)}, bf16[9,2,4608]{2,1,0:T(2,128)(2,1)S(1)}, u32[]{:S(2)}) copy-start(bf16[9,2,4608]{2,1,0:T(2,128)(2,1)S(1)} %collective-permute-done.halo_ref) | copy-start | bytes 497668
  13.1 5.8 %copy-start.7 = (f32[16,4608]{1,0:T(8,128)S(1)}, f32[16,4608]{1,0:T(8,128)}, u32[]{:S(2)}) copy-start(f32[16,4608]{1,0:T(8,128)} %param.12) | copy-start | bytes 884740
  13.1 6.0 %copy-start.8 = (f32[4608]{0:T(1024)S(1)}, f32[4608]{0:T(1024)}, u32[]{:S(2)}) copy-start(f32[4608]{0:T(1024)} %param.13) | copy-start | bytes 55300
  14.5 4.6 %copy-start.4 = (bf16[128,4608]{1,0:T(8,128)(2,1)S(1)}, bf16[128,4608]{1,0:T(8,128)(2,1)}, u32[]{:S(2)}) copy-start(bf16[128,4608]{1,0:T(8,128)(2,1)} %query_ref.3) | copy-start | bytes 3538948
  14.5 12.4 %all-to-all-start = ((bf16[32,2,1152]{2,1,0:T(2,128)(2,1)}), bf16[32,2,1152]{2,1,0:T(2,128)(2,1)S(1)}, u32[]{:S(2)}, u32[]{:S(2)}) async-start(bf16[32,2,1152]{2,1,0:T(2,128)(2,1)} %get-tuple-element.33), calls=%async_computation | async-start | bytes 294912 | tf_op jit(solution)/shard_map/all_to_all | solution.py:634
  23.7 7.2 %copy-start.1 = (bf16[128,4608]{1,0:T(8,128)(2,1)S(1)}, bf16[128,4608]{1,0:T(8,128)(2,1)}, u32[]{:S(2)}) copy-start(bf16[128,4608]{1,0:T(8,128)(2,1)} %get-tuple-element.35.u_ref) | copy-start | bytes 3538948
  27.9 11.3 %all-to-all-start.1 = ((bf16[32,2,1152]{2,1,0:T(2,128)(2,1)}), bf16[32,2,1152]{2,1,0:T(2,128)(2,1)S(1)}, u32[]{:S(2)}, u32[]{:S(2)}) async-start(bf16[32,2,1152]{2,1,0:T(2,128)(2,1)} %prefix.1), calls=%async_computation.1 | async-start | bytes 294912 | tf_op jit(solution)/shard_map/all_to_all | solution.py:634

commit v22 on v21

--- a/solution.py
+++ b/solution.py
@@ -311,7 +311,6 @@
                 place = chunk * (lap // TILES) + number // TILES
                 taps = chunk_taps(wide_ref, place, member, number % TILES, reach + 1)
                 column = column_scr.at[number, member]
-                column[pl.ds(0, 2 * ROWS), :] = jnp.zeros((2 * ROWS, LANES), f32)
                 lay_halo(column, halo_ref, member, lanes)
                 source = (key_ref, value_ref)[member]
                 column[pl.ds(2 * ROWS, ROWS), :] = source[: 2 * ROWS, lanes].astype(f32)[:ROWS]
@@ -323,7 +322,7 @@
                 head = wide(token_scr[number, :1, :])
                 for row in range(1, reach):
                     head = decay * head + wide(token_scr[number, row : row + 1, :])
-                total = state_ref[group : group + ROWS, lanes] + power(decay, tokens - reach) * head
+                total = state_ref[group : group + ROWS, lanes] + jnp.exp(-float(tokens - reach) * rate_ref[group : group + ROWS, lanes]) * head
                 total_scr[group : group + ROWS, lanes] = total
             head_ref[:, lanes] = jnp.concatenate([u, jnp.zeros((ROWS, LANES), f32)], axis=0).astype(bf16)
         return 0

time: 44.2 us -> 44.2 us (level)
  no operation moved by 1% of the time
where the time goes in v22:
time: 44.2 us; the launch traced here: 43.8 us
  Pallas kernels  27.5 us (62%)
  starting transfers between devices  11.3 us (26%)
  waiting for transfers between devices  4.62 us (10%)
    pallas_call x7, Pallas kernels, call(): pl.pallas_call(kernel, in_specs=[beside if at in close else there for at...  27.5 us
    all_to_all x2, starting transfers between devices, swap(): lax.all_to_all(value, axes, split_axis=0, concat_axis=0, axis_index_group...  7.31 us
    ppermute x1, starting transfers between devices, local(): lax.ppermute(packed, axes, [(at, at + 1) for at in range(devices - 1)])  3.95 us
    all_to_all x2, waiting for transfers between devices, swap(): lax.all_to_all(value, axes, split_axis=0, concat_axis=0, axis_index_group...  3.28 us
    ppermute x1, waiting for transfers between devices, local(): lax.ppermute(packed, axes, [(at, at + 1) for at in range(devices - 1)])  1.33 us
  transfers between devices with their start and end apart: 3, of which 2 were waited for; matrix products, arithmetic and copies ran while one was open for 0% of the time, Pallas kernels for 44%

profile of v22, /device:TPU:1, one launch (start us, length us, event | category | flops | bytes accessed | tf_op | source)
XLA Modules:
  0.0 43.8 jit_solution(14969478862990098175)
XLA Ops:
  0.0 0.0 copy-start.6
  0.0 1.3 %pack.1 = bf16[9,2,4608]{2,1,0:T(2,128)(2,1)S(1)} custom-call(bf16[128,4608]{1,0:T(8,128)(2,1)} %key_ref.5, bf16[128,4608]{1,0:T(8,128)(2,1)} %value_ref.5, bf16[128,4608]{1,0:T(8,128)(2,1)} %query_ref.3), custom_call_target="tpu_custom_call" | custom-call | tf_op jit(solution)/shard_map/pack/pallas_call | solution.py:565
  1.3 3.9 %collective-permute-start = (bf16[9,2,4608]{2,1,0:T(2,128)(2,1)S(1)}, bf16[9,2,4608]{2,1,0:T(2,128)(2,1)S(1)}, u32[]{:S(2)}, u32[]{:S(2)}) collective-permute-start(bf16[9,2,4608]{2,1,0:T(2,128)(2,1)S(1)} %pack.1), channel_id=1, source_target_pairs={{0,1},{1,2},{2,3},{3,4},{4,5},{5,6},{6,7},{7,8},{8,9},{9,10},{10,1... | collective-permute-start | bytes 497672 | tf_op jit(solution)/shard_map/ppermute | solution.py:584
  5.2 0.0 copy-done.3
  5.2 0.0 copy-done.2
  5.3 0.0 copy-done
  5.3 0.0 copy-done.6
  5.3 6.5 %signal.1 = (bf16[128,4608]{1,0:T(8,128)(2,1)S(1)}, bf16[128,4608]{1,0:T(8,128)(2,1)}, f32[9,2,8,512]{3,2,1,0:T(8,128)S(1)}, f32[16,4608]{1,0:T(8,128)S(1)}) custom-call(bf16[128,4608]{1,0:T(8,128)(2,1)S(1)} %copy-done.2, bf16[128,4608]{1,0:T(8,128)(2,1)S(1)} %copy-done.3, f32[3,7,288]{2,1,0:T(8,128)S(1)} %copy-done.6, f32[16,4608]{1,0:T(8,128)S(1)} %copy-done), custom_call_target="tpu_custom_call" | custom-call | flops 35389440 | bytes 5898240 | tf_op jit(solution)/shard_map/signal/pallas_call | solution.py:565
  11.8 1.3 %collective-permute-done.halo_ref = bf16[9,2,4608]{2,1,0:T(2,128)(2,1)S(1)} collective-permute-done((bf16[9,2,4608]{2,1,0:T(2,128)(2,1)S(1)}, bf16[9,2,4608]{2,1,0:T(2,128)(2,1)S(1)}, u32[]{:S(2)}, u32[]{:S(2)}) %collective-permute-start) | collective-permute-done | bytes 165920 | tf_op jit(solution)/shard_map/ppermute | solution.py:584
  13.1 1.3 %head.1 = (bf16[32,2,1152]{2,1,0:T(2,128)(2,1)}, bf16[16,4608]{1,0:T(8,128)(2,1)S(1)}, bf16[128,4608]{1,0:T(8,128)(2,1)}) custom-call(bf16[128,4608]{1,0:T(8,128)(2,1)S(1)} %copy-done.2, bf16[128,4608]{1,0:T(8,128)(2,1)S(1)} %copy-done.3, bf16[9,2,4608]{2,1,0:T(2,128)(2,1)S(1)} %collective-permute-done.halo_ref, ...), custom_call_target="tpu_custom_call", output_to_operand_aliasing={{2}: (7, {})} | custom-call | tf_op jit(solution)/shard_map/head/pallas_call | solution.py:565
  14.5 0.0 copy-done.5
  14.5 0.0 copy-start.4
  14.5 4.3 %all-to-all-start = ((bf16[32,2,1152]{2,1,0:T(2,128)(2,1)}), bf16[32,2,1152]{2,1,0:T(2,128)(2,1)S(1)}, u32[]{:S(2)}, u32[]{:S(2)}) async-start(bf16[32,2,1152]{2,1,0:T(2,128)(2,1)} %get-tuple-element.33), calls=%async_computation | async-start | bytes 294912 | tf_op jit(solution)/shard_map/all_to_all | solution.py:633
  18.9 0.2 sqrt_multiply_fusion.coef_ref
  19.1 0.0 copy-done.4
  19.1 4.5 %gate.1 = (bf16[128,4608]{1,0:T(8,128)(2,1)}, f32[128,4608]{1,0:T(8,128)}) custom-call(bf16[128,4608]{1,0:T(8,128)(2,1)S(1)} %copy-done.4, bf16[9,2,4608]{2,1,0:T(2,128)(2,1)} %copy-done.5, f32[3,7,288]{2,1,0:T(8,128)S(1)} %copy-done.6, bf16[128,4608]{1,0:T(8,128)(2,1)} %get-tuple-element.35.u_ref, bf16[16,4608]{1,0:T(8,128)(2,1)S(1)} %get-tuple-element.36.head_ref, ...), custom_call_target="tpu_custom_call" | custom-call | flops 16515072 | bytes 3538944 | tf_op jit(solution)/shard_map/gate/pallas_call | solution.py:565
  23.6 0.0 copy-start.1
  23.6 3.3 %all-to-all-done.piece_ref = bf16[32,2,1152]{2,1,0:T(2,128)(2,1)S(1)} async-done(((bf16[32,2,1152]{2,1,0:T(2,128)(2,1)}), bf16[32,2,1152]{2,1,0:T(2,128)(2,1)S(1)}, u32[]{:S(2)}, u32[]{:S(2)}) %all-to-all-start) | async-done | bytes 147488 | tf_op jit(solution)/shard_map/all_to_all | solution.py:633
  26.9 0.9 %prefix.1 = bf16[32,2,1152]{2,1,0:T(2,128)(2,1)} custom-call(bf16[32,2,1152]{2,1,0:T(2,128)(2,1)S(1)} %all-to-all-done.piece_ref, f32[16,4608]{1,0:T(8,128)S(1)} %copy-done, f32[16,4608]{1,0:T(8,128)S(1)} %sqrt_multiply_fusion.coef_ref), custom_call_target="tpu_custom_call" | custom-call | tf_op jit(solution)/shard_map/prefix/pallas_call | solution.py:565
  27.8 3.0 %all-to-all-start.1 = ((bf16[32,2,1152]{2,1,0:T(2,128)(2,1)}), bf16[32,2,1152]{2,1,0:T(2,128)(2,1)S(1)}, u32[]{:S(2)}, u32[]{:S(2)}) async-start(bf16[32,2,1152]{2,1,0:T(2,128)(2,1)} %prefix.1), calls=%async_computation.1 | async-start | bytes 294912 | tf_op jit(solution)/shard_map/all_to_all | solution.py:633
  30.8 0.0 copy-done.1
  30.8 8.3 %within.1 = (f32[128,4608]{1,0:T(8,128)}, f32[128,512]{1,0:T(8,128)S(1)}, bf16[128,512]{1,0:T(8,128)(2,1)S(1)}) custom-call(bf16[128,4608]{1,0:T(8,128)(2,1)S(1)} %copy-done.1, bf16[16,4608]{1,0:T(8,128)(2,1)S(1)} %get-tuple-element.36.head_ref, f32[16,4608]{1,0:T(8,128)S(1)} %copy-done, ...), custom_call_target="tpu_custom_call", output_to_operand_aliasing={{0}: (6, {})} | custom-call | flops 29491200 | bytes 4718592 | tf_op jit(solution)/shard_map/within/pallas_call | solution.py:565
  39.1 0.0 all-to-all-done.1.piece_ref
  39.2 4.7 %final.1 = bf16[128,4608]{1,0:T(8,128)(2,1)} custom-call(bf16[32,2,1152]{2,1,0:T(2,128)(2,1)S(1)} %all-to-all-done.1.piece_ref, f32[16,4608]{1,0:T(8,128)S(1)} %copy-done, f32[128,512]{1,0:T(8,128)S(1)} %get-tuple-element.48.y_last_ref, bf16[128,512]{1,0:T(8,128)(2,1)S(1)} %get-tuple-element.49.gate_last_ref, f32[128,4608]{1,0:T(8,128)} %get-tuple-element.50.y_ref, ...), custom_call_target="tpu_custom_call" | custom-call | flops 23592960 | bytes 5898240 | tf_op jit(solution)/shard_map/final/pallas_call | solution.py:565
  (9 shorter events, 0.0 us)
Async XLA Ops:
  0.0 5.2 %copy-start.3 = (bf16[128,4608]{1,0:T(8,128)(2,1)S(1)}, bf16[128,4608]{1,0:T(8,128)(2,1)}, u32[]{:S(2)}) copy-start(bf16[128,4608]{1,0:T(8,128)(2,1)} %value_ref.5) | copy-start | bytes 3538948
  0.0 5.2 %copy-start.2 = (bf16[128,4608]{1,0:T(8,128)(2,1)S(1)}, bf16[128,4608]{1,0:T(8,128)(2,1)}, u32[]{:S(2)}) copy-start(bf16[128,4608]{1,0:T(8,128)(2,1)} %key_ref.5) | copy-start | bytes 3538948
  0.0 5.3 %copy-start = (f32[16,4608]{1,0:T(8,128)S(1)}, f32[16,4608]{1,0:T(8,128)}, u32[]{:S(2)}) copy-start(f32[16,4608]{1,0:T(8,128)} %rate_ref.11) | copy-start | bytes 884740
  0.0 5.3 %copy-start.6 = (f32[3,7,288]{2,1,0:T(8,128)S(1)}, f32[3,7,288]{2,1,0:T(8,128)}, u32[]{:S(2)}) copy-start(f32[3,7,288]{2,1,0:T(8,128)} %feat_ref.3) | copy-start | bytes 72580
  1.3 11.8 %collective-permute-start = (bf16[9,2,4608]{2,1,0:T(2,128)(2,1)S(1)}, bf16[9,2,4608]{2,1,0:T(2,128)(2,1)S(1)}, u32[]{:S(2)}, u32[]{:S(2)}) collective-permute-start(bf16[9,2,4608]{2,1,0:T(2,128)(2,1)S(1)} %pack.1), channel_id=1, source_target_pairs={{0,1},{1,2},{2,3},{3,4},{4,5},{5,6},{6,7},{7,8},{8,9},{9,10},{10,1... | collective-permute-start | bytes 497672 | tf_op jit(solution)/shard_map/ppermute | solution.py:584
  13.1 1.4 %copy-start.5 = (bf16[9,2,4608]{2,1,0:T(2,128)(2,1)}, bf16[9,2,4608]{2,1,0:T(2,128)(2,1)S(1)}, u32[]{:S(2)}) copy-start(bf16[9,2,4608]{2,1,0:T(2,128)(2,1)S(1)} %collective-permute-done.halo_ref) | copy-start | bytes 497668
  13.1 5.7 %copy-start.7 = (f32[16,4608]{1,0:T(8,128)S(1)}, f32[16,4608]{1,0:T(8,128)}, u32[]{:S(2)}) copy-start(f32[16,4608]{1,0:T(8,128)} %param.12) | copy-start | bytes 884740
  13.1 5.9 %copy-start.8 = (f32[4608]{0:T(1024)S(1)}, f32[4608]{0:T(1024)}, u32[]{:S(2)}) copy-start(f32[4608]{0:T(1024)} %param.13) | copy-start | bytes 55300
  14.5 4.6 %copy-start.4 = (bf16[128,4608]{1,0:T(8,128)(2,1)S(1)}, bf16[128,4608]{1,0:T(8,128)(2,1)}, u32[]{:S(2)}) copy-start(bf16[128,4608]{1,0:T(8,128)(2,1)} %query_ref.3) | copy-start | bytes 3538948
  14.5 12.4 %all-to-all-start = ((bf16[32,2,1152]{2,1,0:T(2,128)(2,1)}), bf16[32,2,1152]{2,1,0:T(2,128)(2,1)S(1)}, u32[]{:S(2)}, u32[]{:S(2)}) async-start(bf16[32,2,1152]{2,1,0:T(2,128)(2,1)} %get-tuple-element.33), calls=%async_computation | async-start | bytes 294912 | tf_op jit(solution)/shard_map/all_to_all | solution.py:633
  23.6 7.2 %copy-start.1 = (bf16[128,4608]{1,0:T(8,128)(2,1)S(1)}, bf16[128,4608]{1,0:T(8,128)(2,1)}, u32[]{:S(2)}) copy-start(bf16[128,4608]{1,0:T(8,128)(2,1)} %get-tuple-element.35.u_ref) | copy-start | bytes 3538948
  27.8 11.3 %all-to-all-start.1 = ((bf16[32,2,1152]{2,1,0:T(2,128)(2,1)}), bf16[32,2,1152]{2,1,0:T(2,128)(2,1)S(1)}, u32[]{:S(2)}, u32[]{:S(2)}) async-start(bf16[32,2,1152]{2,1,0:T(2,128)(2,1)} %prefix.1), calls=%async_computation.1 | async-start | bytes 294912 | tf_op jit(solution)/shard_map/all_to_all | solution.py:633
